TPU v7x, 32 devices: a whole 2x2x4 slice. The times are simulated.
32 devices in a mesh: space: 8 (over z, x), tm: 4 (over y, core).
Axes of the slice: x: 2, y: 2, z: 4, core: 2. Of those that a mesh axis runs over, the one named last changes fastest.
Arguments:
- snapshots: bfloat16 [81920, 2048], P('space', 'tm'), may hold values from -6 to 6
- modes: bfloat16 [81920, 256], P('space'), may hold values from -0.01953125 to 0.01953125
Outputs:
- gram: float32 [4864, 4864], P('tm', 'space')
- rhs: float32 [4864, 256], P('tm', 'space')
All inputs are finite; a program needn't handle non-finite values.
Results may differ from a plain program's by a relative error of at most 0.0057.
Values may be sent and summed in bfloat16 or wider, within the bound.
No kernel may reach another device: no remote copies, remote signals or barrier semaphores. Data moves between devices by JAX's collectives and lax.ppermute only.
A program may use at most 128 MiB of HBM per device.

v0:
```python
import jax
import jax.numpy as jnp
from jax import lax
from jax.sharding import PartitionSpec as P

LEAD_MODES = 48


ridge_weight = 0.05


def passed_along(value, axis, steps):
    count = lax.axis_size(axis)
    leading, last = (max(0, -steps), min(count, count - steps))
    return lax.ppermute(value, axis, [(source, source + steps) for source in range(leading, last)])


def build_features(current, first, second):
    steps_count = current.shape[1]
    lead = first.shape[0]
    head = current[0:lead].astype(jnp.float32)
    prod_one = (head[:, None, :] * first.astype(jnp.float32)[None, :, :]).reshape(
        lead * lead, steps_count
    )
    prod_two = (head[:, None, :] * second.astype(jnp.float32)[None, :, :]).reshape(
        lead * lead, steps_count
    )
    return jnp.concatenate([current.astype(jnp.float32), prod_one, prod_two], axis=0).astype(
        jnp.bfloat16
    )


def neighbour(values, offset):
    return passed_along(values, "tm", offset)


def contract_rows(left, right):
    return lax.dot_general(
        left, right, (((1,), (1,)), ((), ())), preferred_element_type=jnp.float32
    )


def per_device(snapshots, modes):
    partial_sums = lax.dot_general(
        modes, snapshots, (((0,), (0,)), ((), ())), preferred_element_type=jnp.float32
    )
    coeffs = lax.psum(partial_sums, "space").astype(jnp.bfloat16)
    n_space = lax.axis_size("space")
    n_time = lax.axis_size("tm")
    modes_count = coeffs.shape[0]
    snap_local = coeffs.shape[1]
    total_snaps = snap_local * n_time
    lead = LEAD_MODES
    feature_count = modes_count + 2 * lead * lead
    col_block = feature_count // n_space
    target_block = modes_count // n_space
    row_block = feature_count // n_time
    space_pos = lax.axis_index("space")
    time_pos = lax.axis_index("tm")
    moved = {}
    for offset in (1, 2, -1):
        moved[offset] = neighbour(coeffs, offset)
    phi = build_features(coeffs, moved[1][0:lead], moved[2][0:lead])
    target = moved[-1]
    right = jnp.concatenate(
        [
            lax.dynamic_slice_in_dim(phi, space_pos * col_block, col_block, 0),
            lax.dynamic_slice_in_dim(target, space_pos * target_block, target_block, 0),
        ],
        axis=0,
    )
    joined = lax.psum_scatter(contract_rows(phi, right), "tm", scatter_dimension=0, tiled=True)
    row_global = time_pos * row_block + jnp.arange(row_block, dtype=jnp.int32)
    col_global = space_pos * col_block + jnp.arange(col_block, dtype=jnp.int32)
    diagonal_mask = (row_global[:, None] == col_global[None, :]).astype(jnp.float32)
    gram = joined[:, 0:col_block] / total_snaps + ridge_weight * diagonal_mask
    rhs = joined[:, col_block:] / total_snaps
    return (gram, rhs)


def solution(mesh):
    in_specs = (P("space", "tm"), P("space", None))
    out_specs = (P("tm", "space"), P("tm", "space"))
    return jax.shard_map(
        per_device, mesh=mesh, in_specs=in_specs, out_specs=out_specs, check_vma=False
    )
```

profile of v0, /device:TPU:0, one launch (start us, length us, event | category | flops | bytes accessed | tf_op | source)
XLA Modules:
  0.0 192.0 jit_solution(6195599855826129198)
XLA Ops:
  7.2 0.0 reduce-scatter.2.cloned.1.call-start
  7.2 7.2 %fusion.6 = f32[256,512]{1,0:T(8,128)S(1)} fusion(bf16[10240,256]{1,0:T(8,128)(2,1)} %param.3, bf16[10240,512]{1,0:T(8,128)(2,1)} %param.2), kind=kOutput, calls=%fused_computation.18 | convolution fusion | flops 2684354560 | bytes 16252928 | tf_op jit(solution)/shard_map/dot_general | solution.py:44
  14.4 45.2 %all-reduce.1 = bf16[256,512]{1,0:T(8,128)(2,1)S(1)} all-reduce(f32[256,512]{1,0:T(8,128)S(1)} %fusion.6), channel_id=1, replica_groups=mesh['space'=8,'tm'=4] {'space'}, use_global_device_ids=true, to_apply=%region_0.0 | all-reduce | flops 131072 | bytes 786432 | tf_op jit(solution)/shard_map/psum | solution.py:47
  59.7 3.4 %collective-permute-start.1 = (bf16[256,512]{1,0:T(8,128)(2,1)S(1)}, bf16[256,512]{1,0:T(8,128)(2,1)S(1)}, u32[]{:S(2)}, u32[]{:S(2)}) collective-permute-start(bf16[256,512]{1,0:T(8,128)(2,1)S(1)} %all-reduce.1), channel_id=1, source_target_pairs={{0,2},{1,3},{4,6},{5,7},{8,10},{9,11},{12,14},{13,15},{16,18},{17,... | collective-permute-start | bytes 786440 | tf_op jit(solution)/shard_map/ppermute | solution.py:15
  63.1 1.3 collective-permute-start
  64.5 1.3 collective-permute-start.2
  65.8 3.3 %collective-permute-done.1 = bf16[256,512]{1,0:T(8,128)(2,1)S(1)} collective-permute-done((bf16[256,512]{1,0:T(8,128)(2,1)S(1)}, bf16[256,512]{1,0:T(8,128)(2,1)S(1)}, u32[]{:S(2)}, u32[]{:S(2)}) %collective-permute-start.1) | collective-permute-done | bytes 262176 | tf_op jit(solution)/shard_map/ppermute | solution.py:15
  69.1 0.0 collective-permute-done
  69.2 1.5 multiply_convert_fusion.1
  70.7 0.4 pad_maximum_fusion
  71.1 0.1 constant_dynamic-slice_fusion.1
  71.1 0.0 collective-permute-done.2
  71.1 10.5 %fusion.1 = f32[4864,640]{1,0:T(8,128)} fusion(bf16[32,512]{1,0:T(8,128)(2,1)S(1)} %constant_dynamic-slice_fusion, bf16[608,512]{1,0:T(8,128)(2,1)S(1)} %constant_dynamic-slice_fusion.1, bf16[2304,512]{1,0:T(8,128)(2,1)S(1)} %bitcast.7, bf16[2304,512]{1,0:T(8,128)(2,1)S(1)} %bitcast.5, bf16[256,512]{1,0:T(8,128)(2,1)S(1)} %all-reduce.1), kind=kOutput, calls=%fused_computation.5 | convolution fusion | flops 3203923968 | bytes 18087936 | tf_op jit(solution)/shard_map/dot_general | solution.py:38
  81.7 0.0 reduce-scatter.2.cloned.1.call-update
  81.7 97.2 %reduce-scatter.2.cloned.1.call-done = f32[1216,640]{1,0:T(8,128)} async-done(((f32[4864,640]{1,0:T(8,128)}), f32[1216,640]{1,0:T(8,128)}) %reduce-scatter.2.cloned.1.call-update) | async-done | bytes 3112976 | tf_op jit(solution)/shard_map/reduce_scatter | solution.py:72
  178.9 1.3 slice_multiply_fusion.1
  180.2 0.9 copy.4
  181.1 4.0 %fusion = f32[1216,608]{1,0:T(8,128)} fusion(f32[1216,640]{1,0:T(8,128)} %reduce-scatter.2.cloned.1.call-done, s32[608]{0:T(1024)S(1)} %iota_add_fusion.1, s32[1216]{0:T(1024)S(1)} %iota_add_fusion), kind=kLoop, calls=%fused_computation.4 | loop fusion | flops 2957312 | bytes 5921920 | tf_op jit(solution)/shard_map/add | solution.py:76
  (6 shorter events, 0.1 us)
Async XLA Ops:
  7.2 171.8 %reduce-scatter.2.cloned.1.call-start = ((), (), s32[]{:S(2)}) async-start(), calls=%async_computation.1 | async-start | bytes 15564800 | tf_op jit(solution)/shard_map/reduce_scatter | solution.py:72
  59.7 9.4 %collective-permute-start.1 = (bf16[256,512]{1,0:T(8,128)(2,1)S(1)}, bf16[256,512]{1,0:T(8,128)(2,1)S(1)}, u32[]{:S(2)}, u32[]{:S(2)}) collective-permute-start(bf16[256,512]{1,0:T(8,128)(2,1)S(1)} %all-reduce.1), channel_id=1, source_target_pairs={{0,2},{1,3},{4,6},{5,7},{8,10},{9,11},{12,14},{13,15},{16,18},{17,... | collective-permute-start | bytes 786440 | tf_op jit(solution)/shard_map/ppermute | solution.py:15
  63.1 6.0 %collective-permute-start = (bf16[256,512]{1,0:T(8,128)(2,1)S(1)}, bf16[256,512]{1,0:T(8,128)(2,1)S(1)}, u32[]{:S(2)}, u32[]{:S(2)}) collective-permute-start(bf16[256,512]{1,0:T(8,128)(2,1)S(1)} %all-reduce.1), channel_id=1, source_target_pairs={{0,1},{1,2},{2,3},{4,5},{5,6},{6,7},{8,9},{9,10},{10,11},{12,13},{... | collective-permute-start | bytes 786440 | tf_op jit(solution)/shard_map/ppermute | solution.py:15
  64.5 6.7 %collective-permute-start.2 = (bf16[256,512]{1,0:T(8,128)(2,1)S(1)}, bf16[256,512]{1,0:T(8,128)(2,1)S(1)}, u32[]{:S(2)}, u32[]{:S(2)}) collective-permute-start(bf16[256,512]{1,0:T(8,128)(2,1)S(1)} %all-reduce.1), channel_id=1, source_target_pairs={{1,0},{2,1},{3,2},{5,4},{6,5},{7,6},{9,8},{10,9},{11,10},{13,12},{... | collective-permute-start | bytes 786440 | tf_op jit(solution)/shard_map/ppermute | solution.py:15
Sparse Core Ops, SparseCore 0:
  81.8 97.0 reduce-scatter.1
where the time goes:
time: 192 us
  waiting for transfers between devices  101 us (53%)
  blocking collectives  45.2 us (24%)
  matrix products  17.7 us (9%)
  between operations  14.2 us (7%)
  other arithmetic  7.22 us (4%)
  starting transfers between devices  6.07 us (3%)
    reduce_scatter x1, waiting for transfers between devices, per_device(): lax.psum_scatter(contract_rows(phi, right), 'tm', scatter_dimension=0, ti...  97.2 us
    psum x1, blocking collectives, per_device(): coeffs = lax.psum(partial_sums, 'space').astype(jnp.bfloat16)  45.2 us
    dot_general x1, matrix products, contract_rows(): lax.dot_general(left, right, (((1,), (1,)), ((), ())), preferred_element_...  10.5 us
    dot_general x1, matrix products, per_device(): lax.dot_general(modes, snapshots, (((0,), (0,)), ((), ())), preferred_ele...  7.22 us
    ppermute x3, starting transfers between devices, passed_along(): lax.ppermute(value, axis, [(source, source + steps) for source in range(l...  6.03 us
    add x1, other arithmetic, per_device(): gram = joined[:, 0:col_block] / total_snaps + ridge_weight * diagonal_mask  4 us
  transfers between devices with their start and end apart: 4, of which 2 were waited for; matrix products, arithmetic and copies ran while one was open for 1% of the time, Pallas kernels for 0%

commit v1 on v0

v1 whole, which is shorter than its diff:
```python
import functools

import jax
import jax.numpy as jnp
from jax import lax
from jax.experimental import pallas as pl
from jax.experimental.pallas import tpu as pltpu
from jax.sharding import PartitionSpec as P

LEAD_MODES = 48
RIDGE_WEIGHT = 0.05
ROW_TILE = 16


def swap(value, axis, bit):
    count = lax.axis_size(axis)
    return lax.ppermute(value, axis, [(i, i ^ bit) for i in range(count)])


def bits_of(count):
    return [1 << k for k in range(count.bit_length() - 1)]


def gram_kernel(
    sizes, pos_ref, lead_ref, rest_ref, gram_ref, rhs_ref, delayed, head, rows, cols, side
):
    n_time, snaps, modes, row_block, col_block, target_block = sizes
    total = n_time * snaps
    time_pos, space_pos = pos_ref[0], pos_ref[1]

    def slot(block):
        return jnp.bitwise_xor(time_pos, block)

    def window(block):
        return pl.ds(block * snaps, snaps)

    nothing = jnp.zeros((LEAD_MODES, snaps), jnp.bfloat16)
    for block in range(n_time):
        current = lead_ref[slot(block)]
        head[:, window(block)] = current.astype(jnp.float32)
        for delay in (1, 2):
            if block + delay < n_time:
                delayed[delay - 1, :, window(block + delay)] = current
            if block < delay:
                delayed[delay - 1, :, window(block)] = nothing

    def fill(out, start, extent):
        @pl.when(start == 0)
        def _():
            for block in range(n_time):
                out[pl.ds(LEAD_MODES, LEAD_MODES), window(block)] = lead_ref[slot(block)]
                out[pl.ds(2 * LEAD_MODES, modes - LEAD_MODES), window(block)] = rest_ref[
                    slot(block)
                ]

        def group(q, carry):
            kind, i = lax.div(q, LEAD_MODES), lax.rem(q, LEAD_MODES)
            at = modes + LEAD_MODES * q - start + LEAD_MODES
            factor = jnp.broadcast_to(head[pl.ds(i, 1), :], (ROW_TILE, total)).astype(
                jnp.bfloat16
            )
            for j in range(0, LEAD_MODES, ROW_TILE):
                out[pl.ds(pl.multiple_of(at + j, ROW_TILE), ROW_TILE), :] = (
                    factor * delayed[kind, j : j + ROW_TILE, :]
                )
            return carry

        first = jnp.maximum(0, lax.div(start - modes, LEAD_MODES))
        last = lax.div(start + extent - modes + LEAD_MODES - 1, LEAD_MODES)
        lax.fori_loop(first, last, group, 0)

    fill(cols, space_pos * col_block, col_block)
    fill(rows, time_pos * row_block, row_block)
    wanted = space_pos * target_block
    for block in range(n_time):
        for j in range(0, target_block, ROW_TILE):
            out = cols.at[pl.ds(LEAD_MODES + col_block + j, ROW_TILE), window(block)]
            if block + 1 < n_time:
                mode = wanted + j

                @pl.when(mode < LEAD_MODES)
                def _():
                    out[...] = lead_ref[
                        slot(block + 1), pl.ds(pl.multiple_of(mode, ROW_TILE), ROW_TILE), :
                    ]

                @pl.when(mode >= LEAD_MODES)
                def _():
                    out[...] = rest_ref[
                        slot(block + 1),
                        pl.ds(pl.multiple_of(mode - LEAD_MODES, ROW_TILE), ROW_TILE),
                        :,
                    ]
            else:
                out[...] = jnp.zeros((ROW_TILE, snaps), jnp.bfloat16)

    tile = row_block // 4 if row_block % (4 * ROW_TILE) == 0 else row_block

    def multiply(step, carry):
        top = pl.multiple_of(step * tile, ROW_TILE)
        product = (
            lax.dot_general(
                rows[pl.ds(LEAD_MODES + top, tile), :],
                cols[pl.ds(LEAD_MODES, col_block + target_block), :],
                (((1,), (1,)), ((), ())),
                preferred_element_type=jnp.float32,
            )
            / total
        )
        shape = (tile, col_block)
        row = time_pos * row_block + top + lax.broadcasted_iota(jnp.int32, shape, 0)
        column = space_pos * col_block + lax.broadcasted_iota(jnp.int32, shape, 1)
        gram_ref[pl.ds(top, tile), :] = product[:, 0:col_block] + jnp.where(
            row == column, RIDGE_WEIGHT, 0.0
        )
        side[pl.ds(top, tile), :] = product[:, col_block:]
        return carry

    lax.fori_loop(0, row_block // tile, multiply, 0)
    rhs_ref[...] = side[...].T


def gram_blocks(lead, rest, n_space):
    n_time, _, snaps = lead.shape
    modes = LEAD_MODES + rest.shape[1]
    features = modes + 2 * LEAD_MODES * LEAD_MODES
    row_block, col_block, target_block = features // n_time, features // n_space, modes // n_space
    total = n_time * snaps
    here = jnp.stack([lax.axis_index("tm"), lax.axis_index("space")]).astype(jnp.int32)
    vmem = pl.BlockSpec(memory_space=pltpu.VMEM)
    gram, rhs = pl.pallas_call(
        functools.partial(
            gram_kernel, (n_time, snaps, modes, row_block, col_block, target_block)
        ),
        out_shape=(
            jax.ShapeDtypeStruct((row_block, col_block), jnp.float32),
            jax.ShapeDtypeStruct((target_block, row_block), jnp.float32),
        ),
        in_specs=[pl.BlockSpec(memory_space=pltpu.SMEM), vmem, vmem],
        out_specs=(vmem, vmem),
        scratch_shapes=[
            pltpu.VMEM((2, LEAD_MODES, total), jnp.bfloat16),
            pltpu.VMEM((LEAD_MODES, total), jnp.float32),
            pltpu.VMEM((row_block + 2 * LEAD_MODES, total), jnp.bfloat16),
            pltpu.VMEM((col_block + 2 * LEAD_MODES + target_block, total), jnp.bfloat16),
            pltpu.VMEM((row_block, target_block), jnp.float32),
        ],
        compiler_params=pltpu.CompilerParams(vmem_limit_bytes=56 * 2**20),
    )(here, lead, rest)
    return gram, rhs.T


def per_device(snapshots, modes):
    n_space, n_time = lax.axis_size("space"), lax.axis_size("tm")
    partial_sums = lax.dot_general(
        modes, snapshots, (((0,), (0,)), ((), ())), preferred_element_type=jnp.float32
    )
    lead = partial_sums[0:LEAD_MODES]
    rest = partial_sums[LEAD_MODES:].astype(jnp.bfloat16)
    for bit in bits_of(n_space):
        lead = lead + swap(lead, "space", bit)
        arrived = swap(rest, "space", bit)
        rest = (rest.astype(jnp.float32) + arrived.astype(jnp.float32)).astype(jnp.bfloat16)
    lead = lead.astype(jnp.bfloat16)[None]
    rest = rest[None]
    for bit in reversed(bits_of(n_time)):
        lead = jnp.stack([lead, swap(lead, "tm", bit)], axis=1)
        lead = lead.reshape((-1,) + lead.shape[2:])
        rest = jnp.stack([rest, swap(rest, "tm", bit)], axis=1)
        rest = rest.reshape((-1,) + rest.shape[2:])
    return gram_blocks(lead, rest, n_space)


def solution(mesh):
    in_specs = (P("space", "tm"), P("space", None))
    out_specs = (P("tm", "space"), P("tm", "space"))
    return jax.shard_map(
        per_device, mesh=mesh, in_specs=in_specs, out_specs=out_specs, check_vma=False
    )
```

time: 192 us -> 55.2 us (0.29)
  waiting for transfers between devices: 101 us -> 19.9 us
  blocking collectives: 45.2 us -> 0 us
  between operations: 14.2 us -> 0.71 us
  matrix products: 17.7 us -> 7.22 us
  starting transfers between devices: 6.07 us -> 15.3 us
  Pallas kernels: 0 us -> 9.21 us
  other arithmetic: 7.22 us -> 0.98 us
    reduce_scatter x1 -> x0, waiting for transfers between devices: 97.2 us -> none  [per_device(): lax.psum_scatter(contract_rows(phi, right), 'tm', scatter_dimension=0, ti...]
    psum x1 -> x0, blocking collectives: 45.2 us -> none  [per_device(): coeffs = lax.psum(partial_sums, 'space').astype(jnp.bfloat16)]
    ppermute x3 -> x10, waiting for transfers between devices: 3.34 us -> 19.9 us  [swap(): return lax.ppermute(value, axis, [(i, i ^ bit) for i in range(count)])]
    dot_general x1 -> x0, matrix products: 10.5 us -> none  [contract_rows(): lax.dot_general(left, right, (((1,), (1,)), ((), ())), preferred_element_...]
    ppermute x3 -> x10, starting transfers between devices: 6.03 us -> 15.3 us  [swap(): return lax.ppermute(value, axis, [(i, i ^ bit) for i in range(count)])]
    pallas_call x0 -> x1, Pallas kernels: none -> 9.21 us  [gram_blocks(): pl.pallas_call(functools.partial(gram_kernel, (n_time, snaps, modes, row_...]
    add x3 -> x2, other arithmetic: 4.01 us -> 0.03 us  [per_device(): lead = lead + swap(lead, 'space', bit)]
  transfers between devices with their start and end apart: 4 -> 10, of which waited for: 2 -> 7; matrix products, arithmetic and copies ran while one was open for 1% -> 3% of each run, Pallas kernels for 0% -> 0%
where the time goes in v1:
time: 55.2 us; the launch traced here: 55 us
  waiting for transfers between devices  19.9 us (36%)
  starting transfers between devices  15.3 us (28%)
  Pallas kernels  9.21 us (17%)
  matrix products  7.22 us (13%)
  local copies, waits for them, and re-layouts  1.72 us (3%)
  other arithmetic  0.98 us (2%)
  between operations  0.71 us (1%)
    ppermute x10, waiting for transfers between devices, swap(): return lax.ppermute(value, axis, [(i, i ^ bit) for i in range(count)])  19.9 us
    ppermute x10, starting transfers between devices, swap(): return lax.ppermute(value, axis, [(i, i ^ bit) for i in range(count)])  15.3 us
    pallas_call x1, Pallas kernels, gram_blocks(): pl.pallas_call(functools.partial(gram_kernel, (n_time, snaps, modes, row_...  9.21 us
    dot_general x1, matrix products, per_device(): lax.dot_general(modes, snapshots, (((0,), (0,)), ((), ())), preferred_ele...  7.22 us
  transfers between devices with their start and end apart: 10, of which 7 were waited for; matrix products, arithmetic and copies ran while one was open for 3% of the time, Pallas kernels for 0%

profile of v1, /device:TPU:0, one launch (start us, length us, event | category | flops | bytes accessed | tf_op | source)
XLA Modules:
  0.0 55.0 jit_solution(1856591410652368234)
XLA Ops:
  0.6 7.2 %fusion.6 = f32[256,512]{1,0:T(8,128)S(1)} fusion(bf16[10240,256]{1,0:T(8,128)(2,1)} %param.3, bf16[10240,512]{1,0:T(8,128)(2,1)} %param.2), kind=kOutput, calls=%fused_computation.17 | convolution fusion | flops 2684354560 | bytes 16252928 | tf_op jit(solution)/shard_map/dot_general | solution.py:155
  7.9 3.0 %collective-permute-start.5 = (bf16[208,512]{1,0:T(8,128)(2,1)S(1)}, bf16[208,512]{1,0:T(8,128)(2,1)S(1)}, u32[]{:S(2)}, u32[]{:S(2)}) collective-permute-start(bf16[208,512]{1,0:T(8,128)(2,1)S(1)} %slice.13), channel_id=1, source_target_pairs={{0,4},{4,0},{8,12},{12,8},{16,20},{20,16},{24,28},{28,24},{1,5},{5... | collective-permute-start | bytes 638984 | tf_op jit(solution)/shard_map/ppermute | solution.py:17
  10.9 5.2 %collective-permute-done.5 = bf16[208,512]{1,0:T(8,128)(2,1)S(1)} collective-permute-done((bf16[208,512]{1,0:T(8,128)(2,1)S(1)}, bf16[208,512]{1,0:T(8,128)(2,1)S(1)}, u32[]{:S(2)}, u32[]{:S(2)}) %collective-permute-start.5) | collective-permute-done | bytes 213024 | tf_op jit(solution)/shard_map/ppermute | solution.py:17
  16.1 0.1 add_convert_fusion.2
  16.2 1.9 %collective-permute-start.6 = (bf16[208,512]{1,0:T(8,128)(2,1)S(1)}, bf16[208,512]{1,0:T(8,128)(2,1)S(1)}, u32[]{:S(2)}, u32[]{:S(2)}) collective-permute-start(bf16[208,512]{1,0:T(8,128)(2,1)S(1)} %add_convert_fusion.2), channel_id=1, source_target_pairs={{0,8},{4,12},{8,0},{12,4},{16,24},{20,28},{24,16},{28,20},{1,9},{5... | collective-permute-start | bytes 638984 | tf_op jit(solution)/shard_map/ppermute | solution.py:17
  18.1 1.5 %collective-permute-start = (f32[48,512]{1,0:T(8,128)S(1)}, f32[48,512]{1,0:T(8,128)S(1)}, u32[]{:S(2)}, u32[]{:S(2)}) collective-permute-start(f32[48,512]{1,0:T(8,128)S(1)} %slice.9), channel_id=1, source_target_pairs={{0,4},{4,0},{8,12},{12,8},{16,20},{20,16},{24,28},{28,24},{1,5},{5... | collective-permute-start | bytes 294920 | tf_op jit(solution)/shard_map/ppermute | solution.py:17
  19.7 3.0 %collective-permute-done.6 = bf16[208,512]{1,0:T(8,128)(2,1)S(1)} collective-permute-done((bf16[208,512]{1,0:T(8,128)(2,1)S(1)}, bf16[208,512]{1,0:T(8,128)(2,1)S(1)}, u32[]{:S(2)}, u32[]{:S(2)}) %collective-permute-start.6) | collective-permute-done | bytes 213024 | tf_op jit(solution)/shard_map/ppermute | solution.py:17
  22.7 0.1 add_convert_fusion.1
  22.8 2.6 %collective-permute-start.7 = (bf16[208,512]{1,0:T(8,128)(2,1)S(1)}, bf16[208,512]{1,0:T(8,128)(2,1)S(1)}, u32[]{:S(2)}, u32[]{:S(2)}) collective-permute-start(bf16[208,512]{1,0:T(8,128)(2,1)S(1)} %add_convert_fusion.1), channel_id=1, source_target_pairs={{0,16},{4,20},{8,24},{12,28},{16,0},{20,4},{24,8},{28,12},{1,17},{... | collective-permute-start | bytes 638984 | tf_op jit(solution)/shard_map/ppermute | solution.py:17
  25.4 0.0 collective-permute-done
  25.4 1.6 %collective-permute-start.1 = (f32[48,512]{1,0:T(8,128)S(1)}, f32[48,512]{1,0:T(8,128)S(1)}, u32[]{:S(2)}, u32[]{:S(2)}) collective-permute-start(f32[48,512]{1,0:T(8,128)S(1)} %slice_add_fusion), channel_id=1, source_target_pairs={{0,8},{4,12},{8,0},{12,4},{16,24},{20,28},{24,16},{28,20},{1,9},{5... | collective-permute-start | bytes 294920 | tf_op jit(solution)/shard_map/ppermute | solution.py:17
  27.0 3.8 %collective-permute-done.1 = f32[48,512]{1,0:T(8,128)S(1)} collective-permute-done((f32[48,512]{1,0:T(8,128)S(1)}, f32[48,512]{1,0:T(8,128)S(1)}, u32[]{:S(2)}, u32[]{:S(2)}) %collective-permute-start.1) | collective-permute-done | bytes 98336 | tf_op jit(solution)/shard_map/ppermute | solution.py:17
  30.8 1.9 %collective-permute-start.2 = (f32[48,512]{1,0:T(8,128)S(1)}, f32[48,512]{1,0:T(8,128)S(1)}, u32[]{:S(2)}, u32[]{:S(2)}) collective-permute-start(f32[48,512]{1,0:T(8,128)S(1)} %add.19), channel_id=1, source_target_pairs={{0,16},{4,20},{8,24},{12,28},{16,0},{20,4},{24,8},{28,12},{1,17},{... | collective-permute-start | bytes 294920 | tf_op jit(solution)/shard_map/ppermute | solution.py:17
  32.7 2.9 %collective-permute-done.7 = bf16[208,512]{1,0:T(8,128)(2,1)S(1)} collective-permute-done((bf16[208,512]{1,0:T(8,128)(2,1)S(1)}, bf16[208,512]{1,0:T(8,128)(2,1)S(1)}, u32[]{:S(2)}, u32[]{:S(2)}) %collective-permute-start.7) | collective-permute-done | bytes 213024 | tf_op jit(solution)/shard_map/ppermute | solution.py:17
  35.7 0.1 fusion.3
  35.7 1.5 %collective-permute-start.8 = (bf16[1,208,512]{2,1,0:T(8,128)(2,1)S(1)}, bf16[1,208,512]{2,1,0:T(8,128)(2,1)S(1)}, u32[]{:S(2)}, u32[]{:S(2)}) collective-permute-start(bf16[1,208,512]{2,1,0:T(8,128)(2,1)S(1)} %get-tuple-element.9), channel_id=1, source_target_pairs={{0,2},{1,3},{2,0},{3,1},{4,6},{5,7},{6,4},{7,5},{8,10},{9,11},{10,... | collective-permute-start | bytes 638984 | tf_op jit(solution)/shard_map/ppermute | solution.py:17
  37.2 0.0 collective-permute-done.2
  37.2 1.0 %collective-permute-start.3 = (bf16[1,48,512]{2,1,0:T(8,128)(2,1)S(1)}, bf16[1,48,512]{2,1,0:T(8,128)(2,1)S(1)}, u32[]{:S(2)}, u32[]{:S(2)}) collective-permute-start(bf16[1,48,512]{2,1,0:T(8,128)(2,1)S(1)} %fusion.10), channel_id=1, source_target_pairs={{0,2},{1,3},{2,0},{3,1},{4,6},{5,7},{6,4},{7,5},{8,10},{9,11},{10,... | collective-permute-start | bytes 147464 | tf_op jit(solution)/shard_map/ppermute | solution.py:17
  38.2 3.8 %collective-permute-done.8 = bf16[1,208,512]{2,1,0:T(8,128)(2,1)S(1)} collective-permute-done((bf16[1,208,512]{2,1,0:T(8,128)(2,1)S(1)}, bf16[1,208,512]{2,1,0:T(8,128)(2,1)S(1)}, u32[]{:S(2)}, u32[]{:S(2)}) %collective-permute-start.8) | collective-permute-done | bytes 213024 | tf_op jit(solution)/shard_map/ppermute | solution.py:17
  42.0 0.1 fusion.1
  42.0 0.1 collective-permute-start.9
  42.1 0.4 collective-permute-done.3
  42.5 0.2 collective-permute-start.4
  42.7 0.6 %pad_add_fusion.pos_ref = s32[2]{0:T(128)} fusion(s32[1]{0:T(128)} %bitcast.1, s32[1]{0:T(128)} %bitcast), kind=kLoop, calls=%fused_computation.15 | loop fusion | flops 2 | bytes 16 | tf_op jit(solution)/shard_map/stack | solution.py:129
  43.3 0.7 %collective-permute-done.4 = bf16[2,48,512]{2,1,0:T(8,128)(2,1)S(1)} collective-permute-done((bf16[2,48,512]{2,1,0:T(8,128)(2,1)S(1)}, bf16[2,48,512]{2,1,0:T(8,128)(2,1)S(1)}, u32[]{:S(2)}, u32[]{:S(2)}) %collective-permute-start.4) | collective-permute-done | bytes 98336 | tf_op jit(solution)/shard_map/ppermute | solution.py:17
  44.0 0.7 %copy.4 = bf16[2,2,48,512]{3,2,1,0:T(8,128)(2,1)} copy(bf16[2,2,48,512]{3,2,0,1:T(8,128)(2,1)S(1)} %pad_maximum_fusion.2) | data formatting | bytes 393216 | tf_op jit(solution)/shard_map/stack | solution.py:167
  44.7 0.0 collective-permute-done.9
  44.7 0.1 pad_maximum_fusion
  44.8 1.0 %copy.5 = bf16[2,2,208,512]{3,2,1,0:T(8,128)(2,1)} copy(bf16[2,2,208,512]{3,2,0,1:T(8,128)(2,1)S(1)} %pad_maximum_fusion) | data formatting | bytes 1703936 | tf_op jit(solution)/shard_map/stack | solution.py:169
  45.8 9.2 %shard_map.41 = (f32[1216,608]{1,0:T(8,128)}, f32[32,1216]{1,0:T(8,128)}) custom-call(s32[2]{0:T(128)} %pad_add_fusion.pos_ref, bf16[4,48,512]{2,1,0:T(8,128)(2,1)} %bitcast.28, bf16[4,208,512]{2,1,0:T(8,128)(2,1)} %bitcast.27), custom_call_target="tpu_custom_call" | custom-call | tf_op jit(solution)/shard_map/pallas_call | solution.py:131
  (8 shorter events, 0.1 us)
Async XLA Ops:
  7.9 8.3 %collective-permute-start.5 = (bf16[208,512]{1,0:T(8,128)(2,1)S(1)}, bf16[208,512]{1,0:T(8,128)(2,1)S(1)}, u32[]{:S(2)}, u32[]{:S(2)}) collective-permute-start(bf16[208,512]{1,0:T(8,128)(2,1)S(1)} %slice.13), channel_id=1, source_target_pairs={{0,4},{4,0},{8,12},{12,8},{16,20},{20,16},{24,28},{28,24},{1,5},{5... | collective-permute-start | bytes 638984 | tf_op jit(solution)/shard_map/ppermute | solution.py:17
  16.2 6.5 %collective-permute-start.6 = (bf16[208,512]{1,0:T(8,128)(2,1)S(1)}, bf16[208,512]{1,0:T(8,128)(2,1)S(1)}, u32[]{:S(2)}, u32[]{:S(2)}) collective-permute-start(bf16[208,512]{1,0:T(8,128)(2,1)S(1)} %add_convert_fusion.2), channel_id=1, source_target_pairs={{0,8},{4,12},{8,0},{12,4},{16,24},{20,28},{24,16},{28,20},{1,9},{5... | collective-permute-start | bytes 638984 | tf_op jit(solution)/shard_map/ppermute | solution.py:17
  18.1 7.2 %collective-permute-start = (f32[48,512]{1,0:T(8,128)S(1)}, f32[48,512]{1,0:T(8,128)S(1)}, u32[]{:S(2)}, u32[]{:S(2)}) collective-permute-start(f32[48,512]{1,0:T(8,128)S(1)} %slice.9), channel_id=1, source_target_pairs={{0,4},{4,0},{8,12},{12,8},{16,20},{20,16},{24,28},{28,24},{1,5},{5... | collective-permute-start | bytes 294920 | tf_op jit(solution)/shard_map/ppermute | solution.py:17
  22.8 12.9 %collective-permute-start.7 = (bf16[208,512]{1,0:T(8,128)(2,1)S(1)}, bf16[208,512]{1,0:T(8,128)(2,1)S(1)}, u32[]{:S(2)}, u32[]{:S(2)}) collective-permute-start(bf16[208,512]{1,0:T(8,128)(2,1)S(1)} %add_convert_fusion.1), channel_id=1, source_target_pairs={{0,16},{4,20},{8,24},{12,28},{16,0},{20,4},{24,8},{28,12},{1,17},{... | collective-permute-start | bytes 638984 | tf_op jit(solution)/shard_map/ppermute | solution.py:17
  25.4 5.4 %collective-permute-start.1 = (f32[48,512]{1,0:T(8,128)S(1)}, f32[48,512]{1,0:T(8,128)S(1)}, u32[]{:S(2)}, u32[]{:S(2)}) collective-permute-start(f32[48,512]{1,0:T(8,128)S(1)} %slice_add_fusion), channel_id=1, source_target_pairs={{0,8},{4,12},{8,0},{12,4},{16,24},{20,28},{24,16},{28,20},{1,9},{5... | collective-permute-start | bytes 294920 | tf_op jit(solution)/shard_map/ppermute | solution.py:17
  30.8 6.4 %collective-permute-start.2 = (f32[48,512]{1,0:T(8,128)S(1)}, f32[48,512]{1,0:T(8,128)S(1)}, u32[]{:S(2)}, u32[]{:S(2)}) collective-permute-start(f32[48,512]{1,0:T(8,128)S(1)} %add.19), channel_id=1, source_target_pairs={{0,16},{4,20},{8,24},{12,28},{16,0},{20,4},{24,8},{28,12},{1,17},{... | collective-permute-start | bytes 294920 | tf_op jit(solution)/shard_map/ppermute | solution.py:17
  35.7 6.3 %collective-permute-start.8 = (bf16[1,208,512]{2,1,0:T(8,128)(2,1)S(1)}, bf16[1,208,512]{2,1,0:T(8,128)(2,1)S(1)}, u32[]{:S(2)}, u32[]{:S(2)}) collective-permute-start(bf16[1,208,512]{2,1,0:T(8,128)(2,1)S(1)} %get-tuple-element.9), channel_id=1, source_target_pairs={{0,2},{1,3},{2,0},{3,1},{4,6},{5,7},{6,4},{7,5},{8,10},{9,11},{10,... | collective-permute-start | bytes 638984 | tf_op jit(solution)/shard_map/ppermute | solution.py:17
  37.2 5.3 %collective-permute-start.3 = (bf16[1,48,512]{2,1,0:T(8,128)(2,1)S(1)}, bf16[1,48,512]{2,1,0:T(8,128)(2,1)S(1)}, u32[]{:S(2)}, u32[]{:S(2)}) collective-permute-start(bf16[1,48,512]{2,1,0:T(8,128)(2,1)S(1)} %fusion.10), channel_id=1, source_target_pairs={{0,2},{1,3},{2,0},{3,1},{4,6},{5,7},{6,4},{7,5},{8,10},{9,11},{10,... | collective-permute-start | bytes 147464 | tf_op jit(solution)/shard_map/ppermute | solution.py:17
  42.0 2.7 %collective-permute-start.9 = (bf16[2,208,512]{2,1,0:T(8,128)(2,1)S(1)}, bf16[2,208,512]{2,1,0:T(8,128)(2,1)S(1)}, u32[]{:S(2)}, u32[]{:S(2)}) collective-permute-start(bf16[2,208,512]{2,1,0:T(8,128)(2,1)S(1)} %get-tuple-element.7), channel_id=1, source_target_pairs={{0,1},{1,0},{2,3},{3,2},{4,5},{5,4},{6,7},{7,6},{8,9},{9,8},{10,11... | collective-permute-start | bytes 1277960 | tf_op jit(solution)/shard_map/ppermute | solution.py:17
  42.5 1.5 %collective-permute-start.4 = (bf16[2,48,512]{2,1,0:T(8,128)(2,1)S(1)}, bf16[2,48,512]{2,1,0:T(8,128)(2,1)S(1)}, u32[]{:S(2)}, u32[]{:S(2)}) collective-permute-start(bf16[2,48,512]{2,1,0:T(8,128)(2,1)S(1)} %get-tuple-element.11), channel_id=1, source_target_pairs={{0,1},{1,0},{2,3},{3,2},{4,5},{5,4},{6,7},{7,6},{8,9},{9,8},{10,11... | collective-permute-start | bytes 294920 | tf_op jit(solution)/shard_map/ppermute | solution.py:17

commit v2 on v1

v2 whole, which is shorter than its diff:
```python
import functools

import jax
import jax.numpy as jnp
from jax import lax
from jax.experimental import pallas as pl
from jax.experimental.pallas import tpu as pltpu
from jax.sharding import PartitionSpec as P

LEAD_MODES = 48
RIDGE_WEIGHT = 0.05
ROW_TILE = 16
QUAD = 4


def swap(value, axis, bit):
    count = lax.axis_size(axis)
    return lax.ppermute(value, axis, [(i, i ^ bit) for i in range(count)])


def bits_of(count):
    return [1 << k for k in range(count.bit_length() - 1)]


def gram_kernel(sizes, pos_ref, *refs):
    n_time, snaps, modes, row_block, col_block, target_block = sizes
    half, quarter = n_time // 2, snaps // QUAD
    lead_refs, rest_refs, (gram_ref, rhs_ref) = refs[0:2], refs[2 : 2 + 2 * QUAD], refs[10:12]
    delayed, head, rows, cols, side, rest = refs[12:]
    total = n_time * snaps
    time_pos, space_pos = pos_ref[0], pos_ref[1]
    core = lax.rem(time_pos, 2)
    place = lax.rem(space_pos, QUAD)

    def window(block):
        return pl.ds(pl.multiple_of(block * snaps, snaps), snaps)

    for other in range(2):
        for k in range(half):
            block = jnp.bitwise_xor(time_pos, 2 * k + other)
            current = lead_refs[other][k]
            head[:, window(block)] = current.astype(jnp.float32)
            for delay in (1, 2):

                @pl.when(block + delay < n_time)
                def _():
                    delayed[delay - 1, :, window(block + delay)] = current

            for j in range(QUAD):
                at = block * snaps + jnp.bitwise_xor(place, j) * quarter
                rest[:, pl.ds(pl.multiple_of(at, quarter), quarter)] = rest_refs[
                    other * QUAD + j
                ][k]
    for delay in (1, 2):
        delayed[delay - 1, :, 0 : delay * snaps] = jnp.zeros(
            (LEAD_MODES, delay * snaps), jnp.bfloat16
        )

    def fill(out, start, extent):
        @pl.when(start == 0)
        def _():
            out[pl.ds(LEAD_MODES, LEAD_MODES), :] = head[...].astype(jnp.bfloat16)
            out[pl.ds(2 * LEAD_MODES, modes - LEAD_MODES), :] = rest[...]

        def group(q, carry):
            kind, i = lax.div(q, LEAD_MODES), lax.rem(q, LEAD_MODES)
            at = modes + LEAD_MODES * q - start + LEAD_MODES
            factor = jnp.broadcast_to(head[pl.ds(i, 1), :], (ROW_TILE, total)).astype(
                jnp.bfloat16
            )
            for j in range(0, LEAD_MODES, ROW_TILE):
                out[pl.ds(pl.multiple_of(at + j, ROW_TILE), ROW_TILE), :] = (
                    factor * delayed[kind, j : j + ROW_TILE, :]
                )
            return carry

        first = jnp.maximum(0, lax.div(start - modes, LEAD_MODES))
        last = lax.div(start + extent - modes + LEAD_MODES - 1, LEAD_MODES)
        lax.fori_loop(first, last, group, 0)

    fill(cols, space_pos * col_block, col_block)
    fill(rows, time_pos * row_block, row_block)
    for j in range(0, target_block, ROW_TILE):
        out = cols.at[pl.ds(LEAD_MODES + col_block + j, ROW_TILE), :]
        mode = space_pos * target_block + j
        later = slice(snaps, total)

        @pl.when(mode < LEAD_MODES)
        def _():
            out[:, 0 : total - snaps] = head[
                pl.ds(pl.multiple_of(mode, ROW_TILE), ROW_TILE), later
            ].astype(jnp.bfloat16)

        @pl.when(mode >= LEAD_MODES)
        def _():
            out[:, 0 : total - snaps] = rest[
                pl.ds(pl.multiple_of(mode - LEAD_MODES, ROW_TILE), ROW_TILE), later
            ]

        out[:, total - snaps :] = jnp.zeros((ROW_TILE, snaps), jnp.bfloat16)

    tile = row_block // 4 if row_block % (4 * ROW_TILE) == 0 else row_block

    def multiply(step, carry):
        top = pl.multiple_of(step * tile, ROW_TILE)
        product = (
            lax.dot_general(
                rows[pl.ds(LEAD_MODES + top, tile), :],
                cols[pl.ds(LEAD_MODES, col_block + target_block), :],
                (((1,), (1,)), ((), ())),
                preferred_element_type=jnp.float32,
            )
            / total
        )
        shape = (tile, col_block)
        row = time_pos * row_block + top + lax.broadcasted_iota(jnp.int32, shape, 0)
        column = space_pos * col_block + lax.broadcasted_iota(jnp.int32, shape, 1)
        gram_ref[pl.ds(top, tile), :] = product[:, 0:col_block] + jnp.where(
            row == column, RIDGE_WEIGHT, 0.0
        )
        side[pl.ds(top, tile), :] = product[:, col_block:]
        return carry

    lax.fori_loop(0, row_block // tile, multiply, 0)
    rhs_ref[...] = side[...].T


def gram_blocks(lead, rest, n_time, n_space):
    _, lead_modes, snaps = lead[0].shape
    modes = lead_modes + rest[0].shape[1]
    features = modes + 2 * LEAD_MODES * LEAD_MODES
    row_block, col_block, target_block = features // n_time, features // n_space, modes // n_space
    total = n_time * snaps
    here = jnp.stack([lax.axis_index("tm"), lax.axis_index("space")]).astype(jnp.int32)
    vmem = pl.BlockSpec(memory_space=pltpu.VMEM)
    gram, rhs = pl.pallas_call(
        functools.partial(
            gram_kernel, (n_time, snaps, modes, row_block, col_block, target_block)
        ),
        out_shape=(
            jax.ShapeDtypeStruct((row_block, col_block), jnp.float32),
            jax.ShapeDtypeStruct((target_block, row_block), jnp.float32),
        ),
        in_specs=[pl.BlockSpec(memory_space=pltpu.SMEM)] + [vmem] * (2 + 2 * QUAD),
        out_specs=(vmem, vmem),
        scratch_shapes=[
            pltpu.VMEM((2, LEAD_MODES, total), jnp.bfloat16),
            pltpu.VMEM((LEAD_MODES, total), jnp.float32),
            pltpu.VMEM((row_block + 2 * LEAD_MODES, total), jnp.bfloat16),
            pltpu.VMEM((col_block + 2 * LEAD_MODES + target_block, total), jnp.bfloat16),
            pltpu.VMEM((row_block, target_block), jnp.float32),
            pltpu.VMEM((modes - lead_modes, total), jnp.bfloat16),
        ],
        compiler_params=pltpu.CompilerParams(vmem_limit_bytes=56 * 2**20),
    )(here, *lead, *rest)
    return gram, rhs.T


def to_sum(*parts):
    return functools.reduce(jnp.add, [part.astype(jnp.float32) for part in parts])


def joined(value, axis, bit):
    return jnp.concatenate([value, swap(value, axis, bit)], axis=0)


def per_device(snapshots, modes):
    n_space, n_time = lax.axis_size("space"), lax.axis_size("tm")
    partial_sums = lax.dot_general(
        modes, snapshots, (((0,), (0,)), ((), ())), preferred_element_type=jnp.float32
    )
    snaps = partial_sums.shape[1]
    quarter = snaps // QUAD
    place = lax.rem(lax.axis_index("space"), QUAD)
    lead = partial_sums[0:LEAD_MODES]
    rest = partial_sums[LEAD_MODES:]

    def quarter_of(j):
        start = jnp.bitwise_xor(place, j) * quarter
        return lax.dynamic_slice_in_dim(rest, start, quarter, 1)

    arrived = [
        swap(quarter_of(j).astype(jnp.bfloat16), "space", j) for j in range(1, QUAD)
    ]
    mine = to_sum(quarter_of(0), *arrived).astype(jnp.bfloat16)
    for bit in bits_of(n_space):
        lead = lead + swap(lead, "space", bit)
        if bit >= QUAD:
            mine = to_sum(mine, swap(mine, "space", bit)).astype(jnp.bfloat16)
    lead = lead.astype(jnp.bfloat16)[None]
    mine = mine[None]
    for bit in bits_of(n_time)[1:]:
        lead = joined(lead, "tm", bit)
        mine = joined(mine, "tm", bit)
    rest = [mine] + [swap(mine, "space", j) for j in range(1, QUAD)]
    lead = [lead, swap(lead, "tm", 1)]
    rest = rest + [swap(piece, "tm", 1) for piece in rest]
    return gram_blocks(lead, rest, n_time, n_space)


def solution(mesh):
    in_specs = (P("space", "tm"), P("space", None))
    out_specs = (P("tm", "space"), P("tm", "space"))
    return jax.shard_map(
        per_device, mesh=mesh, in_specs=in_specs, out_specs=out_specs, check_vma=False
    )
```

time: 55.2 us -> 46.7 us (0.85)
  waiting for transfers between devices: 19.9 us -> 7.52 us
  starting transfers between devices: 15.3 us -> 19.5 us
    ppermute x10 -> x17, waiting for transfers between devices: 19.9 us -> 7.52 us  [swap(): return lax.ppermute(value, axis, [(i, i ^ bit) for i in range(count)])]
    ppermute x10 -> x17, starting transfers between devices: 15.3 us -> 19.5 us  [swap(): return lax.ppermute(value, axis, [(i, i ^ bit) for i in range(count)])]
    another operation x2 -> x0, local copies, waits for them, and re-layouts: 1.69 us -> none  [the longest x1 0.99 us: per_device(): rest = jnp.stack([rest, swap(rest, 'tm', bit)], axis=1)]
    unnamed x0 -> x20, local copies, waits for them, and re-layouts: none -> 1.12 us
  transfers between devices with their start and end apart: 10 -> 17, of which waited for: 7 -> 10; matrix products, arithmetic and copies ran while one was open for 3% -> 2% of each run, Pallas kernels for 0% -> 0%
where the time goes in v2:
time: 46.7 us; the launch traced here: 46.5 us
  starting transfers between devices  19.5 us (42%)
  Pallas kernels  9.49 us (20%)
  waiting for transfers between devices  7.52 us (16%)
  matrix products  7.22 us (15%)
  local copies, waits for them, and re-layouts  1.21 us (3%)
  between operations  0.8 us (2%)
  other arithmetic  0.77 us (2%)
    ppermute x17, starting transfers between devices, swap(): return lax.ppermute(value, axis, [(i, i ^ bit) for i in range(count)])  19.5 us
    pallas_call x1, Pallas kernels, gram_blocks(): pl.pallas_call(functools.partial(gram_kernel, (n_time, snaps, modes, row_...  9.49 us
    ppermute x17, waiting for transfers between devices, swap(): return lax.ppermute(value, axis, [(i, i ^ bit) for i in range(count)])  7.52 us
    dot_general x1, matrix products, per_device(): lax.dot_general(modes, snapshots, (((0,), (0,)), ((), ())), preferred_ele...  7.22 us
    unnamed x20, local copies, waits for them, and re-layouts  1.12 us
  transfers between devices with their start and end apart: 17, of which 10 were waited for; matrix products, arithmetic and copies ran while one was open for 2% of the time, Pallas kernels for 0%

profile of v2, /device:TPU:0, one launch (start us, length us, event | category | flops | bytes accessed | tf_op | source)
XLA Modules:
  0.0 46.5 jit_solution(11220524620447252980)
XLA Ops:
  0.7 7.2 %fusion.2 = f32[256,512]{1,0:T(8,128)S(1)} fusion(bf16[10240,256]{1,0:T(8,128)(2,1)} %param.3, bf16[10240,512]{1,0:T(8,128)(2,1)} %param.2), kind=kOutput, calls=%fused_computation.12 | convolution fusion | flops 2684354560 | bytes 16252928 | tf_op jit(solution)/shard_map/dot_general | solution.py:169
  7.9 0.1 dynamic-slice_convert_fusion.2
  8.0 3.0 %collective-permute-start.5 = (bf16[208,128]{1,0:T(8,128)(2,1)S(1)}, bf16[208,128]{1,0:T(8,128)(2,1)S(1)}, u32[]{:S(2)}, u32[]{:S(2)}) collective-permute-start(bf16[208,128]{1,0:T(8,128)(2,1)S(1)} %get-tuple-element.6), channel_id=1, source_target_pairs={{0,4},{4,0},{8,12},{12,8},{16,20},{20,16},{24,28},{28,24},{1,5},{5... | collective-permute-start | bytes 159752 | tf_op jit(solution)/shard_map/ppermute | solution.py:18
  11.0 1.5 %collective-permute-start.7 = (bf16[208,128]{1,0:T(8,128)(2,1)S(1)}, bf16[208,128]{1,0:T(8,128)(2,1)S(1)}, u32[]{:S(2)}, u32[]{:S(2)}) collective-permute-start(bf16[208,128]{1,0:T(8,128)(2,1)S(1)} %get-tuple-element.7), channel_id=1, source_target_pairs={{0,12},{4,8},{8,4},{12,0},{16,28},{20,24},{24,20},{28,16},{1,13},{... | collective-permute-start | bytes 159752 | tf_op jit(solution)/shard_map/ppermute | solution.py:18
  12.5 0.0 collective-permute-start.6
  12.6 2.0 %collective-permute-start = (f32[48,512]{1,0:T(8,128)S(1)}, f32[48,512]{1,0:T(8,128)S(1)}, u32[]{:S(2)}, u32[]{:S(2)}) collective-permute-start(f32[48,512]{1,0:T(8,128)S(1)} %slice.8), channel_id=1, source_target_pairs={{0,4},{4,0},{8,12},{12,8},{16,20},{20,16},{24,28},{28,24},{1,5},{5... | collective-permute-start | bytes 294920 | tf_op jit(solution)/shard_map/ppermute | solution.py:18
  14.6 0.0 collective-permute-done.5
  14.6 2.0 %collective-permute-done.7 = bf16[208,128]{1,0:T(8,128)(2,1)S(1)} collective-permute-done((bf16[208,128]{1,0:T(8,128)(2,1)S(1)}, bf16[208,128]{1,0:T(8,128)(2,1)S(1)}, u32[]{:S(2)}, u32[]{:S(2)}) %collective-permute-start.7) | collective-permute-done | bytes 53280 | tf_op jit(solution)/shard_map/ppermute | solution.py:18
  16.6 0.1 collective-permute-done.6
  16.7 2.7 %collective-permute-start.8 = (bf16[208,128]{1,0:T(8,128)(2,1)S(1)}, bf16[208,128]{1,0:T(8,128)(2,1)S(1)}, u32[]{:S(2)}, u32[]{:S(2)}) collective-permute-start(bf16[208,128]{1,0:T(8,128)(2,1)S(1)} %add_convert_fusion.1), channel_id=1, source_target_pairs={{0,16},{4,20},{8,24},{12,28},{16,0},{20,4},{24,8},{28,12},{1,17},{... | collective-permute-start | bytes 159752 | tf_op jit(solution)/shard_map/ppermute | solution.py:18
  19.4 0.0 collective-permute-done
  19.4 1.1 %collective-permute-start.1 = (f32[48,512]{1,0:T(8,128)S(1)}, f32[48,512]{1,0:T(8,128)S(1)}, u32[]{:S(2)}, u32[]{:S(2)}) collective-permute-start(f32[48,512]{1,0:T(8,128)S(1)} %slice_add_fusion), channel_id=1, source_target_pairs={{0,8},{4,12},{8,0},{12,4},{16,24},{20,28},{24,16},{28,20},{1,9},{5... | collective-permute-start | bytes 294920 | tf_op jit(solution)/shard_map/ppermute | solution.py:18
  20.5 1.4 %collective-permute-done.8 = bf16[208,128]{1,0:T(8,128)(2,1)S(1)} collective-permute-done((bf16[208,128]{1,0:T(8,128)(2,1)S(1)}, bf16[208,128]{1,0:T(8,128)(2,1)S(1)}, u32[]{:S(2)}, u32[]{:S(2)}) %collective-permute-start.8) | collective-permute-done | bytes 53280 | tf_op jit(solution)/shard_map/ppermute | solution.py:18
  21.9 1.6 %collective-permute-start.9 = (bf16[1,208,128]{2,1,0:T(8,128)(2,1)S(1)}, bf16[1,208,128]{2,1,0:T(8,128)(2,1)S(1)}, u32[]{:S(2)}, u32[]{:S(2)}) collective-permute-start(bf16[1,208,128]{2,1,0:T(8,128)(2,1)S(1)} %fusion), channel_id=1, source_target_pairs={{0,2},{1,3},{2,0},{3,1},{4,6},{5,7},{6,4},{7,5},{8,10},{9,11},{10,... | collective-permute-start | bytes 159752 | tf_op jit(solution)/shard_map/ppermute | solution.py:18
  23.5 0.5 %collective-permute-done.1 = f32[48,512]{1,0:T(8,128)S(1)} collective-permute-done((f32[48,512]{1,0:T(8,128)S(1)}, f32[48,512]{1,0:T(8,128)S(1)}, u32[]{:S(2)}, u32[]{:S(2)}) %collective-permute-start.1) | collective-permute-done | bytes 98336 | tf_op jit(solution)/shard_map/ppermute | solution.py:18
  24.1 2.1 %collective-permute-start.2 = (f32[48,512]{1,0:T(8,128)S(1)}, f32[48,512]{1,0:T(8,128)S(1)}, u32[]{:S(2)}, u32[]{:S(2)}) collective-permute-start(f32[48,512]{1,0:T(8,128)S(1)} %add.34), channel_id=1, source_target_pairs={{0,16},{4,20},{8,24},{12,28},{16,0},{20,4},{24,8},{28,12},{1,17},{... | collective-permute-start | bytes 294920 | tf_op jit(solution)/shard_map/ppermute | solution.py:18
  26.2 0.0 collective-permute-done.9
  26.2 0.0 copy-start
  26.2 2.0 %collective-permute-start.12 = (bf16[2,208,128]{2,1,0:T(8,128)(2,1)S(1)}, bf16[2,208,128]{2,1,0:T(8,128)(2,1)S(1)}, u32[]{:S(2)}, u32[]{:S(2)}) collective-permute-start(bf16[2,208,128]{2,1,0:T(8,128)(2,1)S(1)} %pad_maximum_fusion.refs_2_), channel_id=1, source_target_pairs={{0,12},{4,8},{8,4},{12,0},{16,28},{20,24},{24,20},{28,16},{1,13},{... | collective-permute-start | bytes 319496 | tf_op jit(solution)/shard_map/ppermute | solution.py:18
  28.2 1.4 %collective-permute-start.11 = (bf16[2,208,128]{2,1,0:T(8,128)(2,1)S(1)}, bf16[2,208,128]{2,1,0:T(8,128)(2,1)S(1)}, u32[]{:S(2)}, u32[]{:S(2)}) collective-permute-start(bf16[2,208,128]{2,1,0:T(8,128)(2,1)S(1)} %pad_maximum_fusion.refs_2_), channel_id=1, source_target_pairs={{0,8},{4,12},{8,0},{12,4},{16,24},{20,28},{24,16},{28,20},{1,9},{5... | collective-permute-start | bytes 319496 | tf_op jit(solution)/shard_map/ppermute | solution.py:18
  29.6 0.1 collective-permute-start.10
  29.8 0.5 %collective-permute-done.2 = f32[48,512]{1,0:T(8,128)S(1)} collective-permute-done((f32[48,512]{1,0:T(8,128)S(1)}, f32[48,512]{1,0:T(8,128)S(1)}, u32[]{:S(2)}, u32[]{:S(2)}) %collective-permute-start.2) | collective-permute-done | bytes 98336 | tf_op jit(solution)/shard_map/ppermute | solution.py:18
  30.3 1.4 %collective-permute-start.3 = (bf16[1,48,512]{2,1,0:T(8,128)(2,1)S(1)}, bf16[1,48,512]{2,1,0:T(8,128)(2,1)S(1)}, u32[]{:S(2)}, u32[]{:S(2)}) collective-permute-start(bf16[1,48,512]{2,1,0:T(8,128)(2,1)S(1)} %fusion.1), channel_id=1, source_target_pairs={{0,2},{1,3},{2,0},{3,1},{4,6},{5,7},{6,4},{7,5},{8,10},{9,11},{10,... | collective-permute-start | bytes 147464 | tf_op jit(solution)/shard_map/ppermute | solution.py:18
  31.7 0.0 collective-permute-start.13
  31.7 0.6 %collective-permute-done.12.refs_5_ = bf16[2,208,128]{2,1,0:T(8,128)(2,1)S(1)} collective-permute-done((bf16[2,208,128]{2,1,0:T(8,128)(2,1)S(1)}, bf16[2,208,128]{2,1,0:T(8,128)(2,1)S(1)}, u32[]{:S(2)}, u32[]{:S(2)}) %collective-permute-start.12) | collective-permute-done | bytes 106528 | tf_op jit(solution)/shard_map/ppermute | solution.py:18
  32.3 0.0 collective-permute-start.16
  32.3 1.1 %collective-permute-done.11.refs_4_ = bf16[2,208,128]{2,1,0:T(8,128)(2,1)S(1)} collective-permute-done((bf16[2,208,128]{2,1,0:T(8,128)(2,1)S(1)}, bf16[2,208,128]{2,1,0:T(8,128)(2,1)S(1)}, u32[]{:S(2)}, u32[]{:S(2)}) %collective-permute-start.11) | collective-permute-done | bytes 106528 | tf_op jit(solution)/shard_map/ppermute | solution.py:18
  33.5 0.0 collective-permute-start.15
  33.5 0.9 %collective-permute-done.10.refs_3_ = bf16[2,208,128]{2,1,0:T(8,128)(2,1)S(1)} collective-permute-done((bf16[2,208,128]{2,1,0:T(8,128)(2,1)S(1)}, bf16[2,208,128]{2,1,0:T(8,128)(2,1)S(1)}, u32[]{:S(2)}, u32[]{:S(2)}) %collective-permute-start.10) | collective-permute-done | bytes 106528 | tf_op jit(solution)/shard_map/ppermute | solution.py:18
  34.3 0.0 collective-permute-start.14
  34.3 0.1 collective-permute-done.3
  34.5 0.0 copy-start.1
  34.5 0.5 %collective-permute-start.4 = (bf16[2,48,512]{2,1,0:T(8,128)(2,1)S(1)}, bf16[2,48,512]{2,1,0:T(8,128)(2,1)S(1)}, u32[]{:S(2)}, u32[]{:S(2)}) collective-permute-start(bf16[2,48,512]{2,1,0:T(8,128)(2,1)S(1)} %pad_maximum_fusion.1.refs_0_), channel_id=1, source_target_pairs={{0,1},{1,0},{2,3},{3,2},{4,5},{5,4},{6,7},{7,6},{8,9},{9,8},{10,11... | collective-permute-start | bytes 294920 | tf_op jit(solution)/shard_map/ppermute | solution.py:18
  35.0 0.7 %pad_add_fusion.pos_ref = s32[2]{0:T(128)} fusion(s32[1]{0:T(128)} %bitcast.1, s32[1]{0:T(128)} %bitcast), kind=kLoop, calls=%fused_computation.10 | loop fusion | flops 2 | bytes 16 | tf_op jit(solution)/shard_map/stack | solution.py:134
  35.6 0.0 collective-permute-done.13.refs_6_
  35.6 0.0 collective-permute-done.16.refs_9_
  35.6 0.0 copy-start.6
  35.6 0.0 collective-permute-done.15.refs_8_
  35.6 0.0 copy-start.7
  35.6 0.0 collective-permute-done.14.refs_7_
  35.7 0.2 collective-permute-done.4.refs_1_
  35.9 0.0 copy-done.3
  35.9 0.3 copy-done.5
  36.3 0.0 copy-done.6
  36.3 0.0 copy-done.7
  36.3 0.0 copy-done.8
  36.4 0.6 %copy-done.9 = bf16[2,48,512]{2,1,0:T(8,128)(2,1)} copy-done((bf16[2,48,512]{2,1,0:T(8,128)(2,1)}, bf16[2,48,512]{2,1,0:T(8,128)(2,1)S(1)}, u32[]{:S(2)}) %copy-start.9) | copy-done | bytes 98328
  37.0 9.5 %shard_map.41 = (f32[1216,608]{1,0:T(8,128)}, f32[32,1216]{1,0:T(8,128)}) custom-call(s32[2]{0:T(128)} %pad_add_fusion.pos_ref, bf16[2,48,512]{2,1,0:T(8,128)(2,1)} %copy-done.1, bf16[2,48,512]{2,1,0:T(8,128)(2,1)} %copy-done.9, bf16[2,208,128]{2,1,0:T(8,128)(2,1)} %copy-done, bf16[2,208,128]{2,1,0:T(8,128)(2,1)} %copy-done.4, ...), custom_call_target="tpu_custom_call" | custom-call | tf_op jit(solution)/shard_map/pallas_call | solution.py:136
  (19 shorter events, 0.2 us)
Async XLA Ops:
  8.0 6.6 %collective-permute-start.5 = (bf16[208,128]{1,0:T(8,128)(2,1)S(1)}, bf16[208,128]{1,0:T(8,128)(2,1)S(1)}, u32[]{:S(2)}, u32[]{:S(2)}) collective-permute-start(bf16[208,128]{1,0:T(8,128)(2,1)S(1)} %get-tuple-element.6), channel_id=1, source_target_pairs={{0,4},{4,0},{8,12},{12,8},{16,20},{20,16},{24,28},{28,24},{1,5},{5... | collective-permute-start | bytes 159752 | tf_op jit(solution)/shard_map/ppermute | solution.py:18
  11.0 5.6 %collective-permute-start.7 = (bf16[208,128]{1,0:T(8,128)(2,1)S(1)}, bf16[208,128]{1,0:T(8,128)(2,1)S(1)}, u32[]{:S(2)}, u32[]{:S(2)}) collective-permute-start(bf16[208,128]{1,0:T(8,128)(2,1)S(1)} %get-tuple-element.7), channel_id=1, source_target_pairs={{0,12},{4,8},{8,4},{12,0},{16,28},{20,24},{24,20},{28,16},{1,13},{... | collective-permute-start | bytes 159752 | tf_op jit(solution)/shard_map/ppermute | solution.py:18
  12.5 4.1 %collective-permute-start.6 = (bf16[208,128]{1,0:T(8,128)(2,1)S(1)}, bf16[208,128]{1,0:T(8,128)(2,1)S(1)}, u32[]{:S(2)}, u32[]{:S(2)}) collective-permute-start(bf16[208,128]{1,0:T(8,128)(2,1)S(1)} %get-tuple-element.8), channel_id=1, source_target_pairs={{0,8},{4,12},{8,0},{12,4},{16,24},{20,28},{24,16},{28,20},{1,9},{5... | collective-permute-start | bytes 159752 | tf_op jit(solution)/shard_map/ppermute | solution.py:18
  12.6 6.8 %collective-permute-start = (f32[48,512]{1,0:T(8,128)S(1)}, f32[48,512]{1,0:T(8,128)S(1)}, u32[]{:S(2)}, u32[]{:S(2)}) collective-permute-start(f32[48,512]{1,0:T(8,128)S(1)} %slice.8), channel_id=1, source_target_pairs={{0,4},{4,0},{8,12},{12,8},{16,20},{20,16},{24,28},{28,24},{1,5},{5... | collective-permute-start | bytes 294920 | tf_op jit(solution)/shard_map/ppermute | solution.py:18
  16.7 5.2 %collective-permute-start.8 = (bf16[208,128]{1,0:T(8,128)(2,1)S(1)}, bf16[208,128]{1,0:T(8,128)(2,1)S(1)}, u32[]{:S(2)}, u32[]{:S(2)}) collective-permute-start(bf16[208,128]{1,0:T(8,128)(2,1)S(1)} %add_convert_fusion.1), channel_id=1, source_target_pairs={{0,16},{4,20},{8,24},{12,28},{16,0},{20,4},{24,8},{28,12},{1,17},{... | collective-permute-start | bytes 159752 | tf_op jit(solution)/shard_map/ppermute | solution.py:18
  19.4 4.7 %collective-permute-start.1 = (f32[48,512]{1,0:T(8,128)S(1)}, f32[48,512]{1,0:T(8,128)S(1)}, u32[]{:S(2)}, u32[]{:S(2)}) collective-permute-start(f32[48,512]{1,0:T(8,128)S(1)} %slice_add_fusion), channel_id=1, source_target_pairs={{0,8},{4,12},{8,0},{12,4},{16,24},{20,28},{24,16},{28,20},{1,9},{5... | collective-permute-start | bytes 294920 | tf_op jit(solution)/shard_map/ppermute | solution.py:18
  21.9 4.3 %collective-permute-start.9 = (bf16[1,208,128]{2,1,0:T(8,128)(2,1)S(1)}, bf16[1,208,128]{2,1,0:T(8,128)(2,1)S(1)}, u32[]{:S(2)}, u32[]{:S(2)}) collective-permute-start(bf16[1,208,128]{2,1,0:T(8,128)(2,1)S(1)} %fusion), channel_id=1, source_target_pairs={{0,2},{1,3},{2,0},{3,1},{4,6},{5,7},{6,4},{7,5},{8,10},{9,11},{10,... | collective-permute-start | bytes 159752 | tf_op jit(solution)/shard_map/ppermute | solution.py:18
  24.1 6.2 %collective-permute-start.2 = (f32[48,512]{1,0:T(8,128)S(1)}, f32[48,512]{1,0:T(8,128)S(1)}, u32[]{:S(2)}, u32[]{:S(2)}) collective-permute-start(f32[48,512]{1,0:T(8,128)S(1)} %add.34), channel_id=1, source_target_pairs={{0,16},{4,20},{8,24},{12,28},{16,0},{20,4},{24,8},{28,12},{1,17},{... | collective-permute-start | bytes 294920 | tf_op jit(solution)/shard_map/ppermute | solution.py:18
  26.2 9.7 %copy-start = (bf16[2,208,128]{2,1,0:T(8,128)(2,1)}, bf16[2,208,128]{2,1,0:T(8,128)(2,1)S(1)}, u32[]{:S(2)}) copy-start(bf16[2,208,128]{2,1,0:T(8,128)(2,1)S(1)} %pad_maximum_fusion.refs_2_) | copy-start | bytes 319492
  26.2 6.1 %collective-permute-start.12 = (bf16[2,208,128]{2,1,0:T(8,128)(2,1)S(1)}, bf16[2,208,128]{2,1,0:T(8,128)(2,1)S(1)}, u32[]{:S(2)}, u32[]{:S(2)}) collective-permute-start(bf16[2,208,128]{2,1,0:T(8,128)(2,1)S(1)} %pad_maximum_fusion.refs_2_), channel_id=1, source_target_pairs={{0,12},{4,8},{8,4},{12,0},{16,28},{20,24},{24,20},{28,16},{1,13},{... | collective-permute-start | bytes 319496 | tf_op jit(solution)/shard_map/ppermute | solution.py:18
  28.2 5.3 %collective-permute-start.11 = (bf16[2,208,128]{2,1,0:T(8,128)(2,1)S(1)}, bf16[2,208,128]{2,1,0:T(8,128)(2,1)S(1)}, u32[]{:S(2)}, u32[]{:S(2)}) collective-permute-start(bf16[2,208,128]{2,1,0:T(8,128)(2,1)S(1)} %pad_maximum_fusion.refs_2_), channel_id=1, source_target_pairs={{0,8},{4,12},{8,0},{12,4},{16,24},{20,28},{24,16},{28,20},{1,9},{5... | collective-permute-start | bytes 319496 | tf_op jit(solution)/shard_map/ppermute | solution.py:18
  29.6 4.7 %collective-permute-start.10 = (bf16[2,208,128]{2,1,0:T(8,128)(2,1)S(1)}, bf16[2,208,128]{2,1,0:T(8,128)(2,1)S(1)}, u32[]{:S(2)}, u32[]{:S(2)}) collective-permute-start(bf16[2,208,128]{2,1,0:T(8,128)(2,1)S(1)} %pad_maximum_fusion.refs_2_), channel_id=1, source_target_pairs={{0,4},{4,0},{8,12},{12,8},{16,20},{20,16},{24,28},{28,24},{1,5},{5... | collective-permute-start | bytes 319496 | tf_op jit(solution)/shard_map/ppermute | solution.py:18
  30.3 4.2 %collective-permute-start.3 = (bf16[1,48,512]{2,1,0:T(8,128)(2,1)S(1)}, bf16[1,48,512]{2,1,0:T(8,128)(2,1)S(1)}, u32[]{:S(2)}, u32[]{:S(2)}) collective-permute-start(bf16[1,48,512]{2,1,0:T(8,128)(2,1)S(1)} %fusion.1), channel_id=1, source_target_pairs={{0,2},{1,3},{2,0},{3,1},{4,6},{5,7},{6,4},{7,5},{8,10},{9,11},{10,... | collective-permute-start | bytes 147464 | tf_op jit(solution)/shard_map/ppermute | solution.py:18
  31.7 3.9 %collective-permute-start.13 = (bf16[2,208,128]{2,1,0:T(8,128)(2,1)S(1)}, bf16[2,208,128]{2,1,0:T(8,128)(2,1)S(1)}, u32[]{:S(2)}, u32[]{:S(2)}) collective-permute-start(bf16[2,208,128]{2,1,0:T(8,128)(2,1)S(1)} %pad_maximum_fusion.refs_2_), channel_id=1, source_target_pairs={{0,1},{1,0},{2,3},{3,2},{4,5},{5,4},{6,7},{7,6},{8,9},{9,8},{10,11... | collective-permute-start | bytes 319496 | tf_op jit(solution)/shard_map/ppermute | solution.py:18
  32.3 3.6 %copy-start.2 = (bf16[2,208,128]{2,1,0:T(8,128)(2,1)}, bf16[2,208,128]{2,1,0:T(8,128)(2,1)S(1)}, u32[]{:S(2)}) copy-start(bf16[2,208,128]{2,1,0:T(8,128)(2,1)S(1)} %collective-permute-done.12.refs_5_) | copy-start | bytes 319492
  32.3 3.3 %collective-permute-start.16 = (bf16[2,208,128]{2,1,0:T(8,128)(2,1)S(1)}, bf16[2,208,128]{2,1,0:T(8,128)(2,1)S(1)}, u32[]{:S(2)}, u32[]{:S(2)}) collective-permute-start(bf16[2,208,128]{2,1,0:T(8,128)(2,1)S(1)} %collective-permute-done.12.refs_5_), channel_id=1, source_target_pairs={{0,1},{1,0},{2,3},{3,2},{4,5},{5,4},{6,7},{7,6},{8,9},{9,8},{10,11... | collective-permute-start | bytes 319496 | tf_op jit(solution)/shard_map/ppermute | solution.py:18
  33.5 2.4 %copy-start.3 = (bf16[2,208,128]{2,1,0:T(8,128)(2,1)}, bf16[2,208,128]{2,1,0:T(8,128)(2,1)S(1)}, u32[]{:S(2)}) copy-start(bf16[2,208,128]{2,1,0:T(8,128)(2,1)S(1)} %collective-permute-done.11.refs_4_) | copy-start | bytes 319492
  33.5 2.2 %collective-permute-start.15 = (bf16[2,208,128]{2,1,0:T(8,128)(2,1)S(1)}, bf16[2,208,128]{2,1,0:T(8,128)(2,1)S(1)}, u32[]{:S(2)}, u32[]{:S(2)}) collective-permute-start(bf16[2,208,128]{2,1,0:T(8,128)(2,1)S(1)} %collective-permute-done.11.refs_4_), channel_id=1, source_target_pairs={{0,1},{1,0},{2,3},{3,2},{4,5},{5,4},{6,7},{7,6},{8,9},{9,8},{10,11... | collective-permute-start | bytes 319496 | tf_op jit(solution)/shard_map/ppermute | solution.py:18
  34.3 1.6 %copy-start.4 = (bf16[2,208,128]{2,1,0:T(8,128)(2,1)}, bf16[2,208,128]{2,1,0:T(8,128)(2,1)S(1)}, u32[]{:S(2)}) copy-start(bf16[2,208,128]{2,1,0:T(8,128)(2,1)S(1)} %collective-permute-done.10.refs_3_) | copy-start | bytes 319492
  34.3 1.3 %collective-permute-start.14 = (bf16[2,208,128]{2,1,0:T(8,128)(2,1)S(1)}, bf16[2,208,128]{2,1,0:T(8,128)(2,1)S(1)}, u32[]{:S(2)}, u32[]{:S(2)}) collective-permute-start(bf16[2,208,128]{2,1,0:T(8,128)(2,1)S(1)} %collective-permute-done.10.refs_3_), channel_id=1, source_target_pairs={{0,1},{1,0},{2,3},{3,2},{4,5},{5,4},{6,7},{7,6},{8,9},{9,8},{10,11... | collective-permute-start | bytes 319496 | tf_op jit(solution)/shard_map/ppermute | solution.py:18
  34.5 1.5 %copy-start.1 = (bf16[2,48,512]{2,1,0:T(8,128)(2,1)}, bf16[2,48,512]{2,1,0:T(8,128)(2,1)S(1)}, u32[]{:S(2)}) copy-start(bf16[2,48,512]{2,1,0:T(8,128)(2,1)S(1)} %pad_maximum_fusion.1.refs_0_) | copy-start | bytes 294916
  34.5 1.4 %collective-permute-start.4 = (bf16[2,48,512]{2,1,0:T(8,128)(2,1)S(1)}, bf16[2,48,512]{2,1,0:T(8,128)(2,1)S(1)}, u32[]{:S(2)}, u32[]{:S(2)}) collective-permute-start(bf16[2,48,512]{2,1,0:T(8,128)(2,1)S(1)} %pad_maximum_fusion.1.refs_0_), channel_id=1, source_target_pairs={{0,1},{1,0},{2,3},{3,2},{4,5},{5,4},{6,7},{7,6},{8,9},{9,8},{10,11... | collective-permute-start | bytes 294920 | tf_op jit(solution)/shard_map/ppermute | solution.py:18
  35.6 0.7 %copy-start.5 = (bf16[2,208,128]{2,1,0:T(8,128)(2,1)}, bf16[2,208,128]{2,1,0:T(8,128)(2,1)S(1)}, u32[]{:S(2)}) copy-start(bf16[2,208,128]{2,1,0:T(8,128)(2,1)S(1)} %collective-permute-done.13.refs_6_) | copy-start | bytes 319492
  35.6 0.7 %copy-start.6 = (bf16[2,208,128]{2,1,0:T(8,128)(2,1)}, bf16[2,208,128]{2,1,0:T(8,128)(2,1)S(1)}, u32[]{:S(2)}) copy-start(bf16[2,208,128]{2,1,0:T(8,128)(2,1)S(1)} %collective-permute-done.16.refs_9_) | copy-start | bytes 319492
  35.6 0.7 %copy-start.7 = (bf16[2,208,128]{2,1,0:T(8,128)(2,1)}, bf16[2,208,128]{2,1,0:T(8,128)(2,1)S(1)}, u32[]{:S(2)}) copy-start(bf16[2,208,128]{2,1,0:T(8,128)(2,1)S(1)} %collective-permute-done.15.refs_8_) | copy-start | bytes 319492
  35.7 0.7 %copy-start.8 = (bf16[2,208,128]{2,1,0:T(8,128)(2,1)}, bf16[2,208,128]{2,1,0:T(8,128)(2,1)S(1)}, u32[]{:S(2)}) copy-start(bf16[2,208,128]{2,1,0:T(8,128)(2,1)S(1)} %collective-permute-done.14.refs_7_) | copy-start | bytes 319492
  36.4 0.6 %copy-start.9 = (bf16[2,48,512]{2,1,0:T(8,128)(2,1)}, bf16[2,48,512]{2,1,0:T(8,128)(2,1)S(1)}, u32[]{:S(2)}) copy-start(bf16[2,48,512]{2,1,0:T(8,128)(2,1)S(1)} %collective-permute-done.4.refs_1_) | copy-start | bytes 294916

commit v3 on v2

v3 whole, which is shorter than its diff:
```python
import functools

import jax
import jax.numpy as jnp
from jax import lax
from jax.experimental import pallas as pl
from jax.experimental.pallas import tpu as pltpu
from jax.sharding import PartitionSpec as P

LEAD_MODES = 48
RIDGE_WEIGHT = 0.05
ROW_TILE = 16
QUAD = 4


def swap(value, axis, bit):
    count = lax.axis_size(axis)
    return lax.ppermute(value, axis, [(i, i ^ bit) for i in range(count)])


def bits_of(count):
    return [1 << k for k in range(count.bit_length() - 1)]


def gram_kernel(sizes, pos_ref, *refs):
    n_time, snaps, modes, row_block, col_block, target_block = sizes
    half, quarter = n_time // 2, snaps // QUAD
    pieces, (gram_ref, rhs_ref) = refs[0 : 2 * QUAD], refs[2 * QUAD : 2 * QUAD + 2]
    coeffs, delayed, head, rows, cols, side = refs[2 * QUAD + 2 :]
    total = n_time * snaps
    time_pos, space_pos = pos_ref[0], pos_ref[1]
    place = lax.rem(space_pos, QUAD)

    for other in range(2):
        for k in range(half):
            block = jnp.bitwise_xor(time_pos, 2 * k + other)
            for j in range(QUAD):
                at = block * snaps + jnp.bitwise_xor(place, j) * quarter
                coeffs[:, pl.ds(pl.multiple_of(at, quarter), quarter)] = pieces[
                    other * QUAD + j
                ][k]
    head[...] = coeffs[0:LEAD_MODES, :].astype(jnp.float32)
    for delay in (1, 2):
        gap = delay * snaps
        delayed[delay - 1, :, 0:gap] = jnp.zeros((LEAD_MODES, gap), jnp.bfloat16)
        delayed[delay - 1, :, gap:] = coeffs[0:LEAD_MODES, 0 : total - gap]

    def fill(out, start, extent):
        @pl.when(start == 0)
        def _():
            out[pl.ds(LEAD_MODES, modes), :] = coeffs[...]

        def group(q, carry):
            kind, i = lax.div(q, LEAD_MODES), lax.rem(q, LEAD_MODES)
            at = modes + LEAD_MODES * q - start + LEAD_MODES
            factor = jnp.broadcast_to(head[pl.ds(i, 1), :], (ROW_TILE, total)).astype(
                jnp.bfloat16
            )
            for j in range(0, LEAD_MODES, ROW_TILE):
                out[pl.ds(pl.multiple_of(at + j, ROW_TILE), ROW_TILE), :] = (
                    factor * delayed[kind, j : j + ROW_TILE, :]
                )
            return carry

        first = jnp.maximum(0, lax.div(start - modes, LEAD_MODES))
        last = lax.div(start + extent - modes + LEAD_MODES - 1, LEAD_MODES)
        lax.fori_loop(first, last, group, 0)

    fill(cols, space_pos * col_block, col_block)
    fill(rows, time_pos * row_block, row_block)
    wanted = pl.ds(pl.multiple_of(space_pos * target_block, ROW_TILE), target_block)
    at = pl.ds(LEAD_MODES + col_block, target_block)
    cols[at, 0 : total - snaps] = coeffs[wanted, snaps:]
    cols[at, total - snaps :] = jnp.zeros((target_block, snaps), jnp.bfloat16)

    tile = row_block // 4 if row_block % (4 * ROW_TILE) == 0 else row_block

    def multiply(step, carry):
        top = pl.multiple_of(step * tile, ROW_TILE)
        product = (
            lax.dot_general(
                rows[pl.ds(LEAD_MODES + top, tile), :],
                cols[pl.ds(LEAD_MODES, col_block + target_block), :],
                (((1,), (1,)), ((), ())),
                preferred_element_type=jnp.float32,
            )
            / total
        )
        shape = (tile, col_block)
        row = time_pos * row_block + top + lax.broadcasted_iota(jnp.int32, shape, 0)
        column = space_pos * col_block + lax.broadcasted_iota(jnp.int32, shape, 1)
        gram_ref[pl.ds(top, tile), :] = product[:, 0:col_block] + jnp.where(
            row == column, RIDGE_WEIGHT, 0.0
        )
        side[pl.ds(top, tile), :] = product[:, col_block:]
        return carry

    lax.fori_loop(0, row_block // tile, multiply, 0)
    rhs_ref[...] = side[...].T


def gram_blocks(pieces, n_time, n_space):
    half, modes, quarter = pieces[0].shape
    snaps = QUAD * quarter
    features = modes + 2 * LEAD_MODES * LEAD_MODES
    row_block, col_block, target_block = features // n_time, features // n_space, modes // n_space
    total = n_time * snaps
    here = jnp.stack([lax.axis_index("tm"), lax.axis_index("space")]).astype(jnp.int32)
    vmem = pl.BlockSpec(memory_space=pltpu.VMEM)
    gram, rhs = pl.pallas_call(
        functools.partial(
            gram_kernel, (n_time, snaps, modes, row_block, col_block, target_block)
        ),
        out_shape=(
            jax.ShapeDtypeStruct((row_block, col_block), jnp.float32),
            jax.ShapeDtypeStruct((target_block, row_block), jnp.float32),
        ),
        in_specs=[pl.BlockSpec(memory_space=pltpu.SMEM)] + [vmem] * (2 * QUAD),
        out_specs=(vmem, vmem),
        scratch_shapes=[
            pltpu.VMEM((modes, total), jnp.bfloat16),
            pltpu.VMEM((2, LEAD_MODES, total), jnp.bfloat16),
            pltpu.VMEM((LEAD_MODES, total), jnp.float32),
            pltpu.VMEM((row_block + 2 * LEAD_MODES, total), jnp.bfloat16),
            pltpu.VMEM((col_block + 2 * LEAD_MODES + target_block, total), jnp.bfloat16),
            pltpu.VMEM((row_block, target_block), jnp.float32),
        ],
        compiler_params=pltpu.CompilerParams(vmem_limit_bytes=56 * 2**20),
    )(here, *pieces)
    return gram, rhs.T


def rounded(value):
    high = lax.reduce_precision(value, 8, 7)
    left = value[0:LEAD_MODES] - high[0:LEAD_MODES]
    return jnp.concatenate([high, left], axis=0).astype(jnp.bfloat16)


def restored(value):
    modes = value.shape[0] - LEAD_MODES
    whole = value[0:modes].astype(jnp.float32)
    left = value[modes:].astype(jnp.float32)
    return jnp.concatenate([whole[0:LEAD_MODES] + left, whole[LEAD_MODES:]], axis=0)


def joined(value, axis, bit):
    return jnp.concatenate([value, swap(value, axis, bit)], axis=0)


def per_device(snapshots, modes):
    n_space, n_time = lax.axis_size("space"), lax.axis_size("tm")
    partial_sums = lax.dot_general(
        modes, snapshots, (((0,), (0,)), ((), ())), preferred_element_type=jnp.float32
    )
    snaps = partial_sums.shape[1]
    quarter = snaps // QUAD
    place = lax.rem(lax.axis_index("space"), QUAD)

    def quarter_of(j):
        start = jnp.bitwise_xor(place, j) * quarter
        return lax.dynamic_slice_in_dim(partial_sums, start, quarter, 1)

    arrived = [swap(rounded(quarter_of(j)), "space", j) for j in range(1, QUAD)]
    mine = quarter_of(0)
    for part in arrived:
        mine = mine + restored(part)
    for bit in bits_of(n_space)[2:]:
        sent = rounded(mine)
        mine = restored(sent) + restored(swap(sent, "space", bit))
    mine = mine.astype(jnp.bfloat16)[None]
    for bit in bits_of(n_time)[1:]:
        mine = joined(mine, "tm", bit)
    pieces = [mine] + [swap(mine, "space", j) for j in range(1, QUAD)]
    pieces = pieces + [swap(piece, "tm", 1) for piece in pieces]
    return gram_blocks(pieces, n_time, n_space)


def solution(mesh):
    in_specs = (P("space", "tm"), P("space", None))
    out_specs = (P("tm", "space"), P("tm", "space"))
    return jax.shard_map(
        per_device, mesh=mesh, in_specs=in_specs, out_specs=out_specs, check_vma=False
    )
```

time: 46.7 us -> 47.9 us (1.026)
  waiting for transfers between devices: 7.52 us -> 15.9 us
  starting transfers between devices: 19.5 us -> 12.4 us
  local copies, waits for them, and re-layouts: 1.21 us -> 0.71 us
    ppermute x17 -> x12, waiting for transfers between devices: 7.52 us -> 15.9 us  [swap(): return lax.ppermute(value, axis, [(i, i ^ bit) for i in range(count)])]
    ppermute x17 -> x12, starting transfers between devices: 19.5 us -> 12.4 us  [swap(): return lax.ppermute(value, axis, [(i, i ^ bit) for i in range(count)])]
    unnamed x20 -> x16, local copies, waits for them, and re-layouts: 1.12 us -> 0.67 us
  transfers between devices with their start and end apart: 17 -> 12, of which waited for: 10 -> 8; matrix products, arithmetic and copies ran while one was open for 2% -> 1% of each run, Pallas kernels for 0% -> 0%
where the time goes in v3:
time: 47.9 us; the launch traced here: 47.5 us
  waiting for transfers between devices  15.9 us (33%)
  starting transfers between devices  12.4 us (26%)
  Pallas kernels  9.47 us (20%)
  matrix products  7.22 us (15%)
  other arithmetic  0.91 us (2%)
  between operations  0.91 us (2%)
  local copies, waits for them, and re-layouts  0.71 us (1%)
    ppermute x12, waiting for transfers between devices, swap(): return lax.ppermute(value, axis, [(i, i ^ bit) for i in range(count)])  15.9 us
    ppermute x12, starting transfers between devices, swap(): return lax.ppermute(value, axis, [(i, i ^ bit) for i in range(count)])  12.4 us
    pallas_call x1, Pallas kernels, gram_blocks(): pl.pallas_call(functools.partial(gram_kernel, (n_time, snaps, modes, row_...  9.47 us
    dot_general x1, matrix products, per_device(): lax.dot_general(modes, snapshots, (((0,), (0,)), ((), ())), preferred_ele...  7.22 us
  transfers between devices with their start and end apart: 12, of which 8 were waited for; matrix products, arithmetic and copies ran while one was open for 1% of the time, Pallas kernels for 0%

profile of v3, /device:TPU:0, one launch (start us, length us, event | category | flops | bytes accessed | tf_op | source)
XLA Modules:
  0.0 47.5 jit_solution(7287263196236601818)
XLA Ops:
  0.7 7.2 %fusion.16 = f32[256,512]{1,0:T(8,128)S(1)} fusion(bf16[10240,256]{1,0:T(8,128)(2,1)} %param.3, bf16[10240,512]{1,0:T(8,128)(2,1)} %param.2), kind=kOutput, calls=%fused_computation.41 | convolution fusion | flops 2684354560 | bytes 16252928 | tf_op jit(solution)/shard_map/dot_general | solution.py:152
  7.9 0.1 fusion.15
  8.0 3.1 %collective-permute-start.1 = (bf16[304,128]{1,0:T(8,128)(2,1)S(1)}, bf16[304,128]{1,0:T(8,128)(2,1)S(1)}, u32[]{:S(2)}, u32[]{:S(2)}) collective-permute-start(bf16[304,128]{1,0:T(8,128)(2,1)S(1)} %pad_maximum_fusion.2), channel_id=1, source_target_pairs={{0,8},{4,12},{8,0},{12,4},{16,24},{20,28},{24,16},{28,20},{1,9},{5... | collective-permute-start | bytes 233480 | tf_op jit(solution)/shard_map/ppermute | solution.py:18
  11.1 1.5 %collective-permute-start = (bf16[304,128]{1,0:T(8,128)(2,1)S(1)}, bf16[304,128]{1,0:T(8,128)(2,1)S(1)}, u32[]{:S(2)}, u32[]{:S(2)}) collective-permute-start(bf16[304,128]{1,0:T(8,128)(2,1)S(1)} %pad_maximum_fusion.1), channel_id=1, source_target_pairs={{0,4},{4,0},{8,12},{12,8},{16,20},{20,16},{24,28},{28,24},{1,5},{5... | collective-permute-start | bytes 233480 | tf_op jit(solution)/shard_map/ppermute | solution.py:18
  12.6 0.1 collective-permute-start.2
  12.7 3.7 %collective-permute-done = bf16[304,128]{1,0:T(8,128)(2,1)S(1)} collective-permute-done((bf16[304,128]{1,0:T(8,128)(2,1)S(1)}, bf16[304,128]{1,0:T(8,128)(2,1)S(1)}, u32[]{:S(2)}, u32[]{:S(2)}) %collective-permute-start) | collective-permute-done | bytes 77856 | tf_op jit(solution)/shard_map/ppermute | solution.py:18
  16.3 1.6 %collective-permute-done.2 = bf16[304,128]{1,0:T(8,128)(2,1)S(1)} collective-permute-done((bf16[304,128]{1,0:T(8,128)(2,1)S(1)}, bf16[304,128]{1,0:T(8,128)(2,1)S(1)}, u32[]{:S(2)}, u32[]{:S(2)}) %collective-permute-start.2) | collective-permute-done | bytes 77856 | tf_op jit(solution)/shard_map/ppermute | solution.py:18
  17.9 0.0 collective-permute-done.1
  18.0 0.1 fusion.10
  18.1 2.7 %collective-permute-start.3 = (bf16[304,128]{1,0:T(8,128)(2,1)S(1)}, bf16[304,128]{1,0:T(8,128)(2,1)S(1)}, u32[]{:S(2)}, u32[]{:S(2)}) collective-permute-start(bf16[304,128]{1,0:T(8,128)(2,1)S(1)} %pad_maximum_fusion.4), channel_id=1, source_target_pairs={{0,16},{4,20},{8,24},{12,28},{16,0},{20,4},{24,8},{28,12},{1,17},{... | collective-permute-start | bytes 233480 | tf_op jit(solution)/shard_map/ppermute | solution.py:18
  20.8 3.4 %collective-permute-done.3 = bf16[304,128]{1,0:T(8,128)(2,1)S(1)} collective-permute-done((bf16[304,128]{1,0:T(8,128)(2,1)S(1)}, bf16[304,128]{1,0:T(8,128)(2,1)S(1)}, u32[]{:S(2)}, u32[]{:S(2)}) %collective-permute-start.3) | collective-permute-done | bytes 77856 | tf_op jit(solution)/shard_map/ppermute | solution.py:18
  24.3 1.6 %collective-permute-start.4 = (bf16[1,256,128]{2,1,0:T(8,128)(2,1)S(1)}, bf16[1,256,128]{2,1,0:T(8,128)(2,1)S(1)}, u32[]{:S(2)}, u32[]{:S(2)}) collective-permute-start(bf16[1,256,128]{2,1,0:T(8,128)(2,1)S(1)} %fusion.2), channel_id=1, source_target_pairs={{0,2},{1,3},{2,0},{3,1},{4,6},{5,7},{6,4},{7,5},{8,10},{9,11},{10,... | collective-permute-start | bytes 196616 | tf_op jit(solution)/shard_map/ppermute | solution.py:18
  25.9 2.7 %collective-permute-done.4 = bf16[1,256,128]{2,1,0:T(8,128)(2,1)S(1)} collective-permute-done((bf16[1,256,128]{2,1,0:T(8,128)(2,1)S(1)}, bf16[1,256,128]{2,1,0:T(8,128)(2,1)S(1)}, u32[]{:S(2)}, u32[]{:S(2)}) %collective-permute-start.4) | collective-permute-done | bytes 65568 | tf_op jit(solution)/shard_map/ppermute | solution.py:18
  28.7 0.0 copy-start
  28.7 0.1 collective-permute-start.7
  28.7 2.1 %collective-permute-start.6 = (bf16[2,256,128]{2,1,0:T(8,128)(2,1)S(1)}, bf16[2,256,128]{2,1,0:T(8,128)(2,1)S(1)}, u32[]{:S(2)}, u32[]{:S(2)}) collective-permute-start(bf16[2,256,128]{2,1,0:T(8,128)(2,1)S(1)} %pad_maximum_fusion.refs_0_), channel_id=1, source_target_pairs={{0,8},{4,12},{8,0},{12,4},{16,24},{20,28},{24,16},{28,20},{1,9},{5... | collective-permute-start | bytes 393224 | tf_op jit(solution)/shard_map/ppermute | solution.py:18
  30.8 1.4 %collective-permute-start.5 = (bf16[2,256,128]{2,1,0:T(8,128)(2,1)S(1)}, bf16[2,256,128]{2,1,0:T(8,128)(2,1)S(1)}, u32[]{:S(2)}, u32[]{:S(2)}) collective-permute-start(bf16[2,256,128]{2,1,0:T(8,128)(2,1)S(1)} %pad_maximum_fusion.refs_0_), channel_id=1, source_target_pairs={{0,4},{4,0},{8,12},{12,8},{16,20},{20,16},{24,28},{28,24},{1,5},{5... | collective-permute-start | bytes 393224 | tf_op jit(solution)/shard_map/ppermute | solution.py:18
  32.2 0.0 collective-permute-start.8
  32.2 2.4 %collective-permute-done.7.refs_3_ = bf16[2,256,128]{2,1,0:T(8,128)(2,1)S(1)} collective-permute-done((bf16[2,256,128]{2,1,0:T(8,128)(2,1)S(1)}, bf16[2,256,128]{2,1,0:T(8,128)(2,1)S(1)}, u32[]{:S(2)}, u32[]{:S(2)}) %collective-permute-start.7) | collective-permute-done | bytes 131104 | tf_op jit(solution)/shard_map/ppermute | solution.py:18
  34.6 0.0 copy-start.1
  34.6 0.0 collective-permute-start.11
  34.6 0.5 %collective-permute-done.6.refs_2_ = bf16[2,256,128]{2,1,0:T(8,128)(2,1)S(1)} collective-permute-done((bf16[2,256,128]{2,1,0:T(8,128)(2,1)S(1)}, bf16[2,256,128]{2,1,0:T(8,128)(2,1)S(1)}, u32[]{:S(2)}, u32[]{:S(2)}) %collective-permute-start.6) | collective-permute-done | bytes 131104 | tf_op jit(solution)/shard_map/ppermute | solution.py:18
  35.2 0.0 copy-start.2
  35.2 0.0 collective-permute-start.10
  35.2 0.8 %collective-permute-done.5.refs_1_ = bf16[2,256,128]{2,1,0:T(8,128)(2,1)S(1)} collective-permute-done((bf16[2,256,128]{2,1,0:T(8,128)(2,1)S(1)}, bf16[2,256,128]{2,1,0:T(8,128)(2,1)S(1)}, u32[]{:S(2)}, u32[]{:S(2)}) %collective-permute-start.5) | collective-permute-done | bytes 131104 | tf_op jit(solution)/shard_map/ppermute | solution.py:18
  36.0 0.0 copy-start.3
  36.0 0.0 collective-permute-start.9
  36.0 0.6 %pad_add_fusion.pos_ref = s32[2]{0:T(128)} fusion(s32[1]{0:T(128)} %bitcast.1, s32[1]{0:T(128)} %bitcast), kind=kLoop, calls=%fused_computation.34 | loop fusion | flops 2 | bytes 16 | tf_op jit(solution)/shard_map/stack | solution.py:108
  36.6 0.0 collective-permute-done.8.refs_4_
  36.6 0.0 copy-start.4
  36.6 0.0 collective-permute-done.11.refs_7_
  36.6 0.0 copy-start.5
  36.6 0.0 collective-permute-done.10.refs_6_
  36.6 0.0 copy-start.6
  36.6 0.7 %collective-permute-done.9.refs_5_ = bf16[2,256,128]{2,1,0:T(8,128)(2,1)S(1)} collective-permute-done((bf16[2,256,128]{2,1,0:T(8,128)(2,1)S(1)}, bf16[2,256,128]{2,1,0:T(8,128)(2,1)S(1)}, u32[]{:S(2)}, u32[]{:S(2)}) %collective-permute-start.9) | collective-permute-done | bytes 131104 | tf_op jit(solution)/shard_map/ppermute | solution.py:18
  37.3 0.0 copy-done
  37.4 0.0 copy-done.1
  37.4 0.0 copy-done.2
  37.4 0.0 copy-done.3
  37.4 0.0 copy-done.4
  37.4 0.0 copy-done.5
  37.4 0.0 copy-done.6
  37.4 0.0 copy-start.7
  37.4 0.6 %copy-done.7 = bf16[2,256,128]{2,1,0:T(8,128)(2,1)} copy-done((bf16[2,256,128]{2,1,0:T(8,128)(2,1)}, bf16[2,256,128]{2,1,0:T(8,128)(2,1)S(1)}, u32[]{:S(2)}) %copy-start.7) | copy-done | bytes 131096
  38.0 9.5 %shard_map.41 = (f32[1216,608]{1,0:T(8,128)}, f32[32,1216]{1,0:T(8,128)}) custom-call(s32[2]{0:T(128)} %pad_add_fusion.pos_ref, bf16[2,256,128]{2,1,0:T(8,128)(2,1)} %copy-done, bf16[2,256,128]{2,1,0:T(8,128)(2,1)} %copy-done.3, bf16[2,256,128]{2,1,0:T(8,128)(2,1)} %copy-done.2, bf16[2,256,128]{2,1,0:T(8,128)(2,1)} %copy-done.1, ...), custom_call_target="tpu_custom_call" | custom-call | tf_op jit(solution)/shard_map/pallas_call | solution.py:110
  (22 shorter events, 0.2 us)
Async XLA Ops:
  8.0 9.9 %collective-permute-start.1 = (bf16[304,128]{1,0:T(8,128)(2,1)S(1)}, bf16[304,128]{1,0:T(8,128)(2,1)S(1)}, u32[]{:S(2)}, u32[]{:S(2)}) collective-permute-start(bf16[304,128]{1,0:T(8,128)(2,1)S(1)} %pad_maximum_fusion.2), channel_id=1, source_target_pairs={{0,8},{4,12},{8,0},{12,4},{16,24},{20,28},{24,16},{28,20},{1,9},{5... | collective-permute-start | bytes 233480 | tf_op jit(solution)/shard_map/ppermute | solution.py:18
  11.1 5.2 %collective-permute-start = (bf16[304,128]{1,0:T(8,128)(2,1)S(1)}, bf16[304,128]{1,0:T(8,128)(2,1)S(1)}, u32[]{:S(2)}, u32[]{:S(2)}) collective-permute-start(bf16[304,128]{1,0:T(8,128)(2,1)S(1)} %pad_maximum_fusion.1), channel_id=1, source_target_pairs={{0,4},{4,0},{8,12},{12,8},{16,20},{20,16},{24,28},{28,24},{1,5},{5... | collective-permute-start | bytes 233480 | tf_op jit(solution)/shard_map/ppermute | solution.py:18
  12.6 5.3 %collective-permute-start.2 = (bf16[304,128]{1,0:T(8,128)(2,1)S(1)}, bf16[304,128]{1,0:T(8,128)(2,1)S(1)}, u32[]{:S(2)}, u32[]{:S(2)}) collective-permute-start(bf16[304,128]{1,0:T(8,128)(2,1)S(1)} %pad_maximum_fusion.3), channel_id=1, source_target_pairs={{0,12},{4,8},{8,4},{12,0},{16,28},{20,24},{24,20},{28,16},{1,13},{... | collective-permute-start | bytes 233480 | tf_op jit(solution)/shard_map/ppermute | solution.py:18
  18.1 6.1 %collective-permute-start.3 = (bf16[304,128]{1,0:T(8,128)(2,1)S(1)}, bf16[304,128]{1,0:T(8,128)(2,1)S(1)}, u32[]{:S(2)}, u32[]{:S(2)}) collective-permute-start(bf16[304,128]{1,0:T(8,128)(2,1)S(1)} %pad_maximum_fusion.4), channel_id=1, source_target_pairs={{0,16},{4,20},{8,24},{12,28},{16,0},{20,4},{24,8},{28,12},{1,17},{... | collective-permute-start | bytes 233480 | tf_op jit(solution)/shard_map/ppermute | solution.py:18
  24.3 4.3 %collective-permute-start.4 = (bf16[1,256,128]{2,1,0:T(8,128)(2,1)S(1)}, bf16[1,256,128]{2,1,0:T(8,128)(2,1)S(1)}, u32[]{:S(2)}, u32[]{:S(2)}) collective-permute-start(bf16[1,256,128]{2,1,0:T(8,128)(2,1)S(1)} %fusion.2), channel_id=1, source_target_pairs={{0,2},{1,3},{2,0},{3,1},{4,6},{5,7},{6,4},{7,5},{8,10},{9,11},{10,... | collective-permute-start | bytes 196616 | tf_op jit(solution)/shard_map/ppermute | solution.py:18
  28.7 8.7 %copy-start = (bf16[2,256,128]{2,1,0:T(8,128)(2,1)}, bf16[2,256,128]{2,1,0:T(8,128)(2,1)S(1)}, u32[]{:S(2)}) copy-start(bf16[2,256,128]{2,1,0:T(8,128)(2,1)S(1)} %pad_maximum_fusion.refs_0_) | copy-start | bytes 393220
  28.7 6.0 %collective-permute-start.7 = (bf16[2,256,128]{2,1,0:T(8,128)(2,1)S(1)}, bf16[2,256,128]{2,1,0:T(8,128)(2,1)S(1)}, u32[]{:S(2)}, u32[]{:S(2)}) collective-permute-start(bf16[2,256,128]{2,1,0:T(8,128)(2,1)S(1)} %pad_maximum_fusion.refs_0_), channel_id=1, source_target_pairs={{0,12},{4,8},{8,4},{12,0},{16,28},{20,24},{24,20},{28,16},{1,13},{... | collective-permute-start | bytes 393224 | tf_op jit(solution)/shard_map/ppermute | solution.py:18
  28.7 6.4 %collective-permute-start.6 = (bf16[2,256,128]{2,1,0:T(8,128)(2,1)S(1)}, bf16[2,256,128]{2,1,0:T(8,128)(2,1)S(1)}, u32[]{:S(2)}, u32[]{:S(2)}) collective-permute-start(bf16[2,256,128]{2,1,0:T(8,128)(2,1)S(1)} %pad_maximum_fusion.refs_0_), channel_id=1, source_target_pairs={{0,8},{4,12},{8,0},{12,4},{16,24},{20,28},{24,16},{28,20},{1,9},{5... | collective-permute-start | bytes 393224 | tf_op jit(solution)/shard_map/ppermute | solution.py:18
  30.8 5.2 %collective-permute-start.5 = (bf16[2,256,128]{2,1,0:T(8,128)(2,1)S(1)}, bf16[2,256,128]{2,1,0:T(8,128)(2,1)S(1)}, u32[]{:S(2)}, u32[]{:S(2)}) collective-permute-start(bf16[2,256,128]{2,1,0:T(8,128)(2,1)S(1)} %pad_maximum_fusion.refs_0_), channel_id=1, source_target_pairs={{0,4},{4,0},{8,12},{12,8},{16,20},{20,16},{24,28},{28,24},{1,5},{5... | collective-permute-start | bytes 393224 | tf_op jit(solution)/shard_map/ppermute | solution.py:18
  32.2 4.4 %collective-permute-start.8 = (bf16[2,256,128]{2,1,0:T(8,128)(2,1)S(1)}, bf16[2,256,128]{2,1,0:T(8,128)(2,1)S(1)}, u32[]{:S(2)}, u32[]{:S(2)}) collective-permute-start(bf16[2,256,128]{2,1,0:T(8,128)(2,1)S(1)} %pad_maximum_fusion.refs_0_), channel_id=1, source_target_pairs={{0,1},{1,0},{2,3},{3,2},{4,5},{5,4},{6,7},{7,6},{8,9},{9,8},{10,11... | collective-permute-start | bytes 393224 | tf_op jit(solution)/shard_map/ppermute | solution.py:18
  34.6 2.7 %copy-start.1 = (bf16[2,256,128]{2,1,0:T(8,128)(2,1)}, bf16[2,256,128]{2,1,0:T(8,128)(2,1)S(1)}, u32[]{:S(2)}) copy-start(bf16[2,256,128]{2,1,0:T(8,128)(2,1)S(1)} %collective-permute-done.7.refs_3_) | copy-start | bytes 393220
  34.6 2.0 %collective-permute-start.11 = (bf16[2,256,128]{2,1,0:T(8,128)(2,1)S(1)}, bf16[2,256,128]{2,1,0:T(8,128)(2,1)S(1)}, u32[]{:S(2)}, u32[]{:S(2)}) collective-permute-start(bf16[2,256,128]{2,1,0:T(8,128)(2,1)S(1)} %collective-permute-done.7.refs_3_), channel_id=1, source_target_pairs={{0,1},{1,0},{2,3},{3,2},{4,5},{5,4},{6,7},{7,6},{8,9},{9,8},{10,11... | collective-permute-start | bytes 393224 | tf_op jit(solution)/shard_map/ppermute | solution.py:18
  35.2 2.2 %copy-start.2 = (bf16[2,256,128]{2,1,0:T(8,128)(2,1)}, bf16[2,256,128]{2,1,0:T(8,128)(2,1)S(1)}, u32[]{:S(2)}) copy-start(bf16[2,256,128]{2,1,0:T(8,128)(2,1)S(1)} %collective-permute-done.6.refs_2_) | copy-start | bytes 393220
  35.2 1.5 %collective-permute-start.10 = (bf16[2,256,128]{2,1,0:T(8,128)(2,1)S(1)}, bf16[2,256,128]{2,1,0:T(8,128)(2,1)S(1)}, u32[]{:S(2)}, u32[]{:S(2)}) collective-permute-start(bf16[2,256,128]{2,1,0:T(8,128)(2,1)S(1)} %collective-permute-done.6.refs_2_), channel_id=1, source_target_pairs={{0,1},{1,0},{2,3},{3,2},{4,5},{5,4},{6,7},{7,6},{8,9},{9,8},{10,11... | collective-permute-start | bytes 393224 | tf_op jit(solution)/shard_map/ppermute | solution.py:18
  36.0 1.4 %copy-start.3 = (bf16[2,256,128]{2,1,0:T(8,128)(2,1)}, bf16[2,256,128]{2,1,0:T(8,128)(2,1)S(1)}, u32[]{:S(2)}) copy-start(bf16[2,256,128]{2,1,0:T(8,128)(2,1)S(1)} %collective-permute-done.5.refs_1_) | copy-start | bytes 393220
  36.0 1.3 %collective-permute-start.9 = (bf16[2,256,128]{2,1,0:T(8,128)(2,1)S(1)}, bf16[2,256,128]{2,1,0:T(8,128)(2,1)S(1)}, u32[]{:S(2)}, u32[]{:S(2)}) collective-permute-start(bf16[2,256,128]{2,1,0:T(8,128)(2,1)S(1)} %collective-permute-done.5.refs_1_), channel_id=1, source_target_pairs={{0,1},{1,0},{2,3},{3,2},{4,5},{5,4},{6,7},{7,6},{8,9},{9,8},{10,11... | collective-permute-start | bytes 393224 | tf_op jit(solution)/shard_map/ppermute | solution.py:18
  36.6 0.8 %copy-start.4 = (bf16[2,256,128]{2,1,0:T(8,128)(2,1)}, bf16[2,256,128]{2,1,0:T(8,128)(2,1)S(1)}, u32[]{:S(2)}) copy-start(bf16[2,256,128]{2,1,0:T(8,128)(2,1)S(1)} %collective-permute-done.8.refs_4_) | copy-start | bytes 393220
  36.6 0.8 %copy-start.5 = (bf16[2,256,128]{2,1,0:T(8,128)(2,1)}, bf16[2,256,128]{2,1,0:T(8,128)(2,1)S(1)}, u32[]{:S(2)}) copy-start(bf16[2,256,128]{2,1,0:T(8,128)(2,1)S(1)} %collective-permute-done.11.refs_7_) | copy-start | bytes 393220
  36.6 0.8 %copy-start.6 = (bf16[2,256,128]{2,1,0:T(8,128)(2,1)}, bf16[2,256,128]{2,1,0:T(8,128)(2,1)S(1)}, u32[]{:S(2)}) copy-start(bf16[2,256,128]{2,1,0:T(8,128)(2,1)S(1)} %collective-permute-done.10.refs_6_) | copy-start | bytes 393220
  37.4 0.6 %copy-start.7 = (bf16[2,256,128]{2,1,0:T(8,128)(2,1)}, bf16[2,256,128]{2,1,0:T(8,128)(2,1)S(1)}, u32[]{:S(2)}) copy-start(bf16[2,256,128]{2,1,0:T(8,128)(2,1)S(1)} %collective-permute-done.9.refs_5_) | copy-start | bytes 393220

commit v4 on v3

--- a/solution.py
+++ b/solution.py
@@ -11,6 +11,7 @@
 RIDGE_WEIGHT = 0.05
 ROW_TILE = 16
 QUAD = 4
+CUTS = (0, 112)
 
 
 def swap(value, axis, bit):
@@ -25,8 +26,9 @@
 def gram_kernel(sizes, pos_ref, *refs):
     n_time, snaps, modes, row_block, col_block, target_block = sizes
     half, quarter = n_time // 2, snaps // QUAD
-    pieces, (gram_ref, rhs_ref) = refs[0 : 2 * QUAD], refs[2 * QUAD : 2 * QUAD + 2]
-    coeffs, delayed, head, rows, cols, side = refs[2 * QUAD + 2 :]
+    count = 2 * QUAD * len(CUTS)
+    pieces, (gram_ref, rhs_ref) = refs[0:count], refs[count : count + 2]
+    coeffs, delayed, head, rows, cols, side = refs[count + 2 :]
     total = n_time * snaps
     time_pos, space_pos = pos_ref[0], pos_ref[1]
     place = lax.rem(space_pos, QUAD)
@@ -36,9 +38,10 @@
             block = jnp.bitwise_xor(time_pos, 2 * k + other)
             for j in range(QUAD):
                 at = block * snaps + jnp.bitwise_xor(place, j) * quarter
-                coeffs[:, pl.ds(pl.multiple_of(at, quarter), quarter)] = pieces[
-                    other * QUAD + j
-                ][k]
+                at = pl.ds(pl.multiple_of(at, quarter), quarter)
+                for cut, first in enumerate(CUTS):
+                    piece = pieces[(cut * 2 + other) * QUAD + j]
+                    coeffs[first : first + piece.shape[1], at] = piece[k]
     head[...] = coeffs[0:LEAD_MODES, :].astype(jnp.float32)
     for delay in (1, 2):
         gap = delay * snaps
@@ -100,7 +103,8 @@
 
 
 def gram_blocks(pieces, n_time, n_space):
-    half, modes, quarter = pieces[0].shape
+    quarter = pieces[0].shape[2]
+    modes = sum(piece.shape[1] for piece in pieces) // (2 * QUAD)
     snaps = QUAD * quarter
     features = modes + 2 * LEAD_MODES * LEAD_MODES
     row_block, col_block, target_block = features // n_time, features // n_space, modes // n_space
@@ -115,7 +119,7 @@
             jax.ShapeDtypeStruct((row_block, col_block), jnp.float32),
             jax.ShapeDtypeStruct((target_block, row_block), jnp.float32),
         ),
-        in_specs=[pl.BlockSpec(memory_space=pltpu.SMEM)] + [vmem] * (2 * QUAD),
+        in_specs=[pl.BlockSpec(memory_space=pltpu.SMEM)] + [vmem] * len(pieces),
         out_specs=(vmem, vmem),
         scratch_shapes=[
             pltpu.VMEM((modes, total), jnp.bfloat16),
@@ -130,49 +134,55 @@
     return gram, rhs.T
 
 
-def rounded(value):
+def rounded(value, lead):
     high = lax.reduce_precision(value, 8, 7)
-    left = value[0:LEAD_MODES] - high[0:LEAD_MODES]
+    left = value[0:lead] - high[0:lead]
     return jnp.concatenate([high, left], axis=0).astype(jnp.bfloat16)
 
 
-def restored(value):
-    modes = value.shape[0] - LEAD_MODES
+def restored(value, lead):
+    modes = value.shape[0] - lead
     whole = value[0:modes].astype(jnp.float32)
     left = value[modes:].astype(jnp.float32)
-    return jnp.concatenate([whole[0:LEAD_MODES] + left, whole[LEAD_MODES:]], axis=0)
+    return jnp.concatenate([whole[0:lead] + left, whole[lead:]], axis=0)
 
 
 def joined(value, axis, bit):
     return jnp.concatenate([value, swap(value, axis, bit)], axis=0)
 
 
-def per_device(snapshots, modes):
+def gathered(partial_sums, lead):
     n_space, n_time = lax.axis_size("space"), lax.axis_size("tm")
-    partial_sums = lax.dot_general(
-        modes, snapshots, (((0,), (0,)), ((), ())), preferred_element_type=jnp.float32
-    )
-    snaps = partial_sums.shape[1]
-    quarter = snaps // QUAD
+    quarter = partial_sums.shape[1] // QUAD
     place = lax.rem(lax.axis_index("space"), QUAD)
 
     def quarter_of(j):
         start = jnp.bitwise_xor(place, j) * quarter
         return lax.dynamic_slice_in_dim(partial_sums, start, quarter, 1)
 
-    arrived = [swap(rounded(quarter_of(j)), "space", j) for j in range(1, QUAD)]
+    arrived = [swap(rounded(quarter_of(j), lead), "space", j) for j in range(1, QUAD)]
     mine = quarter_of(0)
     for part in arrived:
-        mine = mine + restored(part)
+        mine = mine + restored(part, lead)
     for bit in bits_of(n_space)[2:]:
-        sent = rounded(mine)
-        mine = restored(sent) + restored(swap(sent, "space", bit))
+        sent = rounded(mine, lead)
+        mine = restored(sent, lead) + restored(swap(sent, "space", bit), lead)
     mine = mine.astype(jnp.bfloat16)[None]
     for bit in bits_of(n_time)[1:]:
         mine = joined(mine, "tm", bit)
     pieces = [mine] + [swap(mine, "space", j) for j in range(1, QUAD)]
-    pieces = pieces + [swap(piece, "tm", 1) for piece in pieces]
-    return gram_blocks(pieces, n_time, n_space)
+    return pieces + [swap(piece, "tm", 1) for piece in pieces]
+
+
+def per_device(snapshots, modes):
+    partial_sums = lax.dot_general(
+        modes, snapshots, (((0,), (0,)), ((), ())), preferred_element_type=jnp.float32
+    )
+    ends = CUTS[1:] + (modes.shape[1],)
+    pieces = []
+    for first, end in zip(CUTS, ends):
+        pieces += gathered(partial_sums[first:end], LEAD_MODES if first == 0 else 0)
+    return gram_blocks(pieces, lax.axis_size("tm"), lax.axis_size("space"))
 
 
 def solution(mesh):

time: 47.9 us -> 53.2 us (1.11)
  starting transfers between devices: 12.4 us -> 24.9 us
  waiting for transfers between devices: 15.9 us -> 8.35 us
    ppermute x12 -> x24, starting transfers between devices: 12.4 us -> 24.9 us  [swap(): return lax.ppermute(value, axis, [(i, i ^ bit) for i in range(count)])]
    ppermute x12 -> x24, waiting for transfers between devices: 15.9 us -> 8.35 us  [swap(): return lax.ppermute(value, axis, [(i, i ^ bit) for i in range(count)])]
  transfers between devices with their start and end apart: 12 -> 24, of which waited for: 8 -> 9; matrix products, arithmetic and copies ran while one was open for 1% -> 2% of each run, Pallas kernels for 0% -> 0%
where the time goes in v4:
time: 53.2 us; the launch traced here: 53 us
  starting transfers between devices  24.9 us (47%)
  Pallas kernels  9.49 us (18%)
  waiting for transfers between devices  8.35 us (16%)
  matrix products  7.22 us (14%)
  local copies, waits for them, and re-layouts  1.12 us (2%)
  between operations  1.04 us (2%)
  other arithmetic  0.93 us (2%)
    ppermute x24, starting transfers between devices, swap(): return lax.ppermute(value, axis, [(i, i ^ bit) for i in range(count)])  24.9 us
    pallas_call x1, Pallas kernels, gram_blocks(): pl.pallas_call(functools.partial(gram_kernel, (n_time, snaps, modes, row_...  9.49 us
    ppermute x24, waiting for transfers between devices, swap(): return lax.ppermute(value, axis, [(i, i ^ bit) for i in range(count)])  8.35 us
    dot_general x1, matrix products, per_device(): lax.dot_general(modes, snapshots, (((0,), (0,)), ((), ())), preferred_ele...  7.22 us
  transfers between devices with their start and end apart: 24, of which 9 were waited for; matrix products, arithmetic and copies ran while one was open for 2% of the time, Pallas kernels for 0%

profile of v4, /device:TPU:0, one launch (start us, length us, event | category | flops | bytes accessed | tf_op | source)
XLA Modules:
  0.0 53.0 jit_solution(3530268098362026438)
XLA Ops:
  0.7 7.2 %fusion.17 = f32[256,512]{1,0:T(8,128)S(1)} fusion(bf16[10240,256]{1,0:T(8,128)(2,1)} %param.3, bf16[10240,512]{1,0:T(8,128)(2,1)} %param.2), kind=kOutput, calls=%fused_computation.48 | convolution fusion | flops 2684354560 | bytes 16252928 | tf_op jit(solution)/shard_map/dot_general | solution.py:178
  8.0 3.0 %collective-permute-start.12 = (bf16[144,128]{1,0:T(8,128)(2,1)S(1)}, bf16[144,128]{1,0:T(8,128)(2,1)S(1)}, u32[]{:S(2)}, u32[]{:S(2)}) collective-permute-start(bf16[144,128]{1,0:T(8,128)(2,1)S(1)} %get-tuple-element.18), channel_id=1, source_target_pairs={{0,4},{4,0},{8,12},{12,8},{16,20},{20,16},{24,28},{28,24},{1,5},{5... | collective-permute-start | bytes 110600 | tf_op jit(solution)/shard_map/ppermute | solution.py:19
  11.0 1.5 %collective-permute-start.14 = (bf16[144,128]{1,0:T(8,128)(2,1)S(1)}, bf16[144,128]{1,0:T(8,128)(2,1)S(1)}, u32[]{:S(2)}, u32[]{:S(2)}) collective-permute-start(bf16[144,128]{1,0:T(8,128)(2,1)S(1)} %get-tuple-element.19), channel_id=1, source_target_pairs={{0,12},{4,8},{8,4},{12,0},{16,28},{20,24},{24,20},{28,16},{1,13},{... | collective-permute-start | bytes 110600 | tf_op jit(solution)/shard_map/ppermute | solution.py:19
  12.5 0.0 collective-permute-start.13
  12.7 2.1 %collective-permute-start.1 = (bf16[160,128]{1,0:T(8,128)(2,1)S(1)}, bf16[160,128]{1,0:T(8,128)(2,1)S(1)}, u32[]{:S(2)}, u32[]{:S(2)}) collective-permute-start(bf16[160,128]{1,0:T(8,128)(2,1)S(1)} %pad_maximum_fusion.3), channel_id=1, source_target_pairs={{0,8},{4,12},{8,0},{12,4},{16,24},{20,28},{24,16},{28,20},{1,9},{5... | collective-permute-start | bytes 122888 | tf_op jit(solution)/shard_map/ppermute | solution.py:19
  14.7 1.4 %collective-permute-start.2 = (bf16[160,128]{1,0:T(8,128)(2,1)S(1)}, bf16[160,128]{1,0:T(8,128)(2,1)S(1)}, u32[]{:S(2)}, u32[]{:S(2)}) collective-permute-start(bf16[160,128]{1,0:T(8,128)(2,1)S(1)} %pad_maximum_fusion.4), channel_id=1, source_target_pairs={{0,12},{4,8},{8,4},{12,0},{16,28},{20,24},{24,20},{28,16},{1,13},{... | collective-permute-start | bytes 122888 | tf_op jit(solution)/shard_map/ppermute | solution.py:19
  16.1 0.0 collective-permute-done.12
  16.1 0.2 collective-permute-start
  16.3 0.0 collective-permute-done.14
  16.3 0.1 collective-permute-done.13
  16.5 2.8 %collective-permute-start.15 = (bf16[144,128]{1,0:T(8,128)(2,1)S(1)}, bf16[144,128]{1,0:T(8,128)(2,1)S(1)}, u32[]{:S(2)}, u32[]{:S(2)}) collective-permute-start(bf16[144,128]{1,0:T(8,128)(2,1)S(1)} %reduce-precision_convert_fusion), channel_id=1, source_target_pairs={{0,16},{4,20},{8,24},{12,28},{16,0},{20,4},{24,8},{28,12},{1,17},{... | collective-permute-start | bytes 110600 | tf_op jit(solution)/shard_map/ppermute | solution.py:19
  19.3 0.8 %collective-permute-done = bf16[160,128]{1,0:T(8,128)(2,1)S(1)} collective-permute-done((bf16[160,128]{1,0:T(8,128)(2,1)S(1)}, bf16[160,128]{1,0:T(8,128)(2,1)S(1)}, u32[]{:S(2)}, u32[]{:S(2)}) %collective-permute-start) | collective-permute-done | bytes 40992 | tf_op jit(solution)/shard_map/ppermute | solution.py:19
  20.3 2.7 %collective-permute-start.3 = (bf16[160,128]{1,0:T(8,128)(2,1)S(1)}, bf16[160,128]{1,0:T(8,128)(2,1)S(1)}, u32[]{:S(2)}, u32[]{:S(2)}) collective-permute-start(bf16[160,128]{1,0:T(8,128)(2,1)S(1)} %pad_maximum_fusion.5), channel_id=1, source_target_pairs={{0,16},{4,20},{8,24},{12,28},{16,0},{20,4},{24,8},{28,12},{1,17},{... | collective-permute-start | bytes 122888 | tf_op jit(solution)/shard_map/ppermute | solution.py:19
  23.0 2.3 %collective-permute-done.3 = bf16[160,128]{1,0:T(8,128)(2,1)S(1)} collective-permute-done((bf16[160,128]{1,0:T(8,128)(2,1)S(1)}, bf16[160,128]{1,0:T(8,128)(2,1)S(1)}, u32[]{:S(2)}, u32[]{:S(2)}) %collective-permute-start.3) | collective-permute-done | bytes 40992 | tf_op jit(solution)/shard_map/ppermute | solution.py:19
  25.3 1.6 %collective-permute-start.4 = (bf16[1,112,128]{2,1,0:T(8,128)(2,1)S(1)}, bf16[1,112,128]{2,1,0:T(8,128)(2,1)S(1)}, u32[]{:S(2)}, u32[]{:S(2)}) collective-permute-start(bf16[1,112,128]{2,1,0:T(8,128)(2,1)S(1)} %fusion.2), channel_id=1, source_target_pairs={{0,2},{1,3},{2,0},{3,1},{4,6},{5,7},{6,4},{7,5},{8,10},{9,11},{10,... | collective-permute-start | bytes 86024 | tf_op jit(solution)/shard_map/ppermute | solution.py:19
  26.9 0.0 collective-permute-done.15
  26.9 0.6 %collective-permute-start.16 = (bf16[1,144,128]{2,1,0:T(8,128)(2,1)S(1)}, bf16[1,144,128]{2,1,0:T(8,128)(2,1)S(1)}, u32[]{:S(2)}, u32[]{:S(2)}) collective-permute-start(bf16[1,144,128]{2,1,0:T(8,128)(2,1)S(1)} %fusion.3), channel_id=1, source_target_pairs={{0,2},{1,3},{2,0},{3,1},{4,6},{5,7},{6,4},{7,5},{8,10},{9,11},{10,... | collective-permute-start | bytes 110600 | tf_op jit(solution)/shard_map/ppermute | solution.py:19
  27.5 1.8 %collective-permute-done.4 = bf16[1,112,128]{2,1,0:T(8,128)(2,1)S(1)} collective-permute-done((bf16[1,112,128]{2,1,0:T(8,128)(2,1)S(1)}, bf16[1,112,128]{2,1,0:T(8,128)(2,1)S(1)}, u32[]{:S(2)}, u32[]{:S(2)}) %collective-permute-start.4) | collective-permute-done | bytes 28704 | tf_op jit(solution)/shard_map/ppermute | solution.py:19
  29.3 0.1 collective-permute-start.8
  29.4 1.8 %collective-permute-start.7 = (bf16[2,112,128]{2,1,0:T(8,128)(2,1)S(1)}, bf16[2,112,128]{2,1,0:T(8,128)(2,1)S(1)}, u32[]{:S(2)}, u32[]{:S(2)}) collective-permute-start(bf16[2,112,128]{2,1,0:T(8,128)(2,1)S(1)} %pad_maximum_fusion.1.refs_0_), channel_id=1, source_target_pairs={{0,12},{4,8},{8,4},{12,0},{16,28},{20,24},{24,20},{28,16},{1,13},{... | collective-permute-start | bytes 172040 | tf_op jit(solution)/shard_map/ppermute | solution.py:19
  31.2 0.7 %collective-permute-start.6 = (bf16[2,112,128]{2,1,0:T(8,128)(2,1)S(1)}, bf16[2,112,128]{2,1,0:T(8,128)(2,1)S(1)}, u32[]{:S(2)}, u32[]{:S(2)}) collective-permute-start(bf16[2,112,128]{2,1,0:T(8,128)(2,1)S(1)} %pad_maximum_fusion.1.refs_0_), channel_id=1, source_target_pairs={{0,8},{4,12},{8,0},{12,4},{16,24},{20,28},{24,16},{28,20},{1,9},{5... | collective-permute-start | bytes 172040 | tf_op jit(solution)/shard_map/ppermute | solution.py:19
  31.9 1.0 %collective-permute-start.5 = (bf16[2,112,128]{2,1,0:T(8,128)(2,1)S(1)}, bf16[2,112,128]{2,1,0:T(8,128)(2,1)S(1)}, u32[]{:S(2)}, u32[]{:S(2)}) collective-permute-start(bf16[2,112,128]{2,1,0:T(8,128)(2,1)S(1)} %pad_maximum_fusion.1.refs_0_), channel_id=1, source_target_pairs={{0,4},{4,0},{8,12},{12,8},{16,20},{20,16},{24,28},{28,24},{1,5},{5... | collective-permute-start | bytes 172040 | tf_op jit(solution)/shard_map/ppermute | solution.py:19
  32.9 0.0 collective-permute-done.16
  33.0 0.1 collective-permute-start.20
  33.1 1.8 %collective-permute-start.19 = (bf16[2,144,128]{2,1,0:T(8,128)(2,1)S(1)}, bf16[2,144,128]{2,1,0:T(8,128)(2,1)S(1)}, u32[]{:S(2)}, u32[]{:S(2)}) collective-permute-start(bf16[2,144,128]{2,1,0:T(8,128)(2,1)S(1)} %pad_maximum_fusion.refs_8_), channel_id=1, source_target_pairs={{0,12},{4,8},{8,4},{12,0},{16,28},{20,24},{24,20},{28,16},{1,13},{... | collective-permute-start | bytes 221192 | tf_op jit(solution)/shard_map/ppermute | solution.py:19
  34.8 0.0 collective-permute-done.7.refs_3_
  34.9 1.8 %collective-permute-start.18 = (bf16[2,144,128]{2,1,0:T(8,128)(2,1)S(1)}, bf16[2,144,128]{2,1,0:T(8,128)(2,1)S(1)}, u32[]{:S(2)}, u32[]{:S(2)}) collective-permute-start(bf16[2,144,128]{2,1,0:T(8,128)(2,1)S(1)} %pad_maximum_fusion.refs_8_), channel_id=1, source_target_pairs={{0,8},{4,12},{8,0},{12,4},{16,24},{20,28},{24,16},{28,20},{1,9},{5... | collective-permute-start | bytes 221192 | tf_op jit(solution)/shard_map/ppermute | solution.py:19
  36.6 0.0 collective-permute-done.6.refs_2_
  36.6 0.7 %collective-permute-start.17 = (bf16[2,144,128]{2,1,0:T(8,128)(2,1)S(1)}, bf16[2,144,128]{2,1,0:T(8,128)(2,1)S(1)}, u32[]{:S(2)}, u32[]{:S(2)}) collective-permute-start(bf16[2,144,128]{2,1,0:T(8,128)(2,1)S(1)} %pad_maximum_fusion.refs_8_), channel_id=1, source_target_pairs={{0,4},{4,0},{8,12},{12,8},{16,20},{20,16},{24,28},{28,24},{1,5},{5... | collective-permute-start | bytes 221192 | tf_op jit(solution)/shard_map/ppermute | solution.py:19
  37.4 0.0 collective-permute-start.11
  37.4 0.5 collective-permute-start.10
  37.9 1.0 %collective-permute-done.19.refs_11_ = bf16[2,144,128]{2,1,0:T(8,128)(2,1)S(1)} collective-permute-done((bf16[2,144,128]{2,1,0:T(8,128)(2,1)S(1)}, bf16[2,144,128]{2,1,0:T(8,128)(2,1)S(1)}, u32[]{:S(2)}, u32[]{:S(2)}) %collective-permute-start.19) | collective-permute-done | bytes 73760 | tf_op jit(solution)/shard_map/ppermute | solution.py:19
  38.9 0.0 collective-permute-start.9
  38.9 0.8 %collective-permute-done.18.refs_10_ = bf16[2,144,128]{2,1,0:T(8,128)(2,1)S(1)} collective-permute-done((bf16[2,144,128]{2,1,0:T(8,128)(2,1)S(1)}, bf16[2,144,128]{2,1,0:T(8,128)(2,1)S(1)}, u32[]{:S(2)}, u32[]{:S(2)}) %collective-permute-start.18) | collective-permute-done | bytes 73760 | tf_op jit(solution)/shard_map/ppermute | solution.py:19
  39.7 0.0 collective-permute-start.23
  39.7 1.3 %collective-permute-done.17.refs_9_ = bf16[2,144,128]{2,1,0:T(8,128)(2,1)S(1)} collective-permute-done((bf16[2,144,128]{2,1,0:T(8,128)(2,1)S(1)}, bf16[2,144,128]{2,1,0:T(8,128)(2,1)S(1)}, u32[]{:S(2)}, u32[]{:S(2)}) %collective-permute-start.17) | collective-permute-done | bytes 73760 | tf_op jit(solution)/shard_map/ppermute | solution.py:19
  41.0 0.0 collective-permute-start.22
  41.0 0.5 collective-permute-start.21
  41.5 0.7 %pad_add_fusion.pos_ref = s32[2]{0:T(128)} fusion(s32[1]{0:T(128)} %bitcast.1, s32[1]{0:T(128)} %bitcast), kind=kLoop, calls=%fused_computation.41 | loop fusion | flops 2 | bytes 16 | tf_op jit(solution)/shard_map/stack | solution.py:112
  42.2 0.0 collective-permute-done.10.refs_6_
  42.2 0.1 collective-permute-done.22.refs_14_
  42.3 0.2 collective-permute-done.21.refs_13_
  42.5 0.3 copy-done.14
  42.8 0.0 copy-done.15
  42.8 0.1 copy-done.6
  42.9 0.0 copy-done.7
  42.9 0.6 %copy-done.8 = bf16[2,144,128]{2,1,0:T(8,128)(2,1)} copy-done((bf16[2,144,128]{2,1,0:T(8,128)(2,1)}, bf16[2,144,128]{2,1,0:T(8,128)(2,1)S(1)}, u32[]{:S(2)}) %copy-start.8) | copy-done | bytes 73752
  43.5 9.5 %shard_map.41 = (f32[1216,608]{1,0:T(8,128)}, f32[32,1216]{1,0:T(8,128)}) custom-call(s32[2]{0:T(128)} %pad_add_fusion.pos_ref, bf16[2,112,128]{2,1,0:T(8,128)(2,1)} %copy-done.1, bf16[2,112,128]{2,1,0:T(8,128)(2,1)} %copy-done.12, bf16[2,112,128]{2,1,0:T(8,128)(2,1)} %copy-done.11, bf16[2,112,128]{2,1,0:T(8,128)(2,1)} %copy-done.10, ...), custom_call_target="tpu_custom_call" | custom-call | tf_op jit(solution)/shard_map/pallas_call | solution.py:114
  (65 shorter events, 0.4 us)
Async XLA Ops:
  8.0 8.1 %collective-permute-start.12 = (bf16[144,128]{1,0:T(8,128)(2,1)S(1)}, bf16[144,128]{1,0:T(8,128)(2,1)S(1)}, u32[]{:S(2)}, u32[]{:S(2)}) collective-permute-start(bf16[144,128]{1,0:T(8,128)(2,1)S(1)} %get-tuple-element.18), channel_id=1, source_target_pairs={{0,4},{4,0},{8,12},{12,8},{16,20},{20,16},{24,28},{28,24},{1,5},{5... | collective-permute-start | bytes 110600 | tf_op jit(solution)/shard_map/ppermute | solution.py:19
  11.0 5.4 %collective-permute-start.14 = (bf16[144,128]{1,0:T(8,128)(2,1)S(1)}, bf16[144,128]{1,0:T(8,128)(2,1)S(1)}, u32[]{:S(2)}, u32[]{:S(2)}) collective-permute-start(bf16[144,128]{1,0:T(8,128)(2,1)S(1)} %get-tuple-element.19), channel_id=1, source_target_pairs={{0,12},{4,8},{8,4},{12,0},{16,28},{20,24},{24,20},{28,16},{1,13},{... | collective-permute-start | bytes 110600 | tf_op jit(solution)/shard_map/ppermute | solution.py:19
  12.5 4.0 %collective-permute-start.13 = (bf16[144,128]{1,0:T(8,128)(2,1)S(1)}, bf16[144,128]{1,0:T(8,128)(2,1)S(1)}, u32[]{:S(2)}, u32[]{:S(2)}) collective-permute-start(bf16[144,128]{1,0:T(8,128)(2,1)S(1)} %get-tuple-element.20), channel_id=1, source_target_pairs={{0,8},{4,12},{8,0},{12,4},{16,24},{20,28},{24,16},{28,20},{1,9},{5... | collective-permute-start | bytes 110600 | tf_op jit(solution)/shard_map/ppermute | solution.py:19
  12.7 7.5 %collective-permute-start.1 = (bf16[160,128]{1,0:T(8,128)(2,1)S(1)}, bf16[160,128]{1,0:T(8,128)(2,1)S(1)}, u32[]{:S(2)}, u32[]{:S(2)}) collective-permute-start(bf16[160,128]{1,0:T(8,128)(2,1)S(1)} %pad_maximum_fusion.3), channel_id=1, source_target_pairs={{0,8},{4,12},{8,0},{12,4},{16,24},{20,28},{24,16},{28,20},{1,9},{5... | collective-permute-start | bytes 122888 | tf_op jit(solution)/shard_map/ppermute | solution.py:19
  14.7 5.4 %collective-permute-start.2 = (bf16[160,128]{1,0:T(8,128)(2,1)S(1)}, bf16[160,128]{1,0:T(8,128)(2,1)S(1)}, u32[]{:S(2)}, u32[]{:S(2)}) collective-permute-start(bf16[160,128]{1,0:T(8,128)(2,1)S(1)} %pad_maximum_fusion.4), channel_id=1, source_target_pairs={{0,12},{4,8},{8,4},{12,0},{16,28},{20,24},{24,20},{28,16},{1,13},{... | collective-permute-start | bytes 122888 | tf_op jit(solution)/shard_map/ppermute | solution.py:19
  16.1 4.0 %collective-permute-start = (bf16[160,128]{1,0:T(8,128)(2,1)S(1)}, bf16[160,128]{1,0:T(8,128)(2,1)S(1)}, u32[]{:S(2)}, u32[]{:S(2)}) collective-permute-start(bf16[160,128]{1,0:T(8,128)(2,1)S(1)} %pad_maximum_fusion.2), channel_id=1, source_target_pairs={{0,4},{4,0},{8,12},{12,8},{16,20},{20,16},{24,28},{28,24},{1,5},{5... | collective-permute-start | bytes 122888 | tf_op jit(solution)/shard_map/ppermute | solution.py:19
  16.5 10.4 %collective-permute-start.15 = (bf16[144,128]{1,0:T(8,128)(2,1)S(1)}, bf16[144,128]{1,0:T(8,128)(2,1)S(1)}, u32[]{:S(2)}, u32[]{:S(2)}) collective-permute-start(bf16[144,128]{1,0:T(8,128)(2,1)S(1)} %reduce-precision_convert_fusion), channel_id=1, source_target_pairs={{0,16},{4,20},{8,24},{12,28},{16,0},{20,4},{24,8},{28,12},{1,17},{... | collective-permute-start | bytes 110600 | tf_op jit(solution)/shard_map/ppermute | solution.py:19
  20.3 5.0 %collective-permute-start.3 = (bf16[160,128]{1,0:T(8,128)(2,1)S(1)}, bf16[160,128]{1,0:T(8,128)(2,1)S(1)}, u32[]{:S(2)}, u32[]{:S(2)}) collective-permute-start(bf16[160,128]{1,0:T(8,128)(2,1)S(1)} %pad_maximum_fusion.5), channel_id=1, source_target_pairs={{0,16},{4,20},{8,24},{12,28},{16,0},{20,4},{24,8},{28,12},{1,17},{... | collective-permute-start | bytes 122888 | tf_op jit(solution)/shard_map/ppermute | solution.py:19
  25.3 3.9 %collective-permute-start.4 = (bf16[1,112,128]{2,1,0:T(8,128)(2,1)S(1)}, bf16[1,112,128]{2,1,0:T(8,128)(2,1)S(1)}, u32[]{:S(2)}, u32[]{:S(2)}) collective-permute-start(bf16[1,112,128]{2,1,0:T(8,128)(2,1)S(1)} %fusion.2), channel_id=1, source_target_pairs={{0,2},{1,3},{2,0},{3,1},{4,6},{5,7},{6,4},{7,5},{8,10},{9,11},{10,... | collective-permute-start | bytes 86024 | tf_op jit(solution)/shard_map/ppermute | solution.py:19
  26.9 6.0 %collective-permute-start.16 = (bf16[1,144,128]{2,1,0:T(8,128)(2,1)S(1)}, bf16[1,144,128]{2,1,0:T(8,128)(2,1)S(1)}, u32[]{:S(2)}, u32[]{:S(2)}) collective-permute-start(bf16[1,144,128]{2,1,0:T(8,128)(2,1)S(1)} %fusion.3), channel_id=1, source_target_pairs={{0,2},{1,3},{2,0},{3,1},{4,6},{5,7},{6,4},{7,5},{8,10},{9,11},{10,... | collective-permute-start | bytes 110600 | tf_op jit(solution)/shard_map/ppermute | solution.py:19
  29.3 13.1 %copy-start.1 = (bf16[2,112,128]{2,1,0:T(8,128)(2,1)}, bf16[2,112,128]{2,1,0:T(8,128)(2,1)S(1)}, u32[]{:S(2)}) copy-start(bf16[2,112,128]{2,1,0:T(8,128)(2,1)S(1)} %pad_maximum_fusion.1.refs_0_) | copy-start | bytes 172036
  29.3 3.7 %collective-permute-start.8 = (bf16[2,112,128]{2,1,0:T(8,128)(2,1)S(1)}, bf16[2,112,128]{2,1,0:T(8,128)(2,1)S(1)}, u32[]{:S(2)}, u32[]{:S(2)}) collective-permute-start(bf16[2,112,128]{2,1,0:T(8,128)(2,1)S(1)} %pad_maximum_fusion.1.refs_0_), channel_id=1, source_target_pairs={{0,1},{1,0},{2,3},{3,2},{4,5},{5,4},{6,7},{7,6},{8,9},{9,8},{10,11... | collective-permute-start | bytes 172040 | tf_op jit(solution)/shard_map/ppermute | solution.py:19
  29.4 5.5 %collective-permute-start.7 = (bf16[2,112,128]{2,1,0:T(8,128)(2,1)S(1)}, bf16[2,112,128]{2,1,0:T(8,128)(2,1)S(1)}, u32[]{:S(2)}, u32[]{:S(2)}) collective-permute-start(bf16[2,112,128]{2,1,0:T(8,128)(2,1)S(1)} %pad_maximum_fusion.1.refs_0_), channel_id=1, source_target_pairs={{0,12},{4,8},{8,4},{12,0},{16,28},{20,24},{24,20},{28,16},{1,13},{... | collective-permute-start | bytes 172040 | tf_op jit(solution)/shard_map/ppermute | solution.py:19
  31.2 5.5 %collective-permute-start.6 = (bf16[2,112,128]{2,1,0:T(8,128)(2,1)S(1)}, bf16[2,112,128]{2,1,0:T(8,128)(2,1)S(1)}, u32[]{:S(2)}, u32[]{:S(2)}) collective-permute-start(bf16[2,112,128]{2,1,0:T(8,128)(2,1)S(1)} %pad_maximum_fusion.1.refs_0_), channel_id=1, source_target_pairs={{0,8},{4,12},{8,0},{12,4},{16,24},{20,28},{24,16},{28,20},{1,9},{5... | collective-permute-start | bytes 172040 | tf_op jit(solution)/shard_map/ppermute | solution.py:19
  31.9 5.5 %collective-permute-start.5 = (bf16[2,112,128]{2,1,0:T(8,128)(2,1)S(1)}, bf16[2,112,128]{2,1,0:T(8,128)(2,1)S(1)}, u32[]{:S(2)}, u32[]{:S(2)}) collective-permute-start(bf16[2,112,128]{2,1,0:T(8,128)(2,1)S(1)} %pad_maximum_fusion.1.refs_0_), channel_id=1, source_target_pairs={{0,4},{4,0},{8,12},{12,8},{16,20},{20,16},{24,28},{28,24},{1,5},{5... | collective-permute-start | bytes 172040 | tf_op jit(solution)/shard_map/ppermute | solution.py:19
  32.9 9.5 %copy-start = (bf16[2,144,128]{2,1,0:T(8,128)(2,1)}, bf16[2,144,128]{2,1,0:T(8,128)(2,1)S(1)}, u32[]{:S(2)}) copy-start(bf16[2,144,128]{2,1,0:T(8,128)(2,1)S(1)} %pad_maximum_fusion.refs_8_) | copy-start | bytes 221188
  33.0 4.4 %collective-permute-start.20 = (bf16[2,144,128]{2,1,0:T(8,128)(2,1)S(1)}, bf16[2,144,128]{2,1,0:T(8,128)(2,1)S(1)}, u32[]{:S(2)}, u32[]{:S(2)}) collective-permute-start(bf16[2,144,128]{2,1,0:T(8,128)(2,1)S(1)} %pad_maximum_fusion.refs_8_), channel_id=1, source_target_pairs={{0,1},{1,0},{2,3},{3,2},{4,5},{5,4},{6,7},{7,6},{8,9},{9,8},{10,11... | collective-permute-start | bytes 221192 | tf_op jit(solution)/shard_map/ppermute | solution.py:19
  33.0 9.4 %copy-start.9 = (bf16[2,112,128]{2,1,0:T(8,128)(2,1)}, bf16[2,112,128]{2,1,0:T(8,128)(2,1)S(1)}, u32[]{:S(2)}) copy-start(bf16[2,112,128]{2,1,0:T(8,128)(2,1)S(1)} %collective-permute-done.8.refs_4_) | copy-start | bytes 172036
  33.1 5.9 %collective-permute-start.19 = (bf16[2,144,128]{2,1,0:T(8,128)(2,1)S(1)}, bf16[2,144,128]{2,1,0:T(8,128)(2,1)S(1)}, u32[]{:S(2)}, u32[]{:S(2)}) collective-permute-start(bf16[2,144,128]{2,1,0:T(8,128)(2,1)S(1)} %pad_maximum_fusion.refs_8_), channel_id=1, source_target_pairs={{0,12},{4,8},{8,4},{12,0},{16,28},{20,24},{24,20},{28,16},{1,13},{... | collective-permute-start | bytes 221192 | tf_op jit(solution)/shard_map/ppermute | solution.py:19
  34.9 7.6 %copy-start.10 = (bf16[2,112,128]{2,1,0:T(8,128)(2,1)}, bf16[2,112,128]{2,1,0:T(8,128)(2,1)S(1)}, u32[]{:S(2)}) copy-start(bf16[2,112,128]{2,1,0:T(8,128)(2,1)S(1)} %collective-permute-done.7.refs_3_) | copy-start | bytes 172036
  34.9 4.9 %collective-permute-start.18 = (bf16[2,144,128]{2,1,0:T(8,128)(2,1)S(1)}, bf16[2,144,128]{2,1,0:T(8,128)(2,1)S(1)}, u32[]{:S(2)}, u32[]{:S(2)}) collective-permute-start(bf16[2,144,128]{2,1,0:T(8,128)(2,1)S(1)} %pad_maximum_fusion.refs_8_), channel_id=1, source_target_pairs={{0,8},{4,12},{8,0},{12,4},{16,24},{20,28},{24,16},{28,20},{1,9},{5... | collective-permute-start | bytes 221192 | tf_op jit(solution)/shard_map/ppermute | solution.py:19
  36.6 5.8 %copy-start.11 = (bf16[2,112,128]{2,1,0:T(8,128)(2,1)}, bf16[2,112,128]{2,1,0:T(8,128)(2,1)S(1)}, u32[]{:S(2)}) copy-start(bf16[2,112,128]{2,1,0:T(8,128)(2,1)S(1)} %collective-permute-done.6.refs_2_) | copy-start | bytes 172036
  36.6 4.4 %collective-permute-start.17 = (bf16[2,144,128]{2,1,0:T(8,128)(2,1)S(1)}, bf16[2,144,128]{2,1,0:T(8,128)(2,1)S(1)}, u32[]{:S(2)}, u32[]{:S(2)}) collective-permute-start(bf16[2,144,128]{2,1,0:T(8,128)(2,1)S(1)} %pad_maximum_fusion.refs_8_), channel_id=1, source_target_pairs={{0,4},{4,0},{8,12},{12,8},{16,20},{20,16},{24,28},{28,24},{1,5},{5... | collective-permute-start | bytes 221192 | tf_op jit(solution)/shard_map/ppermute | solution.py:19
  37.4 5.1 %copy-start.12 = (bf16[2,112,128]{2,1,0:T(8,128)(2,1)}, bf16[2,112,128]{2,1,0:T(8,128)(2,1)S(1)}, u32[]{:S(2)}) copy-start(bf16[2,112,128]{2,1,0:T(8,128)(2,1)S(1)} %collective-permute-done.5.refs_1_) | copy-start | bytes 172036
  37.4 3.6 %collective-permute-start.11 = (bf16[2,112,128]{2,1,0:T(8,128)(2,1)S(1)}, bf16[2,112,128]{2,1,0:T(8,128)(2,1)S(1)}, u32[]{:S(2)}, u32[]{:S(2)}) collective-permute-start(bf16[2,112,128]{2,1,0:T(8,128)(2,1)S(1)} %collective-permute-done.7.refs_3_), channel_id=1, source_target_pairs={{0,1},{1,0},{2,3},{3,2},{4,5},{5,4},{6,7},{7,6},{8,9},{9,8},{10,11... | collective-permute-start | bytes 172040 | tf_op jit(solution)/shard_map/ppermute | solution.py:19
  37.4 5.1 %copy-start.2 = (bf16[2,144,128]{2,1,0:T(8,128)(2,1)}, bf16[2,144,128]{2,1,0:T(8,128)(2,1)S(1)}, u32[]{:S(2)}) copy-start(bf16[2,144,128]{2,1,0:T(8,128)(2,1)S(1)} %collective-permute-done.20.refs_12_) | copy-start | bytes 221188
  37.4 4.8 %collective-permute-start.10 = (bf16[2,112,128]{2,1,0:T(8,128)(2,1)S(1)}, bf16[2,112,128]{2,1,0:T(8,128)(2,1)S(1)}, u32[]{:S(2)}, u32[]{:S(2)}) collective-permute-start(bf16[2,112,128]{2,1,0:T(8,128)(2,1)S(1)} %collective-permute-done.6.refs_2_), channel_id=1, source_target_pairs={{0,1},{1,0},{2,3},{3,2},{4,5},{5,4},{6,7},{7,6},{8,9},{9,8},{10,11... | collective-permute-start | bytes 172040 | tf_op jit(solution)/shard_map/ppermute | solution.py:19
  38.9 3.5 %copy-start.3 = (bf16[2,144,128]{2,1,0:T(8,128)(2,1)}, bf16[2,144,128]{2,1,0:T(8,128)(2,1)S(1)}, u32[]{:S(2)}) copy-start(bf16[2,144,128]{2,1,0:T(8,128)(2,1)S(1)} %collective-permute-done.19.refs_11_) | copy-start | bytes 221188
  38.9 3.2 %collective-permute-start.9 = (bf16[2,112,128]{2,1,0:T(8,128)(2,1)S(1)}, bf16[2,112,128]{2,1,0:T(8,128)(2,1)S(1)}, u32[]{:S(2)}, u32[]{:S(2)}) collective-permute-start(bf16[2,112,128]{2,1,0:T(8,128)(2,1)S(1)} %collective-permute-done.5.refs_1_), channel_id=1, source_target_pairs={{0,1},{1,0},{2,3},{3,2},{4,5},{5,4},{6,7},{7,6},{8,9},{9,8},{10,11... | collective-permute-start | bytes 172040 | tf_op jit(solution)/shard_map/ppermute | solution.py:19
  39.7 2.8 %copy-start.4 = (bf16[2,144,128]{2,1,0:T(8,128)(2,1)}, bf16[2,144,128]{2,1,0:T(8,128)(2,1)S(1)}, u32[]{:S(2)}) copy-start(bf16[2,144,128]{2,1,0:T(8,128)(2,1)S(1)} %collective-permute-done.18.refs_10_) | copy-start | bytes 221188
  39.7 2.5 %collective-permute-start.23 = (bf16[2,144,128]{2,1,0:T(8,128)(2,1)S(1)}, bf16[2,144,128]{2,1,0:T(8,128)(2,1)S(1)}, u32[]{:S(2)}, u32[]{:S(2)}) collective-permute-start(bf16[2,144,128]{2,1,0:T(8,128)(2,1)S(1)} %collective-permute-done.19.refs_11_), channel_id=1, source_target_pairs={{0,1},{1,0},{2,3},{3,2},{4,5},{5,4},{6,7},{7,6},{8,9},{9,8},{10,11... | collective-permute-start | bytes 221192 | tf_op jit(solution)/shard_map/ppermute | solution.py:19
  41.0 1.5 %copy-start.5 = (bf16[2,144,128]{2,1,0:T(8,128)(2,1)}, bf16[2,144,128]{2,1,0:T(8,128)(2,1)S(1)}, u32[]{:S(2)}) copy-start(bf16[2,144,128]{2,1,0:T(8,128)(2,1)S(1)} %collective-permute-done.17.refs_9_) | copy-start | bytes 221188
  41.0 1.3 %collective-permute-start.22 = (bf16[2,144,128]{2,1,0:T(8,128)(2,1)S(1)}, bf16[2,144,128]{2,1,0:T(8,128)(2,1)S(1)}, u32[]{:S(2)}, u32[]{:S(2)}) collective-permute-start(bf16[2,144,128]{2,1,0:T(8,128)(2,1)S(1)} %collective-permute-done.18.refs_10_), channel_id=1, source_target_pairs={{0,1},{1,0},{2,3},{3,2},{4,5},{5,4},{6,7},{7,6},{8,9},{9,8},{10,11... | collective-permute-start | bytes 221192 | tf_op jit(solution)/shard_map/ppermute | solution.py:19
  41.0 1.5 %copy-start.13 = (bf16[2,112,128]{2,1,0:T(8,128)(2,1)}, bf16[2,112,128]{2,1,0:T(8,128)(2,1)S(1)}, u32[]{:S(2)}) copy-start(bf16[2,112,128]{2,1,0:T(8,128)(2,1)S(1)} %collective-permute-done.11.refs_7_) | copy-start | bytes 172036
  41.0 1.4 %collective-permute-start.21 = (bf16[2,144,128]{2,1,0:T(8,128)(2,1)S(1)}, bf16[2,144,128]{2,1,0:T(8,128)(2,1)S(1)}, u32[]{:S(2)}, u32[]{:S(2)}) collective-permute-start(bf16[2,144,128]{2,1,0:T(8,128)(2,1)S(1)} %collective-permute-done.17.refs_9_), channel_id=1, source_target_pairs={{0,1},{1,0},{2,3},{3,2},{4,5},{5,4},{6,7},{7,6},{8,9},{9,8},{10,11... | collective-permute-start | bytes 221192 | tf_op jit(solution)/shard_map/ppermute | solution.py:19
  42.2 0.6 %copy-start.14 = (bf16[2,112,128]{2,1,0:T(8,128)(2,1)}, bf16[2,112,128]{2,1,0:T(8,128)(2,1)S(1)}, u32[]{:S(2)}) copy-start(bf16[2,112,128]{2,1,0:T(8,128)(2,1)S(1)} %collective-permute-done.10.refs_6_) | copy-start | bytes 172036
  42.2 0.6 %copy-start.15 = (bf16[2,112,128]{2,1,0:T(8,128)(2,1)}, bf16[2,112,128]{2,1,0:T(8,128)(2,1)S(1)}, u32[]{:S(2)}) copy-start(bf16[2,112,128]{2,1,0:T(8,128)(2,1)S(1)} %collective-permute-done.9.refs_5_) | copy-start | bytes 172036
  42.2 0.7 %copy-start.6 = (bf16[2,144,128]{2,1,0:T(8,128)(2,1)}, bf16[2,144,128]{2,1,0:T(8,128)(2,1)S(1)}, u32[]{:S(2)}) copy-start(bf16[2,144,128]{2,1,0:T(8,128)(2,1)S(1)} %collective-permute-done.23.refs_15_) | copy-start | bytes 221188
  42.3 0.6 %copy-start.7 = (bf16[2,144,128]{2,1,0:T(8,128)(2,1)}, bf16[2,144,128]{2,1,0:T(8,128)(2,1)S(1)}, u32[]{:S(2)}) copy-start(bf16[2,144,128]{2,1,0:T(8,128)(2,1)S(1)} %collective-permute-done.22.refs_14_) | copy-start | bytes 221188
  42.9 0.6 %copy-start.8 = (bf16[2,144,128]{2,1,0:T(8,128)(2,1)}, bf16[2,144,128]{2,1,0:T(8,128)(2,1)S(1)}, u32[]{:S(2)}) copy-start(bf16[2,144,128]{2,1,0:T(8,128)(2,1)S(1)} %collective-permute-done.21.refs_13_) | copy-start | bytes 221188

commit v5 on v3

v5 whole, which is shorter than its diff:
```python
import functools

import jax
import jax.numpy as jnp
from jax import lax
from jax.experimental import pallas as pl
from jax.experimental.pallas import tpu as pltpu
from jax.sharding import PartitionSpec as P

LEAD_MODES = 48
RIDGE_WEIGHT = 0.05
ROW_TILE = 16
QUAD = 4
PROJECTION_STEPS = 10
VMEM_LIMIT = 48 * 2**20


def swap(value, axis, bit):
    count = lax.axis_size(axis)
    return lax.ppermute(value, axis, [(i, i ^ bit) for i in range(count)])


def bits_of(count):
    return [1 << k for k in range(count.bit_length() - 1)]


def in_vmem(value):
    return pltpu.with_memory_space_constraint(value, pltpu.VMEM)


def rounded(value):
    high = lax.reduce_precision(value, 8, 7)
    left = value[0:LEAD_MODES] - high[0:LEAD_MODES]
    return jnp.concatenate([high, left], axis=0).astype(jnp.bfloat16)


def restored(value):
    modes = value.shape[0] - LEAD_MODES
    whole = value[0:modes].astype(jnp.float32)
    left = value[modes:].astype(jnp.float32)
    return jnp.concatenate([whole[0:LEAD_MODES] + left, whole[LEAD_MODES:]], axis=0)


def projection_kernel(modes_hbm, snaps_hbm, own_ref, *refs):
    sent_refs, (modes, snaps, partial_sums, modes_sems, snaps_sems) = refs[0:3], refs[3:]
    depth = modes.shape[0] // PROJECTION_STEPS
    quarter = snaps.shape[1] // QUAD

    def copies(step):
        at = pl.ds(step * depth, depth)
        return (
            pltpu.make_async_copy(modes_hbm.at[at], modes.at[at], modes_sems.at[step]),
            pltpu.make_async_copy(snaps_hbm.at[at], snaps.at[at], snaps_sems.at[step]),
        )

    for step in range(PROJECTION_STEPS):
        for copy in copies(step):
            copy.start()
    for step in range(PROJECTION_STEPS):
        for copy in copies(step):
            copy.wait()
        at = pl.ds(step * depth, depth)
        product = lax.dot_general(
            modes[at, :],
            snaps[at, :],
            (((0,), (0,)), ((), ())),
            preferred_element_type=jnp.float32,
        )
        if step == 0:
            partial_sums[...] = product
        else:
            partial_sums[...] += product
    place = lax.rem(lax.axis_index("space"), QUAD)
    count = partial_sums.shape[0]
    for j in range(QUAD):
        start = pl.multiple_of(jnp.bitwise_xor(place, j) * quarter, quarter)
        part = partial_sums[:, pl.ds(start, quarter)]
        if j == 0:
            own_ref[...] = part
        else:
            high = part.astype(jnp.bfloat16)
            left = part[0:LEAD_MODES] - high[0:LEAD_MODES].astype(jnp.float32)
            sent_refs[j - 1][0:count, :] = high
            sent_refs[j - 1][count:, :] = left.astype(jnp.bfloat16)


def project(modes, snapshots):
    (depth, count), snaps = modes.shape, snapshots.shape[1]
    quarter = snaps // QUAD
    vmem = pl.BlockSpec(memory_space=pltpu.VMEM)
    anywhere = pl.BlockSpec(memory_space=pl.ANY)
    own, *sent = pl.pallas_call(
        projection_kernel,
        out_shape=(pltpu.VMEM((count, quarter), jnp.float32),)
        + (pltpu.VMEM((count + LEAD_MODES, quarter), jnp.bfloat16),) * (QUAD - 1),
        in_specs=[anywhere] * 2,
        out_specs=(vmem,) * QUAD,
        scratch_shapes=[
            pltpu.VMEM((depth, count), jnp.bfloat16),
            pltpu.VMEM((depth, snaps), jnp.bfloat16),
            pltpu.VMEM((count, snaps), jnp.float32),
            pltpu.SemaphoreType.DMA((PROJECTION_STEPS,)),
            pltpu.SemaphoreType.DMA((PROJECTION_STEPS,)),
        ],
        compiler_params=pltpu.CompilerParams(vmem_limit_bytes=VMEM_LIMIT),
        cost_estimate=pl.CostEstimate(
            flops=2 * depth * count * snaps,
            bytes_accessed=2 * depth * (count + snaps),
            transcendentals=0,
        ),
    )(modes, snapshots)
    return own, sent


def gram_kernel(sizes, *refs):
    n_time, snaps, modes, row_block, col_block, target_block, tile = sizes
    half, quarter = n_time // 2, snaps // QUAD
    count = 2 * QUAD
    pieces, (gram_hbm, rhs_ref) = refs[0:count], refs[count : count + 2]
    delayed, head, rows, cols, staged, sems = refs[count + 2 :]
    total = n_time * snaps
    time_pos, space_pos = lax.axis_index("tm"), lax.axis_index("space")
    place = lax.rem(space_pos, QUAD)

    def each_piece(take):
        for other in range(2):
            for k in range(half):
                block = jnp.bitwise_xor(time_pos, 2 * k + other)
                for j in range(QUAD):
                    within = jnp.bitwise_xor(place, j) * quarter
                    take(pieces[other * QUAD + j].at[k], block, within)

    def quarter_at(block, within):
        return pl.ds(pl.multiple_of(block * snaps + within, quarter), quarter)

    for delay in (1, 2):
        gap = delay * snaps
        delayed[delay - 1, :, 0:gap] = jnp.zeros((LEAD_MODES, gap), jnp.bfloat16)

    wanted = pl.ds(pl.multiple_of(space_pos * target_block, ROW_TILE), target_block)
    targets = pl.ds(LEAD_MODES + col_block, target_block)
    cols[targets, total - snaps :] = jnp.zeros((target_block, snaps), jnp.bfloat16)

    def place_lead(piece, block, within):
        current = piece[0:LEAD_MODES, :]
        head[:, quarter_at(block, within)] = current.astype(jnp.float32)
        for delay in (1, 2):

            @pl.when(block + delay < n_time)
            def _():
                delayed[delay - 1, :, quarter_at(block + delay, within)] = current

        @pl.when(block >= 1)
        def _():
            cols[targets, quarter_at(block - 1, within)] = piece[wanted, :]

    each_piece(place_lead)

    def fill(out, start, extent):
        @pl.when(start == 0)
        def _():
            def place_modes(piece, block, within):
                out[pl.ds(LEAD_MODES, modes), quarter_at(block, within)] = piece[...]

            each_piece(place_modes)

        def group(q, carry):
            kind, i = lax.div(q, LEAD_MODES), lax.rem(q, LEAD_MODES)
            at = modes + LEAD_MODES * q - start + LEAD_MODES
            factor = jnp.broadcast_to(head[pl.ds(i, 1), :], (ROW_TILE, total)).astype(
                jnp.bfloat16
            )
            for j in range(0, LEAD_MODES, ROW_TILE):
                out[pl.ds(pl.multiple_of(at + j, ROW_TILE), ROW_TILE), :] = (
                    factor * delayed[kind, j : j + ROW_TILE, :]
                )
            return carry

        first = jnp.maximum(0, lax.div(start - modes, LEAD_MODES))
        last = lax.div(start + extent - modes + LEAD_MODES - 1, LEAD_MODES)
        lax.fori_loop(first, last, group, 0)

    kept = cols[targets, :]
    fill(cols, space_pos * col_block, col_block)
    cols[targets, :] = kept
    fill(rows, time_pos * row_block, row_block)

    writes = []
    for step in range(row_block // tile):
        top = step * tile
        product = lax.dot_general(
            rows[pl.ds(LEAD_MODES + top, tile), :],
            cols[pl.ds(LEAD_MODES, col_block + target_block), :],
            (((1,), (1,)), ((), ())),
            preferred_element_type=jnp.float32,
        ) * (1.0 / total)
        shape = (tile, col_block)
        row = time_pos * row_block + top + lax.broadcasted_iota(jnp.int32, shape, 0)
        column = space_pos * col_block + lax.broadcasted_iota(jnp.int32, shape, 1)
        staged[pl.ds(top, tile), :] = product[:, 0:col_block] + jnp.where(
            row == column, RIDGE_WEIGHT, 0.0
        )
        at = pl.ds(top, tile)
        writes.append(pltpu.make_async_copy(staged.at[at], gram_hbm.at[at], sems.at[step]))
        writes[-1].start()
        rhs_ref[:, top : top + tile] = product[:, col_block:].T
    for write in writes:
        write.wait()


def gram_blocks(pieces, n_time, n_space):
    _, modes, quarter = pieces[0].shape
    snaps = QUAD * quarter
    features = modes + 2 * LEAD_MODES * LEAD_MODES
    row_block, col_block, target_block = features // n_time, features // n_space, modes // n_space
    total = n_time * snaps
    tile = row_block // 2 if row_block % (2 * ROW_TILE) == 0 else row_block
    vmem = pl.BlockSpec(memory_space=pltpu.VMEM)
    gram, rhs = pl.pallas_call(
        functools.partial(
            gram_kernel, (n_time, snaps, modes, row_block, col_block, target_block, tile)
        ),
        out_shape=(
            jax.ShapeDtypeStruct((row_block, col_block), jnp.float32),
            jax.ShapeDtypeStruct((target_block, row_block), jnp.float32),
        ),
        in_specs=[vmem] * len(pieces),
        out_specs=(pl.BlockSpec(memory_space=pl.ANY), vmem),
        scratch_shapes=[
            pltpu.VMEM((2, LEAD_MODES, total), jnp.bfloat16),
            pltpu.VMEM((LEAD_MODES, total), jnp.float32),
            pltpu.VMEM((row_block + 2 * LEAD_MODES, total), jnp.bfloat16),
            pltpu.VMEM((col_block + 2 * LEAD_MODES + target_block, total), jnp.bfloat16),
            pltpu.VMEM((row_block, col_block), jnp.float32),
            pltpu.SemaphoreType.DMA((row_block // tile,)),
        ],
        compiler_params=pltpu.CompilerParams(vmem_limit_bytes=VMEM_LIMIT),
        cost_estimate=pl.CostEstimate(
            flops=2 * row_block * (col_block + target_block) * total,
            bytes_accessed=4 * row_block * (col_block + target_block),
            transcendentals=0,
        ),
    )(*map(in_vmem, pieces))
    return gram, rhs.T


def joined(value, axis, bit):
    return jnp.concatenate([value, swap(value, axis, bit)], axis=0)


def per_device(snapshots, modes):
    n_space, n_time = lax.axis_size("space"), lax.axis_size("tm")
    mine, sent = project(modes, snapshots)
    arrived = [swap(part, "space", j) for j, part in enumerate(sent, 1)]
    for part in arrived:
        mine = mine + restored(part)
    for bit in bits_of(n_space)[2:]:
        out = rounded(mine)
        mine = restored(out) + restored(swap(out, "space", bit))
    mine = mine.astype(jnp.bfloat16)[None]
    for bit in bits_of(n_time)[1:]:
        mine = joined(mine, "tm", bit)
    pieces = [mine] + [swap(mine, "space", j) for j in range(1, QUAD)]
    pieces = pieces + [swap(piece, "tm", 1) for piece in pieces]
    return gram_blocks(pieces, n_time, n_space)


def solution(mesh):
    in_specs = (P("space", "tm"), P("space", None))
    out_specs = (P("tm", "space"), P("tm", "space"))
    return jax.shard_map(
        per_device, mesh=mesh, in_specs=in_specs, out_specs=out_specs, check_vma=False
    )
```

time: 47.9 us -> 45.5 us (0.950)
  matrix products: 7.22 us -> 0 us
  Pallas kernels: 9.47 us -> 13.2 us
  local copies, waits for them, and re-layouts: 0.71 us -> 2.52 us
  other arithmetic: 0.91 us -> 0.18 us
    dot_general x1 -> x0, matrix products: 7.22 us -> none  [per_device(): lax.dot_general(modes, snapshots, (((0,), (0,)), ((), ())), preferred_ele...]
    pallas_call x0 -> x1, Pallas kernels: none -> 5.19 us  [project(): pl.pallas_call(projection_kernel, out_shape=(pltpu.VMEM((count, quarter),...]
    unnamed x16 -> x2, local copies, waits for them, and re-layouts: 0.67 us -> 2.48 us
    pallas_call x1, Pallas kernels: 9.47 us -> 7.96 us  [gram_blocks(): pl.pallas_call(functools.partial(gram_kernel, (n_time, snaps, modes, row_...]
    another operation x3 -> x0, other arithmetic: 0.69 us -> none  [the longest x1 0.6 us: gram_blocks(): jnp.stack([lax.axis_index('tm'), lax.axis_index('space')]).astype(jnp.int32)]
  transfers between devices with their start and end apart: 12 -> 12, of which waited for: 8 -> 9; matrix products, arithmetic and copies ran while one was open for 1% -> 0% of each run, Pallas kernels for 0% -> 0%
where the time goes in v5:
time: 45.5 us; the launch traced here: 45.3 us
  waiting for transfers between devices  16.2 us (36%)
  Pallas kernels  13.2 us (29%)
  starting transfers between devices  12.5 us (27%)
  local copies, waits for them, and re-layouts  2.52 us (6%)
  between operations  0.78 us (2%)
    ppermute x12, waiting for transfers between devices, swap(): return lax.ppermute(value, axis, [(i, i ^ bit) for i in range(count)])  16.2 us
    ppermute x12, starting transfers between devices, swap(): return lax.ppermute(value, axis, [(i, i ^ bit) for i in range(count)])  12.5 us
    pallas_call x1, Pallas kernels, gram_blocks(): pl.pallas_call(functools.partial(gram_kernel, (n_time, snaps, modes, row_...  7.96 us
    pallas_call x1, Pallas kernels, project(): pl.pallas_call(projection_kernel, out_shape=(pltpu.VMEM((count, quarter),...  5.19 us
    unnamed x2, local copies, waits for them, and re-layouts  2.48 us
  transfers between devices with their start and end apart: 12, of which 9 were waited for; matrix products, arithmetic and copies ran while one was open for 0% of the time, Pallas kernels for 0%

profile of v5, /device:TPU:0, one launch (start us, length us, event | category | flops | bytes accessed | tf_op | source)
XLA Modules:
  0.0 45.3 jit_solution(5186150533030313902)
XLA Ops:
  0.6 0.0 copy-start
  0.6 2.5 %copy-done = bf16[10240,256]{1,0:T(8,128)(2,1)S(1)} copy-done((bf16[10240,256]{1,0:T(8,128)(2,1)S(1)}, bf16[10240,256]{1,0:T(8,128)(2,1)}, u32[]{:S(2)}) %copy-start) | copy-done | bytes 5242904
  3.1 5.2 %shard_map.41 = (f32[256,128]{1,0:T(8,128)S(1)}, bf16[304,128]{1,0:T(8,128)(2,1)S(1)}, bf16[304,128]{1,0:T(8,128)(2,1)S(1)}, bf16[304,128]{1,0:T(8,128)(2,1)S(1)}) custom-call(bf16[10240,256]{1,0:T(8,128)(2,1)S(1)} %copy-done, bf16[10240,512]{1,0:T(8,128)(2,1)} %snaps_hbm.1), custom_call_target="tpu_custom_call" | custom-call | flops 2684354560 | bytes 15728640 | tf_op jit(solution)/shard_map/pallas_call | solution.py:92
  8.3 4.0 %collective-permute-start.2 = (bf16[304,128]{1,0:T(8,128)(2,1)S(1)}, bf16[304,128]{1,0:T(8,128)(2,1)S(1)}, u32[]{:S(2)}, u32[]{:S(2)}) collective-permute-start(bf16[304,128]{1,0:T(8,128)(2,1)S(1)} %get-tuple-element.11), channel_id=1, source_target_pairs={{0,12},{4,8},{8,4},{12,0},{16,28},{20,24},{24,20},{28,16},{1,13},{... | collective-permute-start | bytes 233480 | tf_op jit(solution)/shard_map/ppermute | solution.py:20
  12.3 0.5 %collective-permute-start = (bf16[304,128]{1,0:T(8,128)(2,1)S(1)}, bf16[304,128]{1,0:T(8,128)(2,1)S(1)}, u32[]{:S(2)}, u32[]{:S(2)}) collective-permute-start(bf16[304,128]{1,0:T(8,128)(2,1)S(1)} %get-tuple-element.9), channel_id=1, source_target_pairs={{0,4},{4,0},{8,12},{12,8},{16,20},{20,16},{24,28},{28,24},{1,5},{5... | collective-permute-start | bytes 233480 | tf_op jit(solution)/shard_map/ppermute | solution.py:20
  12.9 0.1 collective-permute-start.1
  13.0 1.8 %collective-permute-done.2 = bf16[304,128]{1,0:T(8,128)(2,1)S(1)} collective-permute-done((bf16[304,128]{1,0:T(8,128)(2,1)S(1)}, bf16[304,128]{1,0:T(8,128)(2,1)S(1)}, u32[]{:S(2)}, u32[]{:S(2)}) %collective-permute-start.2) | collective-permute-done | bytes 77856 | tf_op jit(solution)/shard_map/ppermute | solution.py:20
  14.8 2.5 %collective-permute-done.1 = bf16[304,128]{1,0:T(8,128)(2,1)S(1)} collective-permute-done((bf16[304,128]{1,0:T(8,128)(2,1)S(1)}, bf16[304,128]{1,0:T(8,128)(2,1)S(1)}, u32[]{:S(2)}, u32[]{:S(2)}) %collective-permute-start.1) | collective-permute-done | bytes 77856 | tf_op jit(solution)/shard_map/ppermute | solution.py:20
  17.3 0.0 collective-permute-done
  17.5 2.7 %collective-permute-start.3 = (bf16[304,128]{1,0:T(8,128)(2,1)S(1)}, bf16[304,128]{1,0:T(8,128)(2,1)S(1)}, u32[]{:S(2)}, u32[]{:S(2)}) collective-permute-start(bf16[304,128]{1,0:T(8,128)(2,1)S(1)} %pad_maximum_fusion.1), channel_id=1, source_target_pairs={{0,16},{4,20},{8,24},{12,28},{16,0},{20,4},{24,8},{28,12},{1,17},{... | collective-permute-start | bytes 233480 | tf_op jit(solution)/shard_map/ppermute | solution.py:20
  20.2 3.5 %collective-permute-done.3 = bf16[304,128]{1,0:T(8,128)(2,1)S(1)} collective-permute-done((bf16[304,128]{1,0:T(8,128)(2,1)S(1)}, bf16[304,128]{1,0:T(8,128)(2,1)S(1)}, u32[]{:S(2)}, u32[]{:S(2)}) %collective-permute-start.3) | collective-permute-done | bytes 77856 | tf_op jit(solution)/shard_map/ppermute | solution.py:20
  23.8 1.6 %collective-permute-start.4 = (bf16[1,256,128]{2,1,0:T(8,128)(2,1)S(1)}, bf16[1,256,128]{2,1,0:T(8,128)(2,1)S(1)}, u32[]{:S(2)}, u32[]{:S(2)}) collective-permute-start(bf16[1,256,128]{2,1,0:T(8,128)(2,1)S(1)} %fusion.2), channel_id=1, source_target_pairs={{0,2},{1,3},{2,0},{3,1},{4,6},{5,7},{6,4},{7,5},{8,10},{9,11},{10,... | collective-permute-start | bytes 196616 | tf_op jit(solution)/shard_map/ppermute | solution.py:20
  25.3 2.7 %collective-permute-done.4 = bf16[1,256,128]{2,1,0:T(8,128)(2,1)S(1)} collective-permute-done((bf16[1,256,128]{2,1,0:T(8,128)(2,1)S(1)}, bf16[1,256,128]{2,1,0:T(8,128)(2,1)S(1)}, u32[]{:S(2)}, u32[]{:S(2)}) %collective-permute-start.4) | collective-permute-done | bytes 65568 | tf_op jit(solution)/shard_map/ppermute | solution.py:20
  28.1 0.7 %collective-permute-start.7 = (bf16[2,256,128]{2,1,0:T(8,128)(2,1)S(1)}, bf16[2,256,128]{2,1,0:T(8,128)(2,1)S(1)}, u32[]{:S(2)}, u32[]{:S(2)}) collective-permute-start(bf16[2,256,128]{2,1,0:T(8,128)(2,1)S(1)} %pad_maximum_fusion.refs_0_), channel_id=1, source_target_pairs={{0,12},{4,8},{8,4},{12,0},{16,28},{20,24},{24,20},{28,16},{1,13},{... | collective-permute-start | bytes 393224 | tf_op jit(solution)/shard_map/ppermute | solution.py:20
  28.8 2.2 %collective-permute-start.6 = (bf16[2,256,128]{2,1,0:T(8,128)(2,1)S(1)}, bf16[2,256,128]{2,1,0:T(8,128)(2,1)S(1)}, u32[]{:S(2)}, u32[]{:S(2)}) collective-permute-start(bf16[2,256,128]{2,1,0:T(8,128)(2,1)S(1)} %pad_maximum_fusion.refs_0_), channel_id=1, source_target_pairs={{0,8},{4,12},{8,0},{12,4},{16,24},{20,28},{24,16},{28,20},{1,9},{5... | collective-permute-start | bytes 393224 | tf_op jit(solution)/shard_map/ppermute | solution.py:20
  31.0 0.6 %collective-permute-start.5 = (bf16[2,256,128]{2,1,0:T(8,128)(2,1)S(1)}, bf16[2,256,128]{2,1,0:T(8,128)(2,1)S(1)}, u32[]{:S(2)}, u32[]{:S(2)}) collective-permute-start(bf16[2,256,128]{2,1,0:T(8,128)(2,1)S(1)} %pad_maximum_fusion.refs_0_), channel_id=1, source_target_pairs={{0,4},{4,0},{8,12},{12,8},{16,20},{20,16},{24,28},{28,24},{1,5},{5... | collective-permute-start | bytes 393224 | tf_op jit(solution)/shard_map/ppermute | solution.py:20
  31.7 0.0 collective-permute-start.8
  31.7 2.4 %collective-permute-done.7.refs_3_ = bf16[2,256,128]{2,1,0:T(8,128)(2,1)S(1)} collective-permute-done((bf16[2,256,128]{2,1,0:T(8,128)(2,1)S(1)}, bf16[2,256,128]{2,1,0:T(8,128)(2,1)S(1)}, u32[]{:S(2)}, u32[]{:S(2)}) %collective-permute-start.7) | collective-permute-done | bytes 131104 | tf_op jit(solution)/shard_map/ppermute | solution.py:20
  34.0 0.0 collective-permute-start.11
  34.0 1.3 %collective-permute-done.6.refs_2_ = bf16[2,256,128]{2,1,0:T(8,128)(2,1)S(1)} collective-permute-done((bf16[2,256,128]{2,1,0:T(8,128)(2,1)S(1)}, bf16[2,256,128]{2,1,0:T(8,128)(2,1)S(1)}, u32[]{:S(2)}, u32[]{:S(2)}) %collective-permute-start.6) | collective-permute-done | bytes 131104 | tf_op jit(solution)/shard_map/ppermute | solution.py:20
  35.4 0.0 collective-permute-start.10
  35.4 0.6 %collective-permute-done.5.refs_1_ = bf16[2,256,128]{2,1,0:T(8,128)(2,1)S(1)} collective-permute-done((bf16[2,256,128]{2,1,0:T(8,128)(2,1)S(1)}, bf16[2,256,128]{2,1,0:T(8,128)(2,1)S(1)}, u32[]{:S(2)}, u32[]{:S(2)}) %collective-permute-start.5) | collective-permute-done | bytes 131104 | tf_op jit(solution)/shard_map/ppermute | solution.py:20
  36.0 0.0 collective-permute-start.9
  36.0 0.0 collective-permute-done.8.refs_4_
  36.0 0.0 collective-permute-done.11.refs_7_
  36.0 0.7 %collective-permute-done.10.refs_6_ = bf16[2,256,128]{2,1,0:T(8,128)(2,1)S(1)} collective-permute-done((bf16[2,256,128]{2,1,0:T(8,128)(2,1)S(1)}, bf16[2,256,128]{2,1,0:T(8,128)(2,1)S(1)}, u32[]{:S(2)}, u32[]{:S(2)}) %collective-permute-start.10) | collective-permute-done | bytes 131104 | tf_op jit(solution)/shard_map/ppermute | solution.py:20
  36.7 0.6 %collective-permute-done.9.refs_5_ = bf16[2,256,128]{2,1,0:T(8,128)(2,1)S(1)} collective-permute-done((bf16[2,256,128]{2,1,0:T(8,128)(2,1)S(1)}, bf16[2,256,128]{2,1,0:T(8,128)(2,1)S(1)}, u32[]{:S(2)}, u32[]{:S(2)}) %collective-permute-start.9) | collective-permute-done | bytes 131104 | tf_op jit(solution)/shard_map/ppermute | solution.py:20
  37.4 8.0 %shard_map.42 = (f32[1216,608]{1,0:T(8,128)}, f32[32,1216]{1,0:T(8,128)}) custom-call(bf16[2,256,128]{2,1,0:T(8,128)(2,1)S(1)} %pad_maximum_fusion.refs_0_, bf16[2,256,128]{2,1,0:T(8,128)(2,1)S(1)} %collective-permute-done.5.refs_1_, bf16[2,256,128]{2,1,0:T(8,128)(2,1)S(1)} %collective-permute-done.6.refs_2_, ...), custom_call_target="tpu_custom_call" | custom-call | flops 3187671040 | bytes 3112960 | tf_op jit(solution)/shard_map/pallas_call | solution.py:219
  (19 shorter events, 0.2 us)
Async XLA Ops:
  0.6 2.5 %copy-start = (bf16[10240,256]{1,0:T(8,128)(2,1)S(1)}, bf16[10240,256]{1,0:T(8,128)(2,1)}, u32[]{:S(2)}) copy-start(bf16[10240,256]{1,0:T(8,128)(2,1)} %modes_hbm.1) | copy-start | bytes 15728644
  8.3 6.5 %collective-permute-start.2 = (bf16[304,128]{1,0:T(8,128)(2,1)S(1)}, bf16[304,128]{1,0:T(8,128)(2,1)S(1)}, u32[]{:S(2)}, u32[]{:S(2)}) collective-permute-start(bf16[304,128]{1,0:T(8,128)(2,1)S(1)} %get-tuple-element.11), channel_id=1, source_target_pairs={{0,12},{4,8},{8,4},{12,0},{16,28},{20,24},{24,20},{28,16},{1,13},{... | collective-permute-start | bytes 233480 | tf_op jit(solution)/shard_map/ppermute | solution.py:20
  12.3 5.0 %collective-permute-start = (bf16[304,128]{1,0:T(8,128)(2,1)S(1)}, bf16[304,128]{1,0:T(8,128)(2,1)S(1)}, u32[]{:S(2)}, u32[]{:S(2)}) collective-permute-start(bf16[304,128]{1,0:T(8,128)(2,1)S(1)} %get-tuple-element.9), channel_id=1, source_target_pairs={{0,4},{4,0},{8,12},{12,8},{16,20},{20,16},{24,28},{28,24},{1,5},{5... | collective-permute-start | bytes 233480 | tf_op jit(solution)/shard_map/ppermute | solution.py:20
  12.9 4.4 %collective-permute-start.1 = (bf16[304,128]{1,0:T(8,128)(2,1)S(1)}, bf16[304,128]{1,0:T(8,128)(2,1)S(1)}, u32[]{:S(2)}, u32[]{:S(2)}) collective-permute-start(bf16[304,128]{1,0:T(8,128)(2,1)S(1)} %get-tuple-element.10), channel_id=1, source_target_pairs={{0,8},{4,12},{8,0},{12,4},{16,24},{20,28},{24,16},{28,20},{1,9},{5... | collective-permute-start | bytes 233480 | tf_op jit(solution)/shard_map/ppermute | solution.py:20
  17.5 6.2 %collective-permute-start.3 = (bf16[304,128]{1,0:T(8,128)(2,1)S(1)}, bf16[304,128]{1,0:T(8,128)(2,1)S(1)}, u32[]{:S(2)}, u32[]{:S(2)}) collective-permute-start(bf16[304,128]{1,0:T(8,128)(2,1)S(1)} %pad_maximum_fusion.1), channel_id=1, source_target_pairs={{0,16},{4,20},{8,24},{12,28},{16,0},{20,4},{24,8},{28,12},{1,17},{... | collective-permute-start | bytes 233480 | tf_op jit(solution)/shard_map/ppermute | solution.py:20
  23.8 4.3 %collective-permute-start.4 = (bf16[1,256,128]{2,1,0:T(8,128)(2,1)S(1)}, bf16[1,256,128]{2,1,0:T(8,128)(2,1)S(1)}, u32[]{:S(2)}, u32[]{:S(2)}) collective-permute-start(bf16[1,256,128]{2,1,0:T(8,128)(2,1)S(1)} %fusion.2), channel_id=1, source_target_pairs={{0,2},{1,3},{2,0},{3,1},{4,6},{5,7},{6,4},{7,5},{8,10},{9,11},{10,... | collective-permute-start | bytes 196616 | tf_op jit(solution)/shard_map/ppermute | solution.py:20
  28.1 5.9 %collective-permute-start.7 = (bf16[2,256,128]{2,1,0:T(8,128)(2,1)S(1)}, bf16[2,256,128]{2,1,0:T(8,128)(2,1)S(1)}, u32[]{:S(2)}, u32[]{:S(2)}) collective-permute-start(bf16[2,256,128]{2,1,0:T(8,128)(2,1)S(1)} %pad_maximum_fusion.refs_0_), channel_id=1, source_target_pairs={{0,12},{4,8},{8,4},{12,0},{16,28},{20,24},{24,20},{28,16},{1,13},{... | collective-permute-start | bytes 393224 | tf_op jit(solution)/shard_map/ppermute | solution.py:20
  28.8 6.6 %collective-permute-start.6 = (bf16[2,256,128]{2,1,0:T(8,128)(2,1)S(1)}, bf16[2,256,128]{2,1,0:T(8,128)(2,1)S(1)}, u32[]{:S(2)}, u32[]{:S(2)}) collective-permute-start(bf16[2,256,128]{2,1,0:T(8,128)(2,1)S(1)} %pad_maximum_fusion.refs_0_), channel_id=1, source_target_pairs={{0,8},{4,12},{8,0},{12,4},{16,24},{20,28},{24,16},{28,20},{1,9},{5... | collective-permute-start | bytes 393224 | tf_op jit(solution)/shard_map/ppermute | solution.py:20
  31.0 5.0 %collective-permute-start.5 = (bf16[2,256,128]{2,1,0:T(8,128)(2,1)S(1)}, bf16[2,256,128]{2,1,0:T(8,128)(2,1)S(1)}, u32[]{:S(2)}, u32[]{:S(2)}) collective-permute-start(bf16[2,256,128]{2,1,0:T(8,128)(2,1)S(1)} %pad_maximum_fusion.refs_0_), channel_id=1, source_target_pairs={{0,4},{4,0},{8,12},{12,8},{16,20},{20,16},{24,28},{28,24},{1,5},{5... | collective-permute-start | bytes 393224 | tf_op jit(solution)/shard_map/ppermute | solution.py:20
  31.7 4.3 %collective-permute-start.8 = (bf16[2,256,128]{2,1,0:T(8,128)(2,1)S(1)}, bf16[2,256,128]{2,1,0:T(8,128)(2,1)S(1)}, u32[]{:S(2)}, u32[]{:S(2)}) collective-permute-start(bf16[2,256,128]{2,1,0:T(8,128)(2,1)S(1)} %pad_maximum_fusion.refs_0_), channel_id=1, source_target_pairs={{0,1},{1,0},{2,3},{3,2},{4,5},{5,4},{6,7},{7,6},{8,9},{9,8},{10,11... | collective-permute-start | bytes 393224 | tf_op jit(solution)/shard_map/ppermute | solution.py:20
  34.0 2.0 %collective-permute-start.11 = (bf16[2,256,128]{2,1,0:T(8,128)(2,1)S(1)}, bf16[2,256,128]{2,1,0:T(8,128)(2,1)S(1)}, u32[]{:S(2)}, u32[]{:S(2)}) collective-permute-start(bf16[2,256,128]{2,1,0:T(8,128)(2,1)S(1)} %collective-permute-done.7.refs_3_), channel_id=1, source_target_pairs={{0,1},{1,0},{2,3},{3,2},{4,5},{5,4},{6,7},{7,6},{8,9},{9,8},{10,11... | collective-permute-start | bytes 393224 | tf_op jit(solution)/shard_map/ppermute | solution.py:20
  35.4 1.3 %collective-permute-start.10 = (bf16[2,256,128]{2,1,0:T(8,128)(2,1)S(1)}, bf16[2,256,128]{2,1,0:T(8,128)(2,1)S(1)}, u32[]{:S(2)}, u32[]{:S(2)}) collective-permute-start(bf16[2,256,128]{2,1,0:T(8,128)(2,1)S(1)} %collective-permute-done.6.refs_2_), channel_id=1, source_target_pairs={{0,1},{1,0},{2,3},{3,2},{4,5},{5,4},{6,7},{7,6},{8,9},{9,8},{10,11... | collective-permute-start | bytes 393224 | tf_op jit(solution)/shard_map/ppermute | solution.py:20
  36.0 1.3 %collective-permute-start.9 = (bf16[2,256,128]{2,1,0:T(8,128)(2,1)S(1)}, bf16[2,256,128]{2,1,0:T(8,128)(2,1)S(1)}, u32[]{:S(2)}, u32[]{:S(2)}) collective-permute-start(bf16[2,256,128]{2,1,0:T(8,128)(2,1)S(1)} %collective-permute-done.5.refs_1_), channel_id=1, source_target_pairs={{0,1},{1,0},{2,3},{3,2},{4,5},{5,4},{6,7},{7,6},{8,9},{9,8},{10,11... | collective-permute-start | bytes 393224 | tf_op jit(solution)/shard_map/ppermute | solution.py:20

commit v6 on v5

--- a/solution.py
+++ b/solution.py
@@ -22,6 +22,10 @@
 
 def bits_of(count):
     return [1 << k for k in range(count.bit_length() - 1)]
+
+
+def in_hbm(value):
+    return pltpu.with_memory_space_constraint(value, pltpu.HBM)
 
 
 def in_vmem(value):
@@ -88,7 +92,7 @@
     (depth, count), snaps = modes.shape, snapshots.shape[1]
     quarter = snaps // QUAD
     vmem = pl.BlockSpec(memory_space=pltpu.VMEM)
-    anywhere = pl.BlockSpec(memory_space=pl.ANY)
+    anywhere = pl.BlockSpec(memory_space=pltpu.HBM)
     own, *sent = pl.pallas_call(
         projection_kernel,
         out_shape=(pltpu.VMEM((count, quarter), jnp.float32),)
@@ -108,7 +112,7 @@
             bytes_accessed=2 * depth * (count + snaps),
             transcendentals=0,
         ),
-    )(modes, snapshots)
+    )(in_hbm(modes), in_hbm(snapshots))
     return own, sent
 
 
@@ -117,8 +121,8 @@
     half, quarter = n_time // 2, snaps // QUAD
     count = 2 * QUAD
     pieces, (gram_hbm, rhs_ref) = refs[0:count], refs[count : count + 2]
-    delayed, head, rows, cols, staged, sems = refs[count + 2 :]
-    total = n_time * snaps
+    delayed, head, rows, cols, opening, opening_target, staged, side, sems = refs[count + 2 :]
+    later = (n_time - 1) * snaps
     time_pos, space_pos = lax.axis_index("tm"), lax.axis_index("space")
     place = lax.rem(space_pos, QUAD)
 
@@ -127,32 +131,28 @@
             for k in range(half):
                 block = jnp.bitwise_xor(time_pos, 2 * k + other)
                 for j in range(QUAD):
-                    within = jnp.bitwise_xor(place, j) * quarter
+                    within = pl.multiple_of(jnp.bitwise_xor(place, j) * quarter, quarter)
                     take(pieces[other * QUAD + j].at[k], block, within)
 
-    def quarter_at(block, within):
-        return pl.ds(pl.multiple_of(block * snaps + within, quarter), quarter)
-
-    for delay in (1, 2):
-        gap = delay * snaps
-        delayed[delay - 1, :, 0:gap] = jnp.zeros((LEAD_MODES, gap), jnp.bfloat16)
-
+    def later_at(block, within):
+        return pl.ds(pl.multiple_of((block - 1) * snaps + within, quarter), quarter)
+
+    delayed[1, :, 0:snaps] = jnp.zeros((LEAD_MODES, snaps), jnp.bfloat16)
     wanted = pl.ds(pl.multiple_of(space_pos * target_block, ROW_TILE), target_block)
     targets = pl.ds(LEAD_MODES + col_block, target_block)
-    cols[targets, total - snaps :] = jnp.zeros((target_block, snaps), jnp.bfloat16)
 
     def place_lead(piece, block, within):
         current = piece[0:LEAD_MODES, :]
-        head[:, quarter_at(block, within)] = current.astype(jnp.float32)
+
+        @pl.when(block >= 1)
+        def _():
+            head[:, later_at(block, within)] = current.astype(jnp.float32)
+
         for delay in (1, 2):
 
             @pl.when(block + delay < n_time)
             def _():
-                delayed[delay - 1, :, quarter_at(block + delay, within)] = current
-
-        @pl.when(block >= 1)
-        def _():
-            cols[targets, quarter_at(block - 1, within)] = piece[wanted, :]
+                delayed[delay - 1, :, later_at(block + delay, within)] = current
 
     each_piece(place_lead)
 
@@ -160,14 +160,16 @@
         @pl.when(start == 0)
         def _():
             def place_modes(piece, block, within):
-                out[pl.ds(LEAD_MODES, modes), quarter_at(block, within)] = piece[...]
+                @pl.when(block >= 1)
+                def _():
+                    out[pl.ds(LEAD_MODES, modes), later_at(block, within)] = piece[...]
 
             each_piece(place_modes)
 
         def group(q, carry):
             kind, i = lax.div(q, LEAD_MODES), lax.rem(q, LEAD_MODES)
             at = modes + LEAD_MODES * q - start + LEAD_MODES
-            factor = jnp.broadcast_to(head[pl.ds(i, 1), :], (ROW_TILE, total)).astype(
+            factor = jnp.broadcast_to(head[pl.ds(i, 1), :], (ROW_TILE, later)).astype(
                 jnp.bfloat16
             )
             for j in range(0, LEAD_MODES, ROW_TILE):
@@ -180,30 +182,57 @@
         last = lax.div(start + extent - modes + LEAD_MODES - 1, LEAD_MODES)
         lax.fori_loop(first, last, group, 0)
 
-    kept = cols[targets, :]
     fill(cols, space_pos * col_block, col_block)
-    cols[targets, :] = kept
     fill(rows, time_pos * row_block, row_block)
+
+    cols[targets, later - snaps :] = jnp.zeros((target_block, snaps), jnp.bfloat16)
+
+    def place_target(piece, block, within):
+        @pl.when(block >= 2)
+        def _():
+            cols[targets, later_at(block - 1, within)] = piece[wanted, :]
+
+        @pl.when(block == 1)
+        def _():
+            opening_target[:, pl.ds(within, quarter)] = piece[wanted, :]
+
+        @pl.when(block == 0)
+        def _():
+            opening[:, pl.ds(within, quarter)] = piece[...]
+
+    each_piece(place_target)
+
+    def times(left, right):
+        return lax.dot_general(
+            left, right, (((1,), (1,)), ((), ())), preferred_element_type=jnp.float32
+        ) * (1.0 / (n_time * snaps))
 
     writes = []
     for step in range(row_block // tile):
         top = step * tile
-        product = lax.dot_general(
+        at = pl.ds(top, tile)
+        product = times(
             rows[pl.ds(LEAD_MODES + top, tile), :],
             cols[pl.ds(LEAD_MODES, col_block + target_block), :],
-            (((1,), (1,)), ((), ())),
-            preferred_element_type=jnp.float32,
-        ) * (1.0 / total)
+        )
         shape = (tile, col_block)
         row = time_pos * row_block + top + lax.broadcasted_iota(jnp.int32, shape, 0)
         column = space_pos * col_block + lax.broadcasted_iota(jnp.int32, shape, 1)
-        staged[pl.ds(top, tile), :] = product[:, 0:col_block] + jnp.where(
-            row == column, RIDGE_WEIGHT, 0.0
-        )
-        at = pl.ds(top, tile)
+        staged[at, :] = product[:, 0:col_block] + jnp.where(row == column, RIDGE_WEIGHT, 0.0)
+        side[at, :] = product[:, col_block:]
+        if step == 0:
+
+            @pl.when(time_pos == 0)
+            def _():
+                side[0:modes, :] += times(opening[...], opening_target[...])
+
+            @pl.when((time_pos == 0) & (space_pos == 0))
+            def _():
+                staged[0:modes, 0:modes] += times(opening[...], opening[...])
+
         writes.append(pltpu.make_async_copy(staged.at[at], gram_hbm.at[at], sems.at[step]))
         writes[-1].start()
-        rhs_ref[:, top : top + tile] = product[:, col_block:].T
+    rhs_ref[...] = side[...].T
     for write in writes:
         write.wait()
 
@@ -213,8 +242,9 @@
     snaps = QUAD * quarter
     features = modes + 2 * LEAD_MODES * LEAD_MODES
     row_block, col_block, target_block = features // n_time, features // n_space, modes // n_space
-    total = n_time * snaps
+    later = (n_time - 1) * snaps
     tile = row_block // 2 if row_block % (2 * ROW_TILE) == 0 else row_block
+    assert min(tile, col_block) >= modes
     vmem = pl.BlockSpec(memory_space=pltpu.VMEM)
     gram, rhs = pl.pallas_call(
         functools.partial(
@@ -227,16 +257,19 @@
         in_specs=[vmem] * len(pieces),
         out_specs=(pl.BlockSpec(memory_space=pl.ANY), vmem),
         scratch_shapes=[
-            pltpu.VMEM((2, LEAD_MODES, total), jnp.bfloat16),
-            pltpu.VMEM((LEAD_MODES, total), jnp.float32),
-            pltpu.VMEM((row_block + 2 * LEAD_MODES, total), jnp.bfloat16),
-            pltpu.VMEM((col_block + 2 * LEAD_MODES + target_block, total), jnp.bfloat16),
+            pltpu.VMEM((2, LEAD_MODES, later), jnp.bfloat16),
+            pltpu.VMEM((LEAD_MODES, later), jnp.float32),
+            pltpu.VMEM((row_block + 2 * LEAD_MODES, later), jnp.bfloat16),
+            pltpu.VMEM((col_block + 2 * LEAD_MODES + target_block, later), jnp.bfloat16),
+            pltpu.VMEM((modes, snaps), jnp.bfloat16),
+            pltpu.VMEM((target_block, snaps), jnp.bfloat16),
             pltpu.VMEM((row_block, col_block), jnp.float32),
+            pltpu.VMEM((row_block, target_block), jnp.float32),
             pltpu.SemaphoreType.DMA((row_block // tile,)),
         ],
         compiler_params=pltpu.CompilerParams(vmem_limit_bytes=VMEM_LIMIT),
         cost_estimate=pl.CostEstimate(
-            flops=2 * row_block * (col_block + target_block) * total,
+            flops=2 * row_block * (col_block + target_block) * later,
             bytes_accessed=4 * row_block * (col_block + target_block),
             transcendentals=0,
         ),

time: 45.5 us -> 43.3 us (0.952)
  local copies, waits for them, and re-layouts: 2.52 us -> 0.04 us
    unnamed x2 -> x0, local copies, waits for them, and re-layouts: 2.48 us -> none
    pallas_call x1, Pallas kernels: 5.19 us -> 6.24 us  [project(): pl.pallas_call(projection_kernel, out_shape=(pltpu.VMEM((count, quarter),...]
    pallas_call x1, Pallas kernels: 7.96 us -> 7.28 us  [gram_blocks(): pl.pallas_call(functools.partial(gram_kernel, (n_time, snaps, modes, row_...]
where the time goes in v6:
time: 43.3 us; the launch traced here: 43.2 us
  waiting for transfers between devices  16.2 us (37%)
  Pallas kernels  13.5 us (31%)
  starting transfers between devices  12.5 us (29%)
  between operations  0.78 us (2%)
    ppermute x12, waiting for transfers between devices, swap(): return lax.ppermute(value, axis, [(i, i ^ bit) for i in range(count)])  16.2 us
    ppermute x12, starting transfers between devices, swap(): return lax.ppermute(value, axis, [(i, i ^ bit) for i in range(count)])  12.5 us
    pallas_call x1, Pallas kernels, gram_blocks(): pl.pallas_call(functools.partial(gram_kernel, (n_time, snaps, modes, row_...  7.28 us
    pallas_call x1, Pallas kernels, project(): pl.pallas_call(projection_kernel, out_shape=(pltpu.VMEM((count, quarter),...  6.24 us
  transfers between devices with their start and end apart: 12, of which 9 were waited for; matrix products, arithmetic and copies ran while one was open for 0% of the time, Pallas kernels for 0%

profile of v6, /device:TPU:0, one launch (start us, length us, event | category | flops | bytes accessed | tf_op | source)
XLA Modules:
  0.0 43.2 jit_solution(8219382170980700189)
XLA Ops:
  0.6 6.2 %shard_map.41 = (f32[256,128]{1,0:T(8,128)S(1)}, bf16[304,128]{1,0:T(8,128)(2,1)S(1)}, bf16[304,128]{1,0:T(8,128)(2,1)S(1)}, bf16[304,128]{1,0:T(8,128)(2,1)S(1)}) custom-call(bf16[10240,256]{1,0:T(8,128)(2,1)} %modes_hbm.1, bf16[10240,512]{1,0:T(8,128)(2,1)} %snaps_hbm.1), custom_call_target="tpu_custom_call" | custom-call | flops 2684354560 | bytes 15728640 | tf_op jit(solution)/shard_map/pallas_call | solution.py:96
  6.9 4.0 %collective-permute-start.2 = (bf16[304,128]{1,0:T(8,128)(2,1)S(1)}, bf16[304,128]{1,0:T(8,128)(2,1)S(1)}, u32[]{:S(2)}, u32[]{:S(2)}) collective-permute-start(bf16[304,128]{1,0:T(8,128)(2,1)S(1)} %get-tuple-element.11), channel_id=1, source_target_pairs={{0,12},{4,8},{8,4},{12,0},{16,28},{20,24},{24,20},{28,16},{1,13},{... | collective-permute-start | bytes 233480 | tf_op jit(solution)/shard_map/ppermute | solution.py:20
  10.9 0.5 %collective-permute-start = (bf16[304,128]{1,0:T(8,128)(2,1)S(1)}, bf16[304,128]{1,0:T(8,128)(2,1)S(1)}, u32[]{:S(2)}, u32[]{:S(2)}) collective-permute-start(bf16[304,128]{1,0:T(8,128)(2,1)S(1)} %get-tuple-element.9), channel_id=1, source_target_pairs={{0,4},{4,0},{8,12},{12,8},{16,20},{20,16},{24,28},{28,24},{1,5},{5... | collective-permute-start | bytes 233480 | tf_op jit(solution)/shard_map/ppermute | solution.py:20
  11.4 0.1 collective-permute-start.1
  11.6 1.8 %collective-permute-done.2 = bf16[304,128]{1,0:T(8,128)(2,1)S(1)} collective-permute-done((bf16[304,128]{1,0:T(8,128)(2,1)S(1)}, bf16[304,128]{1,0:T(8,128)(2,1)S(1)}, u32[]{:S(2)}, u32[]{:S(2)}) %collective-permute-start.2) | collective-permute-done | bytes 77856 | tf_op jit(solution)/shard_map/ppermute | solution.py:20
  13.4 2.5 %collective-permute-done.1 = bf16[304,128]{1,0:T(8,128)(2,1)S(1)} collective-permute-done((bf16[304,128]{1,0:T(8,128)(2,1)S(1)}, bf16[304,128]{1,0:T(8,128)(2,1)S(1)}, u32[]{:S(2)}, u32[]{:S(2)}) %collective-permute-start.1) | collective-permute-done | bytes 77856 | tf_op jit(solution)/shard_map/ppermute | solution.py:20
  15.9 0.0 collective-permute-done
  16.1 2.7 %collective-permute-start.3 = (bf16[304,128]{1,0:T(8,128)(2,1)S(1)}, bf16[304,128]{1,0:T(8,128)(2,1)S(1)}, u32[]{:S(2)}, u32[]{:S(2)}) collective-permute-start(bf16[304,128]{1,0:T(8,128)(2,1)S(1)} %pad_maximum_fusion.1), channel_id=1, source_target_pairs={{0,16},{4,20},{8,24},{12,28},{16,0},{20,4},{24,8},{28,12},{1,17},{... | collective-permute-start | bytes 233480 | tf_op jit(solution)/shard_map/ppermute | solution.py:20
  18.7 3.5 %collective-permute-done.3 = bf16[304,128]{1,0:T(8,128)(2,1)S(1)} collective-permute-done((bf16[304,128]{1,0:T(8,128)(2,1)S(1)}, bf16[304,128]{1,0:T(8,128)(2,1)S(1)}, u32[]{:S(2)}, u32[]{:S(2)}) %collective-permute-start.3) | collective-permute-done | bytes 77856 | tf_op jit(solution)/shard_map/ppermute | solution.py:20
  22.3 1.6 %collective-permute-start.4 = (bf16[1,256,128]{2,1,0:T(8,128)(2,1)S(1)}, bf16[1,256,128]{2,1,0:T(8,128)(2,1)S(1)}, u32[]{:S(2)}, u32[]{:S(2)}) collective-permute-start(bf16[1,256,128]{2,1,0:T(8,128)(2,1)S(1)} %fusion.2), channel_id=1, source_target_pairs={{0,2},{1,3},{2,0},{3,1},{4,6},{5,7},{6,4},{7,5},{8,10},{9,11},{10,... | collective-permute-start | bytes 196616 | tf_op jit(solution)/shard_map/ppermute | solution.py:20
  23.9 2.7 %collective-permute-done.4 = bf16[1,256,128]{2,1,0:T(8,128)(2,1)S(1)} collective-permute-done((bf16[1,256,128]{2,1,0:T(8,128)(2,1)S(1)}, bf16[1,256,128]{2,1,0:T(8,128)(2,1)S(1)}, u32[]{:S(2)}, u32[]{:S(2)}) %collective-permute-start.4) | collective-permute-done | bytes 65568 | tf_op jit(solution)/shard_map/ppermute | solution.py:20
  26.7 0.7 %collective-permute-start.7 = (bf16[2,256,128]{2,1,0:T(8,128)(2,1)S(1)}, bf16[2,256,128]{2,1,0:T(8,128)(2,1)S(1)}, u32[]{:S(2)}, u32[]{:S(2)}) collective-permute-start(bf16[2,256,128]{2,1,0:T(8,128)(2,1)S(1)} %pad_maximum_fusion.refs_0_), channel_id=1, source_target_pairs={{0,12},{4,8},{8,4},{12,0},{16,28},{20,24},{24,20},{28,16},{1,13},{... | collective-permute-start | bytes 393224 | tf_op jit(solution)/shard_map/ppermute | solution.py:20
  27.4 2.2 %collective-permute-start.6 = (bf16[2,256,128]{2,1,0:T(8,128)(2,1)S(1)}, bf16[2,256,128]{2,1,0:T(8,128)(2,1)S(1)}, u32[]{:S(2)}, u32[]{:S(2)}) collective-permute-start(bf16[2,256,128]{2,1,0:T(8,128)(2,1)S(1)} %pad_maximum_fusion.refs_0_), channel_id=1, source_target_pairs={{0,8},{4,12},{8,0},{12,4},{16,24},{20,28},{24,16},{28,20},{1,9},{5... | collective-permute-start | bytes 393224 | tf_op jit(solution)/shard_map/ppermute | solution.py:20
  29.6 0.6 %collective-permute-start.5 = (bf16[2,256,128]{2,1,0:T(8,128)(2,1)S(1)}, bf16[2,256,128]{2,1,0:T(8,128)(2,1)S(1)}, u32[]{:S(2)}, u32[]{:S(2)}) collective-permute-start(bf16[2,256,128]{2,1,0:T(8,128)(2,1)S(1)} %pad_maximum_fusion.refs_0_), channel_id=1, source_target_pairs={{0,4},{4,0},{8,12},{12,8},{16,20},{20,16},{24,28},{28,24},{1,5},{5... | collective-permute-start | bytes 393224 | tf_op jit(solution)/shard_map/ppermute | solution.py:20
  30.2 0.0 collective-permute-start.8
  30.2 2.4 %collective-permute-done.7.refs_3_ = bf16[2,256,128]{2,1,0:T(8,128)(2,1)S(1)} collective-permute-done((bf16[2,256,128]{2,1,0:T(8,128)(2,1)S(1)}, bf16[2,256,128]{2,1,0:T(8,128)(2,1)S(1)}, u32[]{:S(2)}, u32[]{:S(2)}) %collective-permute-start.7) | collective-permute-done | bytes 131104 | tf_op jit(solution)/shard_map/ppermute | solution.py:20
  32.6 0.0 collective-permute-start.11
  32.6 1.3 %collective-permute-done.6.refs_2_ = bf16[2,256,128]{2,1,0:T(8,128)(2,1)S(1)} collective-permute-done((bf16[2,256,128]{2,1,0:T(8,128)(2,1)S(1)}, bf16[2,256,128]{2,1,0:T(8,128)(2,1)S(1)}, u32[]{:S(2)}, u32[]{:S(2)}) %collective-permute-start.6) | collective-permute-done | bytes 131104 | tf_op jit(solution)/shard_map/ppermute | solution.py:20
  33.9 0.0 collective-permute-start.10
  34.0 0.6 %collective-permute-done.5.refs_1_ = bf16[2,256,128]{2,1,0:T(8,128)(2,1)S(1)} collective-permute-done((bf16[2,256,128]{2,1,0:T(8,128)(2,1)S(1)}, bf16[2,256,128]{2,1,0:T(8,128)(2,1)S(1)}, u32[]{:S(2)}, u32[]{:S(2)}) %collective-permute-start.5) | collective-permute-done | bytes 131104 | tf_op jit(solution)/shard_map/ppermute | solution.py:20
  34.6 0.0 collective-permute-start.9
  34.6 0.0 collective-permute-done.8.refs_4_
  34.6 0.0 collective-permute-done.11.refs_7_
  34.6 0.7 %collective-permute-done.10.refs_6_ = bf16[2,256,128]{2,1,0:T(8,128)(2,1)S(1)} collective-permute-done((bf16[2,256,128]{2,1,0:T(8,128)(2,1)S(1)}, bf16[2,256,128]{2,1,0:T(8,128)(2,1)S(1)}, u32[]{:S(2)}, u32[]{:S(2)}) %collective-permute-start.10) | collective-permute-done | bytes 131104 | tf_op jit(solution)/shard_map/ppermute | solution.py:20
  35.3 0.6 %collective-permute-done.9.refs_5_ = bf16[2,256,128]{2,1,0:T(8,128)(2,1)S(1)} collective-permute-done((bf16[2,256,128]{2,1,0:T(8,128)(2,1)S(1)}, bf16[2,256,128]{2,1,0:T(8,128)(2,1)S(1)}, u32[]{:S(2)}, u32[]{:S(2)}) %collective-permute-start.9) | collective-permute-done | bytes 131104 | tf_op jit(solution)/shard_map/ppermute | solution.py:20
  35.9 7.3 %shard_map.42 = (f32[1216,608]{1,0:T(8,128)}, f32[32,1216]{1,0:T(8,128)}) custom-call(bf16[2,256,128]{2,1,0:T(8,128)(2,1)S(1)} %pad_maximum_fusion.refs_0_, bf16[2,256,128]{2,1,0:T(8,128)(2,1)S(1)} %collective-permute-done.5.refs_1_, bf16[2,256,128]{2,1,0:T(8,128)(2,1)S(1)} %collective-permute-done.6.refs_2_, ...), custom_call_target="tpu_custom_call" | custom-call | flops 2390753280 | bytes 3112960 | tf_op jit(solution)/shard_map/pallas_call | solution.py:249
  (19 shorter events, 0.2 us)
Async XLA Ops:
  6.9 6.5 %collective-permute-start.2 = (bf16[304,128]{1,0:T(8,128)(2,1)S(1)}, bf16[304,128]{1,0:T(8,128)(2,1)S(1)}, u32[]{:S(2)}, u32[]{:S(2)}) collective-permute-start(bf16[304,128]{1,0:T(8,128)(2,1)S(1)} %get-tuple-element.11), channel_id=1, source_target_pairs={{0,12},{4,8},{8,4},{12,0},{16,28},{20,24},{24,20},{28,16},{1,13},{... | collective-permute-start | bytes 233480 | tf_op jit(solution)/shard_map/ppermute | solution.py:20
  10.9 5.0 %collective-permute-start = (bf16[304,128]{1,0:T(8,128)(2,1)S(1)}, bf16[304,128]{1,0:T(8,128)(2,1)S(1)}, u32[]{:S(2)}, u32[]{:S(2)}) collective-permute-start(bf16[304,128]{1,0:T(8,128)(2,1)S(1)} %get-tuple-element.9), channel_id=1, source_target_pairs={{0,4},{4,0},{8,12},{12,8},{16,20},{20,16},{24,28},{28,24},{1,5},{5... | collective-permute-start | bytes 233480 | tf_op jit(solution)/shard_map/ppermute | solution.py:20
  11.4 4.4 %collective-permute-start.1 = (bf16[304,128]{1,0:T(8,128)(2,1)S(1)}, bf16[304,128]{1,0:T(8,128)(2,1)S(1)}, u32[]{:S(2)}, u32[]{:S(2)}) collective-permute-start(bf16[304,128]{1,0:T(8,128)(2,1)S(1)} %get-tuple-element.10), channel_id=1, source_target_pairs={{0,8},{4,12},{8,0},{12,4},{16,24},{20,28},{24,16},{28,20},{1,9},{5... | collective-permute-start | bytes 233480 | tf_op jit(solution)/shard_map/ppermute | solution.py:20
  16.1 6.2 %collective-permute-start.3 = (bf16[304,128]{1,0:T(8,128)(2,1)S(1)}, bf16[304,128]{1,0:T(8,128)(2,1)S(1)}, u32[]{:S(2)}, u32[]{:S(2)}) collective-permute-start(bf16[304,128]{1,0:T(8,128)(2,1)S(1)} %pad_maximum_fusion.1), channel_id=1, source_target_pairs={{0,16},{4,20},{8,24},{12,28},{16,0},{20,4},{24,8},{28,12},{1,17},{... | collective-permute-start | bytes 233480 | tf_op jit(solution)/shard_map/ppermute | solution.py:20
  22.3 4.3 %collective-permute-start.4 = (bf16[1,256,128]{2,1,0:T(8,128)(2,1)S(1)}, bf16[1,256,128]{2,1,0:T(8,128)(2,1)S(1)}, u32[]{:S(2)}, u32[]{:S(2)}) collective-permute-start(bf16[1,256,128]{2,1,0:T(8,128)(2,1)S(1)} %fusion.2), channel_id=1, source_target_pairs={{0,2},{1,3},{2,0},{3,1},{4,6},{5,7},{6,4},{7,5},{8,10},{9,11},{10,... | collective-permute-start | bytes 196616 | tf_op jit(solution)/shard_map/ppermute | solution.py:20
  26.7 5.9 %collective-permute-start.7 = (bf16[2,256,128]{2,1,0:T(8,128)(2,1)S(1)}, bf16[2,256,128]{2,1,0:T(8,128)(2,1)S(1)}, u32[]{:S(2)}, u32[]{:S(2)}) collective-permute-start(bf16[2,256,128]{2,1,0:T(8,128)(2,1)S(1)} %pad_maximum_fusion.refs_0_), channel_id=1, source_target_pairs={{0,12},{4,8},{8,4},{12,0},{16,28},{20,24},{24,20},{28,16},{1,13},{... | collective-permute-start | bytes 393224 | tf_op jit(solution)/shard_map/ppermute | solution.py:20
  27.4 6.6 %collective-permute-start.6 = (bf16[2,256,128]{2,1,0:T(8,128)(2,1)S(1)}, bf16[2,256,128]{2,1,0:T(8,128)(2,1)S(1)}, u32[]{:S(2)}, u32[]{:S(2)}) collective-permute-start(bf16[2,256,128]{2,1,0:T(8,128)(2,1)S(1)} %pad_maximum_fusion.refs_0_), channel_id=1, source_target_pairs={{0,8},{4,12},{8,0},{12,4},{16,24},{20,28},{24,16},{28,20},{1,9},{5... | collective-permute-start | bytes 393224 | tf_op jit(solution)/shard_map/ppermute | solution.py:20
  29.6 5.0 %collective-permute-start.5 = (bf16[2,256,128]{2,1,0:T(8,128)(2,1)S(1)}, bf16[2,256,128]{2,1,0:T(8,128)(2,1)S(1)}, u32[]{:S(2)}, u32[]{:S(2)}) collective-permute-start(bf16[2,256,128]{2,1,0:T(8,128)(2,1)S(1)} %pad_maximum_fusion.refs_0_), channel_id=1, source_target_pairs={{0,4},{4,0},{8,12},{12,8},{16,20},{20,16},{24,28},{28,24},{1,5},{5... | collective-permute-start | bytes 393224 | tf_op jit(solution)/shard_map/ppermute | solution.py:20
  30.2 4.3 %collective-permute-start.8 = (bf16[2,256,128]{2,1,0:T(8,128)(2,1)S(1)}, bf16[2,256,128]{2,1,0:T(8,128)(2,1)S(1)}, u32[]{:S(2)}, u32[]{:S(2)}) collective-permute-start(bf16[2,256,128]{2,1,0:T(8,128)(2,1)S(1)} %pad_maximum_fusion.refs_0_), channel_id=1, source_target_pairs={{0,1},{1,0},{2,3},{3,2},{4,5},{5,4},{6,7},{7,6},{8,9},{9,8},{10,11... | collective-permute-start | bytes 393224 | tf_op jit(solution)/shard_map/ppermute | solution.py:20
  32.6 2.0 %collective-permute-start.11 = (bf16[2,256,128]{2,1,0:T(8,128)(2,1)S(1)}, bf16[2,256,128]{2,1,0:T(8,128)(2,1)S(1)}, u32[]{:S(2)}, u32[]{:S(2)}) collective-permute-start(bf16[2,256,128]{2,1,0:T(8,128)(2,1)S(1)} %collective-permute-done.7.refs_3_), channel_id=1, source_target_pairs={{0,1},{1,0},{2,3},{3,2},{4,5},{5,4},{6,7},{7,6},{8,9},{9,8},{10,11... | collective-permute-start | bytes 393224 | tf_op jit(solution)/shard_map/ppermute | solution.py:20
  33.9 1.3 %collective-permute-start.10 = (bf16[2,256,128]{2,1,0:T(8,128)(2,1)S(1)}, bf16[2,256,128]{2,1,0:T(8,128)(2,1)S(1)}, u32[]{:S(2)}, u32[]{:S(2)}) collective-permute-start(bf16[2,256,128]{2,1,0:T(8,128)(2,1)S(1)} %collective-permute-done.6.refs_2_), channel_id=1, source_target_pairs={{0,1},{1,0},{2,3},{3,2},{4,5},{5,4},{6,7},{7,6},{8,9},{9,8},{10,11... | collective-permute-start | bytes 393224 | tf_op jit(solution)/shard_map/ppermute | solution.py:20
  34.6 1.3 %collective-permute-start.9 = (bf16[2,256,128]{2,1,0:T(8,128)(2,1)S(1)}, bf16[2,256,128]{2,1,0:T(8,128)(2,1)S(1)}, u32[]{:S(2)}, u32[]{:S(2)}) collective-permute-start(bf16[2,256,128]{2,1,0:T(8,128)(2,1)S(1)} %collective-permute-done.5.refs_1_), channel_id=1, source_target_pairs={{0,1},{1,0},{2,3},{3,2},{4,5},{5,4},{6,7},{7,6},{8,9},{9,8},{10,11... | collective-permute-start | bytes 393224 | tf_op jit(solution)/shard_map/ppermute | solution.py:20

commit v7 on v6

--- a/solution.py
+++ b/solution.py
@@ -117,11 +117,11 @@
 
 
 def gram_kernel(sizes, *refs):
-    n_time, snaps, modes, row_block, col_block, target_block, tile = sizes
+    n_time, snaps, modes, row_block, col_block, target_block, tops = sizes
     half, quarter = n_time // 2, snaps // QUAD
     count = 2 * QUAD
     pieces, (gram_hbm, rhs_ref) = refs[0:count], refs[count : count + 2]
-    delayed, head, rows, cols, opening, opening_target, staged, side, sems = refs[count + 2 :]
+    lead, head, target, coeffs, rows, cols, staged, side, sems = refs[count + 2 :]
     later = (n_time - 1) * snaps
     time_pos, space_pos = lax.axis_index("tm"), lax.axis_index("space")
     place = lax.rem(space_pos, QUAD)
@@ -131,50 +131,44 @@
             for k in range(half):
                 block = jnp.bitwise_xor(time_pos, 2 * k + other)
                 for j in range(QUAD):
-                    within = pl.multiple_of(jnp.bitwise_xor(place, j) * quarter, quarter)
-                    take(pieces[other * QUAD + j].at[k], block, within)
-
-    def later_at(block, within):
-        return pl.ds(pl.multiple_of((block - 1) * snaps + within, quarter), quarter)
-
-    delayed[1, :, 0:snaps] = jnp.zeros((LEAD_MODES, snaps), jnp.bfloat16)
+                    at = block * snaps + jnp.bitwise_xor(place, j) * quarter
+                    take(pieces[other * QUAD + j].at[k], pl.multiple_of(at, quarter))
+
+    gap = 2 * snaps
+    lead[:, 0:gap] = jnp.zeros((LEAD_MODES, gap), jnp.bfloat16)
+    target[:, n_time * snaps :] = jnp.zeros((target_block, snaps), jnp.bfloat16)
     wanted = pl.ds(pl.multiple_of(space_pos * target_block, ROW_TILE), target_block)
-    targets = pl.ds(LEAD_MODES + col_block, target_block)
-
-    def place_lead(piece, block, within):
+
+    def place_lead(piece, at):
         current = piece[0:LEAD_MODES, :]
-
-        @pl.when(block >= 1)
-        def _():
-            head[:, later_at(block, within)] = current.astype(jnp.float32)
-
-        for delay in (1, 2):
-
-            @pl.when(block + delay < n_time)
-            def _():
-                delayed[delay - 1, :, later_at(block + delay, within)] = current
+        head[:, pl.ds(at, quarter)] = current.astype(jnp.float32)
+        lead[:, pl.ds(at + gap, quarter)] = current
+        target[:, pl.ds(at, quarter)] = piece[wanted, :]
 
     each_piece(place_lead)
+
+    @pl.when((time_pos == 0) | (space_pos == 0))
+    def _():
+        def place_modes(piece, at):
+            coeffs[:, pl.ds(at, quarter)] = piece[...]
+
+        each_piece(place_modes)
 
     def fill(out, start, extent):
         @pl.when(start == 0)
         def _():
-            def place_modes(piece, block, within):
-                @pl.when(block >= 1)
-                def _():
-                    out[pl.ds(LEAD_MODES, modes), later_at(block, within)] = piece[...]
-
-            each_piece(place_modes)
+            out[pl.ds(LEAD_MODES, modes), :] = coeffs[:, snaps:]
 
         def group(q, carry):
             kind, i = lax.div(q, LEAD_MODES), lax.rem(q, LEAD_MODES)
             at = modes + LEAD_MODES * q - start + LEAD_MODES
-            factor = jnp.broadcast_to(head[pl.ds(i, 1), :], (ROW_TILE, later)).astype(
+            factor = jnp.broadcast_to(head[pl.ds(i, 1), snaps:], (ROW_TILE, later)).astype(
                 jnp.bfloat16
             )
+            shifted = pl.ds(pl.multiple_of(gap - kind * snaps, snaps), later)
             for j in range(0, LEAD_MODES, ROW_TILE):
                 out[pl.ds(pl.multiple_of(at + j, ROW_TILE), ROW_TILE), :] = (
-                    factor * delayed[kind, j : j + ROW_TILE, :]
+                    factor * lead[j : j + ROW_TILE, shifted]
                 )
             return carry
 
@@ -184,23 +178,7 @@
 
     fill(cols, space_pos * col_block, col_block)
     fill(rows, time_pos * row_block, row_block)
-
-    cols[targets, later - snaps :] = jnp.zeros((target_block, snaps), jnp.bfloat16)
-
-    def place_target(piece, block, within):
-        @pl.when(block >= 2)
-        def _():
-            cols[targets, later_at(block - 1, within)] = piece[wanted, :]
-
-        @pl.when(block == 1)
-        def _():
-            opening_target[:, pl.ds(within, quarter)] = piece[wanted, :]
-
-        @pl.when(block == 0)
-        def _():
-            opening[:, pl.ds(within, quarter)] = piece[...]
-
-    each_piece(place_target)
+    cols[pl.ds(LEAD_MODES + col_block, target_block), :] = target[:, gap:]
 
     def times(left, right):
         return lax.dot_general(
@@ -208,8 +186,8 @@
         ) * (1.0 / (n_time * snaps))
 
     writes = []
-    for step in range(row_block // tile):
-        top = step * tile
+    for step, top in enumerate(tops):
+        tile = (tops + (row_block,))[step + 1] - top
         at = pl.ds(top, tile)
         product = times(
             rows[pl.ds(LEAD_MODES + top, tile), :],
@@ -224,11 +202,11 @@
 
             @pl.when(time_pos == 0)
             def _():
-                side[0:modes, :] += times(opening[...], opening_target[...])
+                side[0:modes, :] += times(coeffs[:, 0:snaps], target[:, snaps:gap])
 
             @pl.when((time_pos == 0) & (space_pos == 0))
             def _():
-                staged[0:modes, 0:modes] += times(opening[...], opening[...])
+                staged[0:modes, 0:modes] += times(coeffs[:, 0:snaps], coeffs[:, 0:snaps])
 
         writes.append(pltpu.make_async_copy(staged.at[at], gram_hbm.at[at], sems.at[step]))
         writes[-1].start()
@@ -243,12 +221,13 @@
     features = modes + 2 * LEAD_MODES * LEAD_MODES
     row_block, col_block, target_block = features // n_time, features // n_space, modes // n_space
     later = (n_time - 1) * snaps
-    tile = row_block // 2 if row_block % (2 * ROW_TILE) == 0 else row_block
-    assert min(tile, col_block) >= modes
+    last = row_block // ROW_TILE // 4 * ROW_TILE
+    tops = (0, row_block - last) if row_block - last >= modes else (0,)
+    assert min(row_block, col_block) >= modes
     vmem = pl.BlockSpec(memory_space=pltpu.VMEM)
     gram, rhs = pl.pallas_call(
         functools.partial(
-            gram_kernel, (n_time, snaps, modes, row_block, col_block, target_block, tile)
+            gram_kernel, (n_time, snaps, modes, row_block, col_block, target_block, tops)
         ),
         out_shape=(
             jax.ShapeDtypeStruct((row_block, col_block), jnp.float32),
@@ -257,15 +236,15 @@
         in_specs=[vmem] * len(pieces),
         out_specs=(pl.BlockSpec(memory_space=pl.ANY), vmem),
         scratch_shapes=[
-            pltpu.VMEM((2, LEAD_MODES, later), jnp.bfloat16),
-            pltpu.VMEM((LEAD_MODES, later), jnp.float32),
+            pltpu.VMEM((LEAD_MODES, (n_time + 2) * snaps), jnp.bfloat16),
+            pltpu.VMEM((LEAD_MODES, n_time * snaps), jnp.float32),
+            pltpu.VMEM((target_block, (n_time + 1) * snaps), jnp.bfloat16),
+            pltpu.VMEM((modes, n_time * snaps), jnp.bfloat16),
             pltpu.VMEM((row_block + 2 * LEAD_MODES, later), jnp.bfloat16),
             pltpu.VMEM((col_block + 2 * LEAD_MODES + target_block, later), jnp.bfloat16),
-            pltpu.VMEM((modes, snaps), jnp.bfloat16),
-            pltpu.VMEM((target_block, snaps), jnp.bfloat16),
             pltpu.VMEM((row_block, col_block), jnp.float32),
             pltpu.VMEM((row_block, target_block), jnp.float32),
-            pltpu.SemaphoreType.DMA((row_block // tile,)),
+            pltpu.SemaphoreType.DMA((len(tops),)),
         ],
         compiler_params=pltpu.CompilerParams(vmem_limit_bytes=VMEM_LIMIT),
         cost_estimate=pl.CostEstimate(

time: 43.3 us -> 42.9 us (level)
    pallas_call x1, Pallas kernels: 7.28 us -> 6.82 us  [gram_blocks(): pl.pallas_call(functools.partial(gram_kernel, (n_time, snaps, modes, row_...]
where the time goes in v7:
time: 42.9 us; the launch traced here: 42.7 us
  waiting for transfers between devices  16.2 us (38%)
  Pallas kernels  13.1 us (31%)
  starting transfers between devices  12.5 us (29%)
  between operations  0.78 us (2%)
    ppermute x12, waiting for transfers between devices, swap(): return lax.ppermute(value, axis, [(i, i ^ bit) for i in range(count)])  16.2 us
    ppermute x12, starting transfers between devices, swap(): return lax.ppermute(value, axis, [(i, i ^ bit) for i in range(count)])  12.5 us
    pallas_call x1, Pallas kernels, gram_blocks(): pl.pallas_call(functools.partial(gram_kernel, (n_time, snaps, modes, row_...  6.82 us
    pallas_call x1, Pallas kernels, project(): pl.pallas_call(projection_kernel, out_shape=(pltpu.VMEM((count, quarter),...  6.24 us
  transfers between devices with their start and end apart: 12, of which 9 were waited for; matrix products, arithmetic and copies ran while one was open for 0% of the time, Pallas kernels for 0%

profile of v7, /device:TPU:0, one launch (start us, length us, event | category | flops | bytes accessed | tf_op | source)
XLA Modules:
  0.0 42.7 jit_solution(10145713711769766330)
XLA Ops:
  0.6 6.2 %shard_map.41 = (f32[256,128]{1,0:T(8,128)S(1)}, bf16[304,128]{1,0:T(8,128)(2,1)S(1)}, bf16[304,128]{1,0:T(8,128)(2,1)S(1)}, bf16[304,128]{1,0:T(8,128)(2,1)S(1)}) custom-call(bf16[10240,256]{1,0:T(8,128)(2,1)} %modes_hbm.1, bf16[10240,512]{1,0:T(8,128)(2,1)} %snaps_hbm.1), custom_call_target="tpu_custom_call" | custom-call | flops 2684354560 | bytes 15728640 | tf_op jit(solution)/shard_map/pallas_call | solution.py:96
  6.9 4.0 %collective-permute-start.2 = (bf16[304,128]{1,0:T(8,128)(2,1)S(1)}, bf16[304,128]{1,0:T(8,128)(2,1)S(1)}, u32[]{:S(2)}, u32[]{:S(2)}) collective-permute-start(bf16[304,128]{1,0:T(8,128)(2,1)S(1)} %get-tuple-element.11), channel_id=1, source_target_pairs={{0,12},{4,8},{8,4},{12,0},{16,28},{20,24},{24,20},{28,16},{1,13},{... | collective-permute-start | bytes 233480 | tf_op jit(solution)/shard_map/ppermute | solution.py:20
  10.9 0.5 %collective-permute-start = (bf16[304,128]{1,0:T(8,128)(2,1)S(1)}, bf16[304,128]{1,0:T(8,128)(2,1)S(1)}, u32[]{:S(2)}, u32[]{:S(2)}) collective-permute-start(bf16[304,128]{1,0:T(8,128)(2,1)S(1)} %get-tuple-element.9), channel_id=1, source_target_pairs={{0,4},{4,0},{8,12},{12,8},{16,20},{20,16},{24,28},{28,24},{1,5},{5... | collective-permute-start | bytes 233480 | tf_op jit(solution)/shard_map/ppermute | solution.py:20
  11.4 0.1 collective-permute-start.1
  11.6 1.8 %collective-permute-done.2 = bf16[304,128]{1,0:T(8,128)(2,1)S(1)} collective-permute-done((bf16[304,128]{1,0:T(8,128)(2,1)S(1)}, bf16[304,128]{1,0:T(8,128)(2,1)S(1)}, u32[]{:S(2)}, u32[]{:S(2)}) %collective-permute-start.2) | collective-permute-done | bytes 77856 | tf_op jit(solution)/shard_map/ppermute | solution.py:20
  13.4 2.5 %collective-permute-done.1 = bf16[304,128]{1,0:T(8,128)(2,1)S(1)} collective-permute-done((bf16[304,128]{1,0:T(8,128)(2,1)S(1)}, bf16[304,128]{1,0:T(8,128)(2,1)S(1)}, u32[]{:S(2)}, u32[]{:S(2)}) %collective-permute-start.1) | collective-permute-done | bytes 77856 | tf_op jit(solution)/shard_map/ppermute | solution.py:20
  15.9 0.0 collective-permute-done
  16.1 2.7 %collective-permute-start.3 = (bf16[304,128]{1,0:T(8,128)(2,1)S(1)}, bf16[304,128]{1,0:T(8,128)(2,1)S(1)}, u32[]{:S(2)}, u32[]{:S(2)}) collective-permute-start(bf16[304,128]{1,0:T(8,128)(2,1)S(1)} %pad_maximum_fusion.1), channel_id=1, source_target_pairs={{0,16},{4,20},{8,24},{12,28},{16,0},{20,4},{24,8},{28,12},{1,17},{... | collective-permute-start | bytes 233480 | tf_op jit(solution)/shard_map/ppermute | solution.py:20
  18.7 3.5 %collective-permute-done.3 = bf16[304,128]{1,0:T(8,128)(2,1)S(1)} collective-permute-done((bf16[304,128]{1,0:T(8,128)(2,1)S(1)}, bf16[304,128]{1,0:T(8,128)(2,1)S(1)}, u32[]{:S(2)}, u32[]{:S(2)}) %collective-permute-start.3) | collective-permute-done | bytes 77856 | tf_op jit(solution)/shard_map/ppermute | solution.py:20
  22.3 1.6 %collective-permute-start.4 = (bf16[1,256,128]{2,1,0:T(8,128)(2,1)S(1)}, bf16[1,256,128]{2,1,0:T(8,128)(2,1)S(1)}, u32[]{:S(2)}, u32[]{:S(2)}) collective-permute-start(bf16[1,256,128]{2,1,0:T(8,128)(2,1)S(1)} %fusion.2), channel_id=1, source_target_pairs={{0,2},{1,3},{2,0},{3,1},{4,6},{5,7},{6,4},{7,5},{8,10},{9,11},{10,... | collective-permute-start | bytes 196616 | tf_op jit(solution)/shard_map/ppermute | solution.py:20
  23.9 2.7 %collective-permute-done.4 = bf16[1,256,128]{2,1,0:T(8,128)(2,1)S(1)} collective-permute-done((bf16[1,256,128]{2,1,0:T(8,128)(2,1)S(1)}, bf16[1,256,128]{2,1,0:T(8,128)(2,1)S(1)}, u32[]{:S(2)}, u32[]{:S(2)}) %collective-permute-start.4) | collective-permute-done | bytes 65568 | tf_op jit(solution)/shard_map/ppermute | solution.py:20
  26.7 0.7 %collective-permute-start.7 = (bf16[2,256,128]{2,1,0:T(8,128)(2,1)S(1)}, bf16[2,256,128]{2,1,0:T(8,128)(2,1)S(1)}, u32[]{:S(2)}, u32[]{:S(2)}) collective-permute-start(bf16[2,256,128]{2,1,0:T(8,128)(2,1)S(1)} %pad_maximum_fusion.refs_0_), channel_id=1, source_target_pairs={{0,12},{4,8},{8,4},{12,0},{16,28},{20,24},{24,20},{28,16},{1,13},{... | collective-permute-start | bytes 393224 | tf_op jit(solution)/shard_map/ppermute | solution.py:20
  27.4 2.2 %collective-permute-start.6 = (bf16[2,256,128]{2,1,0:T(8,128)(2,1)S(1)}, bf16[2,256,128]{2,1,0:T(8,128)(2,1)S(1)}, u32[]{:S(2)}, u32[]{:S(2)}) collective-permute-start(bf16[2,256,128]{2,1,0:T(8,128)(2,1)S(1)} %pad_maximum_fusion.refs_0_), channel_id=1, source_target_pairs={{0,8},{4,12},{8,0},{12,4},{16,24},{20,28},{24,16},{28,20},{1,9},{5... | collective-permute-start | bytes 393224 | tf_op jit(solution)/shard_map/ppermute | solution.py:20
  29.6 0.6 %collective-permute-start.5 = (bf16[2,256,128]{2,1,0:T(8,128)(2,1)S(1)}, bf16[2,256,128]{2,1,0:T(8,128)(2,1)S(1)}, u32[]{:S(2)}, u32[]{:S(2)}) collective-permute-start(bf16[2,256,128]{2,1,0:T(8,128)(2,1)S(1)} %pad_maximum_fusion.refs_0_), channel_id=1, source_target_pairs={{0,4},{4,0},{8,12},{12,8},{16,20},{20,16},{24,28},{28,24},{1,5},{5... | collective-permute-start | bytes 393224 | tf_op jit(solution)/shard_map/ppermute | solution.py:20
  30.2 0.0 collective-permute-start.8
  30.2 2.4 %collective-permute-done.7.refs_3_ = bf16[2,256,128]{2,1,0:T(8,128)(2,1)S(1)} collective-permute-done((bf16[2,256,128]{2,1,0:T(8,128)(2,1)S(1)}, bf16[2,256,128]{2,1,0:T(8,128)(2,1)S(1)}, u32[]{:S(2)}, u32[]{:S(2)}) %collective-permute-start.7) | collective-permute-done | bytes 131104 | tf_op jit(solution)/shard_map/ppermute | solution.py:20
  32.6 0.0 collective-permute-start.11
  32.6 1.3 %collective-permute-done.6.refs_2_ = bf16[2,256,128]{2,1,0:T(8,128)(2,1)S(1)} collective-permute-done((bf16[2,256,128]{2,1,0:T(8,128)(2,1)S(1)}, bf16[2,256,128]{2,1,0:T(8,128)(2,1)S(1)}, u32[]{:S(2)}, u32[]{:S(2)}) %collective-permute-start.6) | collective-permute-done | bytes 131104 | tf_op jit(solution)/shard_map/ppermute | solution.py:20
  33.9 0.0 collective-permute-start.10
  34.0 0.6 %collective-permute-done.5.refs_1_ = bf16[2,256,128]{2,1,0:T(8,128)(2,1)S(1)} collective-permute-done((bf16[2,256,128]{2,1,0:T(8,128)(2,1)S(1)}, bf16[2,256,128]{2,1,0:T(8,128)(2,1)S(1)}, u32[]{:S(2)}, u32[]{:S(2)}) %collective-permute-start.5) | collective-permute-done | bytes 131104 | tf_op jit(solution)/shard_map/ppermute | solution.py:20
  34.6 0.0 collective-permute-start.9
  34.6 0.0 collective-permute-done.8.refs_4_
  34.6 0.0 collective-permute-done.11.refs_7_
  34.6 0.7 %collective-permute-done.10.refs_6_ = bf16[2,256,128]{2,1,0:T(8,128)(2,1)S(1)} collective-permute-done((bf16[2,256,128]{2,1,0:T(8,128)(2,1)S(1)}, bf16[2,256,128]{2,1,0:T(8,128)(2,1)S(1)}, u32[]{:S(2)}, u32[]{:S(2)}) %collective-permute-start.10) | collective-permute-done | bytes 131104 | tf_op jit(solution)/shard_map/ppermute | solution.py:20
  35.3 0.6 %collective-permute-done.9.refs_5_ = bf16[2,256,128]{2,1,0:T(8,128)(2,1)S(1)} collective-permute-done((bf16[2,256,128]{2,1,0:T(8,128)(2,1)S(1)}, bf16[2,256,128]{2,1,0:T(8,128)(2,1)S(1)}, u32[]{:S(2)}, u32[]{:S(2)}) %collective-permute-start.9) | collective-permute-done | bytes 131104 | tf_op jit(solution)/shard_map/ppermute | solution.py:20
  35.9 6.8 %shard_map.42 = (f32[1216,608]{1,0:T(8,128)}, f32[32,1216]{1,0:T(8,128)}) custom-call(bf16[2,256,128]{2,1,0:T(8,128)(2,1)S(1)} %pad_maximum_fusion.refs_0_, bf16[2,256,128]{2,1,0:T(8,128)(2,1)S(1)} %collective-permute-done.5.refs_1_, bf16[2,256,128]{2,1,0:T(8,128)(2,1)S(1)} %collective-permute-done.6.refs_2_, ...), custom_call_target="tpu_custom_call" | custom-call | flops 2390753280 | bytes 3112960 | tf_op jit(solution)/shard_map/pallas_call | solution.py:228
  (19 shorter events, 0.2 us)
Async XLA Ops:
  6.9 6.5 %collective-permute-start.2 = (bf16[304,128]{1,0:T(8,128)(2,1)S(1)}, bf16[304,128]{1,0:T(8,128)(2,1)S(1)}, u32[]{:S(2)}, u32[]{:S(2)}) collective-permute-start(bf16[304,128]{1,0:T(8,128)(2,1)S(1)} %get-tuple-element.11), channel_id=1, source_target_pairs={{0,12},{4,8},{8,4},{12,0},{16,28},{20,24},{24,20},{28,16},{1,13},{... | collective-permute-start | bytes 233480 | tf_op jit(solution)/shard_map/ppermute | solution.py:20
  10.9 5.0 %collective-permute-start = (bf16[304,128]{1,0:T(8,128)(2,1)S(1)}, bf16[304,128]{1,0:T(8,128)(2,1)S(1)}, u32[]{:S(2)}, u32[]{:S(2)}) collective-permute-start(bf16[304,128]{1,0:T(8,128)(2,1)S(1)} %get-tuple-element.9), channel_id=1, source_target_pairs={{0,4},{4,0},{8,12},{12,8},{16,20},{20,16},{24,28},{28,24},{1,5},{5... | collective-permute-start | bytes 233480 | tf_op jit(solution)/shard_map/ppermute | solution.py:20
  11.4 4.4 %collective-permute-start.1 = (bf16[304,128]{1,0:T(8,128)(2,1)S(1)}, bf16[304,128]{1,0:T(8,128)(2,1)S(1)}, u32[]{:S(2)}, u32[]{:S(2)}) collective-permute-start(bf16[304,128]{1,0:T(8,128)(2,1)S(1)} %get-tuple-element.10), channel_id=1, source_target_pairs={{0,8},{4,12},{8,0},{12,4},{16,24},{20,28},{24,16},{28,20},{1,9},{5... | collective-permute-start | bytes 233480 | tf_op jit(solution)/shard_map/ppermute | solution.py:20
  16.1 6.2 %collective-permute-start.3 = (bf16[304,128]{1,0:T(8,128)(2,1)S(1)}, bf16[304,128]{1,0:T(8,128)(2,1)S(1)}, u32[]{:S(2)}, u32[]{:S(2)}) collective-permute-start(bf16[304,128]{1,0:T(8,128)(2,1)S(1)} %pad_maximum_fusion.1), channel_id=1, source_target_pairs={{0,16},{4,20},{8,24},{12,28},{16,0},{20,4},{24,8},{28,12},{1,17},{... | collective-permute-start | bytes 233480 | tf_op jit(solution)/shard_map/ppermute | solution.py:20
  22.3 4.3 %collective-permute-start.4 = (bf16[1,256,128]{2,1,0:T(8,128)(2,1)S(1)}, bf16[1,256,128]{2,1,0:T(8,128)(2,1)S(1)}, u32[]{:S(2)}, u32[]{:S(2)}) collective-permute-start(bf16[1,256,128]{2,1,0:T(8,128)(2,1)S(1)} %fusion.2), channel_id=1, source_target_pairs={{0,2},{1,3},{2,0},{3,1},{4,6},{5,7},{6,4},{7,5},{8,10},{9,11},{10,... | collective-permute-start | bytes 196616 | tf_op jit(solution)/shard_map/ppermute | solution.py:20
  26.7 5.9 %collective-permute-start.7 = (bf16[2,256,128]{2,1,0:T(8,128)(2,1)S(1)}, bf16[2,256,128]{2,1,0:T(8,128)(2,1)S(1)}, u32[]{:S(2)}, u32[]{:S(2)}) collective-permute-start(bf16[2,256,128]{2,1,0:T(8,128)(2,1)S(1)} %pad_maximum_fusion.refs_0_), channel_id=1, source_target_pairs={{0,12},{4,8},{8,4},{12,0},{16,28},{20,24},{24,20},{28,16},{1,13},{... | collective-permute-start | bytes 393224 | tf_op jit(solution)/shard_map/ppermute | solution.py:20
  27.4 6.6 %collective-permute-start.6 = (bf16[2,256,128]{2,1,0:T(8,128)(2,1)S(1)}, bf16[2,256,128]{2,1,0:T(8,128)(2,1)S(1)}, u32[]{:S(2)}, u32[]{:S(2)}) collective-permute-start(bf16[2,256,128]{2,1,0:T(8,128)(2,1)S(1)} %pad_maximum_fusion.refs_0_), channel_id=1, source_target_pairs={{0,8},{4,12},{8,0},{12,4},{16,24},{20,28},{24,16},{28,20},{1,9},{5... | collective-permute-start | bytes 393224 | tf_op jit(solution)/shard_map/ppermute | solution.py:20
  29.6 5.0 %collective-permute-start.5 = (bf16[2,256,128]{2,1,0:T(8,128)(2,1)S(1)}, bf16[2,256,128]{2,1,0:T(8,128)(2,1)S(1)}, u32[]{:S(2)}, u32[]{:S(2)}) collective-permute-start(bf16[2,256,128]{2,1,0:T(8,128)(2,1)S(1)} %pad_maximum_fusion.refs_0_), channel_id=1, source_target_pairs={{0,4},{4,0},{8,12},{12,8},{16,20},{20,16},{24,28},{28,24},{1,5},{5... | collective-permute-start | bytes 393224 | tf_op jit(solution)/shard_map/ppermute | solution.py:20
  30.2 4.3 %collective-permute-start.8 = (bf16[2,256,128]{2,1,0:T(8,128)(2,1)S(1)}, bf16[2,256,128]{2,1,0:T(8,128)(2,1)S(1)}, u32[]{:S(2)}, u32[]{:S(2)}) collective-permute-start(bf16[2,256,128]{2,1,0:T(8,128)(2,1)S(1)} %pad_maximum_fusion.refs_0_), channel_id=1, source_target_pairs={{0,1},{1,0},{2,3},{3,2},{4,5},{5,4},{6,7},{7,6},{8,9},{9,8},{10,11... | collective-permute-start | bytes 393224 | tf_op jit(solution)/shard_map/ppermute | solution.py:20
  32.6 2.0 %collective-permute-start.11 = (bf16[2,256,128]{2,1,0:T(8,128)(2,1)S(1)}, bf16[2,256,128]{2,1,0:T(8,128)(2,1)S(1)}, u32[]{:S(2)}, u32[]{:S(2)}) collective-permute-start(bf16[2,256,128]{2,1,0:T(8,128)(2,1)S(1)} %collective-permute-done.7.refs_3_), channel_id=1, source_target_pairs={{0,1},{1,0},{2,3},{3,2},{4,5},{5,4},{6,7},{7,6},{8,9},{9,8},{10,11... | collective-permute-start | bytes 393224 | tf_op jit(solution)/shard_map/ppermute | solution.py:20
  33.9 1.3 %collective-permute-start.10 = (bf16[2,256,128]{2,1,0:T(8,128)(2,1)S(1)}, bf16[2,256,128]{2,1,0:T(8,128)(2,1)S(1)}, u32[]{:S(2)}, u32[]{:S(2)}) collective-permute-start(bf16[2,256,128]{2,1,0:T(8,128)(2,1)S(1)} %collective-permute-done.6.refs_2_), channel_id=1, source_target_pairs={{0,1},{1,0},{2,3},{3,2},{4,5},{5,4},{6,7},{7,6},{8,9},{9,8},{10,11... | collective-permute-start | bytes 393224 | tf_op jit(solution)/shard_map/ppermute | solution.py:20
  34.6 1.3 %collective-permute-start.9 = (bf16[2,256,128]{2,1,0:T(8,128)(2,1)S(1)}, bf16[2,256,128]{2,1,0:T(8,128)(2,1)S(1)}, u32[]{:S(2)}, u32[]{:S(2)}) collective-permute-start(bf16[2,256,128]{2,1,0:T(8,128)(2,1)S(1)} %collective-permute-done.5.refs_1_), channel_id=1, source_target_pairs={{0,1},{1,0},{2,3},{3,2},{4,5},{5,4},{6,7},{7,6},{8,9},{9,8},{10,11... | collective-permute-start | bytes 393224 | tf_op jit(solution)/shard_map/ppermute | solution.py:20

commit v8 on v7

--- a/solution.py
+++ b/solution.py
@@ -117,11 +117,11 @@
 
 
 def gram_kernel(sizes, *refs):
-    n_time, snaps, modes, row_block, col_block, target_block, tops = sizes
+    n_time, snaps, modes, row_block, col_block, target_block, tile = sizes
     half, quarter = n_time // 2, snaps // QUAD
     count = 2 * QUAD
     pieces, (gram_hbm, rhs_ref) = refs[0:count], refs[count : count + 2]
-    lead, head, target, coeffs, rows, cols, staged, side, sems = refs[count + 2 :]
+    lead, head, target, coeffs, *rows, cols, staged, side, sems = refs[count + 2 :]
     later = (n_time - 1) * snaps
     time_pos, space_pos = lax.axis_index("tm"), lax.axis_index("space")
     place = lax.rem(space_pos, QUAD)
@@ -154,30 +154,40 @@
 
         each_piece(place_modes)
 
+    def build_group(out, q, at):
+        kind, i = lax.div(q, LEAD_MODES), lax.rem(q, LEAD_MODES)
+        factor = jnp.broadcast_to(head[pl.ds(i, 1), snaps:], (ROW_TILE, later)).astype(
+            jnp.bfloat16
+        )
+        shifted = pl.ds(pl.multiple_of(gap - kind * snaps, snaps), later)
+        for j in range(0, LEAD_MODES, ROW_TILE):
+            out[pl.ds(pl.multiple_of(at + j, ROW_TILE), ROW_TILE), :] = (
+                factor * lead[j : j + ROW_TILE, shifted]
+            )
+
     def fill(out, start, extent):
         @pl.when(start == 0)
         def _():
             out[pl.ds(LEAD_MODES, modes), :] = coeffs[:, snaps:]
 
         def group(q, carry):
-            kind, i = lax.div(q, LEAD_MODES), lax.rem(q, LEAD_MODES)
-            at = modes + LEAD_MODES * q - start + LEAD_MODES
-            factor = jnp.broadcast_to(head[pl.ds(i, 1), snaps:], (ROW_TILE, later)).astype(
-                jnp.bfloat16
-            )
-            shifted = pl.ds(pl.multiple_of(gap - kind * snaps, snaps), later)
-            for j in range(0, LEAD_MODES, ROW_TILE):
-                out[pl.ds(pl.multiple_of(at + j, ROW_TILE), ROW_TILE), :] = (
-                    factor * lead[j : j + ROW_TILE, shifted]
-                )
+            build_group(out, q, modes + LEAD_MODES * q - start + LEAD_MODES)
             return carry
 
         first = jnp.maximum(0, lax.div(start - modes, LEAD_MODES))
         last = lax.div(start + extent - modes + LEAD_MODES - 1, LEAD_MODES)
         lax.fori_loop(first, last, group, 0)
 
+    def fill_products(out, start, extent):
+        first = lax.div(start - modes, LEAD_MODES)
+        most = 2 * LEAD_MODES - 1
+        for g in range(-(-(extent + LEAD_MODES - ROW_TILE) // LEAD_MODES)):
+            at = modes + LEAD_MODES * (first + g) - start + LEAD_MODES
+            build_group(out, jnp.minimum(first + g, most), at)
+
+    row_start = time_pos * row_block
     fill(cols, space_pos * col_block, col_block)
-    fill(rows, time_pos * row_block, row_block)
+    fill(rows[0], row_start, tile)
     cols[pl.ds(LEAD_MODES + col_block, target_block), :] = target[:, gap:]
 
     def times(left, right):
@@ -186,11 +196,13 @@
         ) * (1.0 / (n_time * snaps))
 
     writes = []
-    for step, top in enumerate(tops):
-        tile = (tops + (row_block,))[step + 1] - top
+    for step in range(row_block // tile):
+        top = step * tile
         at = pl.ds(top, tile)
+        if top + tile < row_block:
+            fill_products(rows[(step + 1) % 2], row_start + top + tile, tile)
         product = times(
-            rows[pl.ds(LEAD_MODES + top, tile), :],
+            rows[step % 2][pl.ds(LEAD_MODES, tile), :],
             cols[pl.ds(LEAD_MODES, col_block + target_block), :],
         )
         shape = (tile, col_block)
@@ -221,13 +233,12 @@
     features = modes + 2 * LEAD_MODES * LEAD_MODES
     row_block, col_block, target_block = features // n_time, features // n_space, modes // n_space
     later = (n_time - 1) * snaps
-    last = row_block // ROW_TILE // 4 * ROW_TILE
-    tops = (0, row_block - last) if row_block - last >= modes else (0,)
-    assert min(row_block, col_block) >= modes
+    tile = row_block // 4 if row_block % (4 * ROW_TILE) == 0 else row_block
+    assert min(tile, col_block) >= modes
     vmem = pl.BlockSpec(memory_space=pltpu.VMEM)
     gram, rhs = pl.pallas_call(
         functools.partial(
-            gram_kernel, (n_time, snaps, modes, row_block, col_block, target_block, tops)
+            gram_kernel, (n_time, snaps, modes, row_block, col_block, target_block, tile)
         ),
         out_shape=(
             jax.ShapeDtypeStruct((row_block, col_block), jnp.float32),
@@ -240,11 +251,12 @@
             pltpu.VMEM((LEAD_MODES, n_time * snaps), jnp.float32),
             pltpu.VMEM((target_block, (n_time + 1) * snaps), jnp.bfloat16),
             pltpu.VMEM((modes, n_time * snaps), jnp.bfloat16),
-            pltpu.VMEM((row_block + 2 * LEAD_MODES, later), jnp.bfloat16),
+            pltpu.VMEM((tile + 2 * LEAD_MODES, later), jnp.bfloat16),
+            pltpu.VMEM((tile + 2 * LEAD_MODES, later), jnp.bfloat16),
             pltpu.VMEM((col_block + 2 * LEAD_MODES + target_block, later), jnp.bfloat16),
             pltpu.VMEM((row_block, col_block), jnp.float32),
             pltpu.VMEM((row_block, target_block), jnp.float32),
-            pltpu.SemaphoreType.DMA((len(tops),)),
+            pltpu.SemaphoreType.DMA((row_block // tile,)),
         ],
         compiler_params=pltpu.CompilerParams(vmem_limit_bytes=VMEM_LIMIT),
         cost_estimate=pl.CostEstimate(

time: 42.9 us -> 42.5 us (level)
  no operation moved by 1% of the time
where the time goes in v8:
time: 42.5 us; the launch traced here: 42.3 us
  waiting for transfers between devices  16.2 us (38%)
  Pallas kernels  12.7 us (30%)
  starting transfers between devices  12.5 us (29%)
  between operations  0.78 us (2%)
    ppermute x12, waiting for transfers between devices, swap(): return lax.ppermute(value, axis, [(i, i ^ bit) for i in range(count)])  16.2 us
    ppermute x12, starting transfers between devices, swap(): return lax.ppermute(value, axis, [(i, i ^ bit) for i in range(count)])  12.5 us
    pallas_call x1, Pallas kernels, gram_blocks(): pl.pallas_call(functools.partial(gram_kernel, (n_time, snaps, modes, row_...  6.42 us
    pallas_call x1, Pallas kernels, project(): pl.pallas_call(projection_kernel, out_shape=(pltpu.VMEM((count, quarter),...  6.24 us
  transfers between devices with their start and end apart: 12, of which 9 were waited for; matrix products, arithmetic and copies ran while one was open for 0% of the time, Pallas kernels for 0%

profile of v8, /device:TPU:0, one launch (start us, length us, event | category | flops | bytes accessed | tf_op | source)
XLA Modules:
  0.0 42.3 jit_solution(6192110458740541380)
XLA Ops:
  0.6 6.2 %shard_map.41 = (f32[256,128]{1,0:T(8,128)S(1)}, bf16[304,128]{1,0:T(8,128)(2,1)S(1)}, bf16[304,128]{1,0:T(8,128)(2,1)S(1)}, bf16[304,128]{1,0:T(8,128)(2,1)S(1)}) custom-call(bf16[10240,256]{1,0:T(8,128)(2,1)} %modes_hbm.1, bf16[10240,512]{1,0:T(8,128)(2,1)} %snaps_hbm.1), custom_call_target="tpu_custom_call" | custom-call | flops 2684354560 | bytes 15728640 | tf_op jit(solution)/shard_map/pallas_call | solution.py:96
  6.9 4.0 %collective-permute-start.2 = (bf16[304,128]{1,0:T(8,128)(2,1)S(1)}, bf16[304,128]{1,0:T(8,128)(2,1)S(1)}, u32[]{:S(2)}, u32[]{:S(2)}) collective-permute-start(bf16[304,128]{1,0:T(8,128)(2,1)S(1)} %get-tuple-element.11), channel_id=1, source_target_pairs={{0,12},{4,8},{8,4},{12,0},{16,28},{20,24},{24,20},{28,16},{1,13},{... | collective-permute-start | bytes 233480 | tf_op jit(solution)/shard_map/ppermute | solution.py:20
  10.9 0.5 %collective-permute-start = (bf16[304,128]{1,0:T(8,128)(2,1)S(1)}, bf16[304,128]{1,0:T(8,128)(2,1)S(1)}, u32[]{:S(2)}, u32[]{:S(2)}) collective-permute-start(bf16[304,128]{1,0:T(8,128)(2,1)S(1)} %get-tuple-element.9), channel_id=1, source_target_pairs={{0,4},{4,0},{8,12},{12,8},{16,20},{20,16},{24,28},{28,24},{1,5},{5... | collective-permute-start | bytes 233480 | tf_op jit(solution)/shard_map/ppermute | solution.py:20
  11.4 0.1 collective-permute-start.1
  11.6 1.8 %collective-permute-done.2 = bf16[304,128]{1,0:T(8,128)(2,1)S(1)} collective-permute-done((bf16[304,128]{1,0:T(8,128)(2,1)S(1)}, bf16[304,128]{1,0:T(8,128)(2,1)S(1)}, u32[]{:S(2)}, u32[]{:S(2)}) %collective-permute-start.2) | collective-permute-done | bytes 77856 | tf_op jit(solution)/shard_map/ppermute | solution.py:20
  13.4 2.5 %collective-permute-done.1 = bf16[304,128]{1,0:T(8,128)(2,1)S(1)} collective-permute-done((bf16[304,128]{1,0:T(8,128)(2,1)S(1)}, bf16[304,128]{1,0:T(8,128)(2,1)S(1)}, u32[]{:S(2)}, u32[]{:S(2)}) %collective-permute-start.1) | collective-permute-done | bytes 77856 | tf_op jit(solution)/shard_map/ppermute | solution.py:20
  15.9 0.0 collective-permute-done
  16.1 2.7 %collective-permute-start.3 = (bf16[304,128]{1,0:T(8,128)(2,1)S(1)}, bf16[304,128]{1,0:T(8,128)(2,1)S(1)}, u32[]{:S(2)}, u32[]{:S(2)}) collective-permute-start(bf16[304,128]{1,0:T(8,128)(2,1)S(1)} %pad_maximum_fusion.1), channel_id=1, source_target_pairs={{0,16},{4,20},{8,24},{12,28},{16,0},{20,4},{24,8},{28,12},{1,17},{... | collective-permute-start | bytes 233480 | tf_op jit(solution)/shard_map/ppermute | solution.py:20
  18.7 3.5 %collective-permute-done.3 = bf16[304,128]{1,0:T(8,128)(2,1)S(1)} collective-permute-done((bf16[304,128]{1,0:T(8,128)(2,1)S(1)}, bf16[304,128]{1,0:T(8,128)(2,1)S(1)}, u32[]{:S(2)}, u32[]{:S(2)}) %collective-permute-start.3) | collective-permute-done | bytes 77856 | tf_op jit(solution)/shard_map/ppermute | solution.py:20
  22.3 1.6 %collective-permute-start.4 = (bf16[1,256,128]{2,1,0:T(8,128)(2,1)S(1)}, bf16[1,256,128]{2,1,0:T(8,128)(2,1)S(1)}, u32[]{:S(2)}, u32[]{:S(2)}) collective-permute-start(bf16[1,256,128]{2,1,0:T(8,128)(2,1)S(1)} %fusion.2), channel_id=1, source_target_pairs={{0,2},{1,3},{2,0},{3,1},{4,6},{5,7},{6,4},{7,5},{8,10},{9,11},{10,... | collective-permute-start | bytes 196616 | tf_op jit(solution)/shard_map/ppermute | solution.py:20
  23.9 2.7 %collective-permute-done.4 = bf16[1,256,128]{2,1,0:T(8,128)(2,1)S(1)} collective-permute-done((bf16[1,256,128]{2,1,0:T(8,128)(2,1)S(1)}, bf16[1,256,128]{2,1,0:T(8,128)(2,1)S(1)}, u32[]{:S(2)}, u32[]{:S(2)}) %collective-permute-start.4) | collective-permute-done | bytes 65568 | tf_op jit(solution)/shard_map/ppermute | solution.py:20
  26.7 0.7 %collective-permute-start.7 = (bf16[2,256,128]{2,1,0:T(8,128)(2,1)S(1)}, bf16[2,256,128]{2,1,0:T(8,128)(2,1)S(1)}, u32[]{:S(2)}, u32[]{:S(2)}) collective-permute-start(bf16[2,256,128]{2,1,0:T(8,128)(2,1)S(1)} %pad_maximum_fusion.refs_0_), channel_id=1, source_target_pairs={{0,12},{4,8},{8,4},{12,0},{16,28},{20,24},{24,20},{28,16},{1,13},{... | collective-permute-start | bytes 393224 | tf_op jit(solution)/shard_map/ppermute | solution.py:20
  27.4 2.2 %collective-permute-start.6 = (bf16[2,256,128]{2,1,0:T(8,128)(2,1)S(1)}, bf16[2,256,128]{2,1,0:T(8,128)(2,1)S(1)}, u32[]{:S(2)}, u32[]{:S(2)}) collective-permute-start(bf16[2,256,128]{2,1,0:T(8,128)(2,1)S(1)} %pad_maximum_fusion.refs_0_), channel_id=1, source_target_pairs={{0,8},{4,12},{8,0},{12,4},{16,24},{20,28},{24,16},{28,20},{1,9},{5... | collective-permute-start | bytes 393224 | tf_op jit(solution)/shard_map/ppermute | solution.py:20
  29.6 0.6 %collective-permute-start.5 = (bf16[2,256,128]{2,1,0:T(8,128)(2,1)S(1)}, bf16[2,256,128]{2,1,0:T(8,128)(2,1)S(1)}, u32[]{:S(2)}, u32[]{:S(2)}) collective-permute-start(bf16[2,256,128]{2,1,0:T(8,128)(2,1)S(1)} %pad_maximum_fusion.refs_0_), channel_id=1, source_target_pairs={{0,4},{4,0},{8,12},{12,8},{16,20},{20,16},{24,28},{28,24},{1,5},{5... | collective-permute-start | bytes 393224 | tf_op jit(solution)/shard_map/ppermute | solution.py:20
  30.2 0.0 collective-permute-start.8
  30.2 2.4 %collective-permute-done.7.refs_3_ = bf16[2,256,128]{2,1,0:T(8,128)(2,1)S(1)} collective-permute-done((bf16[2,256,128]{2,1,0:T(8,128)(2,1)S(1)}, bf16[2,256,128]{2,1,0:T(8,128)(2,1)S(1)}, u32[]{:S(2)}, u32[]{:S(2)}) %collective-permute-start.7) | collective-permute-done | bytes 131104 | tf_op jit(solution)/shard_map/ppermute | solution.py:20
  32.6 0.0 collective-permute-start.11
  32.6 1.3 %collective-permute-done.6.refs_2_ = bf16[2,256,128]{2,1,0:T(8,128)(2,1)S(1)} collective-permute-done((bf16[2,256,128]{2,1,0:T(8,128)(2,1)S(1)}, bf16[2,256,128]{2,1,0:T(8,128)(2,1)S(1)}, u32[]{:S(2)}, u32[]{:S(2)}) %collective-permute-start.6) | collective-permute-done | bytes 131104 | tf_op jit(solution)/shard_map/ppermute | solution.py:20
  33.9 0.0 collective-permute-start.10
  34.0 0.6 %collective-permute-done.5.refs_1_ = bf16[2,256,128]{2,1,0:T(8,128)(2,1)S(1)} collective-permute-done((bf16[2,256,128]{2,1,0:T(8,128)(2,1)S(1)}, bf16[2,256,128]{2,1,0:T(8,128)(2,1)S(1)}, u32[]{:S(2)}, u32[]{:S(2)}) %collective-permute-start.5) | collective-permute-done | bytes 131104 | tf_op jit(solution)/shard_map/ppermute | solution.py:20
  34.6 0.0 collective-permute-start.9
  34.6 0.0 collective-permute-done.8.refs_4_
  34.6 0.0 collective-permute-done.11.refs_7_
  34.6 0.7 %collective-permute-done.10.refs_6_ = bf16[2,256,128]{2,1,0:T(8,128)(2,1)S(1)} collective-permute-done((bf16[2,256,128]{2,1,0:T(8,128)(2,1)S(1)}, bf16[2,256,128]{2,1,0:T(8,128)(2,1)S(1)}, u32[]{:S(2)}, u32[]{:S(2)}) %collective-permute-start.10) | collective-permute-done | bytes 131104 | tf_op jit(solution)/shard_map/ppermute | solution.py:20
  35.3 0.6 %collective-permute-done.9.refs_5_ = bf16[2,256,128]{2,1,0:T(8,128)(2,1)S(1)} collective-permute-done((bf16[2,256,128]{2,1,0:T(8,128)(2,1)S(1)}, bf16[2,256,128]{2,1,0:T(8,128)(2,1)S(1)}, u32[]{:S(2)}, u32[]{:S(2)}) %collective-permute-start.9) | collective-permute-done | bytes 131104 | tf_op jit(solution)/shard_map/ppermute | solution.py:20
  35.9 6.4 %shard_map.42 = (f32[1216,608]{1,0:T(8,128)}, f32[32,1216]{1,0:T(8,128)}) custom-call(bf16[2,256,128]{2,1,0:T(8,128)(2,1)S(1)} %pad_maximum_fusion.refs_0_, bf16[2,256,128]{2,1,0:T(8,128)(2,1)S(1)} %collective-permute-done.5.refs_1_, bf16[2,256,128]{2,1,0:T(8,128)(2,1)S(1)} %collective-permute-done.6.refs_2_, ...), custom_call_target="tpu_custom_call" | custom-call | flops 2390753280 | bytes 3112960 | tf_op jit(solution)/shard_map/pallas_call | solution.py:239
  (19 shorter events, 0.2 us)
Async XLA Ops:
  6.9 6.5 %collective-permute-start.2 = (bf16[304,128]{1,0:T(8,128)(2,1)S(1)}, bf16[304,128]{1,0:T(8,128)(2,1)S(1)}, u32[]{:S(2)}, u32[]{:S(2)}) collective-permute-start(bf16[304,128]{1,0:T(8,128)(2,1)S(1)} %get-tuple-element.11), channel_id=1, source_target_pairs={{0,12},{4,8},{8,4},{12,0},{16,28},{20,24},{24,20},{28,16},{1,13},{... | collective-permute-start | bytes 233480 | tf_op jit(solution)/shard_map/ppermute | solution.py:20
  10.9 5.0 %collective-permute-start = (bf16[304,128]{1,0:T(8,128)(2,1)S(1)}, bf16[304,128]{1,0:T(8,128)(2,1)S(1)}, u32[]{:S(2)}, u32[]{:S(2)}) collective-permute-start(bf16[304,128]{1,0:T(8,128)(2,1)S(1)} %get-tuple-element.9), channel_id=1, source_target_pairs={{0,4},{4,0},{8,12},{12,8},{16,20},{20,16},{24,28},{28,24},{1,5},{5... | collective-permute-start | bytes 233480 | tf_op jit(solution)/shard_map/ppermute | solution.py:20
  11.4 4.4 %collective-permute-start.1 = (bf16[304,128]{1,0:T(8,128)(2,1)S(1)}, bf16[304,128]{1,0:T(8,128)(2,1)S(1)}, u32[]{:S(2)}, u32[]{:S(2)}) collective-permute-start(bf16[304,128]{1,0:T(8,128)(2,1)S(1)} %get-tuple-element.10), channel_id=1, source_target_pairs={{0,8},{4,12},{8,0},{12,4},{16,24},{20,28},{24,16},{28,20},{1,9},{5... | collective-permute-start | bytes 233480 | tf_op jit(solution)/shard_map/ppermute | solution.py:20
  16.1 6.2 %collective-permute-start.3 = (bf16[304,128]{1,0:T(8,128)(2,1)S(1)}, bf16[304,128]{1,0:T(8,128)(2,1)S(1)}, u32[]{:S(2)}, u32[]{:S(2)}) collective-permute-start(bf16[304,128]{1,0:T(8,128)(2,1)S(1)} %pad_maximum_fusion.1), channel_id=1, source_target_pairs={{0,16},{4,20},{8,24},{12,28},{16,0},{20,4},{24,8},{28,12},{1,17},{... | collective-permute-start | bytes 233480 | tf_op jit(solution)/shard_map/ppermute | solution.py:20
  22.3 4.3 %collective-permute-start.4 = (bf16[1,256,128]{2,1,0:T(8,128)(2,1)S(1)}, bf16[1,256,128]{2,1,0:T(8,128)(2,1)S(1)}, u32[]{:S(2)}, u32[]{:S(2)}) collective-permute-start(bf16[1,256,128]{2,1,0:T(8,128)(2,1)S(1)} %fusion.2), channel_id=1, source_target_pairs={{0,2},{1,3},{2,0},{3,1},{4,6},{5,7},{6,4},{7,5},{8,10},{9,11},{10,... | collective-permute-start | bytes 196616 | tf_op jit(solution)/shard_map/ppermute | solution.py:20
  26.7 5.9 %collective-permute-start.7 = (bf16[2,256,128]{2,1,0:T(8,128)(2,1)S(1)}, bf16[2,256,128]{2,1,0:T(8,128)(2,1)S(1)}, u32[]{:S(2)}, u32[]{:S(2)}) collective-permute-start(bf16[2,256,128]{2,1,0:T(8,128)(2,1)S(1)} %pad_maximum_fusion.refs_0_), channel_id=1, source_target_pairs={{0,12},{4,8},{8,4},{12,0},{16,28},{20,24},{24,20},{28,16},{1,13},{... | collective-permute-start | bytes 393224 | tf_op jit(solution)/shard_map/ppermute | solution.py:20
  27.4 6.6 %collective-permute-start.6 = (bf16[2,256,128]{2,1,0:T(8,128)(2,1)S(1)}, bf16[2,256,128]{2,1,0:T(8,128)(2,1)S(1)}, u32[]{:S(2)}, u32[]{:S(2)}) collective-permute-start(bf16[2,256,128]{2,1,0:T(8,128)(2,1)S(1)} %pad_maximum_fusion.refs_0_), channel_id=1, source_target_pairs={{0,8},{4,12},{8,0},{12,4},{16,24},{20,28},{24,16},{28,20},{1,9},{5... | collective-permute-start | bytes 393224 | tf_op jit(solution)/shard_map/ppermute | solution.py:20
  29.6 5.0 %collective-permute-start.5 = (bf16[2,256,128]{2,1,0:T(8,128)(2,1)S(1)}, bf16[2,256,128]{2,1,0:T(8,128)(2,1)S(1)}, u32[]{:S(2)}, u32[]{:S(2)}) collective-permute-start(bf16[2,256,128]{2,1,0:T(8,128)(2,1)S(1)} %pad_maximum_fusion.refs_0_), channel_id=1, source_target_pairs={{0,4},{4,0},{8,12},{12,8},{16,20},{20,16},{24,28},{28,24},{1,5},{5... | collective-permute-start | bytes 393224 | tf_op jit(solution)/shard_map/ppermute | solution.py:20
  30.2 4.3 %collective-permute-start.8 = (bf16[2,256,128]{2,1,0:T(8,128)(2,1)S(1)}, bf16[2,256,128]{2,1,0:T(8,128)(2,1)S(1)}, u32[]{:S(2)}, u32[]{:S(2)}) collective-permute-start(bf16[2,256,128]{2,1,0:T(8,128)(2,1)S(1)} %pad_maximum_fusion.refs_0_), channel_id=1, source_target_pairs={{0,1},{1,0},{2,3},{3,2},{4,5},{5,4},{6,7},{7,6},{8,9},{9,8},{10,11... | collective-permute-start | bytes 393224 | tf_op jit(solution)/shard_map/ppermute | solution.py:20
  32.6 2.0 %collective-permute-start.11 = (bf16[2,256,128]{2,1,0:T(8,128)(2,1)S(1)}, bf16[2,256,128]{2,1,0:T(8,128)(2,1)S(1)}, u32[]{:S(2)}, u32[]{:S(2)}) collective-permute-start(bf16[2,256,128]{2,1,0:T(8,128)(2,1)S(1)} %collective-permute-done.7.refs_3_), channel_id=1, source_target_pairs={{0,1},{1,0},{2,3},{3,2},{4,5},{5,4},{6,7},{7,6},{8,9},{9,8},{10,11... | collective-permute-start | bytes 393224 | tf_op jit(solution)/shard_map/ppermute | solution.py:20
  33.9 1.3 %collective-permute-start.10 = (bf16[2,256,128]{2,1,0:T(8,128)(2,1)S(1)}, bf16[2,256,128]{2,1,0:T(8,128)(2,1)S(1)}, u32[]{:S(2)}, u32[]{:S(2)}) collective-permute-start(bf16[2,256,128]{2,1,0:T(8,128)(2,1)S(1)} %collective-permute-done.6.refs_2_), channel_id=1, source_target_pairs={{0,1},{1,0},{2,3},{3,2},{4,5},{5,4},{6,7},{7,6},{8,9},{9,8},{10,11... | collective-permute-start | bytes 393224 | tf_op jit(solution)/shard_map/ppermute | solution.py:20
  34.6 1.3 %collective-permute-start.9 = (bf16[2,256,128]{2,1,0:T(8,128)(2,1)S(1)}, bf16[2,256,128]{2,1,0:T(8,128)(2,1)S(1)}, u32[]{:S(2)}, u32[]{:S(2)}) collective-permute-start(bf16[2,256,128]{2,1,0:T(8,128)(2,1)S(1)} %collective-permute-done.5.refs_1_), channel_id=1, source_target_pairs={{0,1},{1,0},{2,3},{3,2},{4,5},{5,4},{6,7},{7,6},{8,9},{9,8},{10,11... | collective-permute-start | bytes 393224 | tf_op jit(solution)/shard_map/ppermute | solution.py:20

commit v9 on v8

--- a/solution.py
+++ b/solution.py
@@ -120,8 +120,8 @@
     n_time, snaps, modes, row_block, col_block, target_block, tile = sizes
     half, quarter = n_time // 2, snaps // QUAD
     count = 2 * QUAD
-    pieces, (gram_hbm, rhs_ref) = refs[0:count], refs[count : count + 2]
-    lead, head, target, coeffs, *rows, cols, staged, side, sems = refs[count + 2 :]
+    pieces, (gram_hbm, rhs_hbm) = refs[0:count], refs[count : count + 2]
+    lead, head, target, *rows, cols, staged, side, side_staged, sems = refs[count + 2 :]
     later = (n_time - 1) * snaps
     time_pos, space_pos = lax.axis_index("tm"), lax.axis_index("space")
     place = lax.rem(space_pos, QUAD)
@@ -147,13 +147,6 @@
 
     each_piece(place_lead)
 
-    @pl.when((time_pos == 0) | (space_pos == 0))
-    def _():
-        def place_modes(piece, at):
-            coeffs[:, pl.ds(at, quarter)] = piece[...]
-
-        each_piece(place_modes)
-
     def build_group(out, q, at):
         kind, i = lax.div(q, LEAD_MODES), lax.rem(q, LEAD_MODES)
         factor = jnp.broadcast_to(head[pl.ds(i, 1), snaps:], (ROW_TILE, later)).astype(
@@ -161,14 +154,17 @@
         )
         shifted = pl.ds(pl.multiple_of(gap - kind * snaps, snaps), later)
         for j in range(0, LEAD_MODES, ROW_TILE):
-            out[pl.ds(pl.multiple_of(at + j, ROW_TILE), ROW_TILE), :] = (
+            out[pl.ds(pl.multiple_of(at + j, ROW_TILE), ROW_TILE), snaps:] = (
                 factor * lead[j : j + ROW_TILE, shifted]
             )
 
     def fill(out, start, extent):
         @pl.when(start == 0)
         def _():
-            out[pl.ds(LEAD_MODES, modes), :] = coeffs[:, snaps:]
+            def place_modes(piece, at):
+                out[pl.ds(LEAD_MODES, modes), pl.ds(at, quarter)] = piece[...]
+
+            each_piece(place_modes)
 
         def group(q, carry):
             build_group(out, q, modes + LEAD_MODES * q - start + LEAD_MODES)
@@ -188,13 +184,15 @@
     row_start = time_pos * row_block
     fill(cols, space_pos * col_block, col_block)
     fill(rows[0], row_start, tile)
-    cols[pl.ds(LEAD_MODES + col_block, target_block), :] = target[:, gap:]
+    cols[pl.ds(LEAD_MODES + col_block, target_block), snaps:] = target[:, gap:]
 
     def times(left, right):
         return lax.dot_general(
             left, right, (((1,), (1,)), ((), ())), preferred_element_type=jnp.float32
         ) * (1.0 / (n_time * snaps))
 
+    first_rows = rows[0].at[pl.ds(LEAD_MODES, modes), 0:snaps]
+    first_cols = cols.at[pl.ds(LEAD_MODES, modes), 0:snaps]
     writes = []
     for step in range(row_block // tile):
         top = step * tile
@@ -202,8 +200,8 @@
         if top + tile < row_block:
             fill_products(rows[(step + 1) % 2], row_start + top + tile, tile)
         product = times(
-            rows[step % 2][pl.ds(LEAD_MODES, tile), :],
-            cols[pl.ds(LEAD_MODES, col_block + target_block), :],
+            rows[step % 2][pl.ds(LEAD_MODES, tile), snaps:],
+            cols[pl.ds(LEAD_MODES, col_block + target_block), snaps:],
         )
         shape = (tile, col_block)
         row = time_pos * row_block + top + lax.broadcasted_iota(jnp.int32, shape, 0)
@@ -214,15 +212,19 @@
 
             @pl.when(time_pos == 0)
             def _():
-                side[0:modes, :] += times(coeffs[:, 0:snaps], target[:, snaps:gap])
+                side[0:modes, :] += times(first_rows[...], target[:, snaps:gap])
 
             @pl.when((time_pos == 0) & (space_pos == 0))
             def _():
-                staged[0:modes, 0:modes] += times(coeffs[:, 0:snaps], coeffs[:, 0:snaps])
+                staged[0:modes, 0:modes] += times(
+                    first_rows[...], first_cols[...]
+                )
 
         writes.append(pltpu.make_async_copy(staged.at[at], gram_hbm.at[at], sems.at[step]))
         writes[-1].start()
-    rhs_ref[...] = side[...].T
+    side_staged[...] = side[...].T
+    writes.append(pltpu.make_async_copy(side_staged, rhs_hbm, sems.at[len(writes)]))
+    writes[-1].start()
     for write in writes:
         write.wait()
 
@@ -245,18 +247,18 @@
             jax.ShapeDtypeStruct((target_block, row_block), jnp.float32),
         ),
         in_specs=[vmem] * len(pieces),
-        out_specs=(pl.BlockSpec(memory_space=pl.ANY), vmem),
+        out_specs=(pl.BlockSpec(memory_space=pl.ANY),) * 2,
         scratch_shapes=[
             pltpu.VMEM((LEAD_MODES, (n_time + 2) * snaps), jnp.bfloat16),
             pltpu.VMEM((LEAD_MODES, n_time * snaps), jnp.float32),
             pltpu.VMEM((target_block, (n_time + 1) * snaps), jnp.bfloat16),
-            pltpu.VMEM((modes, n_time * snaps), jnp.bfloat16),
-            pltpu.VMEM((tile + 2 * LEAD_MODES, later), jnp.bfloat16),
-            pltpu.VMEM((tile + 2 * LEAD_MODES, later), jnp.bfloat16),
-            pltpu.VMEM((col_block + 2 * LEAD_MODES + target_block, later), jnp.bfloat16),
+            pltpu.VMEM((tile + 2 * LEAD_MODES, n_time * snaps), jnp.bfloat16),
+            pltpu.VMEM((tile + 2 * LEAD_MODES, n_time * snaps), jnp.bfloat16),
+            pltpu.VMEM((col_block + 2 * LEAD_MODES + target_block, n_time * snaps), jnp.bfloat16),
             pltpu.VMEM((row_block, col_block), jnp.float32),
             pltpu.VMEM((row_block, target_block), jnp.float32),
-            pltpu.SemaphoreType.DMA((row_block // tile,)),
+            pltpu.VMEM((target_block, row_block), jnp.float32),
+            pltpu.SemaphoreType.DMA((row_block // tile + 1,)),
         ],
         compiler_params=pltpu.CompilerParams(vmem_limit_bytes=VMEM_LIMIT),
         cost_estimate=pl.CostEstimate(

time: 42.5 us -> 42.2 us (level)
  no operation moved by 1% of the time
where the time goes in v9:
time: 42.2 us; the launch traced here: 42 us
  waiting for transfers between devices  16.2 us (38%)
  starting transfers between devices  12.5 us (30%)
  Pallas kernels  12.4 us (29%)
  between operations  0.78 us (2%)
    ppermute x12, waiting for transfers between devices, swap(): return lax.ppermute(value, axis, [(i, i ^ bit) for i in range(count)])  16.2 us
    ppermute x12, starting transfers between devices, swap(): return lax.ppermute(value, axis, [(i, i ^ bit) for i in range(count)])  12.5 us
    pallas_call x1, Pallas kernels, project(): pl.pallas_call(projection_kernel, out_shape=(pltpu.VMEM((count, quarter),...  6.24 us
    pallas_call x1, Pallas kernels, gram_blocks(): pl.pallas_call(functools.partial(gram_kernel, (n_time, snaps, modes, row_...  6.12 us
  transfers between devices with their start and end apart: 12, of which 9 were waited for; matrix products, arithmetic and copies ran while one was open for 0% of the time, Pallas kernels for 0%

profile of v9, /device:TPU:0, one launch (start us, length us, event | category | flops | bytes accessed | tf_op | source)
XLA Modules:
  0.0 42.0 jit_solution(2732938298446883770)
XLA Ops:
  0.6 6.2 %shard_map.41 = (f32[256,128]{1,0:T(8,128)S(1)}, bf16[304,128]{1,0:T(8,128)(2,1)S(1)}, bf16[304,128]{1,0:T(8,128)(2,1)S(1)}, bf16[304,128]{1,0:T(8,128)(2,1)S(1)}) custom-call(bf16[10240,256]{1,0:T(8,128)(2,1)} %modes_hbm.1, bf16[10240,512]{1,0:T(8,128)(2,1)} %snaps_hbm.1), custom_call_target="tpu_custom_call" | custom-call | flops 2684354560 | bytes 15728640 | tf_op jit(solution)/shard_map/pallas_call | solution.py:96
  6.9 4.0 %collective-permute-start.2 = (bf16[304,128]{1,0:T(8,128)(2,1)S(1)}, bf16[304,128]{1,0:T(8,128)(2,1)S(1)}, u32[]{:S(2)}, u32[]{:S(2)}) collective-permute-start(bf16[304,128]{1,0:T(8,128)(2,1)S(1)} %get-tuple-element.11), channel_id=1, source_target_pairs={{0,12},{4,8},{8,4},{12,0},{16,28},{20,24},{24,20},{28,16},{1,13},{... | collective-permute-start | bytes 233480 | tf_op jit(solution)/shard_map/ppermute | solution.py:20
  10.9 0.5 %collective-permute-start = (bf16[304,128]{1,0:T(8,128)(2,1)S(1)}, bf16[304,128]{1,0:T(8,128)(2,1)S(1)}, u32[]{:S(2)}, u32[]{:S(2)}) collective-permute-start(bf16[304,128]{1,0:T(8,128)(2,1)S(1)} %get-tuple-element.9), channel_id=1, source_target_pairs={{0,4},{4,0},{8,12},{12,8},{16,20},{20,16},{24,28},{28,24},{1,5},{5... | collective-permute-start | bytes 233480 | tf_op jit(solution)/shard_map/ppermute | solution.py:20
  11.4 0.1 collective-permute-start.1
  11.6 1.8 %collective-permute-done.2 = bf16[304,128]{1,0:T(8,128)(2,1)S(1)} collective-permute-done((bf16[304,128]{1,0:T(8,128)(2,1)S(1)}, bf16[304,128]{1,0:T(8,128)(2,1)S(1)}, u32[]{:S(2)}, u32[]{:S(2)}) %collective-permute-start.2) | collective-permute-done | bytes 77856 | tf_op jit(solution)/shard_map/ppermute | solution.py:20
  13.4 2.5 %collective-permute-done.1 = bf16[304,128]{1,0:T(8,128)(2,1)S(1)} collective-permute-done((bf16[304,128]{1,0:T(8,128)(2,1)S(1)}, bf16[304,128]{1,0:T(8,128)(2,1)S(1)}, u32[]{:S(2)}, u32[]{:S(2)}) %collective-permute-start.1) | collective-permute-done | bytes 77856 | tf_op jit(solution)/shard_map/ppermute | solution.py:20
  15.9 0.0 collective-permute-done
  16.1 2.7 %collective-permute-start.3 = (bf16[304,128]{1,0:T(8,128)(2,1)S(1)}, bf16[304,128]{1,0:T(8,128)(2,1)S(1)}, u32[]{:S(2)}, u32[]{:S(2)}) collective-permute-start(bf16[304,128]{1,0:T(8,128)(2,1)S(1)} %pad_maximum_fusion.1), channel_id=1, source_target_pairs={{0,16},{4,20},{8,24},{12,28},{16,0},{20,4},{24,8},{28,12},{1,17},{... | collective-permute-start | bytes 233480 | tf_op jit(solution)/shard_map/ppermute | solution.py:20
  18.7 3.5 %collective-permute-done.3 = bf16[304,128]{1,0:T(8,128)(2,1)S(1)} collective-permute-done((bf16[304,128]{1,0:T(8,128)(2,1)S(1)}, bf16[304,128]{1,0:T(8,128)(2,1)S(1)}, u32[]{:S(2)}, u32[]{:S(2)}) %collective-permute-start.3) | collective-permute-done | bytes 77856 | tf_op jit(solution)/shard_map/ppermute | solution.py:20
  22.3 1.6 %collective-permute-start.4 = (bf16[1,256,128]{2,1,0:T(8,128)(2,1)S(1)}, bf16[1,256,128]{2,1,0:T(8,128)(2,1)S(1)}, u32[]{:S(2)}, u32[]{:S(2)}) collective-permute-start(bf16[1,256,128]{2,1,0:T(8,128)(2,1)S(1)} %fusion.2), channel_id=1, source_target_pairs={{0,2},{1,3},{2,0},{3,1},{4,6},{5,7},{6,4},{7,5},{8,10},{9,11},{10,... | collective-permute-start | bytes 196616 | tf_op jit(solution)/shard_map/ppermute | solution.py:20
  23.9 2.7 %collective-permute-done.4 = bf16[1,256,128]{2,1,0:T(8,128)(2,1)S(1)} collective-permute-done((bf16[1,256,128]{2,1,0:T(8,128)(2,1)S(1)}, bf16[1,256,128]{2,1,0:T(8,128)(2,1)S(1)}, u32[]{:S(2)}, u32[]{:S(2)}) %collective-permute-start.4) | collective-permute-done | bytes 65568 | tf_op jit(solution)/shard_map/ppermute | solution.py:20
  26.7 0.7 %collective-permute-start.7 = (bf16[2,256,128]{2,1,0:T(8,128)(2,1)S(1)}, bf16[2,256,128]{2,1,0:T(8,128)(2,1)S(1)}, u32[]{:S(2)}, u32[]{:S(2)}) collective-permute-start(bf16[2,256,128]{2,1,0:T(8,128)(2,1)S(1)} %pad_maximum_fusion.refs_0_), channel_id=1, source_target_pairs={{0,12},{4,8},{8,4},{12,0},{16,28},{20,24},{24,20},{28,16},{1,13},{... | collective-permute-start | bytes 393224 | tf_op jit(solution)/shard_map/ppermute | solution.py:20
  27.4 2.2 %collective-permute-start.6 = (bf16[2,256,128]{2,1,0:T(8,128)(2,1)S(1)}, bf16[2,256,128]{2,1,0:T(8,128)(2,1)S(1)}, u32[]{:S(2)}, u32[]{:S(2)}) collective-permute-start(bf16[2,256,128]{2,1,0:T(8,128)(2,1)S(1)} %pad_maximum_fusion.refs_0_), channel_id=1, source_target_pairs={{0,8},{4,12},{8,0},{12,4},{16,24},{20,28},{24,16},{28,20},{1,9},{5... | collective-permute-start | bytes 393224 | tf_op jit(solution)/shard_map/ppermute | solution.py:20
  29.6 0.6 %collective-permute-start.5 = (bf16[2,256,128]{2,1,0:T(8,128)(2,1)S(1)}, bf16[2,256,128]{2,1,0:T(8,128)(2,1)S(1)}, u32[]{:S(2)}, u32[]{:S(2)}) collective-permute-start(bf16[2,256,128]{2,1,0:T(8,128)(2,1)S(1)} %pad_maximum_fusion.refs_0_), channel_id=1, source_target_pairs={{0,4},{4,0},{8,12},{12,8},{16,20},{20,16},{24,28},{28,24},{1,5},{5... | collective-permute-start | bytes 393224 | tf_op jit(solution)/shard_map/ppermute | solution.py:20
  30.2 0.0 collective-permute-start.8
  30.2 2.4 %collective-permute-done.7.refs_3_ = bf16[2,256,128]{2,1,0:T(8,128)(2,1)S(1)} collective-permute-done((bf16[2,256,128]{2,1,0:T(8,128)(2,1)S(1)}, bf16[2,256,128]{2,1,0:T(8,128)(2,1)S(1)}, u32[]{:S(2)}, u32[]{:S(2)}) %collective-permute-start.7) | collective-permute-done | bytes 131104 | tf_op jit(solution)/shard_map/ppermute | solution.py:20
  32.6 0.0 collective-permute-start.11
  32.6 1.3 %collective-permute-done.6.refs_2_ = bf16[2,256,128]{2,1,0:T(8,128)(2,1)S(1)} collective-permute-done((bf16[2,256,128]{2,1,0:T(8,128)(2,1)S(1)}, bf16[2,256,128]{2,1,0:T(8,128)(2,1)S(1)}, u32[]{:S(2)}, u32[]{:S(2)}) %collective-permute-start.6) | collective-permute-done | bytes 131104 | tf_op jit(solution)/shard_map/ppermute | solution.py:20
  33.9 0.0 collective-permute-start.10
  34.0 0.6 %collective-permute-done.5.refs_1_ = bf16[2,256,128]{2,1,0:T(8,128)(2,1)S(1)} collective-permute-done((bf16[2,256,128]{2,1,0:T(8,128)(2,1)S(1)}, bf16[2,256,128]{2,1,0:T(8,128)(2,1)S(1)}, u32[]{:S(2)}, u32[]{:S(2)}) %collective-permute-start.5) | collective-permute-done | bytes 131104 | tf_op jit(solution)/shard_map/ppermute | solution.py:20
  34.6 0.0 collective-permute-start.9
  34.6 0.0 collective-permute-done.8.refs_4_
  34.6 0.0 collective-permute-done.11.refs_7_
  34.6 0.7 %collective-permute-done.10.refs_6_ = bf16[2,256,128]{2,1,0:T(8,128)(2,1)S(1)} collective-permute-done((bf16[2,256,128]{2,1,0:T(8,128)(2,1)S(1)}, bf16[2,256,128]{2,1,0:T(8,128)(2,1)S(1)}, u32[]{:S(2)}, u32[]{:S(2)}) %collective-permute-start.10) | collective-permute-done | bytes 131104 | tf_op jit(solution)/shard_map/ppermute | solution.py:20
  35.3 0.6 %collective-permute-done.9.refs_5_ = bf16[2,256,128]{2,1,0:T(8,128)(2,1)S(1)} collective-permute-done((bf16[2,256,128]{2,1,0:T(8,128)(2,1)S(1)}, bf16[2,256,128]{2,1,0:T(8,128)(2,1)S(1)}, u32[]{:S(2)}, u32[]{:S(2)}) %collective-permute-start.9) | collective-permute-done | bytes 131104 | tf_op jit(solution)/shard_map/ppermute | solution.py:20
  35.9 6.1 %shard_map.42 = (f32[1216,608]{1,0:T(8,128)}, f32[32,1216]{1,0:T(8,128)}) custom-call(bf16[2,256,128]{2,1,0:T(8,128)(2,1)S(1)} %pad_maximum_fusion.refs_0_, bf16[2,256,128]{2,1,0:T(8,128)(2,1)S(1)} %collective-permute-done.5.refs_1_, bf16[2,256,128]{2,1,0:T(8,128)(2,1)S(1)} %collective-permute-done.6.refs_2_, ...), custom_call_target="tpu_custom_call" | custom-call | flops 2390753280 | bytes 3112960 | tf_op jit(solution)/shard_map/pallas_call | solution.py:241
  (19 shorter events, 0.2 us)
Async XLA Ops:
  6.9 6.5 %collective-permute-start.2 = (bf16[304,128]{1,0:T(8,128)(2,1)S(1)}, bf16[304,128]{1,0:T(8,128)(2,1)S(1)}, u32[]{:S(2)}, u32[]{:S(2)}) collective-permute-start(bf16[304,128]{1,0:T(8,128)(2,1)S(1)} %get-tuple-element.11), channel_id=1, source_target_pairs={{0,12},{4,8},{8,4},{12,0},{16,28},{20,24},{24,20},{28,16},{1,13},{... | collective-permute-start | bytes 233480 | tf_op jit(solution)/shard_map/ppermute | solution.py:20
  10.9 5.0 %collective-permute-start = (bf16[304,128]{1,0:T(8,128)(2,1)S(1)}, bf16[304,128]{1,0:T(8,128)(2,1)S(1)}, u32[]{:S(2)}, u32[]{:S(2)}) collective-permute-start(bf16[304,128]{1,0:T(8,128)(2,1)S(1)} %get-tuple-element.9), channel_id=1, source_target_pairs={{0,4},{4,0},{8,12},{12,8},{16,20},{20,16},{24,28},{28,24},{1,5},{5... | collective-permute-start | bytes 233480 | tf_op jit(solution)/shard_map/ppermute | solution.py:20
  11.4 4.4 %collective-permute-start.1 = (bf16[304,128]{1,0:T(8,128)(2,1)S(1)}, bf16[304,128]{1,0:T(8,128)(2,1)S(1)}, u32[]{:S(2)}, u32[]{:S(2)}) collective-permute-start(bf16[304,128]{1,0:T(8,128)(2,1)S(1)} %get-tuple-element.10), channel_id=1, source_target_pairs={{0,8},{4,12},{8,0},{12,4},{16,24},{20,28},{24,16},{28,20},{1,9},{5... | collective-permute-start | bytes 233480 | tf_op jit(solution)/shard_map/ppermute | solution.py:20
  16.1 6.2 %collective-permute-start.3 = (bf16[304,128]{1,0:T(8,128)(2,1)S(1)}, bf16[304,128]{1,0:T(8,128)(2,1)S(1)}, u32[]{:S(2)}, u32[]{:S(2)}) collective-permute-start(bf16[304,128]{1,0:T(8,128)(2,1)S(1)} %pad_maximum_fusion.1), channel_id=1, source_target_pairs={{0,16},{4,20},{8,24},{12,28},{16,0},{20,4},{24,8},{28,12},{1,17},{... | collective-permute-start | bytes 233480 | tf_op jit(solution)/shard_map/ppermute | solution.py:20
  22.3 4.3 %collective-permute-start.4 = (bf16[1,256,128]{2,1,0:T(8,128)(2,1)S(1)}, bf16[1,256,128]{2,1,0:T(8,128)(2,1)S(1)}, u32[]{:S(2)}, u32[]{:S(2)}) collective-permute-start(bf16[1,256,128]{2,1,0:T(8,128)(2,1)S(1)} %fusion.2), channel_id=1, source_target_pairs={{0,2},{1,3},{2,0},{3,1},{4,6},{5,7},{6,4},{7,5},{8,10},{9,11},{10,... | collective-permute-start | bytes 196616 | tf_op jit(solution)/shard_map/ppermute | solution.py:20
  26.7 5.9 %collective-permute-start.7 = (bf16[2,256,128]{2,1,0:T(8,128)(2,1)S(1)}, bf16[2,256,128]{2,1,0:T(8,128)(2,1)S(1)}, u32[]{:S(2)}, u32[]{:S(2)}) collective-permute-start(bf16[2,256,128]{2,1,0:T(8,128)(2,1)S(1)} %pad_maximum_fusion.refs_0_), channel_id=1, source_target_pairs={{0,12},{4,8},{8,4},{12,0},{16,28},{20,24},{24,20},{28,16},{1,13},{... | collective-permute-start | bytes 393224 | tf_op jit(solution)/shard_map/ppermute | solution.py:20
  27.4 6.6 %collective-permute-start.6 = (bf16[2,256,128]{2,1,0:T(8,128)(2,1)S(1)}, bf16[2,256,128]{2,1,0:T(8,128)(2,1)S(1)}, u32[]{:S(2)}, u32[]{:S(2)}) collective-permute-start(bf16[2,256,128]{2,1,0:T(8,128)(2,1)S(1)} %pad_maximum_fusion.refs_0_), channel_id=1, source_target_pairs={{0,8},{4,12},{8,0},{12,4},{16,24},{20,28},{24,16},{28,20},{1,9},{5... | collective-permute-start | bytes 393224 | tf_op jit(solution)/shard_map/ppermute | solution.py:20
  29.6 5.0 %collective-permute-start.5 = (bf16[2,256,128]{2,1,0:T(8,128)(2,1)S(1)}, bf16[2,256,128]{2,1,0:T(8,128)(2,1)S(1)}, u32[]{:S(2)}, u32[]{:S(2)}) collective-permute-start(bf16[2,256,128]{2,1,0:T(8,128)(2,1)S(1)} %pad_maximum_fusion.refs_0_), channel_id=1, source_target_pairs={{0,4},{4,0},{8,12},{12,8},{16,20},{20,16},{24,28},{28,24},{1,5},{5... | collective-permute-start | bytes 393224 | tf_op jit(solution)/shard_map/ppermute | solution.py:20
  30.2 4.3 %collective-permute-start.8 = (bf16[2,256,128]{2,1,0:T(8,128)(2,1)S(1)}, bf16[2,256,128]{2,1,0:T(8,128)(2,1)S(1)}, u32[]{:S(2)}, u32[]{:S(2)}) collective-permute-start(bf16[2,256,128]{2,1,0:T(8,128)(2,1)S(1)} %pad_maximum_fusion.refs_0_), channel_id=1, source_target_pairs={{0,1},{1,0},{2,3},{3,2},{4,5},{5,4},{6,7},{7,6},{8,9},{9,8},{10,11... | collective-permute-start | bytes 393224 | tf_op jit(solution)/shard_map/ppermute | solution.py:20
  32.6 2.0 %collective-permute-start.11 = (bf16[2,256,128]{2,1,0:T(8,128)(2,1)S(1)}, bf16[2,256,128]{2,1,0:T(8,128)(2,1)S(1)}, u32[]{:S(2)}, u32[]{:S(2)}) collective-permute-start(bf16[2,256,128]{2,1,0:T(8,128)(2,1)S(1)} %collective-permute-done.7.refs_3_), channel_id=1, source_target_pairs={{0,1},{1,0},{2,3},{3,2},{4,5},{5,4},{6,7},{7,6},{8,9},{9,8},{10,11... | collective-permute-start | bytes 393224 | tf_op jit(solution)/shard_map/ppermute | solution.py:20
  33.9 1.3 %collective-permute-start.10 = (bf16[2,256,128]{2,1,0:T(8,128)(2,1)S(1)}, bf16[2,256,128]{2,1,0:T(8,128)(2,1)S(1)}, u32[]{:S(2)}, u32[]{:S(2)}) collective-permute-start(bf16[2,256,128]{2,1,0:T(8,128)(2,1)S(1)} %collective-permute-done.6.refs_2_), channel_id=1, source_target_pairs={{0,1},{1,0},{2,3},{3,2},{4,5},{5,4},{6,7},{7,6},{8,9},{9,8},{10,11... | collective-permute-start | bytes 393224 | tf_op jit(solution)/shard_map/ppermute | solution.py:20
  34.6 1.3 %collective-permute-start.9 = (bf16[2,256,128]{2,1,0:T(8,128)(2,1)S(1)}, bf16[2,256,128]{2,1,0:T(8,128)(2,1)S(1)}, u32[]{:S(2)}, u32[]{:S(2)}) collective-permute-start(bf16[2,256,128]{2,1,0:T(8,128)(2,1)S(1)} %collective-permute-done.5.refs_1_), channel_id=1, source_target_pairs={{0,1},{1,0},{2,3},{3,2},{4,5},{5,4},{6,7},{7,6},{8,9},{9,8},{10,11... | collective-permute-start | bytes 393224 | tf_op jit(solution)/shard_map/ppermute | solution.py:20

commit v10 on v9

--- a/solution.py
+++ b/solution.py
@@ -12,6 +12,9 @@
 ROW_TILE = 16
 QUAD = 4
 PROJECTION_STEPS = 10
+EXPONENT_ROWS = 8
+TOP = 9.0
+SMALLEST = 1e-30
 VMEM_LIMIT = 48 * 2**20
 
 
@@ -32,21 +35,20 @@
     return pltpu.with_memory_space_constraint(value, pltpu.VMEM)
 
 
-def rounded(value):
-    high = lax.reduce_precision(value, 8, 7)
-    left = value[0:LEAD_MODES] - high[0:LEAD_MODES]
-    return jnp.concatenate([high, left], axis=0).astype(jnp.bfloat16)
-
-
-def restored(value):
-    modes = value.shape[0] - LEAD_MODES
-    whole = value[0:modes].astype(jnp.float32)
-    left = value[modes:].astype(jnp.float32)
-    return jnp.concatenate([whole[0:LEAD_MODES] + left, whole[LEAD_MODES:]], axis=0)
-
-
-def projection_kernel(modes_hbm, snaps_hbm, own_ref, *refs):
-    sent_refs, (modes, snaps, partial_sums, modes_sems, snaps_sems) = refs[0:3], refs[3:]
+def packed(value, exponent):
+    scaled = value * jnp.exp2(TOP - exponent)
+    return jnp.concatenate([scaled, exponent], axis=0).astype(jnp.float16)
+
+
+def unpacked(value):
+    value = value.astype(jnp.float32)
+    exponent = value[-1:]
+    return value[0:-1] * jnp.exp2(exponent - TOP), exponent
+
+
+def projection_kernel(modes_hbm, snaps_hbm, *refs):
+    part_refs, exponent_ref = refs[0:QUAD], refs[QUAD]
+    modes, snaps, partial_sums, modes_sems, snaps_sems = refs[QUAD + 1 :]
     depth = modes.shape[0] // PROJECTION_STEPS
     quarter = snaps.shape[1] // QUAD
 
@@ -74,31 +76,25 @@
             partial_sums[...] = product
         else:
             partial_sums[...] += product
+    largest = jnp.maximum(jnp.max(jnp.abs(partial_sums[...])), SMALLEST)
+    exponent_ref[...] = jnp.floor(jnp.log2(jnp.full(exponent_ref.shape, largest)))
     place = lax.rem(lax.axis_index("space"), QUAD)
-    count = partial_sums.shape[0]
     for j in range(QUAD):
         start = pl.multiple_of(jnp.bitwise_xor(place, j) * quarter, quarter)
-        part = partial_sums[:, pl.ds(start, quarter)]
-        if j == 0:
-            own_ref[...] = part
-        else:
-            high = part.astype(jnp.bfloat16)
-            left = part[0:LEAD_MODES] - high[0:LEAD_MODES].astype(jnp.float32)
-            sent_refs[j - 1][0:count, :] = high
-            sent_refs[j - 1][count:, :] = left.astype(jnp.bfloat16)
+        part_refs[j][...] = partial_sums[:, pl.ds(start, quarter)]
 
 
 def project(modes, snapshots):
     (depth, count), snaps = modes.shape, snapshots.shape[1]
     quarter = snaps // QUAD
     vmem = pl.BlockSpec(memory_space=pltpu.VMEM)
-    anywhere = pl.BlockSpec(memory_space=pltpu.HBM)
-    own, *sent = pl.pallas_call(
+    hbm = pl.BlockSpec(memory_space=pltpu.HBM)
+    *parts, exponent = pl.pallas_call(
         projection_kernel,
-        out_shape=(pltpu.VMEM((count, quarter), jnp.float32),)
-        + (pltpu.VMEM((count + LEAD_MODES, quarter), jnp.bfloat16),) * (QUAD - 1),
-        in_specs=[anywhere] * 2,
-        out_specs=(vmem,) * QUAD,
+        out_shape=(pltpu.VMEM((count, quarter), jnp.float32),) * QUAD
+        + (pltpu.VMEM((EXPONENT_ROWS, quarter), jnp.float32),),
+        in_specs=[hbm] * 2,
+        out_specs=(vmem,) * (QUAD + 1),
         scratch_shapes=[
             pltpu.VMEM((depth, count), jnp.bfloat16),
             pltpu.VMEM((depth, snaps), jnp.bfloat16),
@@ -113,7 +109,7 @@
             transcendentals=0,
         ),
     )(in_hbm(modes), in_hbm(snapshots))
-    return own, sent
+    return [part.reshape((-1,) + exponent.shape) for part in parts], exponent[None]
 
 
 def gram_kernel(sizes, *refs):
@@ -276,14 +272,16 @@
 
 def per_device(snapshots, modes):
     n_space, n_time = lax.axis_size("space"), lax.axis_size("tm")
-    mine, sent = project(modes, snapshots)
-    arrived = [swap(part, "space", j) for j, part in enumerate(sent, 1)]
+    (mine, *others), exponent = project(modes, snapshots)
+    arrived = [swap(packed(part, exponent), "space", j) for j, part in enumerate(others, 1)]
     for part in arrived:
-        mine = mine + restored(part)
+        value, scale = unpacked(part)
+        mine, exponent = mine + value, jnp.maximum(exponent, scale)
     for bit in bits_of(n_space)[2:]:
-        out = rounded(mine)
-        mine = restored(out) + restored(swap(out, "space", bit))
-    mine = mine.astype(jnp.bfloat16)[None]
+        out = packed(mine, exponent)
+        (mine, own), (value, scale) = unpacked(out), unpacked(swap(out, "space", bit))
+        mine, exponent = mine + value, jnp.maximum(own, scale)
+    mine = mine.astype(jnp.bfloat16).reshape(1, modes.shape[1], -1)
     for bit in bits_of(n_time)[1:]:
         mine = joined(mine, "tm", bit)
     pieces = [mine] + [swap(mine, "space", j) for j in range(1, QUAD)]

time: 42.2 us -> 42.2 us (level)
  transfers between devices with their start and end apart: 12 -> 12, of which waited for: 9 -> 10; matrix products, arithmetic and copies ran while one was open for 0% -> 0% of each run, Pallas kernels for 0% -> 0%
where the time goes in v10:
time: 42.2 us; the launch traced here: 42 us
  waiting for transfers between devices  16.2 us (38%)
  Pallas kernels  12.4 us (29%)
  starting transfers between devices  12.4 us (29%)
  between operations  0.73 us (2%)
    ppermute x12, waiting for transfers between devices, swap(): return lax.ppermute(value, axis, [(i, i ^ bit) for i in range(count)])  16.2 us
    ppermute x12, starting transfers between devices, swap(): return lax.ppermute(value, axis, [(i, i ^ bit) for i in range(count)])  12.4 us
    pallas_call x1, Pallas kernels, project(): pl.pallas_call(projection_kernel, out_shape=(pltpu.VMEM((count, quarter),...  6.28 us
    pallas_call x1, Pallas kernels, gram_blocks(): pl.pallas_call(functools.partial(gram_kernel, (n_time, snaps, modes, row_...  6.12 us
  transfers between devices with their start and end apart: 12, of which 10 were waited for; matrix products, arithmetic and copies ran while one was open for 0% of the time, Pallas kernels for 0%

profile of v10, /device:TPU:0, one launch (start us, length us, event | category | flops | bytes accessed | tf_op | source)
XLA Modules:
  0.0 42.0 jit_solution(18213020528358180727)
XLA Ops:
  0.6 6.3 %shard_map.41 = (f32[256,128]{1,0:T(8,128)S(1)}, f32[256,128]{1,0:T(8,128)S(1)}, f32[256,128]{1,0:T(8,128)S(1)}, f32[256,128]{1,0:T(8,128)S(1)}, f32[8,128]{1,0:T(8,128)S(1)}) custom-call(bf16[10240,256]{1,0:T(8,128)(2,1)} %modes_hbm.1, bf16[10240,512]{1,0:T(8,128)(2,1)} %snaps_hbm.1), custom_call_target="tpu_custom_call" | custom-call | flops 2684354560 | bytes 15728640 | tf_op jit(solution)/shard_map/pallas_call | solution.py:92
  7.0 0.1 pad_maximum_fusion.3
  7.0 3.0 %collective-permute-start = (f16[33,8,128]{2,1,0:T(8,128)(2,1)S(1)}, f16[33,8,128]{2,1,0:T(8,128)(2,1)S(1)}, u32[]{:S(2)}, u32[]{:S(2)}) collective-permute-start(f16[33,8,128]{2,1,0:T(8,128)(2,1)S(1)} %get-tuple-element.28), channel_id=1, source_target_pairs={{0,4},{4,0},{8,12},{12,8},{16,20},{20,16},{24,28},{28,24},{1,5},{5... | collective-permute-start | bytes 202760 | tf_op jit(solution)/shard_map/ppermute | solution.py:23
  10.1 1.6 %collective-permute-start.1 = (f16[33,8,128]{2,1,0:T(8,128)(2,1)S(1)}, f16[33,8,128]{2,1,0:T(8,128)(2,1)S(1)}, u32[]{:S(2)}, u32[]{:S(2)}) collective-permute-start(f16[33,8,128]{2,1,0:T(8,128)(2,1)S(1)} %get-tuple-element.29), channel_id=1, source_target_pairs={{0,8},{4,12},{8,0},{12,4},{16,24},{20,28},{24,16},{28,20},{1,9},{5... | collective-permute-start | bytes 202760 | tf_op jit(solution)/shard_map/ppermute | solution.py:23
  11.6 0.0 collective-permute-start.2
  11.6 0.7 %collective-permute-done = f16[33,8,128]{2,1,0:T(8,128)(2,1)S(1)} collective-permute-done((f16[33,8,128]{2,1,0:T(8,128)(2,1)S(1)}, f16[33,8,128]{2,1,0:T(8,128)(2,1)S(1)}, u32[]{:S(2)}, u32[]{:S(2)}) %collective-permute-start) | collective-permute-done | bytes 67616 | tf_op jit(solution)/shard_map/ppermute | solution.py:23
  12.3 2.6 %collective-permute-done.1 = f16[33,8,128]{2,1,0:T(8,128)(2,1)S(1)} collective-permute-done((f16[33,8,128]{2,1,0:T(8,128)(2,1)S(1)}, f16[33,8,128]{2,1,0:T(8,128)(2,1)S(1)}, u32[]{:S(2)}, u32[]{:S(2)}) %collective-permute-start.1) | collective-permute-done | bytes 67616 | tf_op jit(solution)/shard_map/ppermute | solution.py:23
  14.9 1.9 %collective-permute-done.2 = f16[33,8,128]{2,1,0:T(8,128)(2,1)S(1)} collective-permute-done((f16[33,8,128]{2,1,0:T(8,128)(2,1)S(1)}, f16[33,8,128]{2,1,0:T(8,128)(2,1)S(1)}, u32[]{:S(2)}, u32[]{:S(2)}) %collective-permute-start.2) | collective-permute-done | bytes 67616 | tf_op jit(solution)/shard_map/ppermute | solution.py:23
  16.9 0.1 fusion.4
  17.0 2.7 %collective-permute-start.3 = (f16[33,8,128]{2,1,0:T(8,128)(2,1)S(1)}, f16[33,8,128]{2,1,0:T(8,128)(2,1)S(1)}, u32[]{:S(2)}, u32[]{:S(2)}) collective-permute-start(f16[33,8,128]{2,1,0:T(8,128)(2,1)S(1)} %get-tuple-element.22), channel_id=1, source_target_pairs={{0,16},{4,20},{8,24},{12,28},{16,0},{20,4},{24,8},{28,12},{1,17},{... | collective-permute-start | bytes 202760 | tf_op jit(solution)/shard_map/ppermute | solution.py:23
  19.6 3.2 %collective-permute-done.3 = f16[33,8,128]{2,1,0:T(8,128)(2,1)S(1)} collective-permute-done((f16[33,8,128]{2,1,0:T(8,128)(2,1)S(1)}, f16[33,8,128]{2,1,0:T(8,128)(2,1)S(1)}, u32[]{:S(2)}, u32[]{:S(2)}) %collective-permute-start.3) | collective-permute-done | bytes 67616 | tf_op jit(solution)/shard_map/ppermute | solution.py:23
  22.9 1.6 %collective-permute-start.4 = (bf16[1,256,128]{2,1,0:T(8,128)(2,1)S(1)}, bf16[1,256,128]{2,1,0:T(8,128)(2,1)S(1)}, u32[]{:S(2)}, u32[]{:S(2)}) collective-permute-start(bf16[1,256,128]{2,1,0:T(8,128)(2,1)S(1)} %fusion.10), channel_id=1, source_target_pairs={{0,2},{1,3},{2,0},{3,1},{4,6},{5,7},{6,4},{7,5},{8,10},{9,11},{10,... | collective-permute-start | bytes 196616 | tf_op jit(solution)/shard_map/ppermute | solution.py:23
  24.5 2.7 %collective-permute-done.4 = bf16[1,256,128]{2,1,0:T(8,128)(2,1)S(1)} collective-permute-done((bf16[1,256,128]{2,1,0:T(8,128)(2,1)S(1)}, bf16[1,256,128]{2,1,0:T(8,128)(2,1)S(1)}, u32[]{:S(2)}, u32[]{:S(2)}) %collective-permute-start.4) | collective-permute-done | bytes 65568 | tf_op jit(solution)/shard_map/ppermute | solution.py:23
  27.2 0.3 collective-permute-start.7
  27.5 1.9 %collective-permute-start.6 = (bf16[2,256,128]{2,1,0:T(8,128)(2,1)S(1)}, bf16[2,256,128]{2,1,0:T(8,128)(2,1)S(1)}, u32[]{:S(2)}, u32[]{:S(2)}) collective-permute-start(bf16[2,256,128]{2,1,0:T(8,128)(2,1)S(1)} %pad_maximum_fusion.refs_0_), channel_id=1, source_target_pairs={{0,8},{4,12},{8,0},{12,4},{16,24},{20,28},{24,16},{28,20},{1,9},{5... | collective-permute-start | bytes 393224 | tf_op jit(solution)/shard_map/ppermute | solution.py:23
  29.4 1.4 %collective-permute-start.5 = (bf16[2,256,128]{2,1,0:T(8,128)(2,1)S(1)}, bf16[2,256,128]{2,1,0:T(8,128)(2,1)S(1)}, u32[]{:S(2)}, u32[]{:S(2)}) collective-permute-start(bf16[2,256,128]{2,1,0:T(8,128)(2,1)S(1)} %pad_maximum_fusion.refs_0_), channel_id=1, source_target_pairs={{0,4},{4,0},{8,12},{12,8},{16,20},{20,16},{24,28},{28,24},{1,5},{5... | collective-permute-start | bytes 393224 | tf_op jit(solution)/shard_map/ppermute | solution.py:23
  30.8 0.0 collective-permute-start.8
  30.8 2.4 %collective-permute-done.7.refs_3_ = bf16[2,256,128]{2,1,0:T(8,128)(2,1)S(1)} collective-permute-done((bf16[2,256,128]{2,1,0:T(8,128)(2,1)S(1)}, bf16[2,256,128]{2,1,0:T(8,128)(2,1)S(1)}, u32[]{:S(2)}, u32[]{:S(2)}) %collective-permute-start.7) | collective-permute-done | bytes 131104 | tf_op jit(solution)/shard_map/ppermute | solution.py:23
  33.2 0.0 collective-permute-start.11
  33.2 0.6 %collective-permute-done.6.refs_2_ = bf16[2,256,128]{2,1,0:T(8,128)(2,1)S(1)} collective-permute-done((bf16[2,256,128]{2,1,0:T(8,128)(2,1)S(1)}, bf16[2,256,128]{2,1,0:T(8,128)(2,1)S(1)}, u32[]{:S(2)}, u32[]{:S(2)}) %collective-permute-start.6) | collective-permute-done | bytes 131104 | tf_op jit(solution)/shard_map/ppermute | solution.py:23
  33.7 0.0 collective-permute-start.10
  33.7 0.8 %collective-permute-done.5.refs_1_ = bf16[2,256,128]{2,1,0:T(8,128)(2,1)S(1)} collective-permute-done((bf16[2,256,128]{2,1,0:T(8,128)(2,1)S(1)}, bf16[2,256,128]{2,1,0:T(8,128)(2,1)S(1)}, u32[]{:S(2)}, u32[]{:S(2)}) %collective-permute-start.5) | collective-permute-done | bytes 131104 | tf_op jit(solution)/shard_map/ppermute | solution.py:23
  34.6 0.0 collective-permute-start.9
  34.6 0.0 collective-permute-done.8.refs_4_
  34.6 0.0 collective-permute-done.11.refs_7_
  34.6 0.5 %collective-permute-done.10.refs_6_ = bf16[2,256,128]{2,1,0:T(8,128)(2,1)S(1)} collective-permute-done((bf16[2,256,128]{2,1,0:T(8,128)(2,1)S(1)}, bf16[2,256,128]{2,1,0:T(8,128)(2,1)S(1)}, u32[]{:S(2)}, u32[]{:S(2)}) %collective-permute-start.10) | collective-permute-done | bytes 131104 | tf_op jit(solution)/shard_map/ppermute | solution.py:23
  35.1 0.8 %collective-permute-done.9.refs_5_ = bf16[2,256,128]{2,1,0:T(8,128)(2,1)S(1)} collective-permute-done((bf16[2,256,128]{2,1,0:T(8,128)(2,1)S(1)}, bf16[2,256,128]{2,1,0:T(8,128)(2,1)S(1)}, u32[]{:S(2)}, u32[]{:S(2)}) %collective-permute-start.9) | collective-permute-done | bytes 131104 | tf_op jit(solution)/shard_map/ppermute | solution.py:23
  35.9 6.1 %shard_map.42 = (f32[1216,608]{1,0:T(8,128)}, f32[32,1216]{1,0:T(8,128)}) custom-call(bf16[2,256,128]{2,1,0:T(8,128)(2,1)S(1)} %pad_maximum_fusion.refs_0_, bf16[2,256,128]{2,1,0:T(8,128)(2,1)S(1)} %collective-permute-done.5.refs_1_, bf16[2,256,128]{2,1,0:T(8,128)(2,1)S(1)} %collective-permute-done.6.refs_2_, ...), custom_call_target="tpu_custom_call" | custom-call | flops 2390753280 | bytes 3112960 | tf_op jit(solution)/shard_map/pallas_call | solution.py:237
  (13 shorter events, 0.2 us)
Async XLA Ops:
  7.0 5.3 %collective-permute-start = (f16[33,8,128]{2,1,0:T(8,128)(2,1)S(1)}, f16[33,8,128]{2,1,0:T(8,128)(2,1)S(1)}, u32[]{:S(2)}, u32[]{:S(2)}) collective-permute-start(f16[33,8,128]{2,1,0:T(8,128)(2,1)S(1)} %get-tuple-element.28), channel_id=1, source_target_pairs={{0,4},{4,0},{8,12},{12,8},{16,20},{20,16},{24,28},{28,24},{1,5},{5... | collective-permute-start | bytes 202760 | tf_op jit(solution)/shard_map/ppermute | solution.py:23
  10.1 4.9 %collective-permute-start.1 = (f16[33,8,128]{2,1,0:T(8,128)(2,1)S(1)}, f16[33,8,128]{2,1,0:T(8,128)(2,1)S(1)}, u32[]{:S(2)}, u32[]{:S(2)}) collective-permute-start(f16[33,8,128]{2,1,0:T(8,128)(2,1)S(1)} %get-tuple-element.29), channel_id=1, source_target_pairs={{0,8},{4,12},{8,0},{12,4},{16,24},{20,28},{24,16},{28,20},{1,9},{5... | collective-permute-start | bytes 202760 | tf_op jit(solution)/shard_map/ppermute | solution.py:23
  11.6 5.2 %collective-permute-start.2 = (f16[33,8,128]{2,1,0:T(8,128)(2,1)S(1)}, f16[33,8,128]{2,1,0:T(8,128)(2,1)S(1)}, u32[]{:S(2)}, u32[]{:S(2)}) collective-permute-start(f16[33,8,128]{2,1,0:T(8,128)(2,1)S(1)} %get-tuple-element.30), channel_id=1, source_target_pairs={{0,12},{4,8},{8,4},{12,0},{16,28},{20,24},{24,20},{28,16},{1,13},{... | collective-permute-start | bytes 202760 | tf_op jit(solution)/shard_map/ppermute | solution.py:23
  17.0 5.9 %collective-permute-start.3 = (f16[33,8,128]{2,1,0:T(8,128)(2,1)S(1)}, f16[33,8,128]{2,1,0:T(8,128)(2,1)S(1)}, u32[]{:S(2)}, u32[]{:S(2)}) collective-permute-start(f16[33,8,128]{2,1,0:T(8,128)(2,1)S(1)} %get-tuple-element.22), channel_id=1, source_target_pairs={{0,16},{4,20},{8,24},{12,28},{16,0},{20,4},{24,8},{28,12},{1,17},{... | collective-permute-start | bytes 202760 | tf_op jit(solution)/shard_map/ppermute | solution.py:23
  22.9 4.3 %collective-permute-start.4 = (bf16[1,256,128]{2,1,0:T(8,128)(2,1)S(1)}, bf16[1,256,128]{2,1,0:T(8,128)(2,1)S(1)}, u32[]{:S(2)}, u32[]{:S(2)}) collective-permute-start(bf16[1,256,128]{2,1,0:T(8,128)(2,1)S(1)} %fusion.10), channel_id=1, source_target_pairs={{0,2},{1,3},{2,0},{3,1},{4,6},{5,7},{6,4},{7,5},{8,10},{9,11},{10,... | collective-permute-start | bytes 196616 | tf_op jit(solution)/shard_map/ppermute | solution.py:23
  27.2 5.9 %collective-permute-start.7 = (bf16[2,256,128]{2,1,0:T(8,128)(2,1)S(1)}, bf16[2,256,128]{2,1,0:T(8,128)(2,1)S(1)}, u32[]{:S(2)}, u32[]{:S(2)}) collective-permute-start(bf16[2,256,128]{2,1,0:T(8,128)(2,1)S(1)} %pad_maximum_fusion.refs_0_), channel_id=1, source_target_pairs={{0,12},{4,8},{8,4},{12,0},{16,28},{20,24},{24,20},{28,16},{1,13},{... | collective-permute-start | bytes 393224 | tf_op jit(solution)/shard_map/ppermute | solution.py:23
  27.5 6.2 %collective-permute-start.6 = (bf16[2,256,128]{2,1,0:T(8,128)(2,1)S(1)}, bf16[2,256,128]{2,1,0:T(8,128)(2,1)S(1)}, u32[]{:S(2)}, u32[]{:S(2)}) collective-permute-start(bf16[2,256,128]{2,1,0:T(8,128)(2,1)S(1)} %pad_maximum_fusion.refs_0_), channel_id=1, source_target_pairs={{0,8},{4,12},{8,0},{12,4},{16,24},{20,28},{24,16},{28,20},{1,9},{5... | collective-permute-start | bytes 393224 | tf_op jit(solution)/shard_map/ppermute | solution.py:23
  29.4 5.2 %collective-permute-start.5 = (bf16[2,256,128]{2,1,0:T(8,128)(2,1)S(1)}, bf16[2,256,128]{2,1,0:T(8,128)(2,1)S(1)}, u32[]{:S(2)}, u32[]{:S(2)}) collective-permute-start(bf16[2,256,128]{2,1,0:T(8,128)(2,1)S(1)} %pad_maximum_fusion.refs_0_), channel_id=1, source_target_pairs={{0,4},{4,0},{8,12},{12,8},{16,20},{20,16},{24,28},{28,24},{1,5},{5... | collective-permute-start | bytes 393224 | tf_op jit(solution)/shard_map/ppermute | solution.py:23
  30.8 3.8 %collective-permute-start.8 = (bf16[2,256,128]{2,1,0:T(8,128)(2,1)S(1)}, bf16[2,256,128]{2,1,0:T(8,128)(2,1)S(1)}, u32[]{:S(2)}, u32[]{:S(2)}) collective-permute-start(bf16[2,256,128]{2,1,0:T(8,128)(2,1)S(1)} %pad_maximum_fusion.refs_0_), channel_id=1, source_target_pairs={{0,1},{1,0},{2,3},{3,2},{4,5},{5,4},{6,7},{7,6},{8,9},{9,8},{10,11... | collective-permute-start | bytes 393224 | tf_op jit(solution)/shard_map/ppermute | solution.py:23
  33.2 1.4 %collective-permute-start.11 = (bf16[2,256,128]{2,1,0:T(8,128)(2,1)S(1)}, bf16[2,256,128]{2,1,0:T(8,128)(2,1)S(1)}, u32[]{:S(2)}, u32[]{:S(2)}) collective-permute-start(bf16[2,256,128]{2,1,0:T(8,128)(2,1)S(1)} %collective-permute-done.7.refs_3_), channel_id=1, source_target_pairs={{0,1},{1,0},{2,3},{3,2},{4,5},{5,4},{6,7},{7,6},{8,9},{9,8},{10,11... | collective-permute-start | bytes 393224 | tf_op jit(solution)/shard_map/ppermute | solution.py:23
  33.7 1.3 %collective-permute-start.10 = (bf16[2,256,128]{2,1,0:T(8,128)(2,1)S(1)}, bf16[2,256,128]{2,1,0:T(8,128)(2,1)S(1)}, u32[]{:S(2)}, u32[]{:S(2)}) collective-permute-start(bf16[2,256,128]{2,1,0:T(8,128)(2,1)S(1)} %collective-permute-done.6.refs_2_), channel_id=1, source_target_pairs={{0,1},{1,0},{2,3},{3,2},{4,5},{5,4},{6,7},{7,6},{8,9},{9,8},{10,11... | collective-permute-start | bytes 393224 | tf_op jit(solution)/shard_map/ppermute | solution.py:23
  34.6 1.3 %collective-permute-start.9 = (bf16[2,256,128]{2,1,0:T(8,128)(2,1)S(1)}, bf16[2,256,128]{2,1,0:T(8,128)(2,1)S(1)}, u32[]{:S(2)}, u32[]{:S(2)}) collective-permute-start(bf16[2,256,128]{2,1,0:T(8,128)(2,1)S(1)} %collective-permute-done.5.refs_1_), channel_id=1, source_target_pairs={{0,1},{1,0},{2,3},{3,2},{4,5},{5,4},{6,7},{7,6},{8,9},{9,8},{10,11... | collective-permute-start | bytes 393224 | tf_op jit(solution)/shard_map/ppermute | solution.py:23

commit v11 on v10

--- a/solution.py
+++ b/solution.py
@@ -11,6 +11,8 @@
 RIDGE_WEIGHT = 0.05
 ROW_TILE = 16
 QUAD = 4
+SUM_PARTNERS = ((0, 3, 2, 1), (0, 3, 1, 2))
+GATHER_PARTNERS = ((0, 2, 3, 1), (0, 3, 2, 1))
 PROJECTION_STEPS = 10
 EXPONENT_ROWS = 8
 TOP = 9.0
@@ -21,6 +23,21 @@
 def swap(value, axis, bit):
     count = lax.axis_size(axis)
     return lax.ppermute(value, axis, [(i, i ^ bit) for i in range(count)])
+
+
+def swap_quad(value, partners, turn):
+    n_space, n_time = lax.axis_size("space"), lax.axis_size("tm")
+    pairs = [
+        (s * n_time + t, (s ^ partners[t % 2][turn]) * n_time + t)
+        for s in range(n_space)
+        for t in range(n_time)
+    ]
+    return lax.ppermute(value, ("space", "tm"), pairs)
+
+
+def partner(partners, core, turn):
+    even, odd = partners[0][turn], partners[1][turn]
+    return even if even == odd else jnp.where(core == 0, even, odd)
 
 
 def bits_of(count):
@@ -79,8 +96,9 @@
     largest = jnp.maximum(jnp.max(jnp.abs(partial_sums[...])), SMALLEST)
     exponent_ref[...] = jnp.floor(jnp.log2(jnp.full(exponent_ref.shape, largest)))
     place = lax.rem(lax.axis_index("space"), QUAD)
+    core = lax.rem(lax.axis_index("tm"), 2)
     for j in range(QUAD):
-        start = pl.multiple_of(jnp.bitwise_xor(place, j) * quarter, quarter)
+        start = pl.multiple_of(jnp.bitwise_xor(place, partner(SUM_PARTNERS, core, j)) * quarter, quarter)
         part_refs[j][...] = partial_sums[:, pl.ds(start, quarter)]
 
 
@@ -120,14 +138,15 @@
     lead, head, target, *rows, cols, staged, side, side_staged, sems = refs[count + 2 :]
     later = (n_time - 1) * snaps
     time_pos, space_pos = lax.axis_index("tm"), lax.axis_index("space")
-    place = lax.rem(space_pos, QUAD)
+    place, core = lax.rem(space_pos, QUAD), lax.rem(time_pos, 2)
 
     def each_piece(take):
         for other in range(2):
             for k in range(half):
                 block = jnp.bitwise_xor(time_pos, 2 * k + other)
                 for j in range(QUAD):
-                    at = block * snaps + jnp.bitwise_xor(place, j) * quarter
+                    source = partner(GATHER_PARTNERS, jnp.bitwise_xor(core, other), j)
+                    at = block * snaps + jnp.bitwise_xor(place, source) * quarter
                     take(pieces[other * QUAD + j].at[k], pl.multiple_of(at, quarter))
 
     gap = 2 * snaps
@@ -273,7 +292,7 @@
 def per_device(snapshots, modes):
     n_space, n_time = lax.axis_size("space"), lax.axis_size("tm")
     (mine, *others), exponent = project(modes, snapshots)
-    arrived = [swap(packed(part, exponent), "space", j) for j, part in enumerate(others, 1)]
+    arrived = [swap_quad(packed(part, exponent), SUM_PARTNERS, j) for j, part in enumerate(others, 1)]
     for part in arrived:
         value, scale = unpacked(part)
         mine, exponent = mine + value, jnp.maximum(exponent, scale)
@@ -284,7 +303,7 @@
     mine = mine.astype(jnp.bfloat16).reshape(1, modes.shape[1], -1)
     for bit in bits_of(n_time)[1:]:
         mine = joined(mine, "tm", bit)
-    pieces = [mine] + [swap(mine, "space", j) for j in range(1, QUAD)]
+    pieces = [mine] + [swap_quad(mine, GATHER_PARTNERS, j) for j in range(1, QUAD)]
     pieces = pieces + [swap(piece, "tm", 1) for piece in pieces]
     return gram_blocks(pieces, n_time, n_space)
 

time: 42.2 us -> 41.3 us (0.979)
  waiting for transfers between devices: 16.2 us -> 15.2 us
    ppermute x12 -> x6, waiting for transfers between devices: 16.2 us -> 6.59 us  [swap(): return lax.ppermute(value, axis, [(i, i ^ bit) for i in range(count)])]
    ppermute x0 -> x6, waiting for transfers between devices: none -> 8.57 us  [swap_quad(): return lax.ppermute(value, ('space', 'tm'), pairs)]
    ppermute x0 -> x6, starting transfers between devices: none -> 8.22 us  [swap_quad(): return lax.ppermute(value, ('space', 'tm'), pairs)]
    ppermute x12 -> x6, starting transfers between devices: 12.4 us -> 4.34 us  [swap(): return lax.ppermute(value, axis, [(i, i ^ bit) for i in range(count)])]
where the time goes in v11:
time: 41.3 us; the launch traced here: 41.2 us
  waiting for transfers between devices  15.2 us (37%)
  starting transfers between devices  12.6 us (31%)
  Pallas kernels  12.4 us (30%)
  between operations  0.73 us (2%)
    ppermute x6, waiting for transfers between devices, swap_quad(): return lax.ppermute(value, ('space', 'tm'), pairs)  8.57 us
    ppermute x6, starting transfers between devices, swap_quad(): return lax.ppermute(value, ('space', 'tm'), pairs)  8.22 us
    ppermute x6, waiting for transfers between devices, swap(): return lax.ppermute(value, axis, [(i, i ^ bit) for i in range(count)])  6.59 us
    pallas_call x1, Pallas kernels, project(): pl.pallas_call(projection_kernel, out_shape=(pltpu.VMEM((count, quarter),...  6.28 us
    pallas_call x1, Pallas kernels, gram_blocks(): pl.pallas_call(functools.partial(gram_kernel, (n_time, snaps, modes, row_...  6.13 us
    ppermute x6, starting transfers between devices, swap(): return lax.ppermute(value, axis, [(i, i ^ bit) for i in range(count)])  4.34 us
  transfers between devices with their start and end apart: 12, of which 10 were waited for; matrix products, arithmetic and copies ran while one was open for 0% of the time, Pallas kernels for 0%

profile of v11, /device:TPU:0, one launch (start us, length us, event | category | flops | bytes accessed | tf_op | source)
XLA Modules:
  0.0 41.2 jit_solution(11186590678074154321)
XLA Ops:
  0.6 6.3 %shard_map.41 = (f32[256,128]{1,0:T(8,128)S(1)}, f32[256,128]{1,0:T(8,128)S(1)}, f32[256,128]{1,0:T(8,128)S(1)}, f32[256,128]{1,0:T(8,128)S(1)}, f32[8,128]{1,0:T(8,128)S(1)}) custom-call(bf16[10240,256]{1,0:T(8,128)(2,1)} %modes_hbm.1, bf16[10240,512]{1,0:T(8,128)(2,1)} %snaps_hbm.1), custom_call_target="tpu_custom_call" | custom-call | flops 2684354560 | bytes 15728640 | tf_op jit(solution)/shard_map/pallas_call | solution.py:110
  7.0 0.1 pad_maximum_fusion.3
  7.0 4.0 %collective-permute-start = (f16[33,8,128]{2,1,0:T(8,128)(2,1)S(1)}, f16[33,8,128]{2,1,0:T(8,128)(2,1)S(1)}, u32[]{:S(2)}, u32[]{:S(2)}) collective-permute-start(f16[33,8,128]{2,1,0:T(8,128)(2,1)S(1)} %get-tuple-element.28), channel_id=1, source_target_pairs={{0,12},{1,13},{2,14},{3,15},{4,8},{5,9},{6,10},{7,11},{8,4},{9,5},... | collective-permute-start | bytes 202760 | tf_op jit(solution)/shard_map/ppermute | solution.py:35
  11.1 0.4 %collective-permute-start.1 = (f16[33,8,128]{2,1,0:T(8,128)(2,1)S(1)}, f16[33,8,128]{2,1,0:T(8,128)(2,1)S(1)}, u32[]{:S(2)}, u32[]{:S(2)}) collective-permute-start(f16[33,8,128]{2,1,0:T(8,128)(2,1)S(1)} %get-tuple-element.29), channel_id=1, source_target_pairs={{0,8},{1,5},{2,10},{3,7},{4,12},{5,1},{6,14},{7,3},{8,0},{9,13},{1... | collective-permute-start | bytes 202760 | tf_op jit(solution)/shard_map/ppermute | solution.py:35
  11.5 0.2 collective-permute-start.2
  11.7 1.6 %collective-permute-done = f16[33,8,128]{2,1,0:T(8,128)(2,1)S(1)} collective-permute-done((f16[33,8,128]{2,1,0:T(8,128)(2,1)S(1)}, f16[33,8,128]{2,1,0:T(8,128)(2,1)S(1)}, u32[]{:S(2)}, u32[]{:S(2)}) %collective-permute-start) | collective-permute-done | bytes 67616 | tf_op jit(solution)/shard_map/ppermute | solution.py:35
  13.4 2.0 %collective-permute-done.1 = f16[33,8,128]{2,1,0:T(8,128)(2,1)S(1)} collective-permute-done((f16[33,8,128]{2,1,0:T(8,128)(2,1)S(1)}, f16[33,8,128]{2,1,0:T(8,128)(2,1)S(1)}, u32[]{:S(2)}, u32[]{:S(2)}) %collective-permute-start.1) | collective-permute-done | bytes 67616 | tf_op jit(solution)/shard_map/ppermute | solution.py:35
  15.4 0.4 %collective-permute-done.2 = f16[33,8,128]{2,1,0:T(8,128)(2,1)S(1)} collective-permute-done((f16[33,8,128]{2,1,0:T(8,128)(2,1)S(1)}, f16[33,8,128]{2,1,0:T(8,128)(2,1)S(1)}, u32[]{:S(2)}, u32[]{:S(2)}) %collective-permute-start.2) | collective-permute-done | bytes 67616 | tf_op jit(solution)/shard_map/ppermute | solution.py:35
  15.9 0.1 fusion.4
  15.9 2.7 %collective-permute-start.3 = (f16[33,8,128]{2,1,0:T(8,128)(2,1)S(1)}, f16[33,8,128]{2,1,0:T(8,128)(2,1)S(1)}, u32[]{:S(2)}, u32[]{:S(2)}) collective-permute-start(f16[33,8,128]{2,1,0:T(8,128)(2,1)S(1)} %get-tuple-element.22), channel_id=1, source_target_pairs={{0,16},{4,20},{8,24},{12,28},{16,0},{20,4},{24,8},{28,12},{1,17},{... | collective-permute-start | bytes 202760 | tf_op jit(solution)/shard_map/ppermute | solution.py:25
  18.6 2.6 %collective-permute-done.3 = f16[33,8,128]{2,1,0:T(8,128)(2,1)S(1)} collective-permute-done((f16[33,8,128]{2,1,0:T(8,128)(2,1)S(1)}, f16[33,8,128]{2,1,0:T(8,128)(2,1)S(1)}, u32[]{:S(2)}, u32[]{:S(2)}) %collective-permute-start.3) | collective-permute-done | bytes 67616 | tf_op jit(solution)/shard_map/ppermute | solution.py:25
  21.3 1.6 %collective-permute-start.4 = (bf16[1,256,128]{2,1,0:T(8,128)(2,1)S(1)}, bf16[1,256,128]{2,1,0:T(8,128)(2,1)S(1)}, u32[]{:S(2)}, u32[]{:S(2)}) collective-permute-start(bf16[1,256,128]{2,1,0:T(8,128)(2,1)S(1)} %fusion.10), channel_id=1, source_target_pairs={{0,2},{1,3},{2,0},{3,1},{4,6},{5,7},{6,4},{7,5},{8,10},{9,11},{10,... | collective-permute-start | bytes 196616 | tf_op jit(solution)/shard_map/ppermute | solution.py:25
  22.8 2.7 %collective-permute-done.4 = bf16[1,256,128]{2,1,0:T(8,128)(2,1)S(1)} collective-permute-done((bf16[1,256,128]{2,1,0:T(8,128)(2,1)S(1)}, bf16[1,256,128]{2,1,0:T(8,128)(2,1)S(1)}, u32[]{:S(2)}, u32[]{:S(2)}) %collective-permute-start.4) | collective-permute-done | bytes 65568 | tf_op jit(solution)/shard_map/ppermute | solution.py:25
  25.6 1.8 %collective-permute-start.7 = (bf16[2,256,128]{2,1,0:T(8,128)(2,1)S(1)}, bf16[2,256,128]{2,1,0:T(8,128)(2,1)S(1)}, u32[]{:S(2)}, u32[]{:S(2)}) collective-permute-start(bf16[2,256,128]{2,1,0:T(8,128)(2,1)S(1)} %pad_maximum_fusion.refs_0_), channel_id=1, source_target_pairs={{0,4},{1,5},{2,6},{3,7},{4,0},{5,1},{6,2},{7,3},{8,12},{9,13},{10,... | collective-permute-start | bytes 393224 | tf_op jit(solution)/shard_map/ppermute | solution.py:35
  27.4 1.3 %collective-permute-start.6 = (bf16[2,256,128]{2,1,0:T(8,128)(2,1)S(1)}, bf16[2,256,128]{2,1,0:T(8,128)(2,1)S(1)}, u32[]{:S(2)}, u32[]{:S(2)}) collective-permute-start(bf16[2,256,128]{2,1,0:T(8,128)(2,1)S(1)} %pad_maximum_fusion.refs_0_), channel_id=1, source_target_pairs={{0,12},{1,9},{2,14},{3,11},{4,8},{5,13},{6,10},{7,15},{8,4},{9,1},... | collective-permute-start | bytes 393224 | tf_op jit(solution)/shard_map/ppermute | solution.py:35
  28.7 0.4 %collective-permute-start.5 = (bf16[2,256,128]{2,1,0:T(8,128)(2,1)S(1)}, bf16[2,256,128]{2,1,0:T(8,128)(2,1)S(1)}, u32[]{:S(2)}, u32[]{:S(2)}) collective-permute-start(bf16[2,256,128]{2,1,0:T(8,128)(2,1)S(1)} %pad_maximum_fusion.refs_0_), channel_id=1, source_target_pairs={{0,8},{1,13},{2,10},{3,15},{4,12},{5,9},{6,14},{7,11},{8,0},{9,5},... | collective-permute-start | bytes 393224 | tf_op jit(solution)/shard_map/ppermute | solution.py:35
  29.2 0.0 collective-permute-start.8
  29.2 3.0 %collective-permute-done.7.refs_3_ = bf16[2,256,128]{2,1,0:T(8,128)(2,1)S(1)} collective-permute-done((bf16[2,256,128]{2,1,0:T(8,128)(2,1)S(1)}, bf16[2,256,128]{2,1,0:T(8,128)(2,1)S(1)}, u32[]{:S(2)}, u32[]{:S(2)}) %collective-permute-start.7) | collective-permute-done | bytes 131104 | tf_op jit(solution)/shard_map/ppermute | solution.py:35
  32.2 0.0 collective-permute-start.11
  32.2 1.1 %collective-permute-done.6.refs_2_ = bf16[2,256,128]{2,1,0:T(8,128)(2,1)S(1)} collective-permute-done((bf16[2,256,128]{2,1,0:T(8,128)(2,1)S(1)}, bf16[2,256,128]{2,1,0:T(8,128)(2,1)S(1)}, u32[]{:S(2)}, u32[]{:S(2)}) %collective-permute-start.6) | collective-permute-done | bytes 131104 | tf_op jit(solution)/shard_map/ppermute | solution.py:35
  33.3 0.0 collective-permute-start.10
  33.3 0.4 %collective-permute-done.5.refs_1_ = bf16[2,256,128]{2,1,0:T(8,128)(2,1)S(1)} collective-permute-done((bf16[2,256,128]{2,1,0:T(8,128)(2,1)S(1)}, bf16[2,256,128]{2,1,0:T(8,128)(2,1)S(1)}, u32[]{:S(2)}, u32[]{:S(2)}) %collective-permute-start.5) | collective-permute-done | bytes 131104 | tf_op jit(solution)/shard_map/ppermute | solution.py:35
  33.7 0.1 collective-permute-start.9
  33.8 0.0 collective-permute-done.8.refs_4_
  33.8 0.0 collective-permute-done.11.refs_7_
  33.8 0.8 %collective-permute-done.10.refs_6_ = bf16[2,256,128]{2,1,0:T(8,128)(2,1)S(1)} collective-permute-done((bf16[2,256,128]{2,1,0:T(8,128)(2,1)S(1)}, bf16[2,256,128]{2,1,0:T(8,128)(2,1)S(1)}, u32[]{:S(2)}, u32[]{:S(2)}) %collective-permute-start.10) | collective-permute-done | bytes 131104 | tf_op jit(solution)/shard_map/ppermute | solution.py:25
  34.6 0.4 %collective-permute-done.9.refs_5_ = bf16[2,256,128]{2,1,0:T(8,128)(2,1)S(1)} collective-permute-done((bf16[2,256,128]{2,1,0:T(8,128)(2,1)S(1)}, bf16[2,256,128]{2,1,0:T(8,128)(2,1)S(1)}, u32[]{:S(2)}, u32[]{:S(2)}) %collective-permute-start.9) | collective-permute-done | bytes 131104 | tf_op jit(solution)/shard_map/ppermute | solution.py:25
  35.0 6.1 %shard_map.42 = (f32[1216,608]{1,0:T(8,128)}, f32[32,1216]{1,0:T(8,128)}) custom-call(bf16[2,256,128]{2,1,0:T(8,128)(2,1)S(1)} %pad_maximum_fusion.refs_0_, bf16[2,256,128]{2,1,0:T(8,128)(2,1)S(1)} %collective-permute-done.5.refs_1_, bf16[2,256,128]{2,1,0:T(8,128)(2,1)S(1)} %collective-permute-done.6.refs_2_, ...), custom_call_target="tpu_custom_call" | custom-call | flops 2390753280 | bytes 3112960 | tf_op jit(solution)/shard_map/pallas_call | solution.py:256
  (13 shorter events, 0.2 us)
Async XLA Ops:
  7.0 6.3 %collective-permute-start = (f16[33,8,128]{2,1,0:T(8,128)(2,1)S(1)}, f16[33,8,128]{2,1,0:T(8,128)(2,1)S(1)}, u32[]{:S(2)}, u32[]{:S(2)}) collective-permute-start(f16[33,8,128]{2,1,0:T(8,128)(2,1)S(1)} %get-tuple-element.28), channel_id=1, source_target_pairs={{0,12},{1,13},{2,14},{3,15},{4,8},{5,9},{6,10},{7,11},{8,4},{9,5},... | collective-permute-start | bytes 202760 | tf_op jit(solution)/shard_map/ppermute | solution.py:35
  11.1 4.3 %collective-permute-start.1 = (f16[33,8,128]{2,1,0:T(8,128)(2,1)S(1)}, f16[33,8,128]{2,1,0:T(8,128)(2,1)S(1)}, u32[]{:S(2)}, u32[]{:S(2)}) collective-permute-start(f16[33,8,128]{2,1,0:T(8,128)(2,1)S(1)} %get-tuple-element.29), channel_id=1, source_target_pairs={{0,8},{1,5},{2,10},{3,7},{4,12},{5,1},{6,14},{7,3},{8,0},{9,13},{1... | collective-permute-start | bytes 202760 | tf_op jit(solution)/shard_map/ppermute | solution.py:35
  11.5 4.3 %collective-permute-start.2 = (f16[33,8,128]{2,1,0:T(8,128)(2,1)S(1)}, f16[33,8,128]{2,1,0:T(8,128)(2,1)S(1)}, u32[]{:S(2)}, u32[]{:S(2)}) collective-permute-start(f16[33,8,128]{2,1,0:T(8,128)(2,1)S(1)} %get-tuple-element.30), channel_id=1, source_target_pairs={{0,4},{1,9},{2,6},{3,11},{4,0},{5,13},{6,2},{7,15},{8,12},{9,1},{1... | collective-permute-start | bytes 202760 | tf_op jit(solution)/shard_map/ppermute | solution.py:35
  15.9 5.3 %collective-permute-start.3 = (f16[33,8,128]{2,1,0:T(8,128)(2,1)S(1)}, f16[33,8,128]{2,1,0:T(8,128)(2,1)S(1)}, u32[]{:S(2)}, u32[]{:S(2)}) collective-permute-start(f16[33,8,128]{2,1,0:T(8,128)(2,1)S(1)} %get-tuple-element.22), channel_id=1, source_target_pairs={{0,16},{4,20},{8,24},{12,28},{16,0},{20,4},{24,8},{28,12},{1,17},{... | collective-permute-start | bytes 202760 | tf_op jit(solution)/shard_map/ppermute | solution.py:25
  21.3 4.3 %collective-permute-start.4 = (bf16[1,256,128]{2,1,0:T(8,128)(2,1)S(1)}, bf16[1,256,128]{2,1,0:T(8,128)(2,1)S(1)}, u32[]{:S(2)}, u32[]{:S(2)}) collective-permute-start(bf16[1,256,128]{2,1,0:T(8,128)(2,1)S(1)} %fusion.10), channel_id=1, source_target_pairs={{0,2},{1,3},{2,0},{3,1},{4,6},{5,7},{6,4},{7,5},{8,10},{9,11},{10,... | collective-permute-start | bytes 196616 | tf_op jit(solution)/shard_map/ppermute | solution.py:25
  25.6 6.6 %collective-permute-start.7 = (bf16[2,256,128]{2,1,0:T(8,128)(2,1)S(1)}, bf16[2,256,128]{2,1,0:T(8,128)(2,1)S(1)}, u32[]{:S(2)}, u32[]{:S(2)}) collective-permute-start(bf16[2,256,128]{2,1,0:T(8,128)(2,1)S(1)} %pad_maximum_fusion.refs_0_), channel_id=1, source_target_pairs={{0,4},{1,5},{2,6},{3,7},{4,0},{5,1},{6,2},{7,3},{8,12},{9,13},{10,... | collective-permute-start | bytes 393224 | tf_op jit(solution)/shard_map/ppermute | solution.py:35
  27.4 5.9 %collective-permute-start.6 = (bf16[2,256,128]{2,1,0:T(8,128)(2,1)S(1)}, bf16[2,256,128]{2,1,0:T(8,128)(2,1)S(1)}, u32[]{:S(2)}, u32[]{:S(2)}) collective-permute-start(bf16[2,256,128]{2,1,0:T(8,128)(2,1)S(1)} %pad_maximum_fusion.refs_0_), channel_id=1, source_target_pairs={{0,12},{1,9},{2,14},{3,11},{4,8},{5,13},{6,10},{7,15},{8,4},{9,1},... | collective-permute-start | bytes 393224 | tf_op jit(solution)/shard_map/ppermute | solution.py:35
  28.7 5.0 %collective-permute-start.5 = (bf16[2,256,128]{2,1,0:T(8,128)(2,1)S(1)}, bf16[2,256,128]{2,1,0:T(8,128)(2,1)S(1)}, u32[]{:S(2)}, u32[]{:S(2)}) collective-permute-start(bf16[2,256,128]{2,1,0:T(8,128)(2,1)S(1)} %pad_maximum_fusion.refs_0_), channel_id=1, source_target_pairs={{0,8},{1,13},{2,10},{3,15},{4,12},{5,9},{6,14},{7,11},{8,0},{9,5},... | collective-permute-start | bytes 393224 | tf_op jit(solution)/shard_map/ppermute | solution.py:35
  29.2 4.6 %collective-permute-start.8 = (bf16[2,256,128]{2,1,0:T(8,128)(2,1)S(1)}, bf16[2,256,128]{2,1,0:T(8,128)(2,1)S(1)}, u32[]{:S(2)}, u32[]{:S(2)}) collective-permute-start(bf16[2,256,128]{2,1,0:T(8,128)(2,1)S(1)} %pad_maximum_fusion.refs_0_), channel_id=1, source_target_pairs={{0,1},{1,0},{2,3},{3,2},{4,5},{5,4},{6,7},{7,6},{8,9},{9,8},{10,11... | collective-permute-start | bytes 393224 | tf_op jit(solution)/shard_map/ppermute | solution.py:25
  32.2 1.6 %collective-permute-start.11 = (bf16[2,256,128]{2,1,0:T(8,128)(2,1)S(1)}, bf16[2,256,128]{2,1,0:T(8,128)(2,1)S(1)}, u32[]{:S(2)}, u32[]{:S(2)}) collective-permute-start(bf16[2,256,128]{2,1,0:T(8,128)(2,1)S(1)} %collective-permute-done.7.refs_3_), channel_id=1, source_target_pairs={{0,1},{1,0},{2,3},{3,2},{4,5},{5,4},{6,7},{7,6},{8,9},{9,8},{10,11... | collective-permute-start | bytes 393224 | tf_op jit(solution)/shard_map/ppermute | solution.py:25
  33.3 1.3 %collective-permute-start.10 = (bf16[2,256,128]{2,1,0:T(8,128)(2,1)S(1)}, bf16[2,256,128]{2,1,0:T(8,128)(2,1)S(1)}, u32[]{:S(2)}, u32[]{:S(2)}) collective-permute-start(bf16[2,256,128]{2,1,0:T(8,128)(2,1)S(1)} %collective-permute-done.6.refs_2_), channel_id=1, source_target_pairs={{0,1},{1,0},{2,3},{3,2},{4,5},{5,4},{6,7},{7,6},{8,9},{9,8},{10,11... | collective-permute-start | bytes 393224 | tf_op jit(solution)/shard_map/ppermute | solution.py:25
  33.7 1.3 %collective-permute-start.9 = (bf16[2,256,128]{2,1,0:T(8,128)(2,1)S(1)}, bf16[2,256,128]{2,1,0:T(8,128)(2,1)S(1)}, u32[]{:S(2)}, u32[]{:S(2)}) collective-permute-start(bf16[2,256,128]{2,1,0:T(8,128)(2,1)S(1)} %collective-permute-done.5.refs_1_), channel_id=1, source_target_pairs={{0,1},{1,0},{2,3},{3,2},{4,5},{5,4},{6,7},{7,6},{8,9},{9,8},{10,11... | collective-permute-start | bytes 393224 | tf_op jit(solution)/shard_map/ppermute | solution.py:25

commit v12 on v11

--- a/solution.py
+++ b/solution.py
@@ -18,6 +18,8 @@
 TOP = 9.0
 SMALLEST = 1e-30
 VMEM_LIMIT = 48 * 2**20
+GRAM_VMEM_LIMIT = 32 * 2**20
+EAGERNESS = 20
 
 
 def swap(value, axis, bit):
@@ -130,24 +132,38 @@
     return [part.reshape((-1,) + exponent.shape) for part in parts], exponent[None]
 
 
-def gram_kernel(sizes, *refs):
-    n_time, snaps, modes, row_block, col_block, target_block, tile = sizes
-    half, quarter = n_time // 2, snaps // QUAD
-    count = 2 * QUAD
-    pieces, (gram_hbm, rhs_hbm) = refs[0:count], refs[count : count + 2]
-    lead, head, target, *rows, cols, staged, side, side_staged, sems = refs[count + 2 :]
+def gram_kernel(sizes, turns, *refs):
+    n_time, quarter, modes, row_block, col_block, target_block, tile = sizes
+    half, snaps, is_last = n_time // 2, quarter * len(turns), 0 not in turns
+    refs = list(refs)
+
+    def taken(count):
+        return [refs.pop(0) for _ in range(count)]
+
+    pieces = taken(2 * len(turns))
+    (before,) = taken(1) if is_last else (None,)
+    outs = taken(2 if is_last else 1)
+    lead, head, target, *rows, cols = taken(6)
+    if is_last:
+        (gram_hbm, rhs_hbm), (staged, side, side_staged, sems) = outs, refs
+        scale = 1.0 / (n_time * QUAD * quarter)
+    else:
+        staged = side = outs[0]
+        scale = 1.0
+    aside = slice(0, target_block) if is_last else slice(col_block, col_block + target_block)
     later = (n_time - 1) * snaps
     time_pos, space_pos = lax.axis_index("tm"), lax.axis_index("space")
-    place, core = lax.rem(space_pos, QUAD), lax.rem(time_pos, 2)
+    core = lax.rem(time_pos, 2)
 
     def each_piece(take):
         for other in range(2):
             for k in range(half):
                 block = jnp.bitwise_xor(time_pos, 2 * k + other)
-                for j in range(QUAD):
-                    source = partner(GATHER_PARTNERS, jnp.bitwise_xor(core, other), j)
-                    at = block * snaps + jnp.bitwise_xor(place, source) * quarter
-                    take(pieces[other * QUAD + j].at[k], pl.multiple_of(at, quarter))
+                for j, turn in enumerate(turns):
+                    source = partner(GATHER_PARTNERS, jnp.bitwise_xor(core, other), turn)
+                    at = block * snaps + (source - min(turns)) * quarter
+                    piece = pieces[other * len(turns) + j].at[k]
+                    take(piece, pl.multiple_of(at, quarter))
 
     gap = 2 * snaps
     lead[:, 0:gap] = jnp.zeros((LEAD_MODES, gap), jnp.bfloat16)
@@ -204,7 +220,7 @@
     def times(left, right):
         return lax.dot_general(
             left, right, (((1,), (1,)), ((), ())), preferred_element_type=jnp.float32
-        ) * (1.0 / (n_time * snaps))
+        )
 
     first_rows = rows[0].at[pl.ds(LEAD_MODES, modes), 0:snaps]
     first_cols = cols.at[pl.ds(LEAD_MODES, modes), 0:snaps]
@@ -218,25 +234,35 @@
             rows[step % 2][pl.ds(LEAD_MODES, tile), snaps:],
             cols[pl.ds(LEAD_MODES, col_block + target_block), snaps:],
         )
+        if is_last:
+            product = (product + before[at, :]) * scale
         shape = (tile, col_block)
         row = time_pos * row_block + top + lax.broadcasted_iota(jnp.int32, shape, 0)
         column = space_pos * col_block + lax.broadcasted_iota(jnp.int32, shape, 1)
-        staged[at, :] = product[:, 0:col_block] + jnp.where(row == column, RIDGE_WEIGHT, 0.0)
-        side[at, :] = product[:, col_block:]
+        if is_last:
+            ridge = jnp.where(row == column, RIDGE_WEIGHT, 0.0)
+            staged[at, :] = product[:, 0:col_block] + ridge
+            side[at, :] = product[:, col_block:]
+        else:
+            staged[at, :] = product
         if step == 0:
 
             @pl.when(time_pos == 0)
             def _():
-                side[0:modes, :] += times(first_rows[...], target[:, snaps:gap])
+                extra = times(first_rows[...], target[:, snaps:gap]) * scale
+                side[0:modes, aside] += extra
 
             @pl.when((time_pos == 0) & (space_pos == 0))
             def _():
-                staged[0:modes, 0:modes] += times(
-                    first_rows[...], first_cols[...]
-                )
-
+                extra = times(first_rows[...], first_cols[...]) * scale
+                staged[0:modes, 0:modes] += extra
+
+        if not is_last:
+            continue
         writes.append(pltpu.make_async_copy(staged.at[at], gram_hbm.at[at], sems.at[step]))
         writes[-1].start()
+    if not is_last:
+        return
     side_staged[...] = side[...].T
     writes.append(pltpu.make_async_copy(side_staged, rhs_hbm, sems.at[len(writes)]))
     writes[-1].start()
@@ -244,45 +270,56 @@
         write.wait()
 
 
-def gram_blocks(pieces, n_time, n_space):
+def add_quarters(turns, pieces, before, n_time, n_space):
     _, modes, quarter = pieces[0].shape
-    snaps = QUAD * quarter
     features = modes + 2 * LEAD_MODES * LEAD_MODES
     row_block, col_block, target_block = features // n_time, features // n_space, modes // n_space
-    later = (n_time - 1) * snaps
     tile = row_block // 4 if row_block % (4 * ROW_TILE) == 0 else row_block
     assert min(tile, col_block) >= modes
+    snaps, is_last = quarter * len(turns), before is not None
+    width = col_block + target_block
+    total = n_time * snaps
+    scratch = [
+        pltpu.VMEM((LEAD_MODES, total + 2 * snaps), jnp.bfloat16),
+        pltpu.VMEM((LEAD_MODES, total), jnp.float32),
+        pltpu.VMEM((target_block, total + snaps), jnp.bfloat16),
+        pltpu.VMEM((tile + 2 * LEAD_MODES, total), jnp.bfloat16),
+        pltpu.VMEM((tile + 2 * LEAD_MODES, total), jnp.bfloat16),
+        pltpu.VMEM((width + 2 * LEAD_MODES, total), jnp.bfloat16),
+    ]
     vmem = pl.BlockSpec(memory_space=pltpu.VMEM)
-    gram, rhs = pl.pallas_call(
-        functools.partial(
-            gram_kernel, (n_time, snaps, modes, row_block, col_block, target_block, tile)
-        ),
-        out_shape=(
+    if is_last:
+        out_shape = (
             jax.ShapeDtypeStruct((row_block, col_block), jnp.float32),
             jax.ShapeDtypeStruct((target_block, row_block), jnp.float32),
-        ),
-        in_specs=[vmem] * len(pieces),
-        out_specs=(pl.BlockSpec(memory_space=pl.ANY),) * 2,
-        scratch_shapes=[
-            pltpu.VMEM((LEAD_MODES, (n_time + 2) * snaps), jnp.bfloat16),
-            pltpu.VMEM((LEAD_MODES, n_time * snaps), jnp.float32),
-            pltpu.VMEM((target_block, (n_time + 1) * snaps), jnp.bfloat16),
-            pltpu.VMEM((tile + 2 * LEAD_MODES, n_time * snaps), jnp.bfloat16),
-            pltpu.VMEM((tile + 2 * LEAD_MODES, n_time * snaps), jnp.bfloat16),
-            pltpu.VMEM((col_block + 2 * LEAD_MODES + target_block, n_time * snaps), jnp.bfloat16),
+        )
+        out_specs = (pl.BlockSpec(memory_space=pl.ANY),) * 2
+        scratch += [
             pltpu.VMEM((row_block, col_block), jnp.float32),
             pltpu.VMEM((row_block, target_block), jnp.float32),
             pltpu.VMEM((target_block, row_block), jnp.float32),
             pltpu.SemaphoreType.DMA((row_block // tile + 1,)),
-        ],
-        compiler_params=pltpu.CompilerParams(vmem_limit_bytes=VMEM_LIMIT),
+        ]
+    else:
+        out_shape, out_specs = pltpu.VMEM((row_block, width), jnp.float32), vmem
+    operands = pieces + ([before] if is_last else [])
+    return pl.pallas_call(
+        functools.partial(
+            gram_kernel,
+            (n_time, quarter, modes, row_block, col_block, target_block, tile),
+            turns,
+        ),
+        out_shape=out_shape,
+        in_specs=[vmem] * len(operands),
+        out_specs=out_specs,
+        scratch_shapes=scratch,
+        compiler_params=pltpu.CompilerParams(vmem_limit_bytes=GRAM_VMEM_LIMIT),
         cost_estimate=pl.CostEstimate(
-            flops=2 * row_block * (col_block + target_block) * later,
-            bytes_accessed=4 * row_block * (col_block + target_block),
+            flops=EAGERNESS * row_block * width * total,
+            bytes_accessed=4 * row_block * width,
             transcendentals=0,
         ),
-    )(*map(in_vmem, pieces))
-    return gram, rhs.T
+    )(*map(in_vmem, operands))
 
 
 def joined(value, axis, bit):
@@ -303,9 +340,11 @@
     mine = mine.astype(jnp.bfloat16).reshape(1, modes.shape[1], -1)
     for bit in bits_of(n_time)[1:]:
         mine = joined(mine, "tm", bit)
-    pieces = [mine] + [swap_quad(mine, GATHER_PARTNERS, j) for j in range(1, QUAD)]
-    pieces = pieces + [swap(piece, "tm", 1) for piece in pieces]
-    return gram_blocks(pieces, n_time, n_space)
+    others = [swap_quad(mine, GATHER_PARTNERS, j) for j in range(1, QUAD)]
+    total = add_quarters((0,), [mine, swap(mine, "tm", 1)], None, n_time, n_space)
+    pieces = others + [swap(piece, "tm", 1) for piece in others]
+    gram, rhs = add_quarters((1, 2, 3), pieces, total, n_time, n_space)
+    return gram, rhs.T
 
 
 def solution(mesh):

time: 41.3 us -> 41 us (level)
  waiting for transfers between devices: 15.2 us -> 13.9 us
  Pallas kernels: 12.4 us -> 13.4 us
    ppermute x6, waiting for transfers between devices: 6.59 us -> 5.35 us  [swap(): return lax.ppermute(value, axis, [(i, i ^ bit) for i in range(count)])]
    pallas_call x1 -> x2, Pallas kernels: 6.13 us -> 7.08 us  [add_quarters(): pl.pallas_call(functools.partial(gram_kernel, (n_time, quarter, modes, ro...]
  transfers between devices with their start and end apart: 12 -> 12, of which waited for: 10 -> 8; matrix products, arithmetic and copies ran while one was open for 0% -> 0% of each run, Pallas kernels for 0% -> 5%
where the time goes in v12:
time: 41 us; the launch traced here: 40.9 us
  waiting for transfers between devices  13.9 us (34%)
  Pallas kernels  13.4 us (33%)
  starting transfers between devices  12.6 us (31%)
  between operations  0.75 us (2%)
    ppermute x6, waiting for transfers between devices, swap_quad(): return lax.ppermute(value, ('space', 'tm'), pairs)  8.57 us
    ppermute x6, starting transfers between devices, swap_quad(): return lax.ppermute(value, ('space', 'tm'), pairs)  8.22 us
    pallas_call x2, Pallas kernels, add_quarters(): pl.pallas_call(functools.partial(gram_kernel, (n_time, quarter, modes, ro...  7.08 us
    pallas_call x1, Pallas kernels, project(): pl.pallas_call(projection_kernel, out_shape=(pltpu.VMEM((count, quarter),...  6.28 us
    ppermute x6, waiting for transfers between devices, swap(): return lax.ppermute(value, axis, [(i, i ^ bit) for i in range(count)])  5.35 us
    ppermute x6, starting transfers between devices, swap(): return lax.ppermute(value, axis, [(i, i ^ bit) for i in range(count)])  4.34 us
  transfers between devices with their start and end apart: 12, of which 8 were waited for; matrix products, arithmetic and copies ran while one was open for 0% of the time, Pallas kernels for 5%

profile of v12, /device:TPU:0, one launch (start us, length us, event | category | flops | bytes accessed | tf_op | source)
XLA Modules:
  0.0 40.9 jit_solution(3718875098817786476)
XLA Ops:
  0.6 6.3 %shard_map.41 = (f32[256,128]{1,0:T(8,128)S(1)}, f32[256,128]{1,0:T(8,128)S(1)}, f32[256,128]{1,0:T(8,128)S(1)}, f32[256,128]{1,0:T(8,128)S(1)}, f32[8,128]{1,0:T(8,128)S(1)}) custom-call(bf16[10240,256]{1,0:T(8,128)(2,1)} %modes_hbm.1, bf16[10240,512]{1,0:T(8,128)(2,1)} %snaps_hbm.1), custom_call_target="tpu_custom_call" | custom-call | flops 2684354560 | bytes 15728640 | tf_op jit(solution)/shard_map/pallas_call | solution.py:112
  7.0 0.1 pad_maximum_fusion.3
  7.0 4.0 %collective-permute-start = (f16[33,8,128]{2,1,0:T(8,128)(2,1)S(1)}, f16[33,8,128]{2,1,0:T(8,128)(2,1)S(1)}, u32[]{:S(2)}, u32[]{:S(2)}) collective-permute-start(f16[33,8,128]{2,1,0:T(8,128)(2,1)S(1)} %get-tuple-element.28), channel_id=1, source_target_pairs={{0,12},{1,13},{2,14},{3,15},{4,8},{5,9},{6,10},{7,11},{8,4},{9,5},... | collective-permute-start | bytes 202760 | tf_op jit(solution)/shard_map/ppermute | solution.py:37
  11.1 0.4 %collective-permute-start.1 = (f16[33,8,128]{2,1,0:T(8,128)(2,1)S(1)}, f16[33,8,128]{2,1,0:T(8,128)(2,1)S(1)}, u32[]{:S(2)}, u32[]{:S(2)}) collective-permute-start(f16[33,8,128]{2,1,0:T(8,128)(2,1)S(1)} %get-tuple-element.29), channel_id=1, source_target_pairs={{0,8},{1,5},{2,10},{3,7},{4,12},{5,1},{6,14},{7,3},{8,0},{9,13},{1... | collective-permute-start | bytes 202760 | tf_op jit(solution)/shard_map/ppermute | solution.py:37
  11.5 0.2 collective-permute-start.2
  11.7 1.6 %collective-permute-done = f16[33,8,128]{2,1,0:T(8,128)(2,1)S(1)} collective-permute-done((f16[33,8,128]{2,1,0:T(8,128)(2,1)S(1)}, f16[33,8,128]{2,1,0:T(8,128)(2,1)S(1)}, u32[]{:S(2)}, u32[]{:S(2)}) %collective-permute-start) | collective-permute-done | bytes 67616 | tf_op jit(solution)/shard_map/ppermute | solution.py:37
  13.4 2.0 %collective-permute-done.1 = f16[33,8,128]{2,1,0:T(8,128)(2,1)S(1)} collective-permute-done((f16[33,8,128]{2,1,0:T(8,128)(2,1)S(1)}, f16[33,8,128]{2,1,0:T(8,128)(2,1)S(1)}, u32[]{:S(2)}, u32[]{:S(2)}) %collective-permute-start.1) | collective-permute-done | bytes 67616 | tf_op jit(solution)/shard_map/ppermute | solution.py:37
  15.4 0.4 %collective-permute-done.2 = f16[33,8,128]{2,1,0:T(8,128)(2,1)S(1)} collective-permute-done((f16[33,8,128]{2,1,0:T(8,128)(2,1)S(1)}, f16[33,8,128]{2,1,0:T(8,128)(2,1)S(1)}, u32[]{:S(2)}, u32[]{:S(2)}) %collective-permute-start.2) | collective-permute-done | bytes 67616 | tf_op jit(solution)/shard_map/ppermute | solution.py:37
  15.9 0.1 fusion.4
  15.9 2.7 %collective-permute-start.3 = (f16[33,8,128]{2,1,0:T(8,128)(2,1)S(1)}, f16[33,8,128]{2,1,0:T(8,128)(2,1)S(1)}, u32[]{:S(2)}, u32[]{:S(2)}) collective-permute-start(f16[33,8,128]{2,1,0:T(8,128)(2,1)S(1)} %get-tuple-element.22), channel_id=1, source_target_pairs={{0,16},{4,20},{8,24},{12,28},{16,0},{20,4},{24,8},{28,12},{1,17},{... | collective-permute-start | bytes 202760 | tf_op jit(solution)/shard_map/ppermute | solution.py:27
  18.6 2.6 %collective-permute-done.3 = f16[33,8,128]{2,1,0:T(8,128)(2,1)S(1)} collective-permute-done((f16[33,8,128]{2,1,0:T(8,128)(2,1)S(1)}, f16[33,8,128]{2,1,0:T(8,128)(2,1)S(1)}, u32[]{:S(2)}, u32[]{:S(2)}) %collective-permute-start.3) | collective-permute-done | bytes 67616 | tf_op jit(solution)/shard_map/ppermute | solution.py:27
  21.3 1.6 %collective-permute-start.4 = (bf16[1,256,128]{2,1,0:T(8,128)(2,1)S(1)}, bf16[1,256,128]{2,1,0:T(8,128)(2,1)S(1)}, u32[]{:S(2)}, u32[]{:S(2)}) collective-permute-start(bf16[1,256,128]{2,1,0:T(8,128)(2,1)S(1)} %fusion.10), channel_id=1, source_target_pairs={{0,2},{1,3},{2,0},{3,1},{4,6},{5,7},{6,4},{7,5},{8,10},{9,11},{10,... | collective-permute-start | bytes 196616 | tf_op jit(solution)/shard_map/ppermute | solution.py:27
  22.8 2.7 %collective-permute-done.4 = bf16[1,256,128]{2,1,0:T(8,128)(2,1)S(1)} collective-permute-done((bf16[1,256,128]{2,1,0:T(8,128)(2,1)S(1)}, bf16[1,256,128]{2,1,0:T(8,128)(2,1)S(1)}, u32[]{:S(2)}, u32[]{:S(2)}) %collective-permute-start.4) | collective-permute-done | bytes 65568 | tf_op jit(solution)/shard_map/ppermute | solution.py:27
  25.6 1.8 %collective-permute-start.7 = (bf16[2,256,128]{2,1,0:T(8,128)(2,1)S(1)}, bf16[2,256,128]{2,1,0:T(8,128)(2,1)S(1)}, u32[]{:S(2)}, u32[]{:S(2)}) collective-permute-start(bf16[2,256,128]{2,1,0:T(8,128)(2,1)S(1)} %pad_maximum_fusion.refs_0_), channel_id=1, source_target_pairs={{0,4},{1,5},{2,6},{3,7},{4,0},{5,1},{6,2},{7,3},{8,12},{9,13},{10,... | collective-permute-start | bytes 393224 | tf_op jit(solution)/shard_map/ppermute | solution.py:37
  27.4 1.3 %collective-permute-start.6 = (bf16[2,256,128]{2,1,0:T(8,128)(2,1)S(1)}, bf16[2,256,128]{2,1,0:T(8,128)(2,1)S(1)}, u32[]{:S(2)}, u32[]{:S(2)}) collective-permute-start(bf16[2,256,128]{2,1,0:T(8,128)(2,1)S(1)} %pad_maximum_fusion.refs_0_), channel_id=1, source_target_pairs={{0,12},{1,9},{2,14},{3,11},{4,8},{5,13},{6,10},{7,15},{8,4},{9,1},... | collective-permute-start | bytes 393224 | tf_op jit(solution)/shard_map/ppermute | solution.py:37
  28.7 0.4 %collective-permute-start.5 = (bf16[2,256,128]{2,1,0:T(8,128)(2,1)S(1)}, bf16[2,256,128]{2,1,0:T(8,128)(2,1)S(1)}, u32[]{:S(2)}, u32[]{:S(2)}) collective-permute-start(bf16[2,256,128]{2,1,0:T(8,128)(2,1)S(1)} %pad_maximum_fusion.refs_0_), channel_id=1, source_target_pairs={{0,8},{1,13},{2,10},{3,15},{4,12},{5,9},{6,14},{7,11},{8,0},{9,5},... | collective-permute-start | bytes 393224 | tf_op jit(solution)/shard_map/ppermute | solution.py:37
  29.2 0.0 collective-permute-start.11
  29.2 3.0 %collective-permute-done.7.refs_2_ = bf16[2,256,128]{2,1,0:T(8,128)(2,1)S(1)} collective-permute-done((bf16[2,256,128]{2,1,0:T(8,128)(2,1)S(1)}, bf16[2,256,128]{2,1,0:T(8,128)(2,1)S(1)}, u32[]{:S(2)}, u32[]{:S(2)}) %collective-permute-start.7) | collective-permute-done | bytes 131104 | tf_op jit(solution)/shard_map/ppermute | solution.py:37
  32.2 0.0 collective-permute-start.10
  32.2 1.1 %collective-permute-done.6.refs_1_ = bf16[2,256,128]{2,1,0:T(8,128)(2,1)S(1)} collective-permute-done((bf16[2,256,128]{2,1,0:T(8,128)(2,1)S(1)}, bf16[2,256,128]{2,1,0:T(8,128)(2,1)S(1)}, u32[]{:S(2)}, u32[]{:S(2)}) %collective-permute-start.6) | collective-permute-done | bytes 131104 | tf_op jit(solution)/shard_map/ppermute | solution.py:37
  33.3 0.0 collective-permute-start.9
  33.3 0.4 %collective-permute-done.5.refs_0_ = bf16[2,256,128]{2,1,0:T(8,128)(2,1)S(1)} collective-permute-done((bf16[2,256,128]{2,1,0:T(8,128)(2,1)S(1)}, bf16[2,256,128]{2,1,0:T(8,128)(2,1)S(1)}, u32[]{:S(2)}, u32[]{:S(2)}) %collective-permute-start.5) | collective-permute-done | bytes 131104 | tf_op jit(solution)/shard_map/ppermute | solution.py:37
  33.7 0.1 collective-permute-start.8
  33.8 0.0 collective-permute-done.11.refs_1_
  33.8 2.0 %shard_map.42.refs_6_ = f32[1216,640]{1,0:T(8,128)S(1)} custom-call(bf16[2,256,128]{2,1,0:T(8,128)(2,1)S(1)} %pad_maximum_fusion.refs_0_, bf16[2,256,128]{2,1,0:T(8,128)(2,1)S(1)} %collective-permute-done.11.refs_1_), custom_call_target="tpu_custom_call" | custom-call | flops 7969177600 | bytes 3112960 | tf_op jit(solution)/shard_map/pallas_call | solution.py:306
  35.8 0.0 collective-permute-done.10.refs_5_
  35.8 0.0 collective-permute-done.9.refs_4_
  35.8 0.0 collective-permute-done.8.refs_3_
  35.8 5.1 %shard_map.43 = (f32[1216,608]{1,0:T(8,128)}, f32[32,1216]{1,0:T(8,128)}) custom-call(bf16[2,256,128]{2,1,0:T(8,128)(2,1)S(1)} %collective-permute-done.5.refs_0_, bf16[2,256,128]{2,1,0:T(8,128)(2,1)S(1)} %collective-permute-done.6.refs_1_, bf16[2,256,128]{2,1,0:T(8,128)(2,1)S(1)} %collective-permute-done.7.refs_2_, ...), custom_call_target="tpu_custom_call" | custom-call | flops 23907532800 | bytes 3112960 | tf_op jit(solution)/shard_map/pallas_call | solution.py:306
  (13 shorter events, 0.2 us)
Async XLA Ops:
  7.0 6.3 %collective-permute-start = (f16[33,8,128]{2,1,0:T(8,128)(2,1)S(1)}, f16[33,8,128]{2,1,0:T(8,128)(2,1)S(1)}, u32[]{:S(2)}, u32[]{:S(2)}) collective-permute-start(f16[33,8,128]{2,1,0:T(8,128)(2,1)S(1)} %get-tuple-element.28), channel_id=1, source_target_pairs={{0,12},{1,13},{2,14},{3,15},{4,8},{5,9},{6,10},{7,11},{8,4},{9,5},... | collective-permute-start | bytes 202760 | tf_op jit(solution)/shard_map/ppermute | solution.py:37
  11.1 4.3 %collective-permute-start.1 = (f16[33,8,128]{2,1,0:T(8,128)(2,1)S(1)}, f16[33,8,128]{2,1,0:T(8,128)(2,1)S(1)}, u32[]{:S(2)}, u32[]{:S(2)}) collective-permute-start(f16[33,8,128]{2,1,0:T(8,128)(2,1)S(1)} %get-tuple-element.29), channel_id=1, source_target_pairs={{0,8},{1,5},{2,10},{3,7},{4,12},{5,1},{6,14},{7,3},{8,0},{9,13},{1... | collective-permute-start | bytes 202760 | tf_op jit(solution)/shard_map/ppermute | solution.py:37
  11.5 4.3 %collective-permute-start.2 = (f16[33,8,128]{2,1,0:T(8,128)(2,1)S(1)}, f16[33,8,128]{2,1,0:T(8,128)(2,1)S(1)}, u32[]{:S(2)}, u32[]{:S(2)}) collective-permute-start(f16[33,8,128]{2,1,0:T(8,128)(2,1)S(1)} %get-tuple-element.30), channel_id=1, source_target_pairs={{0,4},{1,9},{2,6},{3,11},{4,0},{5,13},{6,2},{7,15},{8,12},{9,1},{1... | collective-permute-start | bytes 202760 | tf_op jit(solution)/shard_map/ppermute | solution.py:37
  15.9 5.3 %collective-permute-start.3 = (f16[33,8,128]{2,1,0:T(8,128)(2,1)S(1)}, f16[33,8,128]{2,1,0:T(8,128)(2,1)S(1)}, u32[]{:S(2)}, u32[]{:S(2)}) collective-permute-start(f16[33,8,128]{2,1,0:T(8,128)(2,1)S(1)} %get-tuple-element.22), channel_id=1, source_target_pairs={{0,16},{4,20},{8,24},{12,28},{16,0},{20,4},{24,8},{28,12},{1,17},{... | collective-permute-start | bytes 202760 | tf_op jit(solution)/shard_map/ppermute | solution.py:27
  21.3 4.3 %collective-permute-start.4 = (bf16[1,256,128]{2,1,0:T(8,128)(2,1)S(1)}, bf16[1,256,128]{2,1,0:T(8,128)(2,1)S(1)}, u32[]{:S(2)}, u32[]{:S(2)}) collective-permute-start(bf16[1,256,128]{2,1,0:T(8,128)(2,1)S(1)} %fusion.10), channel_id=1, source_target_pairs={{0,2},{1,3},{2,0},{3,1},{4,6},{5,7},{6,4},{7,5},{8,10},{9,11},{10,... | collective-permute-start | bytes 196616 | tf_op jit(solution)/shard_map/ppermute | solution.py:27
  25.6 6.6 %collective-permute-start.7 = (bf16[2,256,128]{2,1,0:T(8,128)(2,1)S(1)}, bf16[2,256,128]{2,1,0:T(8,128)(2,1)S(1)}, u32[]{:S(2)}, u32[]{:S(2)}) collective-permute-start(bf16[2,256,128]{2,1,0:T(8,128)(2,1)S(1)} %pad_maximum_fusion.refs_0_), channel_id=1, source_target_pairs={{0,4},{1,5},{2,6},{3,7},{4,0},{5,1},{6,2},{7,3},{8,12},{9,13},{10,... | collective-permute-start | bytes 393224 | tf_op jit(solution)/shard_map/ppermute | solution.py:37
  27.4 5.9 %collective-permute-start.6 = (bf16[2,256,128]{2,1,0:T(8,128)(2,1)S(1)}, bf16[2,256,128]{2,1,0:T(8,128)(2,1)S(1)}, u32[]{:S(2)}, u32[]{:S(2)}) collective-permute-start(bf16[2,256,128]{2,1,0:T(8,128)(2,1)S(1)} %pad_maximum_fusion.refs_0_), channel_id=1, source_target_pairs={{0,12},{1,9},{2,14},{3,11},{4,8},{5,13},{6,10},{7,15},{8,4},{9,1},... | collective-permute-start | bytes 393224 | tf_op jit(solution)/shard_map/ppermute | solution.py:37
  28.7 5.0 %collective-permute-start.5 = (bf16[2,256,128]{2,1,0:T(8,128)(2,1)S(1)}, bf16[2,256,128]{2,1,0:T(8,128)(2,1)S(1)}, u32[]{:S(2)}, u32[]{:S(2)}) collective-permute-start(bf16[2,256,128]{2,1,0:T(8,128)(2,1)S(1)} %pad_maximum_fusion.refs_0_), channel_id=1, source_target_pairs={{0,8},{1,13},{2,10},{3,15},{4,12},{5,9},{6,14},{7,11},{8,0},{9,5},... | collective-permute-start | bytes 393224 | tf_op jit(solution)/shard_map/ppermute | solution.py:37
  29.2 4.6 %collective-permute-start.11 = (bf16[2,256,128]{2,1,0:T(8,128)(2,1)S(1)}, bf16[2,256,128]{2,1,0:T(8,128)(2,1)S(1)}, u32[]{:S(2)}, u32[]{:S(2)}) collective-permute-start(bf16[2,256,128]{2,1,0:T(8,128)(2,1)S(1)} %pad_maximum_fusion.refs_0_), channel_id=1, source_target_pairs={{0,1},{1,0},{2,3},{3,2},{4,5},{5,4},{6,7},{7,6},{8,9},{9,8},{10,11... | collective-permute-start | bytes 393224 | tf_op jit(solution)/shard_map/ppermute | solution.py:27
  32.2 3.6 %collective-permute-start.10 = (bf16[2,256,128]{2,1,0:T(8,128)(2,1)S(1)}, bf16[2,256,128]{2,1,0:T(8,128)(2,1)S(1)}, u32[]{:S(2)}, u32[]{:S(2)}) collective-permute-start(bf16[2,256,128]{2,1,0:T(8,128)(2,1)S(1)} %collective-permute-done.7.refs_2_), channel_id=1, source_target_pairs={{0,1},{1,0},{2,3},{3,2},{4,5},{5,4},{6,7},{7,6},{8,9},{9,8},{10,11... | collective-permute-start | bytes 393224 | tf_op jit(solution)/shard_map/ppermute | solution.py:27
  33.3 2.5 %collective-permute-start.9 = (bf16[2,256,128]{2,1,0:T(8,128)(2,1)S(1)}, bf16[2,256,128]{2,1,0:T(8,128)(2,1)S(1)}, u32[]{:S(2)}, u32[]{:S(2)}) collective-permute-start(bf16[2,256,128]{2,1,0:T(8,128)(2,1)S(1)} %collective-permute-done.6.refs_1_), channel_id=1, source_target_pairs={{0,1},{1,0},{2,3},{3,2},{4,5},{5,4},{6,7},{7,6},{8,9},{9,8},{10,11... | collective-permute-start | bytes 393224 | tf_op jit(solution)/shard_map/ppermute | solution.py:27
  33.7 2.1 %collective-permute-start.8 = (bf16[2,256,128]{2,1,0:T(8,128)(2,1)S(1)}, bf16[2,256,128]{2,1,0:T(8,128)(2,1)S(1)}, u32[]{:S(2)}, u32[]{:S(2)}) collective-permute-start(bf16[2,256,128]{2,1,0:T(8,128)(2,1)S(1)} %collective-permute-done.5.refs_0_), channel_id=1, source_target_pairs={{0,1},{1,0},{2,3},{3,2},{4,5},{5,4},{6,7},{7,6},{8,9},{9,8},{10,11... | collective-permute-start | bytes 393224 | tf_op jit(solution)/shard_map/ppermute | solution.py:27

commit v13 on v12

--- a/solution.py
+++ b/solution.py
@@ -223,7 +223,6 @@
         )
 
     first_rows = rows[0].at[pl.ds(LEAD_MODES, modes), 0:snaps]
-    first_cols = cols.at[pl.ds(LEAD_MODES, modes), 0:snaps]
     writes = []
     for step in range(row_block // tile):
         top = step * tile
@@ -247,15 +246,19 @@
             staged[at, :] = product
         if step == 0:
 
-            @pl.when(time_pos == 0)
+            @pl.when((time_pos == 0) & (space_pos == 0))
+            def _():
+                end = LEAD_MODES + modes
+                cols[end : end + target_block, 0:snaps] = target[:, snaps:gap]
+                right = cols[LEAD_MODES : end + target_block, 0:snaps]
+                extra = times(first_rows[...], right) * scale
+                staged[0:modes, 0:modes] += extra[:, 0:modes]
+                side[0:modes, aside] += extra[:, modes:]
+
+            @pl.when((time_pos == 0) & (space_pos != 0))
             def _():
                 extra = times(first_rows[...], target[:, snaps:gap]) * scale
                 side[0:modes, aside] += extra
-
-            @pl.when((time_pos == 0) & (space_pos == 0))
-            def _():
-                extra = times(first_rows[...], first_cols[...]) * scale
-                staged[0:modes, 0:modes] += extra
 
         if not is_last:
             continue

time: 41 us -> 40.8 us (level)
  no operation moved by 1% of the time
where the time goes in v13:
time: 40.8 us; the launch traced here: 40.7 us
  waiting for transfers between devices  13.9 us (34%)
  Pallas kernels  13.1 us (32%)
  starting transfers between devices  12.6 us (31%)
  between operations  0.75 us (2%)
    ppermute x6, waiting for transfers between devices, swap_quad(): return lax.ppermute(value, ('space', 'tm'), pairs)  8.57 us
    ppermute x6, starting transfers between devices, swap_quad(): return lax.ppermute(value, ('space', 'tm'), pairs)  8.22 us
    pallas_call x2, Pallas kernels, add_quarters(): pl.pallas_call(functools.partial(gram_kernel, (n_time, quarter, modes, ro...  6.86 us
    pallas_call x1, Pallas kernels, project(): pl.pallas_call(projection_kernel, out_shape=(pltpu.VMEM((count, quarter),...  6.28 us
    ppermute x6, waiting for transfers between devices, swap(): return lax.ppermute(value, axis, [(i, i ^ bit) for i in range(count)])  5.35 us
    ppermute x6, starting transfers between devices, swap(): return lax.ppermute(value, axis, [(i, i ^ bit) for i in range(count)])  4.34 us
  transfers between devices with their start and end apart: 12, of which 8 were waited for; matrix products, arithmetic and copies ran while one was open for 0% of the time, Pallas kernels for 5%

profile of v13, /device:TPU:0, one launch (start us, length us, event | category | flops | bytes accessed | tf_op | source)
XLA Modules:
  0.0 40.7 jit_solution(2243149073467077846)
XLA Ops:
  0.6 6.3 %shard_map.41 = (f32[256,128]{1,0:T(8,128)S(1)}, f32[256,128]{1,0:T(8,128)S(1)}, f32[256,128]{1,0:T(8,128)S(1)}, f32[256,128]{1,0:T(8,128)S(1)}, f32[8,128]{1,0:T(8,128)S(1)}) custom-call(bf16[10240,256]{1,0:T(8,128)(2,1)} %modes_hbm.1, bf16[10240,512]{1,0:T(8,128)(2,1)} %snaps_hbm.1), custom_call_target="tpu_custom_call" | custom-call | flops 2684354560 | bytes 15728640 | tf_op jit(solution)/shard_map/pallas_call | solution.py:112
  7.0 0.1 pad_maximum_fusion.3
  7.0 4.0 %collective-permute-start = (f16[33,8,128]{2,1,0:T(8,128)(2,1)S(1)}, f16[33,8,128]{2,1,0:T(8,128)(2,1)S(1)}, u32[]{:S(2)}, u32[]{:S(2)}) collective-permute-start(f16[33,8,128]{2,1,0:T(8,128)(2,1)S(1)} %get-tuple-element.28), channel_id=1, source_target_pairs={{0,12},{1,13},{2,14},{3,15},{4,8},{5,9},{6,10},{7,11},{8,4},{9,5},... | collective-permute-start | bytes 202760 | tf_op jit(solution)/shard_map/ppermute | solution.py:37
  11.1 0.4 %collective-permute-start.1 = (f16[33,8,128]{2,1,0:T(8,128)(2,1)S(1)}, f16[33,8,128]{2,1,0:T(8,128)(2,1)S(1)}, u32[]{:S(2)}, u32[]{:S(2)}) collective-permute-start(f16[33,8,128]{2,1,0:T(8,128)(2,1)S(1)} %get-tuple-element.29), channel_id=1, source_target_pairs={{0,8},{1,5},{2,10},{3,7},{4,12},{5,1},{6,14},{7,3},{8,0},{9,13},{1... | collective-permute-start | bytes 202760 | tf_op jit(solution)/shard_map/ppermute | solution.py:37
  11.5 0.2 collective-permute-start.2
  11.7 1.6 %collective-permute-done = f16[33,8,128]{2,1,0:T(8,128)(2,1)S(1)} collective-permute-done((f16[33,8,128]{2,1,0:T(8,128)(2,1)S(1)}, f16[33,8,128]{2,1,0:T(8,128)(2,1)S(1)}, u32[]{:S(2)}, u32[]{:S(2)}) %collective-permute-start) | collective-permute-done | bytes 67616 | tf_op jit(solution)/shard_map/ppermute | solution.py:37
  13.4 2.0 %collective-permute-done.1 = f16[33,8,128]{2,1,0:T(8,128)(2,1)S(1)} collective-permute-done((f16[33,8,128]{2,1,0:T(8,128)(2,1)S(1)}, f16[33,8,128]{2,1,0:T(8,128)(2,1)S(1)}, u32[]{:S(2)}, u32[]{:S(2)}) %collective-permute-start.1) | collective-permute-done | bytes 67616 | tf_op jit(solution)/shard_map/ppermute | solution.py:37
  15.4 0.4 %collective-permute-done.2 = f16[33,8,128]{2,1,0:T(8,128)(2,1)S(1)} collective-permute-done((f16[33,8,128]{2,1,0:T(8,128)(2,1)S(1)}, f16[33,8,128]{2,1,0:T(8,128)(2,1)S(1)}, u32[]{:S(2)}, u32[]{:S(2)}) %collective-permute-start.2) | collective-permute-done | bytes 67616 | tf_op jit(solution)/shard_map/ppermute | solution.py:37
  15.9 0.1 fusion.4
  15.9 2.7 %collective-permute-start.3 = (f16[33,8,128]{2,1,0:T(8,128)(2,1)S(1)}, f16[33,8,128]{2,1,0:T(8,128)(2,1)S(1)}, u32[]{:S(2)}, u32[]{:S(2)}) collective-permute-start(f16[33,8,128]{2,1,0:T(8,128)(2,1)S(1)} %get-tuple-element.22), channel_id=1, source_target_pairs={{0,16},{4,20},{8,24},{12,28},{16,0},{20,4},{24,8},{28,12},{1,17},{... | collective-permute-start | bytes 202760 | tf_op jit(solution)/shard_map/ppermute | solution.py:27
  18.6 2.6 %collective-permute-done.3 = f16[33,8,128]{2,1,0:T(8,128)(2,1)S(1)} collective-permute-done((f16[33,8,128]{2,1,0:T(8,128)(2,1)S(1)}, f16[33,8,128]{2,1,0:T(8,128)(2,1)S(1)}, u32[]{:S(2)}, u32[]{:S(2)}) %collective-permute-start.3) | collective-permute-done | bytes 67616 | tf_op jit(solution)/shard_map/ppermute | solution.py:27
  21.3 1.6 %collective-permute-start.4 = (bf16[1,256,128]{2,1,0:T(8,128)(2,1)S(1)}, bf16[1,256,128]{2,1,0:T(8,128)(2,1)S(1)}, u32[]{:S(2)}, u32[]{:S(2)}) collective-permute-start(bf16[1,256,128]{2,1,0:T(8,128)(2,1)S(1)} %fusion.10), channel_id=1, source_target_pairs={{0,2},{1,3},{2,0},{3,1},{4,6},{5,7},{6,4},{7,5},{8,10},{9,11},{10,... | collective-permute-start | bytes 196616 | tf_op jit(solution)/shard_map/ppermute | solution.py:27
  22.8 2.7 %collective-permute-done.4 = bf16[1,256,128]{2,1,0:T(8,128)(2,1)S(1)} collective-permute-done((bf16[1,256,128]{2,1,0:T(8,128)(2,1)S(1)}, bf16[1,256,128]{2,1,0:T(8,128)(2,1)S(1)}, u32[]{:S(2)}, u32[]{:S(2)}) %collective-permute-start.4) | collective-permute-done | bytes 65568 | tf_op jit(solution)/shard_map/ppermute | solution.py:27
  25.6 1.8 %collective-permute-start.7 = (bf16[2,256,128]{2,1,0:T(8,128)(2,1)S(1)}, bf16[2,256,128]{2,1,0:T(8,128)(2,1)S(1)}, u32[]{:S(2)}, u32[]{:S(2)}) collective-permute-start(bf16[2,256,128]{2,1,0:T(8,128)(2,1)S(1)} %pad_maximum_fusion.refs_0_), channel_id=1, source_target_pairs={{0,4},{1,5},{2,6},{3,7},{4,0},{5,1},{6,2},{7,3},{8,12},{9,13},{10,... | collective-permute-start | bytes 393224 | tf_op jit(solution)/shard_map/ppermute | solution.py:37
  27.4 1.3 %collective-permute-start.6 = (bf16[2,256,128]{2,1,0:T(8,128)(2,1)S(1)}, bf16[2,256,128]{2,1,0:T(8,128)(2,1)S(1)}, u32[]{:S(2)}, u32[]{:S(2)}) collective-permute-start(bf16[2,256,128]{2,1,0:T(8,128)(2,1)S(1)} %pad_maximum_fusion.refs_0_), channel_id=1, source_target_pairs={{0,12},{1,9},{2,14},{3,11},{4,8},{5,13},{6,10},{7,15},{8,4},{9,1},... | collective-permute-start | bytes 393224 | tf_op jit(solution)/shard_map/ppermute | solution.py:37
  28.7 0.4 %collective-permute-start.5 = (bf16[2,256,128]{2,1,0:T(8,128)(2,1)S(1)}, bf16[2,256,128]{2,1,0:T(8,128)(2,1)S(1)}, u32[]{:S(2)}, u32[]{:S(2)}) collective-permute-start(bf16[2,256,128]{2,1,0:T(8,128)(2,1)S(1)} %pad_maximum_fusion.refs_0_), channel_id=1, source_target_pairs={{0,8},{1,13},{2,10},{3,15},{4,12},{5,9},{6,14},{7,11},{8,0},{9,5},... | collective-permute-start | bytes 393224 | tf_op jit(solution)/shard_map/ppermute | solution.py:37
  29.2 0.0 collective-permute-start.11
  29.2 3.0 %collective-permute-done.7.refs_2_ = bf16[2,256,128]{2,1,0:T(8,128)(2,1)S(1)} collective-permute-done((bf16[2,256,128]{2,1,0:T(8,128)(2,1)S(1)}, bf16[2,256,128]{2,1,0:T(8,128)(2,1)S(1)}, u32[]{:S(2)}, u32[]{:S(2)}) %collective-permute-start.7) | collective-permute-done | bytes 131104 | tf_op jit(solution)/shard_map/ppermute | solution.py:37
  32.2 0.0 collective-permute-start.10
  32.2 1.1 %collective-permute-done.6.refs_1_ = bf16[2,256,128]{2,1,0:T(8,128)(2,1)S(1)} collective-permute-done((bf16[2,256,128]{2,1,0:T(8,128)(2,1)S(1)}, bf16[2,256,128]{2,1,0:T(8,128)(2,1)S(1)}, u32[]{:S(2)}, u32[]{:S(2)}) %collective-permute-start.6) | collective-permute-done | bytes 131104 | tf_op jit(solution)/shard_map/ppermute | solution.py:37
  33.3 0.0 collective-permute-start.9
  33.3 0.4 %collective-permute-done.5.refs_0_ = bf16[2,256,128]{2,1,0:T(8,128)(2,1)S(1)} collective-permute-done((bf16[2,256,128]{2,1,0:T(8,128)(2,1)S(1)}, bf16[2,256,128]{2,1,0:T(8,128)(2,1)S(1)}, u32[]{:S(2)}, u32[]{:S(2)}) %collective-permute-start.5) | collective-permute-done | bytes 131104 | tf_op jit(solution)/shard_map/ppermute | solution.py:37
  33.7 0.1 collective-permute-start.8
  33.8 0.0 collective-permute-done.11.refs_1_
  33.8 1.9 %shard_map.42.refs_6_ = f32[1216,640]{1,0:T(8,128)S(1)} custom-call(bf16[2,256,128]{2,1,0:T(8,128)(2,1)S(1)} %pad_maximum_fusion.refs_0_, bf16[2,256,128]{2,1,0:T(8,128)(2,1)S(1)} %collective-permute-done.11.refs_1_), custom_call_target="tpu_custom_call" | custom-call | flops 7969177600 | bytes 3112960 | tf_op jit(solution)/shard_map/pallas_call | solution.py:309
  35.6 0.0 collective-permute-done.10.refs_5_
  35.7 0.0 collective-permute-done.9.refs_4_
  35.7 0.0 collective-permute-done.8.refs_3_
  35.7 5.0 %shard_map.43 = (f32[1216,608]{1,0:T(8,128)}, f32[32,1216]{1,0:T(8,128)}) custom-call(bf16[2,256,128]{2,1,0:T(8,128)(2,1)S(1)} %collective-permute-done.5.refs_0_, bf16[2,256,128]{2,1,0:T(8,128)(2,1)S(1)} %collective-permute-done.6.refs_1_, bf16[2,256,128]{2,1,0:T(8,128)(2,1)S(1)} %collective-permute-done.7.refs_2_, ...), custom_call_target="tpu_custom_call" | custom-call | flops 23907532800 | bytes 3112960 | tf_op jit(solution)/shard_map/pallas_call | solution.py:309
  (13 shorter events, 0.2 us)
Async XLA Ops:
  7.0 6.3 %collective-permute-start = (f16[33,8,128]{2,1,0:T(8,128)(2,1)S(1)}, f16[33,8,128]{2,1,0:T(8,128)(2,1)S(1)}, u32[]{:S(2)}, u32[]{:S(2)}) collective-permute-start(f16[33,8,128]{2,1,0:T(8,128)(2,1)S(1)} %get-tuple-element.28), channel_id=1, source_target_pairs={{0,12},{1,13},{2,14},{3,15},{4,8},{5,9},{6,10},{7,11},{8,4},{9,5},... | collective-permute-start | bytes 202760 | tf_op jit(solution)/shard_map/ppermute | solution.py:37
  11.1 4.3 %collective-permute-start.1 = (f16[33,8,128]{2,1,0:T(8,128)(2,1)S(1)}, f16[33,8,128]{2,1,0:T(8,128)(2,1)S(1)}, u32[]{:S(2)}, u32[]{:S(2)}) collective-permute-start(f16[33,8,128]{2,1,0:T(8,128)(2,1)S(1)} %get-tuple-element.29), channel_id=1, source_target_pairs={{0,8},{1,5},{2,10},{3,7},{4,12},{5,1},{6,14},{7,3},{8,0},{9,13},{1... | collective-permute-start | bytes 202760 | tf_op jit(solution)/shard_map/ppermute | solution.py:37
  11.5 4.3 %collective-permute-start.2 = (f16[33,8,128]{2,1,0:T(8,128)(2,1)S(1)}, f16[33,8,128]{2,1,0:T(8,128)(2,1)S(1)}, u32[]{:S(2)}, u32[]{:S(2)}) collective-permute-start(f16[33,8,128]{2,1,0:T(8,128)(2,1)S(1)} %get-tuple-element.30), channel_id=1, source_target_pairs={{0,4},{1,9},{2,6},{3,11},{4,0},{5,13},{6,2},{7,15},{8,12},{9,1},{1... | collective-permute-start | bytes 202760 | tf_op jit(solution)/shard_map/ppermute | solution.py:37
  15.9 5.3 %collective-permute-start.3 = (f16[33,8,128]{2,1,0:T(8,128)(2,1)S(1)}, f16[33,8,128]{2,1,0:T(8,128)(2,1)S(1)}, u32[]{:S(2)}, u32[]{:S(2)}) collective-permute-start(f16[33,8,128]{2,1,0:T(8,128)(2,1)S(1)} %get-tuple-element.22), channel_id=1, source_target_pairs={{0,16},{4,20},{8,24},{12,28},{16,0},{20,4},{24,8},{28,12},{1,17},{... | collective-permute-start | bytes 202760 | tf_op jit(solution)/shard_map/ppermute | solution.py:27
  21.3 4.3 %collective-permute-start.4 = (bf16[1,256,128]{2,1,0:T(8,128)(2,1)S(1)}, bf16[1,256,128]{2,1,0:T(8,128)(2,1)S(1)}, u32[]{:S(2)}, u32[]{:S(2)}) collective-permute-start(bf16[1,256,128]{2,1,0:T(8,128)(2,1)S(1)} %fusion.10), channel_id=1, source_target_pairs={{0,2},{1,3},{2,0},{3,1},{4,6},{5,7},{6,4},{7,5},{8,10},{9,11},{10,... | collective-permute-start | bytes 196616 | tf_op jit(solution)/shard_map/ppermute | solution.py:27
  25.6 6.6 %collective-permute-start.7 = (bf16[2,256,128]{2,1,0:T(8,128)(2,1)S(1)}, bf16[2,256,128]{2,1,0:T(8,128)(2,1)S(1)}, u32[]{:S(2)}, u32[]{:S(2)}) collective-permute-start(bf16[2,256,128]{2,1,0:T(8,128)(2,1)S(1)} %pad_maximum_fusion.refs_0_), channel_id=1, source_target_pairs={{0,4},{1,5},{2,6},{3,7},{4,0},{5,1},{6,2},{7,3},{8,12},{9,13},{10,... | collective-permute-start | bytes 393224 | tf_op jit(solution)/shard_map/ppermute | solution.py:37
  27.4 5.9 %collective-permute-start.6 = (bf16[2,256,128]{2,1,0:T(8,128)(2,1)S(1)}, bf16[2,256,128]{2,1,0:T(8,128)(2,1)S(1)}, u32[]{:S(2)}, u32[]{:S(2)}) collective-permute-start(bf16[2,256,128]{2,1,0:T(8,128)(2,1)S(1)} %pad_maximum_fusion.refs_0_), channel_id=1, source_target_pairs={{0,12},{1,9},{2,14},{3,11},{4,8},{5,13},{6,10},{7,15},{8,4},{9,1},... | collective-permute-start | bytes 393224 | tf_op jit(solution)/shard_map/ppermute | solution.py:37
  28.7 5.0 %collective-permute-start.5 = (bf16[2,256,128]{2,1,0:T(8,128)(2,1)S(1)}, bf16[2,256,128]{2,1,0:T(8,128)(2,1)S(1)}, u32[]{:S(2)}, u32[]{:S(2)}) collective-permute-start(bf16[2,256,128]{2,1,0:T(8,128)(2,1)S(1)} %pad_maximum_fusion.refs_0_), channel_id=1, source_target_pairs={{0,8},{1,13},{2,10},{3,15},{4,12},{5,9},{6,14},{7,11},{8,0},{9,5},... | collective-permute-start | bytes 393224 | tf_op jit(solution)/shard_map/ppermute | solution.py:37
  29.2 4.6 %collective-permute-start.11 = (bf16[2,256,128]{2,1,0:T(8,128)(2,1)S(1)}, bf16[2,256,128]{2,1,0:T(8,128)(2,1)S(1)}, u32[]{:S(2)}, u32[]{:S(2)}) collective-permute-start(bf16[2,256,128]{2,1,0:T(8,128)(2,1)S(1)} %pad_maximum_fusion.refs_0_), channel_id=1, source_target_pairs={{0,1},{1,0},{2,3},{3,2},{4,5},{5,4},{6,7},{7,6},{8,9},{9,8},{10,11... | collective-permute-start | bytes 393224 | tf_op jit(solution)/shard_map/ppermute | solution.py:27
  32.2 3.5 %collective-permute-start.10 = (bf16[2,256,128]{2,1,0:T(8,128)(2,1)S(1)}, bf16[2,256,128]{2,1,0:T(8,128)(2,1)S(1)}, u32[]{:S(2)}, u32[]{:S(2)}) collective-permute-start(bf16[2,256,128]{2,1,0:T(8,128)(2,1)S(1)} %collective-permute-done.7.refs_2_), channel_id=1, source_target_pairs={{0,1},{1,0},{2,3},{3,2},{4,5},{5,4},{6,7},{7,6},{8,9},{9,8},{10,11... | collective-permute-start | bytes 393224 | tf_op jit(solution)/shard_map/ppermute | solution.py:27
  33.3 2.4 %collective-permute-start.9 = (bf16[2,256,128]{2,1,0:T(8,128)(2,1)S(1)}, bf16[2,256,128]{2,1,0:T(8,128)(2,1)S(1)}, u32[]{:S(2)}, u32[]{:S(2)}) collective-permute-start(bf16[2,256,128]{2,1,0:T(8,128)(2,1)S(1)} %collective-permute-done.6.refs_1_), channel_id=1, source_target_pairs={{0,1},{1,0},{2,3},{3,2},{4,5},{5,4},{6,7},{7,6},{8,9},{9,8},{10,11... | collective-permute-start | bytes 393224 | tf_op jit(solution)/shard_map/ppermute | solution.py:27
  33.7 2.0 %collective-permute-start.8 = (bf16[2,256,128]{2,1,0:T(8,128)(2,1)S(1)}, bf16[2,256,128]{2,1,0:T(8,128)(2,1)S(1)}, u32[]{:S(2)}, u32[]{:S(2)}) collective-permute-start(bf16[2,256,128]{2,1,0:T(8,128)(2,1)S(1)} %collective-permute-done.5.refs_0_), channel_id=1, source_target_pairs={{0,1},{1,0},{2,3},{3,2},{4,5},{5,4},{6,7},{7,6},{8,9},{9,8},{10,11... | collective-permute-start | bytes 393224 | tf_op jit(solution)/shard_map/ppermute | solution.py:27

commit v14 on v13

--- a/solution.py
+++ b/solution.py
@@ -11,9 +11,9 @@
 RIDGE_WEIGHT = 0.05
 ROW_TILE = 16
 QUAD = 4
-SUM_PARTNERS = ((0, 3, 2, 1), (0, 3, 1, 2))
+SUM_PARTNERS = ((0, 3, 2, 1), (0, 3, 2, 1))
 GATHER_PARTNERS = ((0, 2, 3, 1), (0, 3, 2, 1))
-PROJECTION_STEPS = 10
+PROJECTION_STEPS = 16
 EXPONENT_ROWS = 8
 TOP = 9.0
 SMALLEST = 1e-30

time: 40.8 us -> 40.7 us (level)
  no operation moved by 1% of the time
where the time goes in v14:
time: 40.7 us; the launch traced here: 40.6 us
  waiting for transfers between devices  13.9 us (34%)
  Pallas kernels  13.2 us (32%)
  starting transfers between devices  12.5 us (31%)
  between operations  0.75 us (2%)
    ppermute x6, waiting for transfers between devices, swap_quad(): return lax.ppermute(value, ('space', 'tm'), pairs)  8.57 us
    ppermute x6, starting transfers between devices, swap_quad(): return lax.ppermute(value, ('space', 'tm'), pairs)  8.22 us
    pallas_call x2, Pallas kernels, add_quarters(): pl.pallas_call(functools.partial(gram_kernel, (n_time, quarter, modes, ro...  6.87 us
    pallas_call x1, Pallas kernels, project(): pl.pallas_call(projection_kernel, out_shape=(pltpu.VMEM((count, quarter),...  6.29 us
    ppermute x6, waiting for transfers between devices, swap(): return lax.ppermute(value, axis, [(i, i ^ bit) for i in range(count)])  5.35 us
    ppermute x6, starting transfers between devices, swap(): return lax.ppermute(value, axis, [(i, i ^ bit) for i in range(count)])  4.25 us
  transfers between devices with their start and end apart: 12, of which 8 were waited for; matrix products, arithmetic and copies ran while one was open for 0% of the time, Pallas kernels for 5%

profile of v14, /device:TPU:0, one launch (start us, length us, event | category | flops | bytes accessed | tf_op | source)
XLA Modules:
  0.0 40.6 jit_solution(12045449290301383253)
XLA Ops:
  0.6 6.3 %shard_map.41 = (f32[256,128]{1,0:T(8,128)S(1)}, f32[256,128]{1,0:T(8,128)S(1)}, f32[256,128]{1,0:T(8,128)S(1)}, f32[256,128]{1,0:T(8,128)S(1)}, f32[8,128]{1,0:T(8,128)S(1)}) custom-call(bf16[10240,256]{1,0:T(8,128)(2,1)} %modes_hbm.1, bf16[10240,512]{1,0:T(8,128)(2,1)} %snaps_hbm.1), custom_call_target="tpu_custom_call" | custom-call | flops 2684354560 | bytes 15728640 | tf_op jit(solution)/shard_map/pallas_call | solution.py:112
  7.0 0.1 pad_maximum_fusion.3
  7.1 4.0 %collective-permute-start = (f16[33,8,128]{2,1,0:T(8,128)(2,1)S(1)}, f16[33,8,128]{2,1,0:T(8,128)(2,1)S(1)}, u32[]{:S(2)}, u32[]{:S(2)}) collective-permute-start(f16[33,8,128]{2,1,0:T(8,128)(2,1)S(1)} %get-tuple-element.28), channel_id=1, source_target_pairs={{0,12},{1,13},{2,14},{3,15},{4,8},{5,9},{6,10},{7,11},{8,4},{9,5},... | collective-permute-start | bytes 202760 | tf_op jit(solution)/shard_map/ppermute | solution.py:37
  11.1 0.4 %collective-permute-start.1 = (f16[33,8,128]{2,1,0:T(8,128)(2,1)S(1)}, f16[33,8,128]{2,1,0:T(8,128)(2,1)S(1)}, u32[]{:S(2)}, u32[]{:S(2)}) collective-permute-start(f16[33,8,128]{2,1,0:T(8,128)(2,1)S(1)} %get-tuple-element.29), channel_id=1, source_target_pairs={{0,8},{1,9},{2,10},{3,11},{4,12},{5,13},{6,14},{7,15},{8,0},{9,1},... | collective-permute-start | bytes 202760 | tf_op jit(solution)/shard_map/ppermute | solution.py:37
  11.5 0.2 collective-permute-start.2
  11.7 1.8 %collective-permute-done = f16[33,8,128]{2,1,0:T(8,128)(2,1)S(1)} collective-permute-done((f16[33,8,128]{2,1,0:T(8,128)(2,1)S(1)}, f16[33,8,128]{2,1,0:T(8,128)(2,1)S(1)}, u32[]{:S(2)}, u32[]{:S(2)}) %collective-permute-start) | collective-permute-done | bytes 67616 | tf_op jit(solution)/shard_map/ppermute | solution.py:37
  13.6 1.8 %collective-permute-done.1 = f16[33,8,128]{2,1,0:T(8,128)(2,1)S(1)} collective-permute-done((f16[33,8,128]{2,1,0:T(8,128)(2,1)S(1)}, f16[33,8,128]{2,1,0:T(8,128)(2,1)S(1)}, u32[]{:S(2)}, u32[]{:S(2)}) %collective-permute-start.1) | collective-permute-done | bytes 67616 | tf_op jit(solution)/shard_map/ppermute | solution.py:37
  15.4 0.4 %collective-permute-done.2 = f16[33,8,128]{2,1,0:T(8,128)(2,1)S(1)} collective-permute-done((f16[33,8,128]{2,1,0:T(8,128)(2,1)S(1)}, f16[33,8,128]{2,1,0:T(8,128)(2,1)S(1)}, u32[]{:S(2)}, u32[]{:S(2)}) %collective-permute-start.2) | collective-permute-done | bytes 67616 | tf_op jit(solution)/shard_map/ppermute | solution.py:37
  15.9 0.1 fusion.4
  15.9 2.7 %collective-permute-start.3 = (f16[33,8,128]{2,1,0:T(8,128)(2,1)S(1)}, f16[33,8,128]{2,1,0:T(8,128)(2,1)S(1)}, u32[]{:S(2)}, u32[]{:S(2)}) collective-permute-start(f16[33,8,128]{2,1,0:T(8,128)(2,1)S(1)} %get-tuple-element.22), channel_id=1, source_target_pairs={{0,16},{4,20},{8,24},{12,28},{16,0},{20,4},{24,8},{28,12},{1,17},{... | collective-permute-start | bytes 202760 | tf_op jit(solution)/shard_map/ppermute | solution.py:27
  18.6 2.6 %collective-permute-done.3 = f16[33,8,128]{2,1,0:T(8,128)(2,1)S(1)} collective-permute-done((f16[33,8,128]{2,1,0:T(8,128)(2,1)S(1)}, f16[33,8,128]{2,1,0:T(8,128)(2,1)S(1)}, u32[]{:S(2)}, u32[]{:S(2)}) %collective-permute-start.3) | collective-permute-done | bytes 67616 | tf_op jit(solution)/shard_map/ppermute | solution.py:27
  21.3 1.6 %collective-permute-start.4 = (bf16[1,256,128]{2,1,0:T(8,128)(2,1)S(1)}, bf16[1,256,128]{2,1,0:T(8,128)(2,1)S(1)}, u32[]{:S(2)}, u32[]{:S(2)}) collective-permute-start(bf16[1,256,128]{2,1,0:T(8,128)(2,1)S(1)} %fusion.10), channel_id=1, source_target_pairs={{0,2},{1,3},{2,0},{3,1},{4,6},{5,7},{6,4},{7,5},{8,10},{9,11},{10,... | collective-permute-start | bytes 196616 | tf_op jit(solution)/shard_map/ppermute | solution.py:27
  22.8 2.7 %collective-permute-done.4 = bf16[1,256,128]{2,1,0:T(8,128)(2,1)S(1)} collective-permute-done((bf16[1,256,128]{2,1,0:T(8,128)(2,1)S(1)}, bf16[1,256,128]{2,1,0:T(8,128)(2,1)S(1)}, u32[]{:S(2)}, u32[]{:S(2)}) %collective-permute-start.4) | collective-permute-done | bytes 65568 | tf_op jit(solution)/shard_map/ppermute | solution.py:27
  25.6 0.5 %collective-permute-start.7 = (bf16[2,256,128]{2,1,0:T(8,128)(2,1)S(1)}, bf16[2,256,128]{2,1,0:T(8,128)(2,1)S(1)}, u32[]{:S(2)}, u32[]{:S(2)}) collective-permute-start(bf16[2,256,128]{2,1,0:T(8,128)(2,1)S(1)} %pad_maximum_fusion.refs_0_), channel_id=1, source_target_pairs={{0,4},{1,5},{2,6},{3,7},{4,0},{5,1},{6,2},{7,3},{8,12},{9,13},{10,... | collective-permute-start | bytes 393224 | tf_op jit(solution)/shard_map/ppermute | solution.py:37
  26.1 2.6 %collective-permute-start.6 = (bf16[2,256,128]{2,1,0:T(8,128)(2,1)S(1)}, bf16[2,256,128]{2,1,0:T(8,128)(2,1)S(1)}, u32[]{:S(2)}, u32[]{:S(2)}) collective-permute-start(bf16[2,256,128]{2,1,0:T(8,128)(2,1)S(1)} %pad_maximum_fusion.refs_0_), channel_id=1, source_target_pairs={{0,12},{1,9},{2,14},{3,11},{4,8},{5,13},{6,10},{7,15},{8,4},{9,1},... | collective-permute-start | bytes 393224 | tf_op jit(solution)/shard_map/ppermute | solution.py:37
  28.7 0.4 %collective-permute-start.5 = (bf16[2,256,128]{2,1,0:T(8,128)(2,1)S(1)}, bf16[2,256,128]{2,1,0:T(8,128)(2,1)S(1)}, u32[]{:S(2)}, u32[]{:S(2)}) collective-permute-start(bf16[2,256,128]{2,1,0:T(8,128)(2,1)S(1)} %pad_maximum_fusion.refs_0_), channel_id=1, source_target_pairs={{0,8},{1,13},{2,10},{3,15},{4,12},{5,9},{6,14},{7,11},{8,0},{9,5},... | collective-permute-start | bytes 393224 | tf_op jit(solution)/shard_map/ppermute | solution.py:37
  29.2 0.0 collective-permute-start.11
  29.2 1.5 %collective-permute-done.7.refs_2_ = bf16[2,256,128]{2,1,0:T(8,128)(2,1)S(1)} collective-permute-done((bf16[2,256,128]{2,1,0:T(8,128)(2,1)S(1)}, bf16[2,256,128]{2,1,0:T(8,128)(2,1)S(1)}, u32[]{:S(2)}, u32[]{:S(2)}) %collective-permute-start.7) | collective-permute-done | bytes 131104 | tf_op jit(solution)/shard_map/ppermute | solution.py:37
  30.7 0.0 collective-permute-start.10
  30.7 1.4 %collective-permute-done.6.refs_1_ = bf16[2,256,128]{2,1,0:T(8,128)(2,1)S(1)} collective-permute-done((bf16[2,256,128]{2,1,0:T(8,128)(2,1)S(1)}, bf16[2,256,128]{2,1,0:T(8,128)(2,1)S(1)}, u32[]{:S(2)}, u32[]{:S(2)}) %collective-permute-start.6) | collective-permute-done | bytes 131104 | tf_op jit(solution)/shard_map/ppermute | solution.py:37
  32.0 0.0 collective-permute-start.9
  32.0 1.6 %collective-permute-done.5.refs_0_ = bf16[2,256,128]{2,1,0:T(8,128)(2,1)S(1)} collective-permute-done((bf16[2,256,128]{2,1,0:T(8,128)(2,1)S(1)}, bf16[2,256,128]{2,1,0:T(8,128)(2,1)S(1)}, u32[]{:S(2)}, u32[]{:S(2)}) %collective-permute-start.5) | collective-permute-done | bytes 131104 | tf_op jit(solution)/shard_map/ppermute | solution.py:37
  33.7 0.0 collective-permute-start.8
  33.7 0.0 collective-permute-done.11.refs_1_
  33.7 1.9 %shard_map.42.refs_6_ = f32[1216,640]{1,0:T(8,128)S(1)} custom-call(bf16[2,256,128]{2,1,0:T(8,128)(2,1)S(1)} %pad_maximum_fusion.refs_0_, bf16[2,256,128]{2,1,0:T(8,128)(2,1)S(1)} %collective-permute-done.11.refs_1_), custom_call_target="tpu_custom_call" | custom-call | flops 7969177600 | bytes 3112960 | tf_op jit(solution)/shard_map/pallas_call | solution.py:309
  35.6 0.0 collective-permute-done.10.refs_5_
  35.6 0.0 collective-permute-done.9.refs_4_
  35.6 0.0 collective-permute-done.8.refs_3_
  35.6 5.0 %shard_map.43 = (f32[1216,608]{1,0:T(8,128)}, f32[32,1216]{1,0:T(8,128)}) custom-call(bf16[2,256,128]{2,1,0:T(8,128)(2,1)S(1)} %collective-permute-done.5.refs_0_, bf16[2,256,128]{2,1,0:T(8,128)(2,1)S(1)} %collective-permute-done.6.refs_1_, bf16[2,256,128]{2,1,0:T(8,128)(2,1)S(1)} %collective-permute-done.7.refs_2_, ...), custom_call_target="tpu_custom_call" | custom-call | flops 23907532800 | bytes 3112960 | tf_op jit(solution)/shard_map/pallas_call | solution.py:309
  (13 shorter events, 0.2 us)
Async XLA Ops:
  7.1 6.5 %collective-permute-start = (f16[33,8,128]{2,1,0:T(8,128)(2,1)S(1)}, f16[33,8,128]{2,1,0:T(8,128)(2,1)S(1)}, u32[]{:S(2)}, u32[]{:S(2)}) collective-permute-start(f16[33,8,128]{2,1,0:T(8,128)(2,1)S(1)} %get-tuple-element.28), channel_id=1, source_target_pairs={{0,12},{1,13},{2,14},{3,15},{4,8},{5,9},{6,10},{7,11},{8,4},{9,5},... | collective-permute-start | bytes 202760 | tf_op jit(solution)/shard_map/ppermute | solution.py:37
  11.1 4.3 %collective-permute-start.1 = (f16[33,8,128]{2,1,0:T(8,128)(2,1)S(1)}, f16[33,8,128]{2,1,0:T(8,128)(2,1)S(1)}, u32[]{:S(2)}, u32[]{:S(2)}) collective-permute-start(f16[33,8,128]{2,1,0:T(8,128)(2,1)S(1)} %get-tuple-element.29), channel_id=1, source_target_pairs={{0,8},{1,9},{2,10},{3,11},{4,12},{5,13},{6,14},{7,15},{8,0},{9,1},... | collective-permute-start | bytes 202760 | tf_op jit(solution)/shard_map/ppermute | solution.py:37
  11.5 4.3 %collective-permute-start.2 = (f16[33,8,128]{2,1,0:T(8,128)(2,1)S(1)}, f16[33,8,128]{2,1,0:T(8,128)(2,1)S(1)}, u32[]{:S(2)}, u32[]{:S(2)}) collective-permute-start(f16[33,8,128]{2,1,0:T(8,128)(2,1)S(1)} %get-tuple-element.30), channel_id=1, source_target_pairs={{0,4},{1,5},{2,6},{3,7},{4,0},{5,1},{6,2},{7,3},{8,12},{9,13},{10,... | collective-permute-start | bytes 202760 | tf_op jit(solution)/shard_map/ppermute | solution.py:37
  15.9 5.3 %collective-permute-start.3 = (f16[33,8,128]{2,1,0:T(8,128)(2,1)S(1)}, f16[33,8,128]{2,1,0:T(8,128)(2,1)S(1)}, u32[]{:S(2)}, u32[]{:S(2)}) collective-permute-start(f16[33,8,128]{2,1,0:T(8,128)(2,1)S(1)} %get-tuple-element.22), channel_id=1, source_target_pairs={{0,16},{4,20},{8,24},{12,28},{16,0},{20,4},{24,8},{28,12},{1,17},{... | collective-permute-start | bytes 202760 | tf_op jit(solution)/shard_map/ppermute | solution.py:27
  21.3 4.3 %collective-permute-start.4 = (bf16[1,256,128]{2,1,0:T(8,128)(2,1)S(1)}, bf16[1,256,128]{2,1,0:T(8,128)(2,1)S(1)}, u32[]{:S(2)}, u32[]{:S(2)}) collective-permute-start(bf16[1,256,128]{2,1,0:T(8,128)(2,1)S(1)} %fusion.10), channel_id=1, source_target_pairs={{0,2},{1,3},{2,0},{3,1},{4,6},{5,7},{6,4},{7,5},{8,10},{9,11},{10,... | collective-permute-start | bytes 196616 | tf_op jit(solution)/shard_map/ppermute | solution.py:27
  25.6 5.0 %collective-permute-start.7 = (bf16[2,256,128]{2,1,0:T(8,128)(2,1)S(1)}, bf16[2,256,128]{2,1,0:T(8,128)(2,1)S(1)}, u32[]{:S(2)}, u32[]{:S(2)}) collective-permute-start(bf16[2,256,128]{2,1,0:T(8,128)(2,1)S(1)} %pad_maximum_fusion.refs_0_), channel_id=1, source_target_pairs={{0,4},{1,5},{2,6},{3,7},{4,0},{5,1},{6,2},{7,3},{8,12},{9,13},{10,... | collective-permute-start | bytes 393224 | tf_op jit(solution)/shard_map/ppermute | solution.py:37
  26.1 5.9 %collective-permute-start.6 = (bf16[2,256,128]{2,1,0:T(8,128)(2,1)S(1)}, bf16[2,256,128]{2,1,0:T(8,128)(2,1)S(1)}, u32[]{:S(2)}, u32[]{:S(2)}) collective-permute-start(bf16[2,256,128]{2,1,0:T(8,128)(2,1)S(1)} %pad_maximum_fusion.refs_0_), channel_id=1, source_target_pairs={{0,12},{1,9},{2,14},{3,11},{4,8},{5,13},{6,10},{7,15},{8,4},{9,1},... | collective-permute-start | bytes 393224 | tf_op jit(solution)/shard_map/ppermute | solution.py:37
  28.7 5.0 %collective-permute-start.5 = (bf16[2,256,128]{2,1,0:T(8,128)(2,1)S(1)}, bf16[2,256,128]{2,1,0:T(8,128)(2,1)S(1)}, u32[]{:S(2)}, u32[]{:S(2)}) collective-permute-start(bf16[2,256,128]{2,1,0:T(8,128)(2,1)S(1)} %pad_maximum_fusion.refs_0_), channel_id=1, source_target_pairs={{0,8},{1,13},{2,10},{3,15},{4,12},{5,9},{6,14},{7,11},{8,0},{9,5},... | collective-permute-start | bytes 393224 | tf_op jit(solution)/shard_map/ppermute | solution.py:37
  29.2 4.5 %collective-permute-start.11 = (bf16[2,256,128]{2,1,0:T(8,128)(2,1)S(1)}, bf16[2,256,128]{2,1,0:T(8,128)(2,1)S(1)}, u32[]{:S(2)}, u32[]{:S(2)}) collective-permute-start(bf16[2,256,128]{2,1,0:T(8,128)(2,1)S(1)} %pad_maximum_fusion.refs_0_), channel_id=1, source_target_pairs={{0,1},{1,0},{2,3},{3,2},{4,5},{5,4},{6,7},{7,6},{8,9},{9,8},{10,11... | collective-permute-start | bytes 393224 | tf_op jit(solution)/shard_map/ppermute | solution.py:27
  30.7 4.9 %collective-permute-start.10 = (bf16[2,256,128]{2,1,0:T(8,128)(2,1)S(1)}, bf16[2,256,128]{2,1,0:T(8,128)(2,1)S(1)}, u32[]{:S(2)}, u32[]{:S(2)}) collective-permute-start(bf16[2,256,128]{2,1,0:T(8,128)(2,1)S(1)} %collective-permute-done.7.refs_2_), channel_id=1, source_target_pairs={{0,1},{1,0},{2,3},{3,2},{4,5},{5,4},{6,7},{7,6},{8,9},{9,8},{10,11... | collective-permute-start | bytes 393224 | tf_op jit(solution)/shard_map/ppermute | solution.py:27
  32.0 3.5 %collective-permute-start.9 = (bf16[2,256,128]{2,1,0:T(8,128)(2,1)S(1)}, bf16[2,256,128]{2,1,0:T(8,128)(2,1)S(1)}, u32[]{:S(2)}, u32[]{:S(2)}) collective-permute-start(bf16[2,256,128]{2,1,0:T(8,128)(2,1)S(1)} %collective-permute-done.6.refs_1_), channel_id=1, source_target_pairs={{0,1},{1,0},{2,3},{3,2},{4,5},{5,4},{6,7},{7,6},{8,9},{9,8},{10,11... | collective-permute-start | bytes 393224 | tf_op jit(solution)/shard_map/ppermute | solution.py:27
  33.7 1.9 %collective-permute-start.8 = (bf16[2,256,128]{2,1,0:T(8,128)(2,1)S(1)}, bf16[2,256,128]{2,1,0:T(8,128)(2,1)S(1)}, u32[]{:S(2)}, u32[]{:S(2)}) collective-permute-start(bf16[2,256,128]{2,1,0:T(8,128)(2,1)S(1)} %collective-permute-done.5.refs_0_), channel_id=1, source_target_pairs={{0,1},{1,0},{2,3},{3,2},{4,5},{5,4},{6,7},{7,6},{8,9},{9,8},{10,11... | collective-permute-start | bytes 393224 | tf_op jit(solution)/shard_map/ppermute | solution.py:27

commit v15 on v14

--- a/solution.py
+++ b/solution.py
@@ -12,7 +12,7 @@
 ROW_TILE = 16
 QUAD = 4
 SUM_PARTNERS = ((0, 3, 2, 1), (0, 3, 2, 1))
-GATHER_PARTNERS = ((0, 2, 3, 1), (0, 3, 2, 1))
+GATHER_PARTNERS = ((0, 2, 3, 1), (0, 2, 3, 1))
 PROJECTION_STEPS = 16
 EXPONENT_ROWS = 8
 TOP = 9.0

time: 40.7 us -> 40.7 us (level)
  no operation moved by 1% of the time
where the time goes in v15:
time: 40.7 us; the launch traced here: 40.6 us
  waiting for transfers between devices  13.9 us (34%)
  Pallas kernels  13.2 us (32%)
  starting transfers between devices  12.5 us (31%)
  between operations  0.75 us (2%)
    ppermute x6, waiting for transfers between devices, swap_quad(): return lax.ppermute(value, ('space', 'tm'), pairs)  8.57 us
    ppermute x6, starting transfers between devices, swap_quad(): return lax.ppermute(value, ('space', 'tm'), pairs)  8.22 us
    pallas_call x2, Pallas kernels, add_quarters(): pl.pallas_call(functools.partial(gram_kernel, (n_time, quarter, modes, ro...  6.87 us
    pallas_call x1, Pallas kernels, project(): pl.pallas_call(projection_kernel, out_shape=(pltpu.VMEM((count, quarter),...  6.29 us
    ppermute x6, waiting for transfers between devices, swap(): return lax.ppermute(value, axis, [(i, i ^ bit) for i in range(count)])  5.35 us
    ppermute x6, starting transfers between devices, swap(): return lax.ppermute(value, axis, [(i, i ^ bit) for i in range(count)])  4.25 us
  transfers between devices with their start and end apart: 12, of which 8 were waited for; matrix products, arithmetic and copies ran while one was open for 0% of the time, Pallas kernels for 5%

profile of v15, /device:TPU:0, one launch (start us, length us, event | category | flops | bytes accessed | tf_op | source)
XLA Modules:
  0.0 40.6 jit_solution(11259901755384415252)
XLA Ops:
  0.6 6.3 %shard_map.41 = (f32[256,128]{1,0:T(8,128)S(1)}, f32[256,128]{1,0:T(8,128)S(1)}, f32[256,128]{1,0:T(8,128)S(1)}, f32[256,128]{1,0:T(8,128)S(1)}, f32[8,128]{1,0:T(8,128)S(1)}) custom-call(bf16[10240,256]{1,0:T(8,128)(2,1)} %modes_hbm.1, bf16[10240,512]{1,0:T(8,128)(2,1)} %snaps_hbm.1), custom_call_target="tpu_custom_call" | custom-call | flops 2684354560 | bytes 15728640 | tf_op jit(solution)/shard_map/pallas_call | solution.py:112
  7.0 0.1 pad_maximum_fusion.3
  7.1 4.0 %collective-permute-start = (f16[33,8,128]{2,1,0:T(8,128)(2,1)S(1)}, f16[33,8,128]{2,1,0:T(8,128)(2,1)S(1)}, u32[]{:S(2)}, u32[]{:S(2)}) collective-permute-start(f16[33,8,128]{2,1,0:T(8,128)(2,1)S(1)} %get-tuple-element.28), channel_id=1, source_target_pairs={{0,12},{1,13},{2,14},{3,15},{4,8},{5,9},{6,10},{7,11},{8,4},{9,5},... | collective-permute-start | bytes 202760 | tf_op jit(solution)/shard_map/ppermute | solution.py:37
  11.1 0.4 %collective-permute-start.1 = (f16[33,8,128]{2,1,0:T(8,128)(2,1)S(1)}, f16[33,8,128]{2,1,0:T(8,128)(2,1)S(1)}, u32[]{:S(2)}, u32[]{:S(2)}) collective-permute-start(f16[33,8,128]{2,1,0:T(8,128)(2,1)S(1)} %get-tuple-element.29), channel_id=1, source_target_pairs={{0,8},{1,9},{2,10},{3,11},{4,12},{5,13},{6,14},{7,15},{8,0},{9,1},... | collective-permute-start | bytes 202760 | tf_op jit(solution)/shard_map/ppermute | solution.py:37
  11.5 0.2 collective-permute-start.2
  11.7 1.8 %collective-permute-done = f16[33,8,128]{2,1,0:T(8,128)(2,1)S(1)} collective-permute-done((f16[33,8,128]{2,1,0:T(8,128)(2,1)S(1)}, f16[33,8,128]{2,1,0:T(8,128)(2,1)S(1)}, u32[]{:S(2)}, u32[]{:S(2)}) %collective-permute-start) | collective-permute-done | bytes 67616 | tf_op jit(solution)/shard_map/ppermute | solution.py:37
  13.6 1.8 %collective-permute-done.1 = f16[33,8,128]{2,1,0:T(8,128)(2,1)S(1)} collective-permute-done((f16[33,8,128]{2,1,0:T(8,128)(2,1)S(1)}, f16[33,8,128]{2,1,0:T(8,128)(2,1)S(1)}, u32[]{:S(2)}, u32[]{:S(2)}) %collective-permute-start.1) | collective-permute-done | bytes 67616 | tf_op jit(solution)/shard_map/ppermute | solution.py:37
  15.4 0.4 %collective-permute-done.2 = f16[33,8,128]{2,1,0:T(8,128)(2,1)S(1)} collective-permute-done((f16[33,8,128]{2,1,0:T(8,128)(2,1)S(1)}, f16[33,8,128]{2,1,0:T(8,128)(2,1)S(1)}, u32[]{:S(2)}, u32[]{:S(2)}) %collective-permute-start.2) | collective-permute-done | bytes 67616 | tf_op jit(solution)/shard_map/ppermute | solution.py:37
  15.9 0.1 fusion.4
  15.9 2.7 %collective-permute-start.3 = (f16[33,8,128]{2,1,0:T(8,128)(2,1)S(1)}, f16[33,8,128]{2,1,0:T(8,128)(2,1)S(1)}, u32[]{:S(2)}, u32[]{:S(2)}) collective-permute-start(f16[33,8,128]{2,1,0:T(8,128)(2,1)S(1)} %get-tuple-element.22), channel_id=1, source_target_pairs={{0,16},{4,20},{8,24},{12,28},{16,0},{20,4},{24,8},{28,12},{1,17},{... | collective-permute-start | bytes 202760 | tf_op jit(solution)/shard_map/ppermute | solution.py:27
  18.6 2.6 %collective-permute-done.3 = f16[33,8,128]{2,1,0:T(8,128)(2,1)S(1)} collective-permute-done((f16[33,8,128]{2,1,0:T(8,128)(2,1)S(1)}, f16[33,8,128]{2,1,0:T(8,128)(2,1)S(1)}, u32[]{:S(2)}, u32[]{:S(2)}) %collective-permute-start.3) | collective-permute-done | bytes 67616 | tf_op jit(solution)/shard_map/ppermute | solution.py:27
  21.3 1.6 %collective-permute-start.4 = (bf16[1,256,128]{2,1,0:T(8,128)(2,1)S(1)}, bf16[1,256,128]{2,1,0:T(8,128)(2,1)S(1)}, u32[]{:S(2)}, u32[]{:S(2)}) collective-permute-start(bf16[1,256,128]{2,1,0:T(8,128)(2,1)S(1)} %fusion.10), channel_id=1, source_target_pairs={{0,2},{1,3},{2,0},{3,1},{4,6},{5,7},{6,4},{7,5},{8,10},{9,11},{10,... | collective-permute-start | bytes 196616 | tf_op jit(solution)/shard_map/ppermute | solution.py:27
  22.8 2.7 %collective-permute-done.4 = bf16[1,256,128]{2,1,0:T(8,128)(2,1)S(1)} collective-permute-done((bf16[1,256,128]{2,1,0:T(8,128)(2,1)S(1)}, bf16[1,256,128]{2,1,0:T(8,128)(2,1)S(1)}, u32[]{:S(2)}, u32[]{:S(2)}) %collective-permute-start.4) | collective-permute-done | bytes 65568 | tf_op jit(solution)/shard_map/ppermute | solution.py:27
  25.6 0.5 %collective-permute-start.7 = (bf16[2,256,128]{2,1,0:T(8,128)(2,1)S(1)}, bf16[2,256,128]{2,1,0:T(8,128)(2,1)S(1)}, u32[]{:S(2)}, u32[]{:S(2)}) collective-permute-start(bf16[2,256,128]{2,1,0:T(8,128)(2,1)S(1)} %pad_maximum_fusion.refs_0_), channel_id=1, source_target_pairs={{0,4},{1,5},{2,6},{3,7},{4,0},{5,1},{6,2},{7,3},{8,12},{9,13},{10,... | collective-permute-start | bytes 393224 | tf_op jit(solution)/shard_map/ppermute | solution.py:37
  26.1 2.6 %collective-permute-start.6 = (bf16[2,256,128]{2,1,0:T(8,128)(2,1)S(1)}, bf16[2,256,128]{2,1,0:T(8,128)(2,1)S(1)}, u32[]{:S(2)}, u32[]{:S(2)}) collective-permute-start(bf16[2,256,128]{2,1,0:T(8,128)(2,1)S(1)} %pad_maximum_fusion.refs_0_), channel_id=1, source_target_pairs={{0,12},{1,13},{2,14},{3,15},{4,8},{5,9},{6,10},{7,11},{8,4},{9,5},... | collective-permute-start | bytes 393224 | tf_op jit(solution)/shard_map/ppermute | solution.py:37
  28.7 0.4 %collective-permute-start.5 = (bf16[2,256,128]{2,1,0:T(8,128)(2,1)S(1)}, bf16[2,256,128]{2,1,0:T(8,128)(2,1)S(1)}, u32[]{:S(2)}, u32[]{:S(2)}) collective-permute-start(bf16[2,256,128]{2,1,0:T(8,128)(2,1)S(1)} %pad_maximum_fusion.refs_0_), channel_id=1, source_target_pairs={{0,8},{1,9},{2,10},{3,11},{4,12},{5,13},{6,14},{7,15},{8,0},{9,1},... | collective-permute-start | bytes 393224 | tf_op jit(solution)/shard_map/ppermute | solution.py:37
  29.2 0.0 collective-permute-start.11
  29.2 1.5 %collective-permute-done.7.refs_2_ = bf16[2,256,128]{2,1,0:T(8,128)(2,1)S(1)} collective-permute-done((bf16[2,256,128]{2,1,0:T(8,128)(2,1)S(1)}, bf16[2,256,128]{2,1,0:T(8,128)(2,1)S(1)}, u32[]{:S(2)}, u32[]{:S(2)}) %collective-permute-start.7) | collective-permute-done | bytes 131104 | tf_op jit(solution)/shard_map/ppermute | solution.py:37
  30.7 0.0 collective-permute-start.10
  30.7 1.4 %collective-permute-done.6.refs_1_ = bf16[2,256,128]{2,1,0:T(8,128)(2,1)S(1)} collective-permute-done((bf16[2,256,128]{2,1,0:T(8,128)(2,1)S(1)}, bf16[2,256,128]{2,1,0:T(8,128)(2,1)S(1)}, u32[]{:S(2)}, u32[]{:S(2)}) %collective-permute-start.6) | collective-permute-done | bytes 131104 | tf_op jit(solution)/shard_map/ppermute | solution.py:37
  32.0 0.0 collective-permute-start.9
  32.0 1.6 %collective-permute-done.5.refs_0_ = bf16[2,256,128]{2,1,0:T(8,128)(2,1)S(1)} collective-permute-done((bf16[2,256,128]{2,1,0:T(8,128)(2,1)S(1)}, bf16[2,256,128]{2,1,0:T(8,128)(2,1)S(1)}, u32[]{:S(2)}, u32[]{:S(2)}) %collective-permute-start.5) | collective-permute-done | bytes 131104 | tf_op jit(solution)/shard_map/ppermute | solution.py:37
  33.7 0.0 collective-permute-start.8
  33.7 0.0 collective-permute-done.11.refs_1_
  33.7 1.9 %shard_map.42.refs_6_ = f32[1216,640]{1,0:T(8,128)S(1)} custom-call(bf16[2,256,128]{2,1,0:T(8,128)(2,1)S(1)} %pad_maximum_fusion.refs_0_, bf16[2,256,128]{2,1,0:T(8,128)(2,1)S(1)} %collective-permute-done.11.refs_1_), custom_call_target="tpu_custom_call" | custom-call | flops 7969177600 | bytes 3112960 | tf_op jit(solution)/shard_map/pallas_call | solution.py:309
  35.6 0.0 collective-permute-done.10.refs_5_
  35.6 0.0 collective-permute-done.9.refs_4_
  35.6 0.0 collective-permute-done.8.refs_3_
  35.6 5.0 %shard_map.43 = (f32[1216,608]{1,0:T(8,128)}, f32[32,1216]{1,0:T(8,128)}) custom-call(bf16[2,256,128]{2,1,0:T(8,128)(2,1)S(1)} %collective-permute-done.5.refs_0_, bf16[2,256,128]{2,1,0:T(8,128)(2,1)S(1)} %collective-permute-done.6.refs_1_, bf16[2,256,128]{2,1,0:T(8,128)(2,1)S(1)} %collective-permute-done.7.refs_2_, ...), custom_call_target="tpu_custom_call" | custom-call | flops 23907532800 | bytes 3112960 | tf_op jit(solution)/shard_map/pallas_call | solution.py:309
  (13 shorter events, 0.2 us)
Async XLA Ops:
  7.1 6.5 %collective-permute-start = (f16[33,8,128]{2,1,0:T(8,128)(2,1)S(1)}, f16[33,8,128]{2,1,0:T(8,128)(2,1)S(1)}, u32[]{:S(2)}, u32[]{:S(2)}) collective-permute-start(f16[33,8,128]{2,1,0:T(8,128)(2,1)S(1)} %get-tuple-element.28), channel_id=1, source_target_pairs={{0,12},{1,13},{2,14},{3,15},{4,8},{5,9},{6,10},{7,11},{8,4},{9,5},... | collective-permute-start | bytes 202760 | tf_op jit(solution)/shard_map/ppermute | solution.py:37
  11.1 4.3 %collective-permute-start.1 = (f16[33,8,128]{2,1,0:T(8,128)(2,1)S(1)}, f16[33,8,128]{2,1,0:T(8,128)(2,1)S(1)}, u32[]{:S(2)}, u32[]{:S(2)}) collective-permute-start(f16[33,8,128]{2,1,0:T(8,128)(2,1)S(1)} %get-tuple-element.29), channel_id=1, source_target_pairs={{0,8},{1,9},{2,10},{3,11},{4,12},{5,13},{6,14},{7,15},{8,0},{9,1},... | collective-permute-start | bytes 202760 | tf_op jit(solution)/shard_map/ppermute | solution.py:37
  11.5 4.3 %collective-permute-start.2 = (f16[33,8,128]{2,1,0:T(8,128)(2,1)S(1)}, f16[33,8,128]{2,1,0:T(8,128)(2,1)S(1)}, u32[]{:S(2)}, u32[]{:S(2)}) collective-permute-start(f16[33,8,128]{2,1,0:T(8,128)(2,1)S(1)} %get-tuple-element.30), channel_id=1, source_target_pairs={{0,4},{1,5},{2,6},{3,7},{4,0},{5,1},{6,2},{7,3},{8,12},{9,13},{10,... | collective-permute-start | bytes 202760 | tf_op jit(solution)/shard_map/ppermute | solution.py:37
  15.9 5.3 %collective-permute-start.3 = (f16[33,8,128]{2,1,0:T(8,128)(2,1)S(1)}, f16[33,8,128]{2,1,0:T(8,128)(2,1)S(1)}, u32[]{:S(2)}, u32[]{:S(2)}) collective-permute-start(f16[33,8,128]{2,1,0:T(8,128)(2,1)S(1)} %get-tuple-element.22), channel_id=1, source_target_pairs={{0,16},{4,20},{8,24},{12,28},{16,0},{20,4},{24,8},{28,12},{1,17},{... | collective-permute-start | bytes 202760 | tf_op jit(solution)/shard_map/ppermute | solution.py:27
  21.3 4.3 %collective-permute-start.4 = (bf16[1,256,128]{2,1,0:T(8,128)(2,1)S(1)}, bf16[1,256,128]{2,1,0:T(8,128)(2,1)S(1)}, u32[]{:S(2)}, u32[]{:S(2)}) collective-permute-start(bf16[1,256,128]{2,1,0:T(8,128)(2,1)S(1)} %fusion.10), channel_id=1, source_target_pairs={{0,2},{1,3},{2,0},{3,1},{4,6},{5,7},{6,4},{7,5},{8,10},{9,11},{10,... | collective-permute-start | bytes 196616 | tf_op jit(solution)/shard_map/ppermute | solution.py:27
  25.6 5.0 %collective-permute-start.7 = (bf16[2,256,128]{2,1,0:T(8,128)(2,1)S(1)}, bf16[2,256,128]{2,1,0:T(8,128)(2,1)S(1)}, u32[]{:S(2)}, u32[]{:S(2)}) collective-permute-start(bf16[2,256,128]{2,1,0:T(8,128)(2,1)S(1)} %pad_maximum_fusion.refs_0_), channel_id=1, source_target_pairs={{0,4},{1,5},{2,6},{3,7},{4,0},{5,1},{6,2},{7,3},{8,12},{9,13},{10,... | collective-permute-start | bytes 393224 | tf_op jit(solution)/shard_map/ppermute | solution.py:37
  26.1 5.9 %collective-permute-start.6 = (bf16[2,256,128]{2,1,0:T(8,128)(2,1)S(1)}, bf16[2,256,128]{2,1,0:T(8,128)(2,1)S(1)}, u32[]{:S(2)}, u32[]{:S(2)}) collective-permute-start(bf16[2,256,128]{2,1,0:T(8,128)(2,1)S(1)} %pad_maximum_fusion.refs_0_), channel_id=1, source_target_pairs={{0,12},{1,13},{2,14},{3,15},{4,8},{5,9},{6,10},{7,11},{8,4},{9,5},... | collective-permute-start | bytes 393224 | tf_op jit(solution)/shard_map/ppermute | solution.py:37
  28.7 5.0 %collective-permute-start.5 = (bf16[2,256,128]{2,1,0:T(8,128)(2,1)S(1)}, bf16[2,256,128]{2,1,0:T(8,128)(2,1)S(1)}, u32[]{:S(2)}, u32[]{:S(2)}) collective-permute-start(bf16[2,256,128]{2,1,0:T(8,128)(2,1)S(1)} %pad_maximum_fusion.refs_0_), channel_id=1, source_target_pairs={{0,8},{1,9},{2,10},{3,11},{4,12},{5,13},{6,14},{7,15},{8,0},{9,1},... | collective-permute-start | bytes 393224 | tf_op jit(solution)/shard_map/ppermute | solution.py:37
  29.2 4.5 %collective-permute-start.11 = (bf16[2,256,128]{2,1,0:T(8,128)(2,1)S(1)}, bf16[2,256,128]{2,1,0:T(8,128)(2,1)S(1)}, u32[]{:S(2)}, u32[]{:S(2)}) collective-permute-start(bf16[2,256,128]{2,1,0:T(8,128)(2,1)S(1)} %pad_maximum_fusion.refs_0_), channel_id=1, source_target_pairs={{0,1},{1,0},{2,3},{3,2},{4,5},{5,4},{6,7},{7,6},{8,9},{9,8},{10,11... | collective-permute-start | bytes 393224 | tf_op jit(solution)/shard_map/ppermute | solution.py:27
  30.7 4.9 %collective-permute-start.10 = (bf16[2,256,128]{2,1,0:T(8,128)(2,1)S(1)}, bf16[2,256,128]{2,1,0:T(8,128)(2,1)S(1)}, u32[]{:S(2)}, u32[]{:S(2)}) collective-permute-start(bf16[2,256,128]{2,1,0:T(8,128)(2,1)S(1)} %collective-permute-done.7.refs_2_), channel_id=1, source_target_pairs={{0,1},{1,0},{2,3},{3,2},{4,5},{5,4},{6,7},{7,6},{8,9},{9,8},{10,11... | collective-permute-start | bytes 393224 | tf_op jit(solution)/shard_map/ppermute | solution.py:27
  32.0 3.5 %collective-permute-start.9 = (bf16[2,256,128]{2,1,0:T(8,128)(2,1)S(1)}, bf16[2,256,128]{2,1,0:T(8,128)(2,1)S(1)}, u32[]{:S(2)}, u32[]{:S(2)}) collective-permute-start(bf16[2,256,128]{2,1,0:T(8,128)(2,1)S(1)} %collective-permute-done.6.refs_1_), channel_id=1, source_target_pairs={{0,1},{1,0},{2,3},{3,2},{4,5},{5,4},{6,7},{7,6},{8,9},{9,8},{10,11... | collective-permute-start | bytes 393224 | tf_op jit(solution)/shard_map/ppermute | solution.py:27
  33.7 1.9 %collective-permute-start.8 = (bf16[2,256,128]{2,1,0:T(8,128)(2,1)S(1)}, bf16[2,256,128]{2,1,0:T(8,128)(2,1)S(1)}, u32[]{:S(2)}, u32[]{:S(2)}) collective-permute-start(bf16[2,256,128]{2,1,0:T(8,128)(2,1)S(1)} %collective-permute-done.5.refs_0_), channel_id=1, source_target_pairs={{0,1},{1,0},{2,3},{3,2},{4,5},{5,4},{6,7},{7,6},{8,9},{9,8},{10,11... | collective-permute-start | bytes 393224 | tf_op jit(solution)/shard_map/ppermute | solution.py:27
